TPU v7x, 128 devices: a whole 4x4x4 slice. The times are simulated.
128 devices in a mesh: row: 8 (over y, x_lo), col: 16 (over x_hi, z, core).
Axes of the slice: x: 4 (x_hi: 2, x_lo: 2; x = x_hi * 2 + x_lo), y: 4, z: 4, core: 2. Of those that a mesh axis runs over, the one named last changes fastest.
Arguments:
- vectors: float32 [32768, 128], P(('row', 'col')), may hold values from -6 to 6
- widths: int32 [256], P(('row', 'col')), may hold values from 64 to 128, as said below
- tiles: bfloat16 [8, 16, 256, 128, 128], P('row', 'col'), may hold values from -0.03125 to 0.03125
- block_rows: int32 [8, 16, 256], P('row', 'col'), may hold values from 0 to 31, as said below
- block_cols: int32 [8, 16, 256], P('row', 'col'), may hold values from 0 to 15
- block_count: int32 [8, 16], P('row', 'col'), may hold values from 64 to 256, as said below
Outputs:
- filtered: float32 [32768, 128], P(('row', 'col'))
Inputs may be any that keep to these rules, and one draw needn't show every extreme that they name: `widths`: every atom has a width from 64 to 128; both ends occur. `block_rows`: used slots of one tile name distinct blocks (a, b) of global atom row a and column b; a block is stored only where a <= b with a + b even, or a > b with a + b odd, so each mirror pair is stored at most once. `block_count`: some tile uses all 256 slots and some tile 256 // 4.
All inputs are finite; a program needn't handle non-finite values.
Results may differ from a plain program's by a relative error of at most 0.0042.
Values may be sent and summed in bfloat16 or wider, within the bound.
No kernel may reach another device: no remote copies, remote signals or barrier semaphores. Data moves between devices by JAX's collectives and lax.ppermute only.
A program may use at most 128 MiB of HBM per device.

v0:
```python
import jax
import jax.numpy as jnp
from jax import lax
from jax.sharding import PartitionSpec as P

center = 0.25


def local(vectors, widths, tiles, block_rows, block_cols, block_count):
    piece_rows, vector_count = vectors.shape
    atom_rows = tiles.shape[-1]
    slot_count = tiles.shape[2]
    rows_total = lax.axis_size("row")
    cols_total = lax.axis_size("col")
    ratio = cols_total // rows_total
    row_place = lax.axis_index("row")
    col_place = lax.axis_index("col")
    tile_set = tiles[0, 0]
    slot_rows = block_rows[0, 0]
    slot_cols = block_cols[0, 0]
    live_slots = (jnp.arange(slot_count) < block_count[0, 0]).astype(jnp.float32)[:, None, None]
    row_keep = (
        (jnp.arange(atom_rows)[None, :] < widths[:, None])
        .astype(jnp.float32)
        .reshape(piece_rows, 1)
    )
    row_atoms = cols_total * piece_rows // atom_rows
    col_atoms = rows_total * piece_rows // atom_rows

    def apply_matrix(current):
        rounded = current.astype(jnp.bfloat16)
        whole = lax.all_gather(rounded, ("row", "col"), axis=0, tiled=True)
        row_block = lax.dynamic_slice_in_dim(
            whole, row_place * cols_total * piece_rows, cols_total * piece_rows, 0
        )
        col_block = lax.dynamic_slice_in_dim(
            whole, col_place * rows_total * piece_rows, rows_total * piece_rows, 0
        )
        row_blocks = row_block.reshape(row_atoms, atom_rows, vector_count)
        col_blocks = col_block.reshape(col_atoms, atom_rows, vector_count)
        direct = (
            jnp.einsum(
                "sab,sbk->sak", tile_set, col_blocks[slot_cols], preferred_element_type=jnp.float32
            )
            * live_slots
        )
        mirror = (
            jnp.einsum(
                "sab,sak->sbk", tile_set, row_blocks[slot_rows], preferred_element_type=jnp.float32
            )
            * live_slots
        )
        direct_rows = jax.ops.segment_sum(direct, slot_rows, num_segments=row_atoms).reshape(
            row_atoms * atom_rows, vector_count
        )
        mirror_cols = jax.ops.segment_sum(mirror, slot_cols, num_segments=col_atoms).reshape(
            1, rows_total, piece_rows, vector_count
        )
        own_part = lax.psum_scatter(direct_rows, "col", scatter_dimension=0, tiled=True)
        target = (jnp.arange(ratio) == col_place % ratio).astype(jnp.float32)[:, None, None, None]
        sending = (mirror_cols * target).reshape(cols_total * piece_rows, vector_count)
        received = lax.all_to_all(sending, "col", split_axis=0, concat_axis=0, tiled=True)
        received = received.reshape(rows_total, ratio, piece_rows, vector_count)
        picked = lax.dynamic_index_in_dim(received, col_place // rows_total, 1, keepdims=False)
        picked = picked.reshape(rows_total * piece_rows, vector_count)
        other_part = lax.psum_scatter(picked, "row", scatter_dimension=0, tiled=True)
        return (own_part + other_part) * row_keep

    first = vectors * row_keep
    second = apply_matrix(first) - center * first
    third = apply_matrix(second)
    return 2.0 * (third - center * second) - first


def solution(mesh):
    return jax.shard_map(
        local,
        mesh=mesh,
        in_specs=(
            P(("row", "col"), None),
            P(("row", "col")),
            P("row", "col", None, None, None),
            P("row", "col", None),
            P("row", "col", None),
            P("row", "col"),
        ),
        out_specs=P(("row", "col"), None),
        check_vma=False,
    )
```

profile of v0, /device:TPU:25, one launch (start us, length us, event | category | flops | bytes accessed | tf_op | source)
XLA Modules:
  0.0 874.7 jit_solution(17649060559877223293)
XLA Ops:
  6.5 0.0 all-gather.3.cloned.1.call-start
  6.5 0.7 fusion.4
  7.3 1.6 multiply_convert_fusion
  8.9 0.0 all-gather.3.cloned.1.call-update
  8.9 0.0 reduce-scatter.5.cloned.1.call-start
  9.0 0.1 mul.134
  9.1 0.1 mul.135
  9.8 0.7 compare_select_fusion
  10.5 0.7 compare_select_fusion.1
  11.2 201.7 %all-gather.3.cloned.1.call-done = bf16[32768,128]{1,0:T(8,128)(2,1)} async-done(((bf16[256,128]{1,0:T(8,128)(2,1)}), bf16[32768,128]{1,0:T(8,128)(2,1)}) %all-gather.3.cloned.1.call-update) | async-done | bytes 8388624 | tf_op jit(solution)/shard_map/all_gather | solution.py:32
  212.9 1.1 constant_dynamic-slice_fusion.5
  214.0 8.6 gather_fusion
  222.6 13.0 %multiply_bitcast_fusion.3 = f32[256,128,128]{1,2,0:T(8,128)} fusion(bf16[256,128,128]{2,1,0:T(8,128)(2,1)} %gather_fusion, bf16[1,1,256,128,128]{4,3,2,1,0:T(8,128)(2,1)} %param.8, f32[256]{0:T(256)S(1)} %compare_convert_fusion.1), kind=kOutput, calls=%fused_computation.11 | convolution fusion | flops 1077936128 | bytes 33555456 | tf_op jit(solution)/shard_map/sab,sbk->sak/dot_general | solution.py:42
  235.6 17.5 %copy.12 = f32[256,128,128]{2,1,0:T(8,128)} copy(f32[256,128,128]{1,2,0:T(8,128)} %multiply_bitcast_fusion.3) | data formatting | bytes 33554432 | tf_op jit(solution)/shard_map/mul | solution.py:42
  253.0 0.2 broadcast.78.clone
  253.3 0.0 copy-done.5
  253.3 33.2 %scatter_fusion = f32[32,128,128]{2,1,0:T(8,128)S(1)} fusion(f32[32,128,128]{2,1,0:T(8,128)S(1)} %broadcast.78.clone, s32[256]{0:T(256)S(1)} %bitcast.61, f32[256,128,128]{2,1,0:T(8,128)} %copy.12), kind=kCustom, calls=%fused_computation.4 | custom fusion | flops 4194304 | bytes 50332672 | tf_op jit(solution)/shard_map/scatter-add | solution.py:53
  286.5 0.0 copy-start
  286.5 1.3 copy-done
  287.8 0.0 reduce-scatter.5.cloned.1.call-update
  287.9 1.3 constant_dynamic-slice_fusion.4
  289.2 8.7 gather_fusion.1
  297.9 15.9 %multiply_bitcast_fusion.2 = f32[256,128,128]{1,2,0:T(8,128)} fusion(bf16[256,128,128]{2,1,0:T(8,128)(2,1)} %gather_fusion.1, bf16[1,1,256,128,128]{4,3,2,1,0:T(8,128)(2,1)} %param.8, f32[256]{0:T(256)S(1)} %compare_convert_fusion.1), kind=kOutput, calls=%fused_computation.10 | convolution fusion | flops 1077936128 | bytes 33555456 | tf_op jit(solution)/shard_map/sab,sak->sbk/dot_general | solution.py:48
  313.7 17.5 %copy.14 = f32[256,128,128]{2,1,0:T(8,128)} copy(f32[256,128,128]{1,2,0:T(8,128)} %multiply_bitcast_fusion.2) | data formatting | bytes 33554432 | tf_op jit(solution)/shard_map/mul | solution.py:48
  331.3 0.1 broadcast.81.clone
  331.4 0.0 copy-done.6
  331.4 33.2 %scatter_fusion.1 = f32[16,128,128]{2,1,0:T(8,128)S(1)} fusion(f32[16,128,128]{2,1,0:T(8,128)S(1)} %broadcast.81.clone, s32[256]{0:T(256)S(1)} %bitcast.63, f32[256,128,128]{2,1,0:T(8,128)} %copy.14), kind=kCustom, calls=%fused_computation.5 | custom fusion | flops 4194304 | bytes 50332672 | tf_op jit(solution)/shard_map/scatter-add | solution.py:56
  364.6 0.0 copy-start.2
  364.6 1.6 bitcast_multiply_fusion.1
  366.3 5.9 all-to-all-start
  372.1 0.0 reduce-scatter.7.cloned.1.call-start
  372.2 28.4 %all-to-all-done = f32[16,256,128]{2,1,0:T(8,128)S(1)} async-done(((f32[16,256,128]{2,1,0:T(8,128)}), f32[16,256,128]{2,1,0:T(8,128)S(1)}, u32[]{:S(2)}, u32[]{:S(2)}) %all-to-all-start) | async-done | bytes 2097184 | tf_op jit(solution)/shard_map/all_to_all | solution.py:62
  400.6 1.0 constant_dynamic-slice_fusion.3
  401.7 0.0 reduce-scatter.7.cloned.1.call-update
  401.7 0.0 all-gather.5.cloned.1.call-start
  401.7 0.0 reduce-scatter.5.cloned.1.call-done
  401.8 35.6 %reduce-scatter.7.cloned.1.call-done = f32[256,128]{1,0:T(8,128)} async-done(((f32[2048,128]{1,0:T(8,128)}), f32[256,128]{1,0:T(8,128)}) %reduce-scatter.7.cloned.1.call-update) | async-done | bytes 131088 | tf_op jit(solution)/shard_map/reduce_scatter | solution.py:66
  437.4 0.0 copy-done.2
  437.4 1.7 fusion.5
  439.1 0.0 all-gather.5.cloned.1.call-update
  439.1 0.0 reduce-scatter.9.cloned.1.call-start
  439.2 207.3 %all-gather.5.cloned.1.call-done = bf16[32768,128]{1,0:T(8,128)(2,1)} async-done(((bf16[256,128]{1,0:T(8,128)(2,1)}), bf16[32768,128]{1,0:T(8,128)(2,1)}) %all-gather.5.cloned.1.call-update) | async-done | bytes 8388624 | tf_op jit(solution)/shard_map/all_gather | solution.py:32
  646.4 1.3 constant_dynamic-slice_fusion.1
  647.7 8.8 %gather_fusion.3 = bf16[256,128,128]{2,1,0:T(8,128)(2,1)} fusion(bf16[32,128,128]{2,1,0:T(8,128)(2,1)S(1)} %bitcast.55, s32[1024]{0:T(1024)S(1)} %pad_clamp_fusion), kind=kCustom, calls=%fused_computation.3 | custom fusion | bytes 16778240 | tf_op jit(solution)/shard_map/gather | solution.py:49
  656.6 1.1 constant_dynamic-slice_fusion.2
  657.6 8.6 gather_fusion.2
  666.2 13.0 %multiply_bitcast_fusion.1 = f32[256,128,128]{1,2,0:T(8,128)} fusion(bf16[256,128,128]{2,1,0:T(8,128)(2,1)} %gather_fusion.2, bf16[1,1,256,128,128]{4,3,2,1,0:T(8,128)(2,1)} %param.8, f32[256]{0:T(256)S(1)} %compare_convert_fusion.1), kind=kOutput, calls=%fused_computation.9 | convolution fusion | flops 1077936128 | bytes 33555456 | tf_op jit(solution)/shard_map/sab,sbk->sak/dot_general | solution.py:42
  679.2 17.5 %copy.16 = f32[256,128,128]{2,1,0:T(8,128)} copy(f32[256,128,128]{1,2,0:T(8,128)} %multiply_bitcast_fusion.1) | data formatting | bytes 33554432 | tf_op jit(solution)/shard_map/mul | solution.py:42
  696.7 0.2 broadcast.78
  696.9 33.2 %scatter_fusion.2 = f32[32,128,128]{2,1,0:T(8,128)S(1)} fusion(f32[32,128,128]{2,1,0:T(8,128)S(1)} %broadcast.78, s32[256]{0:T(256)S(1)} %bitcast.62, f32[256,128,128]{2,1,0:T(8,128)} %copy.16), kind=kCustom, calls=%fused_computation.6 | custom fusion | flops 4194304 | bytes 50332672 | tf_op jit(solution)/shard_map/scatter-add | solution.py:53
  730.2 1.3 copy-done.1
  731.5 0.0 reduce-scatter.9.cloned.1.call-update
  731.5 0.3 reduce-scatter.11.cloned.1.call-start
  731.8 15.7 %multiply_bitcast_fusion = f32[256,128,128]{1,2,0:T(8,128)} fusion(bf16[256,128,128]{2,1,0:T(8,128)(2,1)} %gather_fusion.3, bf16[1,1,256,128,128]{4,3,2,1,0:T(8,128)(2,1)} %param.8, f32[256]{0:T(256)S(1)} %compare_convert_fusion.1), kind=kOutput, calls=%fused_computation.8 | convolution fusion | flops 1077936128 | bytes 33555456 | tf_op jit(solution)/shard_map/sab,sak->sbk/dot_general | solution.py:48
  747.6 17.6 %copy.18 = f32[256,128,128]{2,1,0:T(8,128)} copy(f32[256,128,128]{1,2,0:T(8,128)} %multiply_bitcast_fusion) | data formatting | bytes 33554432 | tf_op jit(solution)/shard_map/mul | solution.py:48
  765.2 0.1 broadcast.81
  765.3 33.2 %scatter_fusion.3 = f32[16,128,128]{2,1,0:T(8,128)S(1)} fusion(f32[16,128,128]{2,1,0:T(8,128)S(1)} %broadcast.81, s32[256]{0:T(256)S(1)} %bitcast.64, f32[256,128,128]{2,1,0:T(8,128)} %copy.18), kind=kCustom, calls=%fused_computation.7 | custom fusion | flops 4194304 | bytes 50332672 | tf_op jit(solution)/shard_map/scatter-add | solution.py:56
  798.5 0.3 bitcast_multiply_fusion
  798.8 33.8 %all_to_all.12 = f32[16,256,128]{2,1,0:T(8,128)S(1)} all-to-all(f32[16,256,128]{2,1,0:T(8,128)S(1)} %bitcast_multiply_fusion), channel_id=1, replica_groups=mesh['row'=8,'col'=16] {'col'}, dimensions={0} | all-to-all | bytes 4194304 | tf_op jit(solution)/shard_map/all_to_all | solution.py:62
  832.6 1.0 constant_dynamic-slice_fusion
  833.7 0.0 reduce-scatter.11.cloned.1.call-update
  833.7 0.0 reduce-scatter.9.cloned.1.call-done
  833.7 32.4 %reduce-scatter.11.cloned.1.call-done = f32[256,128]{1,0:T(8,128)} async-done(((f32[2048,128]{1,0:T(8,128)}), f32[256,128]{1,0:T(8,128)}) %reduce-scatter.11.cloned.1.call-update) | async-done | bytes 131088 | tf_op jit(solution)/shard_map/reduce_scatter | solution.py:66
  866.1 1.7 multiply_subtract_fusion
  (11 shorter events, 0.0 us)
Async XLA Ops:
  6.5 206.3 %all-gather.3.cloned.1.call-start = ((), (), s32[]{:S(2)}) async-start(), calls=%async_computation.6 | async-start | bytes 8454144 | tf_op jit(solution)/shard_map/all_gather | solution.py:32
  8.9 392.8 %reduce-scatter.5.cloned.1.call-start = ((), (), s32[]{:S(2)}) async-start(), calls=%async_computation.7 | async-start | bytes 2228224 | tf_op jit(solution)/shard_map/reduce_scatter | solution.py:59
  235.6 17.7 %copy-start.5 = (s32[1,1,256]{2,1,0:T(1,128)S(1)}, s32[1,1,256]{2,1,0:T(1,128)}, u32[]{:S(2)}) copy-start(s32[1,1,256]{2,1,0:T(1,128)} %param.9) | copy-start | bytes 3076
  286.5 1.3 copy-start
  313.7 17.7 %copy-start.6 = (s32[1,1,256]{2,1,0:T(1,128)S(1)}, s32[1,1,256]{2,1,0:T(1,128)}, u32[]{:S(2)}) copy-start(s32[1,1,256]{2,1,0:T(1,128)} %param.10) | copy-start | bytes 3076
  364.6 72.8 %copy-start.2 = (f32[256,128]{1,0:T(8,128)S(1)}, f32[256,128]{1,0:T(8,128)}, u32[]{:S(2)}) copy-start(f32[256,128]{1,0:T(8,128)} %param.6) | copy-start | bytes 393220
  366.3 34.3 %all-to-all-start = ((f32[16,256,128]{2,1,0:T(8,128)}), f32[16,256,128]{2,1,0:T(8,128)S(1)}, u32[]{:S(2)}, u32[]{:S(2)}) async-start(f32[16,256,128]{2,1,0:T(8,128)} %bitcast_multiply_fusion.1), calls=%async_computation.1 | async-start | bytes 4194304 | tf_op jit(solution)/shard_map/all_to_all | solution.py:62
  372.1 65.2 %reduce-scatter.7.cloned.1.call-start = ((), (), s32[]{:S(2)}) async-start(), calls=%async_computation.8 | async-start | bytes 1179648 | tf_op jit(solution)/shard_map/reduce_scatter | solution.py:66
  401.7 244.8 %all-gather.5.cloned.1.call-start = ((), (), s32[]{:S(2)}) async-start(), calls=%async_computation.9 | async-start | bytes 8454144 | tf_op jit(solution)/shard_map/all_gather | solution.py:32
  439.1 394.6 %reduce-scatter.9.cloned.1.call-start = ((), (), s32[]{:S(2)}) async-start(), calls=%async_computation.10 | async-start | bytes 2228224 | tf_op jit(solution)/shard_map/reduce_scatter | solution.py:59
  730.2 1.3 copy-start.1
  731.5 134.6 %reduce-scatter.11.cloned.1.call-start = ((), (), s32[]{:S(2)}) async-start(), calls=%async_computation.11 | async-start | bytes 1179648 | tf_op jit(solution)/shard_map/reduce_scatter | solution.py:66
  798.5 67.6 %copy-start.3 = (f32[256,128]{1,0:T(8,128)S(1)}, f32[256,128]{1,0:T(8,128)}, u32[]{:S(2)}) copy-start(f32[256,128]{1,0:T(8,128)} %reduce-scatter.5.cloned.1.call-done) | copy-start | bytes 393220
  798.5 67.6 %copy-start.4 = (f32[256,128]{1,0:T(8,128)S(1)}, f32[256,128]{1,0:T(8,128)}, u32[]{:S(2)}) copy-start(f32[256,128]{1,0:T(8,128)} %reduce-scatter.7.cloned.1.call-done) | copy-start | bytes 393220
Sparse Core Ops, SparseCore 0:
  9.1 203.7 all-gather.2
  288.0 69.1 reduce-scatter.4
  401.8 35.5 reduce-scatter.6
  439.2 207.1 all-gather.4
  731.6 69.1 reduce-scatter.8
  833.8 32.2 reduce-scatter.10
where the time goes:
time: 886 us; the launch traced here: 875 us
  waiting for transfers between devices  506 us (57%)
  other arithmetic  142 us (16%)
  local copies, waits for them, and re-layouts  115 us (13%)
  matrix products  57.6 us (7%)
  blocking collectives  33.8 us (4%)
  between operations  14.3 us (2%)
    all_gather x2, waiting for transfers between devices, apply_matrix(): whole = lax.all_gather(rounded, ('row', 'col'), axis=0, tiled=True)  409 us
    reduce_scatter x2, waiting for transfers between devices, apply_matrix(): lax.psum_scatter(picked, 'row', scatter_dimension=0, tiled=True)  68 us
    scatter-add x2, other arithmetic, apply_matrix(): jax.ops.segment_sum(mirror, slot_cols, num_segments=col_atoms)  66.5 us
    scatter-add x2, other arithmetic, apply_matrix(): jax.ops.segment_sum(direct, slot_rows, num_segments=row_atoms)  66.4 us
    mul x2, local copies, waits for them, and re-layouts, apply_matrix(): jnp.einsum('sab,sak->sbk', tile_set, row_blocks[slot_rows], preferred_ele...  35.1 us
    mul x2, local copies, waits for them, and re-layouts, apply_matrix(): jnp.einsum('sab,sbk->sak', tile_set, col_blocks[slot_cols], preferred_ele...  34.9 us
    all_to_all x1, blocking collectives, apply_matrix(): lax.all_to_all(sending, 'col', split_axis=0, concat_axis=0, tiled=True)  33.8 us
    dot_general x2, matrix products, apply_matrix(): jnp.einsum('sab,sak->sbk', tile_set, row_blocks[slot_rows], preferred_ele...  31.6 us
  transfers between devices with their start and end apart: 7, of which 5 were waited for; matrix products, arithmetic and copies ran while one was open for 17% of the time, Pallas kernels for 0%

commit v1 on v0

v1 whole, which is shorter than its diff:
```python
import functools

import jax
import jax.numpy as jnp
from jax import lax
from jax.experimental import pallas as pl
from jax.experimental.pallas import tpu as pltpu
from jax.sharding import Mesh
from jax.sharding import PartitionSpec as P

CENTER = 0.25
ATOM = 128
VECS = 128
AR = 32
AC = 16
SLOTS = 256
N_ROW = 8
N_COL = 16
BF = jnp.bfloat16
F32 = jnp.float32
ROWS = ("y", "xl")
COLS = ("xh", "z", "co")
ALL = ROWS + COLS
D_LEN = 9
M_LEN = 17


def tables(slot_rows, slot_cols, count, row, col):
    place = jnp.where(jnp.arange(SLOTS) < count, slot_rows * AC + slot_cols, -1)

    def pack(rows, cols, index, zero):
        want = (rows * AC + cols).reshape(-1, 1)
        entry = jnp.arange(SLOTS)[None, :] * 64 + index.reshape(-1, 1) - zero
        return zero + jnp.sum(jnp.where(place[None, :] == want, entry, 0), axis=1)

    a = jnp.arange(AR)[:, None]
    q = jnp.arange(D_LEN)[None, :]
    ga = row * AR + a
    gb = col * AC + 2 * q
    odd = ga % 2 == 1
    main = 2 * q + jnp.where(odd, ga <= gb + 1, ga > gb).astype(jnp.int32)
    extra = ga - 1 - col * AC
    extra = jnp.where(odd & (extra >= 0) & (extra < AC), extra, -AC * AR)
    b = jnp.where(q < 8, main, extra)
    direct = pack(a + 0 * b, b, b, AC)

    b = jnp.arange(AC)[:, None]
    q = jnp.arange(M_LEN)[None, :]
    gb = col * AC + b
    ga = row * AR + 2 * q
    odd = gb % 2 == 1
    main = 2 * q + jnp.where(odd, ga + 1 <= gb, ga > gb).astype(jnp.int32)
    extra = gb + 1 - row * AR
    extra = jnp.where((~odd) & (extra >= 0) & (extra < AR), extra, -AR)
    a = jnp.where(q < 16, main, extra)
    mirror = pack(a, b + 0 * a, a, AR)
    return direct, mirror


def direct_kernel(tab, core, x_ref, t_ref, mine_ref, other_ref, held):
    held[:AC] = x_ref[...].reshape(AC, ATOM, VECS)
    held[AC] = jnp.zeros((ATOM, VECS), BF)
    co = core[0]

    def product(a, q, n):
        blocks, xs = [], []
        for k in range(n):
            e = tab[a * D_LEN + q + k]
            blocks.append(t_ref[lax.shift_right_logical(e, 6)])
            xs.append(held[jnp.bitwise_and(e, 63)])
        if n == 1:
            left, right = blocks[0], xs[0]
        else:
            left, right = jnp.concatenate(blocks, 1), jnp.concatenate(xs, 0)
        return jnp.dot(left, right, preferred_element_type=F32)

    def step(xz, carry):
        for which, out in ((0, mine_ref), (1, other_ref)):
            for t in range(2):
                a = 4 * xz + 2 * (co if which == 0 else 1 - co) + t
                total = product(a, 0, 8)
                if t:
                    total = total + product(a, 8, 1)
                out[xz, t * ATOM:(t + 1) * ATOM, :] = total.astype(out.dtype)
        return carry

    lax.fori_loop(0, 8, step, 0)


def mirror_kernel(tab, x_ref, y_ref, core, t_ref, out_ref, held):
    co = core[0]
    for xz in range(8):
        held[pl.ds(4 * xz + 2 * co, 2)] = x_ref[xz]
        held[pl.ds(4 * xz + 2 - 2 * co, 2)] = y_ref[xz]
    held[AR] = jnp.zeros((VECS, ATOM), BF)

    def product(b, q, n):
        blocks, xs = [], []
        for k in range(n):
            e = tab[b * M_LEN + q + k]
            blocks.append(t_ref[lax.shift_right_logical(e, 6)])
            xs.append(held[jnp.bitwise_and(e, 63)])
        if n == 1:
            left, right = xs[0], blocks[0]
        else:
            left, right = jnp.concatenate(xs, 1), jnp.concatenate(blocks, 0)
        return jnp.dot(left, right, preferred_element_type=F32)

    def step(k, carry):
        for t in range(2):
            b = 2 * k + t
            total = product(b, 0, 8) + product(b, 8, 8)
            if not t:
                total = total + product(b, 16, 1)
            out_ref[k, t] = total.astype(out_ref.dtype)
        return carry

    lax.fori_loop(0, 8, step, 0)


SMEM = pl.BlockSpec(memory_space=pltpu.SMEM)
VMEM = pl.BlockSpec(memory_space=pltpu.VMEM)
PARAMS = pltpu.CompilerParams(vmem_limit_bytes=32 * 1024 * 1024)


def direct_call(tab, core, x, tiles):
    return pl.pallas_call(
        direct_kernel,
        out_shape=(
            jax.ShapeDtypeStruct((8, 2 * ATOM, VECS), F32),
            jax.ShapeDtypeStruct((8, 2 * ATOM, VECS), BF),
        ),
        in_specs=[SMEM, SMEM, VMEM, VMEM],
        out_specs=(VMEM, VMEM),
        scratch_shapes=[pltpu.VMEM((AC + 1, ATOM, VECS), BF)],
        compiler_params=PARAMS,
        cost_estimate=pl.CostEstimate(
            flops=2 * SLOTS * ATOM**3, bytes_accessed=2**23, transcendentals=0
        ),
        name="direct",
    )(tab, core, x, tiles)


def mirror_call(tab, core, x, y, tiles):
    return pl.pallas_call(
        mirror_kernel,
        out_shape=jax.ShapeDtypeStruct((8, 2, VECS, ATOM), BF),
        in_specs=[SMEM, VMEM, VMEM, SMEM, VMEM],
        out_specs=VMEM,
        scratch_shapes=[pltpu.VMEM((AR + 1, VECS, ATOM), BF)],
        compiler_params=PARAMS,
        cost_estimate=pl.CostEstimate(
            flops=2 * SLOTS * ATOM**3, bytes_accessed=2**23, transcendentals=0
        ),
        name="mirror",
    )(tab, x, y, core, tiles)


TO_COL = [(r * 16 + c, (c % 8) * 16 + 2 * r + c // 8) for r in range(8) for c in range(16)]
TO_ROW = [(d, s) for s, d in TO_COL]
SWAP = [(0, 1), (1, 0)]


def local(vectors, widths, tiles, block_rows, block_cols, block_count):
    row = lax.axis_index(ROWS)
    col = lax.axis_index(COLS)
    core = lax.axis_index("co").astype(jnp.int32).reshape(1)
    tile_set = tiles[0, 0]
    direct_tab, mirror_tab = tables(
        block_rows[0, 0], block_cols[0, 0], block_count[0, 0], row, col
    )
    keep = (jnp.arange(ATOM)[None, :] < widths[:, None]).astype(F32).reshape(2 * ATOM, 1)

    def flip(x):
        return x.reshape(2, ATOM, VECS).swapaxes(1, 2)

    def copies(x):
        return jnp.broadcast_to(x[None], (8, *x.shape))

    def exchange(x, axes):
        return lax.all_to_all(x, axes, split_axis=0, concat_axis=0, tiled=True)

    def apply_matrix(current):
        rounded = current.astype(BF)
        piece = lax.ppermute(rounded, ALL, TO_COL)
        near = exchange(copies(flip(rounded)), ("xh", "z"))
        far = lax.ppermute(near, "co", SWAP)
        piece, near = lax.optimization_barrier((piece, near))
        col_block = exchange(copies(piece), ROWS)
        mirror = mirror_call(mirror_tab, core, near, far, tile_set)
        mine, other = direct_call(direct_tab, core, col_block, tile_set)
        theirs = lax.ppermute(other, "co", SWAP)
        got = exchange(mirror, ROWS)
        got = flip(jnp.sum(got.astype(F32), axis=0)).reshape(2 * ATOM, VECS)
        back = lax.ppermute(got.astype(BF), ALL, TO_ROW)
        both = (mine + theirs.astype(F32)).astype(BF)
        own = jnp.sum(exchange(both, ("xh", "z")).astype(F32), axis=0)
        return (own + back.astype(F32)) * keep

    first = vectors * keep
    second = apply_matrix(first) - CENTER * first
    third = apply_matrix(second)
    return 2.0 * (third - CENTER * second) - first


def solution(mesh):
    split = Mesh(mesh.devices.reshape(4, 2, 2, 4, 2), ALL)
    return jax.shard_map(
        local,
        mesh=split,
        in_specs=(
            P(ALL, None),
            P(ALL),
            P(ROWS, COLS, None, None, None),
            P(ROWS, COLS, None),
            P(ROWS, COLS, None),
            P(ROWS, COLS),
        ),
        out_specs=P(ALL, None),
        check_vma=False,
    )
```

time: 886 us -> 171 us (0.19); the launches traced: 875 us -> 170 us
  waiting for transfers between devices: 506 us -> 43.4 us
  other arithmetic: 142 us -> 8.25 us
  local copies, waits for them, and re-layouts: 115 us -> 14.7 us
  starting transfers between devices: 6.33 us -> 84.1 us
  matrix products: 57.6 us -> 0 us
  blocking collectives: 33.8 us -> 0 us
  Pallas kernels: 0 us -> 18.5 us
  between operations: 14.3 us -> 0.96 us
    all_gather x2 -> x0, waiting for transfers between devices: 409 us -> none  [apply_matrix(): whole = lax.all_gather(rounded, ('row', 'col'), axis=0, tiled=True)]
    scatter-add x4 -> x0, other arithmetic: 133 us -> none  [the longest x2 66.5 us: apply_matrix(): jax.ops.segment_sum(mirror, slot_cols, num_segments=col_atoms)]
    mul x6 -> x0, local copies, waits for them, and re-layouts: 70.2 us -> none  [the longest x2 35.1 us: apply_matrix(): jnp.einsum('sab,sak->sbk', tile_set, row_blocks[slot_rows], preferred_ele...]
    reduce_scatter x4 -> x0, waiting for transfers between devices: 68 us -> none  [the longest x2 68 us: apply_matrix(): lax.psum_scatter(picked, 'row', scatter_dimension=0, tiled=True)]
    dot_general x4 -> x0, matrix products: 57.6 us -> none  [the longest x2 31.6 us: apply_matrix(): jnp.einsum('sab,sak->sbk', tile_set, row_blocks[slot_rows], preferred_ele...]
    ppermute x0 -> x8, starting transfers between devices: none -> 46.1 us  [the longest x2 20.2 us: apply_matrix(): back = lax.ppermute(got.astype(BF), ALL, TO_ROW)]
    gather x4 -> x0, local copies, waits for them, and re-layouts: 34.7 us -> none  [the longest x2 17.5 us: apply_matrix(): row_blocks[slot_rows]]
    all_to_all x1 -> x0, blocking collectives: 33.8 us -> none  [apply_matrix(): lax.all_to_all(sending, 'col', split_axis=0, concat_axis=0, tiled=True)]
  transfers between devices with their start and end apart: 7 -> 16, of which waited for: 5 -> 8; matrix products, arithmetic and copies ran while one was open for 17% -> 4% of each run, Pallas kernels for 0% -> 11%
where the time goes in v1:
time: 171 us; the launch traced here: 170 us
  starting transfers between devices  84.1 us (49%)
  waiting for transfers between devices  43.4 us (25%)
  Pallas kernels  18.5 us (11%)
  local copies, waits for them, and re-layouts  14.7 us (9%)
  other arithmetic  8.25 us (5%)
    all_to_all x8, starting transfers between devices, exchange(): return lax.all_to_all(x, axes, split_axis=0, concat_axis=0, tiled=True)  38 us
    all_to_all x8, waiting for transfers between devices, exchange(): return lax.all_to_all(x, axes, split_axis=0, concat_axis=0, tiled=True)  29.5 us
    ppermute x2, starting transfers between devices, apply_matrix(): back = lax.ppermute(got.astype(BF), ALL, TO_ROW)  20.2 us
    ppermute x2, starting transfers between devices, apply_matrix(): piece = lax.ppermute(rounded, ALL, TO_COL)  17.9 us
    unnamed x10, local copies, waits for them, and re-layouts  10.2 us
    ppermute x2, waiting for transfers between devices, apply_matrix(): back = lax.ppermute(got.astype(BF), ALL, TO_ROW)  10.1 us
    pallas_call x2, Pallas kernels, mirror_call(): pl.pallas_call(mirror_kernel, out_shape=jax.ShapeDtypeStruct((8, 2, VECS,...  10.1 us
    pallas_call x2, Pallas kernels, direct_call(): pl.pallas_call(direct_kernel, out_shape=(jax.ShapeDtypeStruct((8, 2 * ATO...  8.44 us
  transfers between devices with their start and end apart: 16, of which 8 were waited for; matrix products, arithmetic and copies ran while one was open for 4% of the time, Pallas kernels for 11%

profile of v1, /device:TPU:25, one launch (start us, length us, event | category | flops | bytes accessed | tf_op | source)
XLA Modules:
  0.0 169.8 jit_solution(12230321306287754180)
XLA Ops:
  0.0 0.7 fusion.1
  0.7 1.0 multiply_convert_fusion
  1.7 7.9 %collective-permute-start = (bf16[256,128]{1,0:T(8,128)(2,1)S(1)}, bf16[256,128]{1,0:T(8,128)(2,1)S(1)}, u32[]{:S(2)}, u32[]{:S(2)}) collective-permute-start(bf16[256,128]{1,0:T(8,128)(2,1)S(1)} %multiply_convert_fusion), channel_id=1, source_target_pairs={{0,0},{1,16},{2,32},{3,48},{4,64},{5,80},{6,96},{7,112},{8,1},{9,1... | collective-permute-start | bytes 196616 | tf_op jit(solution)/shard_map/ppermute | solution.py:185
  9.7 0.1 copy.17
  9.8 0.9 broadcast_in_dim.118
  10.7 3.5 %all-to-all-start = ((bf16[8,2,128,128]{3,2,1,0:T(8,128)(2,1)}), bf16[8,2,128,128]{3,2,1,0:T(8,128)(2,1)S(1)}, u32[]{:S(2)}, u32[]{:S(2)}) async-start(bf16[8,2,128,128]{3,2,1,0:T(8,128)(2,1)} %broadcast_in_dim.118), calls=%async_computation | async-start | bytes 1048576 | tf_op jit(solution)/shard_map/all_to_all | solution.py:181
  15.0 0.7 multiply_add_fusion.1
  15.7 0.1 add_select_fusion
  15.8 0.1 reshape.393
  15.9 0.1 add_select_fusion.1
  16.0 0.1 add.257
  16.1 0.1 add.258
  16.2 7.5 %all-to-all-done.x_ref = bf16[8,2,128,128]{3,2,1,0:T(8,128)(2,1)S(1)} async-done(((bf16[8,2,128,128]{3,2,1,0:T(8,128)(2,1)}), bf16[8,2,128,128]{3,2,1,0:T(8,128)(2,1)S(1)}, u32[]{:S(2)}, u32[]{:S(2)}) %all-to-all-start) | async-done | bytes 524320 | tf_op jit(solution)/shard_map/all_to_all | solution.py:181
  23.7 0.9 broadcast_in_dim.119
  24.6 5.3 %all-to-all-start.1 = ((bf16[8,256,128]{2,1,0:T(8,128)(2,1)}), bf16[8,256,128]{2,1,0:T(8,128)(2,1)S(1)}, u32[]{:S(2)}, u32[]{:S(2)}) async-start(bf16[8,256,128]{2,1,0:T(8,128)(2,1)} %broadcast_in_dim.119), calls=%async_computation.1 | async-start | bytes 1048576 | tf_op jit(solution)/shard_map/all_to_all | solution.py:181
  29.9 0.2 select_reduce_fusion
  30.2 0.1 reshape.395
  30.3 0.1 add.289
  30.4 1.6 collective-permute-start.2
  32.0 4.7 %all-to-all-done.1.x_ref = bf16[8,256,128]{2,1,0:T(8,128)(2,1)S(1)} async-done(((bf16[8,256,128]{2,1,0:T(8,128)(2,1)}), bf16[8,256,128]{2,1,0:T(8,128)(2,1)S(1)}, u32[]{:S(2)}, u32[]{:S(2)}) %all-to-all-start.1) | async-done | bytes 524320 | tf_op jit(solution)/shard_map/all_to_all | solution.py:181
  36.7 3.4 %copy-done = bf16[1,1,256,128,128]{4,3,2,1,0:T(8,128)(2,1)S(1)} copy-done((bf16[1,1,256,128,128]{4,3,2,1,0:T(8,128)(2,1)S(1)}, bf16[1,1,256,128,128]{4,3,2,1,0:T(8,128)(2,1)}, u32[]{:S(2)}) %copy-start) | copy-done | bytes 8388632
  40.1 4.2 %direct.2 = (f32[8,256,128]{2,1,0:T(8,128)S(1)}, bf16[8,256,128]{2,1,0:T(8,128)(2,1)S(1)}) custom-call(s32[288]{0:T(512)S(1)} %broadcast_add_fusion.1.tab, s32[1]{0:T(128)} %bitcast.2.core, bf16[8,256,128]{2,1,0:T(8,128)(2,1)S(1)} %all-to-all-done.1.x_ref, bf16[256,128,128]{2,1,0:T(8,128)(2,1)S(1)} %bitcast.15), custom_call_target="tpu_custom_call" | custom-call | flops 1073741824 | bytes 8388608 | tf_op jit(solution)/shard_map/direct/pallas_call | solution.py:127
  44.3 0.0 copy-start.4
  44.3 2.3 %collective-permute-start.1 = (bf16[8,256,128]{2,1,0:T(8,128)(2,1)S(1)}, bf16[8,256,128]{2,1,0:T(8,128)(2,1)}, u32[]{:S(2)}, u32[]{:S(2)}) collective-permute-start(bf16[8,256,128]{2,1,0:T(8,128)(2,1)S(1)} %get-tuple-element.15), channel_id=1, source_target_pairs={{0,1},{1,0},{2,3},{3,2},{4,5},{5,4},{6,7},{7,6},{8,9},{9,8},{10,11... | collective-permute-start | bytes 1572872 | tf_op jit(solution)/shard_map/ppermute | solution.py:192
  46.6 0.2 select_reduce_fusion.1
  46.9 5.0 %mirror.2 = bf16[8,2,128,128]{3,2,1,0:T(8,128)(2,1)} custom-call(s32[272]{0:T(512)S(1)} %broadcast_add_fusion.tab, bf16[8,2,128,128]{3,2,1,0:T(8,128)(2,1)S(1)} %all-to-all-done.x_ref, bf16[8,2,128,128]{3,2,1,0:T(8,128)(2,1)S(1)} %collective-permute-done.2.y_ref, s32[1]{0:T(128)} %bitcast.2.core, bf16[256,128,128]{2,1,0:T(8,128)(2,1)S(1)} %bitcast.16), custom_call_target="tpu_custom_call" | custom-call | flops 1073741824 | bytes 8388608 | tf_op jit(solution)/shard_map/mirror/pallas_call | solution.py:145
  51.9 5.5 %all-to-all-start.3 = ((bf16[8,2,128,128]{3,2,1,0:T(8,128)(2,1)}), bf16[8,2,128,128]{3,2,1,0:T(8,128)(2,1)S(1)}, u32[]{:S(2)}, u32[]{:S(2)}) async-start(bf16[8,2,128,128]{3,2,1,0:T(8,128)(2,1)} %mirror.2), calls=%async_computation.3 | async-start | bytes 1048576 | tf_op jit(solution)/shard_map/all_to_all | solution.py:181
  57.4 0.0 collective-permute-done.1
  57.4 1.9 %add_convert_fusion.1 = bf16[8,256,128]{2,1,0:T(8,128)(2,1)} fusion(f32[8,256,128]{2,1,0:T(8,128)S(1)} %get-tuple-element.14, bf16[8,256,128]{2,1,0:T(8,128)(2,1)} %collective-permute-done.1), kind=kLoop, calls=%fused_computation.3 | loop fusion | flops 786432 | bytes 2097152 | tf_op jit(solution)/shard_map/convert_element_type | solution.py:196
  59.4 6.2 %all-to-all-done.3 = bf16[8,2,128,128]{3,2,1,0:T(8,128)(2,1)S(1)} async-done(((bf16[8,2,128,128]{3,2,1,0:T(8,128)(2,1)}), bf16[8,2,128,128]{3,2,1,0:T(8,128)(2,1)S(1)}, u32[]{:S(2)}, u32[]{:S(2)}) %all-to-all-start.3) | async-done | bytes 524320 | tf_op jit(solution)/shard_map/all_to_all | solution.py:181
  65.6 4.5 %all-to-all-start.2 = ((bf16[8,256,128]{2,1,0:T(8,128)(2,1)}), bf16[8,256,128]{2,1,0:T(8,128)(2,1)S(1)}, u32[]{:S(2)}, u32[]{:S(2)}) async-start(bf16[8,256,128]{2,1,0:T(8,128)(2,1)} %add_convert_fusion.1), calls=%async_computation.2 | async-start | bytes 1048576 | tf_op jit(solution)/shard_map/all_to_all | solution.py:181
  70.0 0.1 reduce_sum.63
  70.1 0.1 copy.18
  70.2 10.1 %collective-permute-start.3 = (bf16[256,128]{1,0:T(8,128)(2,1)S(1)}, bf16[256,128]{1,0:T(8,128)(2,1)S(1)}, u32[]{:S(2)}, u32[]{:S(2)}) collective-permute-start(bf16[256,128]{1,0:T(8,128)(2,1)S(1)} %bitcast.25), channel_id=1, source_target_pairs={{0,0},{16,1},{32,2},{48,3},{64,4},{80,5},{96,6},{112,7},{1,8},{17,... | collective-permute-start | bytes 196616 | tf_op jit(solution)/shard_map/ppermute | solution.py:195
  80.3 0.0 all-to-all-done.2
  80.4 0.1 convert_reduce_fusion.1
  80.4 5.1 %collective-permute-done.3 = bf16[256,128]{1,0:T(8,128)(2,1)S(1)} collective-permute-done((bf16[256,128]{1,0:T(8,128)(2,1)S(1)}, bf16[256,128]{1,0:T(8,128)(2,1)S(1)}, u32[]{:S(2)}, u32[]{:S(2)}) %collective-permute-start.3) | collective-permute-done | bytes 65568 | tf_op jit(solution)/shard_map/ppermute | solution.py:195
  85.5 0.1 fusion
  85.6 0.1 copy.19
  85.8 0.9 broadcast_in_dim.127
  86.7 3.5 %all-to-all-start.4 = ((bf16[8,2,128,128]{3,2,1,0:T(8,128)(2,1)}), bf16[8,2,128,128]{3,2,1,0:T(8,128)(2,1)S(1)}, u32[]{:S(2)}, u32[]{:S(2)}) async-start(bf16[8,2,128,128]{3,2,1,0:T(8,128)(2,1)} %broadcast_in_dim.127), calls=%async_computation.4 | async-start | bytes 1048576 | tf_op jit(solution)/shard_map/all_to_all | solution.py:181
  90.2 10.0 %collective-permute-start.4 = (bf16[256,128]{1,0:T(8,128)(2,1)S(1)}, bf16[256,128]{1,0:T(8,128)(2,1)S(1)}, u32[]{:S(2)}, u32[]{:S(2)}) collective-permute-start(bf16[256,128]{1,0:T(8,128)(2,1)S(1)} %fusion), channel_id=1, source_target_pairs={{0,0},{1,16},{2,32},{3,48},{4,64},{5,80},{6,96},{7,112},{8,1},{9,1... | collective-permute-start | bytes 196616 | tf_op jit(solution)/shard_map/ppermute | solution.py:185
  100.2 3.7 %collective-permute-done.4 = bf16[256,128]{1,0:T(8,128)(2,1)S(1)} collective-permute-done((bf16[256,128]{1,0:T(8,128)(2,1)S(1)}, bf16[256,128]{1,0:T(8,128)(2,1)S(1)}, u32[]{:S(2)}, u32[]{:S(2)}) %collective-permute-start.4) | collective-permute-done | bytes 65568 | tf_op jit(solution)/shard_map/ppermute | solution.py:185
  103.9 0.0 all-to-all-done.4.x_ref
  103.9 0.9 broadcast_in_dim.128
  104.7 4.7 %all-to-all-start.5 = ((bf16[8,256,128]{2,1,0:T(8,128)(2,1)}), bf16[8,256,128]{2,1,0:T(8,128)(2,1)S(1)}, u32[]{:S(2)}, u32[]{:S(2)}) async-start(bf16[8,256,128]{2,1,0:T(8,128)(2,1)} %broadcast_in_dim.128), calls=%async_computation.5 | async-start | bytes 1048576 | tf_op jit(solution)/shard_map/all_to_all | solution.py:181
  109.4 1.7 collective-permute-start.6
  111.1 5.0 %all-to-all-done.5.x_ref = bf16[8,256,128]{2,1,0:T(8,128)(2,1)S(1)} async-done(((bf16[8,256,128]{2,1,0:T(8,128)(2,1)}), bf16[8,256,128]{2,1,0:T(8,128)(2,1)S(1)}, u32[]{:S(2)}, u32[]{:S(2)}) %all-to-all-start.5) | async-done | bytes 524320 | tf_op jit(solution)/shard_map/all_to_all | solution.py:181
  116.0 3.4 %copy-done.2 = bf16[1,1,256,128,128]{4,3,2,1,0:T(8,128)(2,1)S(1)} copy-done((bf16[1,1,256,128,128]{4,3,2,1,0:T(8,128)(2,1)S(1)}, bf16[1,1,256,128,128]{4,3,2,1,0:T(8,128)(2,1)}, u32[]{:S(2)}) %copy-start.2) | copy-done | bytes 8388632
  119.4 4.2 %direct.3 = (f32[8,256,128]{2,1,0:T(8,128)S(1)}, bf16[8,256,128]{2,1,0:T(8,128)(2,1)S(1)}) custom-call(s32[288]{0:T(512)S(1)} %broadcast_add_fusion.1.tab, s32[1]{0:T(128)} %bitcast.2.core, bf16[8,256,128]{2,1,0:T(8,128)(2,1)S(1)} %all-to-all-done.5.x_ref, bf16[256,128,128]{2,1,0:T(8,128)(2,1)S(1)} %bitcast.17), custom_call_target="tpu_custom_call" | custom-call | flops 1073741824 | bytes 8388608 | tf_op jit(solution)/shard_map/direct/pallas_call | solution.py:127
  123.6 2.4 %collective-permute-start.5 = (bf16[8,256,128]{2,1,0:T(8,128)(2,1)S(1)}, bf16[8,256,128]{2,1,0:T(8,128)(2,1)}, u32[]{:S(2)}, u32[]{:S(2)}) collective-permute-start(bf16[8,256,128]{2,1,0:T(8,128)(2,1)S(1)} %get-tuple-element.19), channel_id=1, source_target_pairs={{0,1},{1,0},{2,3},{3,2},{4,5},{5,4},{6,7},{7,6},{8,9},{9,8},{10,11... | collective-permute-start | bytes 1572872 | tf_op jit(solution)/shard_map/ppermute | solution.py:192
  126.0 0.0 collective-permute-done.6.y_ref
  126.0 3.4 %copy-done.3 = bf16[1,1,256,128,128]{4,3,2,1,0:T(8,128)(2,1)S(1)} copy-done((bf16[1,1,256,128,128]{4,3,2,1,0:T(8,128)(2,1)S(1)}, bf16[1,1,256,128,128]{4,3,2,1,0:T(8,128)(2,1)}, u32[]{:S(2)}) %copy-start.3) | copy-done | bytes 8388632
  129.4 5.0 %mirror.3 = bf16[8,2,128,128]{3,2,1,0:T(8,128)(2,1)} custom-call(s32[272]{0:T(512)S(1)} %broadcast_add_fusion.tab, bf16[8,2,128,128]{3,2,1,0:T(8,128)(2,1)S(1)} %all-to-all-done.4.x_ref, bf16[8,2,128,128]{3,2,1,0:T(8,128)(2,1)S(1)} %collective-permute-done.6.y_ref, s32[1]{0:T(128)} %bitcast.2.core, bf16[256,128,128]{2,1,0:T(8,128)(2,1)S(1)} %bitcast.18), custom_call_target="tpu_custom_call" | custom-call | flops 1073741824 | bytes 8388608 | tf_op jit(solution)/shard_map/mirror/pallas_call | solution.py:145
  134.4 5.5 %all-to-all-start.7 = ((bf16[8,2,128,128]{3,2,1,0:T(8,128)(2,1)}), bf16[8,2,128,128]{3,2,1,0:T(8,128)(2,1)S(1)}, u32[]{:S(2)}, u32[]{:S(2)}) async-start(bf16[8,2,128,128]{3,2,1,0:T(8,128)(2,1)} %mirror.3), calls=%async_computation.7 | async-start | bytes 1048576 | tf_op jit(solution)/shard_map/all_to_all | solution.py:181
  140.0 1.9 %add_convert_fusion = bf16[8,256,128]{2,1,0:T(8,128)(2,1)} fusion(f32[8,256,128]{2,1,0:T(8,128)S(1)} %get-tuple-element.18, bf16[8,256,128]{2,1,0:T(8,128)(2,1)} %collective-permute-done.5), kind=kLoop, calls=%fused_computation.1 | loop fusion | flops 786432 | bytes 2097152 | tf_op jit(solution)/shard_map/convert_element_type | solution.py:196
  141.9 6.2 %all-to-all-done.7 = bf16[8,2,128,128]{3,2,1,0:T(8,128)(2,1)S(1)} async-done(((bf16[8,2,128,128]{3,2,1,0:T(8,128)(2,1)}), bf16[8,2,128,128]{3,2,1,0:T(8,128)(2,1)S(1)}, u32[]{:S(2)}, u32[]{:S(2)}) %all-to-all-start.7) | async-done | bytes 524320 | tf_op jit(solution)/shard_map/all_to_all | solution.py:181
  148.1 5.5 %all-to-all-start.6 = ((bf16[8,256,128]{2,1,0:T(8,128)(2,1)}), bf16[8,256,128]{2,1,0:T(8,128)(2,1)S(1)}, u32[]{:S(2)}, u32[]{:S(2)}) async-start(bf16[8,256,128]{2,1,0:T(8,128)(2,1)} %add_convert_fusion), calls=%async_computation.6 | async-start | bytes 1048576 | tf_op jit(solution)/shard_map/all_to_all | solution.py:181
  153.6 0.1 reduce_sum.65
  153.7 0.1 copy.20
  153.8 10.1 %collective-permute-start.7 = (bf16[256,128]{1,0:T(8,128)(2,1)S(1)}, bf16[256,128]{1,0:T(8,128)(2,1)S(1)}, u32[]{:S(2)}, u32[]{:S(2)}) collective-permute-start(bf16[256,128]{1,0:T(8,128)(2,1)S(1)} %bitcast.26), channel_id=1, source_target_pairs={{0,0},{16,1},{32,2},{48,3},{64,4},{80,5},{96,6},{112,7},{1,8},{17,... | collective-permute-start | bytes 196616 | tf_op jit(solution)/shard_map/ppermute | solution.py:195
  163.9 0.1 convert_reduce_fusion
  164.0 5.1 %collective-permute-done.7 = bf16[256,128]{1,0:T(8,128)(2,1)S(1)} collective-permute-done((bf16[256,128]{1,0:T(8,128)(2,1)S(1)}, bf16[256,128]{1,0:T(8,128)(2,1)S(1)}, u32[]{:S(2)}, u32[]{:S(2)}) %collective-permute-start.7) | collective-permute-done | bytes 65568 | tf_op jit(solution)/shard_map/ppermute | solution.py:195
  169.0 0.8 multiply_subtract_fusion
  (27 shorter events, 0.1 us)
Async XLA Ops:
  1.7 14.5 %collective-permute-start = (bf16[256,128]{1,0:T(8,128)(2,1)S(1)}, bf16[256,128]{1,0:T(8,128)(2,1)S(1)}, u32[]{:S(2)}, u32[]{:S(2)}) collective-permute-start(bf16[256,128]{1,0:T(8,128)(2,1)S(1)} %multiply_convert_fusion), channel_id=1, source_target_pairs={{0,0},{1,16},{2,32},{3,48},{4,64},{5,80},{6,96},{7,112},{8,1},{9,1... | collective-permute-start | bytes 196616 | tf_op jit(solution)/shard_map/ppermute | solution.py:185
  10.7 13.0 %all-to-all-start = ((bf16[8,2,128,128]{3,2,1,0:T(8,128)(2,1)}), bf16[8,2,128,128]{3,2,1,0:T(8,128)(2,1)S(1)}, u32[]{:S(2)}, u32[]{:S(2)}) async-start(bf16[8,2,128,128]{3,2,1,0:T(8,128)(2,1)} %broadcast_in_dim.118), calls=%async_computation | async-start | bytes 1048576 | tf_op jit(solution)/shard_map/all_to_all | solution.py:181
  24.6 12.1 %all-to-all-start.1 = ((bf16[8,256,128]{2,1,0:T(8,128)(2,1)}), bf16[8,256,128]{2,1,0:T(8,128)(2,1)S(1)}, u32[]{:S(2)}, u32[]{:S(2)}) async-start(bf16[8,256,128]{2,1,0:T(8,128)(2,1)} %broadcast_in_dim.119), calls=%async_computation.1 | async-start | bytes 1048576 | tf_op jit(solution)/shard_map/all_to_all | solution.py:181
  30.4 16.4 %collective-permute-start.2 = (bf16[8,2,128,128]{3,2,1,0:T(8,128)(2,1)S(1)}, bf16[8,2,128,128]{3,2,1,0:T(8,128)(2,1)S(1)}, u32[]{:S(2)}, u32[]{:S(2)}) collective-permute-start(bf16[8,2,128,128]{3,2,1,0:T(8,128)(2,1)S(1)} %all-to-all-done.x_ref), channel_id=1, source_target_pairs={{0,1},{1,0},{2,3},{3,2},{4,5},{5,4},{6,7},{7,6},{8,9},{9,8},{10,11... | collective-permute-start | bytes 1572872 | tf_op jit(solution)/shard_map/ppermute | solution.py:187
  36.7 3.4 %copy-start = (bf16[1,1,256,128,128]{4,3,2,1,0:T(8,128)(2,1)S(1)}, bf16[1,1,256,128,128]{4,3,2,1,0:T(8,128)(2,1)}, u32[]{:S(2)}) copy-start(bf16[1,1,256,128,128]{4,3,2,1,0:T(8,128)(2,1)} %param.8) | copy-start | bytes 25165828
  40.1 6.8 %copy-start.1 = (bf16[1,1,256,128,128]{4,3,2,1,0:T(8,128)(2,1)S(1)}, bf16[1,1,256,128,128]{4,3,2,1,0:T(8,128)(2,1)}, u32[]{:S(2)}) copy-start(bf16[1,1,256,128,128]{4,3,2,1,0:T(8,128)(2,1)} %param.8) | copy-start | bytes 25165828
  44.3 41.2 %copy-start.4 = (f32[256,128]{1,0:T(8,128)S(1)}, f32[256,128]{1,0:T(8,128)}, u32[]{:S(2)}) copy-start(f32[256,128]{1,0:T(8,128)} %param.6) | copy-start | bytes 393220
  44.3 13.1 %collective-permute-start.1 = (bf16[8,256,128]{2,1,0:T(8,128)(2,1)S(1)}, bf16[8,256,128]{2,1,0:T(8,128)(2,1)}, u32[]{:S(2)}, u32[]{:S(2)}) collective-permute-start(bf16[8,256,128]{2,1,0:T(8,128)(2,1)S(1)} %get-tuple-element.15), channel_id=1, source_target_pairs={{0,1},{1,0},{2,3},{3,2},{4,5},{5,4},{6,7},{7,6},{8,9},{9,8},{10,11... | collective-permute-start | bytes 1572872 | tf_op jit(solution)/shard_map/ppermute | solution.py:192
  51.9 13.7 %all-to-all-start.3 = ((bf16[8,2,128,128]{3,2,1,0:T(8,128)(2,1)}), bf16[8,2,128,128]{3,2,1,0:T(8,128)(2,1)S(1)}, u32[]{:S(2)}, u32[]{:S(2)}) async-start(bf16[8,2,128,128]{3,2,1,0:T(8,128)(2,1)} %mirror.2), calls=%async_computation.3 | async-start | bytes 1048576 | tf_op jit(solution)/shard_map/all_to_all | solution.py:181
  65.6 14.8 %all-to-all-start.2 = ((bf16[8,256,128]{2,1,0:T(8,128)(2,1)}), bf16[8,256,128]{2,1,0:T(8,128)(2,1)S(1)}, u32[]{:S(2)}, u32[]{:S(2)}) async-start(bf16[8,256,128]{2,1,0:T(8,128)(2,1)} %add_convert_fusion.1), calls=%async_computation.2 | async-start | bytes 1048576 | tf_op jit(solution)/shard_map/all_to_all | solution.py:181
  70.2 15.3 %collective-permute-start.3 = (bf16[256,128]{1,0:T(8,128)(2,1)S(1)}, bf16[256,128]{1,0:T(8,128)(2,1)S(1)}, u32[]{:S(2)}, u32[]{:S(2)}) collective-permute-start(bf16[256,128]{1,0:T(8,128)(2,1)S(1)} %bitcast.25), channel_id=1, source_target_pairs={{0,0},{16,1},{32,2},{48,3},{64,4},{80,5},{96,6},{112,7},{1,8},{17,... | collective-permute-start | bytes 196616 | tf_op jit(solution)/shard_map/ppermute | solution.py:195
  86.7 17.2 %all-to-all-start.4 = ((bf16[8,2,128,128]{3,2,1,0:T(8,128)(2,1)}), bf16[8,2,128,128]{3,2,1,0:T(8,128)(2,1)S(1)}, u32[]{:S(2)}, u32[]{:S(2)}) async-start(bf16[8,2,128,128]{3,2,1,0:T(8,128)(2,1)} %broadcast_in_dim.127), calls=%async_computation.4 | async-start | bytes 1048576 | tf_op jit(solution)/shard_map/all_to_all | solution.py:181
  90.2 13.7 %collective-permute-start.4 = (bf16[256,128]{1,0:T(8,128)(2,1)S(1)}, bf16[256,128]{1,0:T(8,128)(2,1)S(1)}, u32[]{:S(2)}, u32[]{:S(2)}) collective-permute-start(bf16[256,128]{1,0:T(8,128)(2,1)S(1)} %fusion), channel_id=1, source_target_pairs={{0,0},{1,16},{2,32},{3,48},{4,64},{5,80},{6,96},{7,112},{8,1},{9,1... | collective-permute-start | bytes 196616 | tf_op jit(solution)/shard_map/ppermute | solution.py:185
  104.7 11.3 %all-to-all-start.5 = ((bf16[8,256,128]{2,1,0:T(8,128)(2,1)}), bf16[8,256,128]{2,1,0:T(8,128)(2,1)S(1)}, u32[]{:S(2)}, u32[]{:S(2)}) async-start(bf16[8,256,128]{2,1,0:T(8,128)(2,1)} %broadcast_in_dim.128), calls=%async_computation.5 | async-start | bytes 1048576 | tf_op jit(solution)/shard_map/all_to_all | solution.py:181
  109.4 16.6 %collective-permute-start.6 = (bf16[8,2,128,128]{3,2,1,0:T(8,128)(2,1)S(1)}, bf16[8,2,128,128]{3,2,1,0:T(8,128)(2,1)S(1)}, u32[]{:S(2)}, u32[]{:S(2)}) collective-permute-start(bf16[8,2,128,128]{3,2,1,0:T(8,128)(2,1)S(1)} %all-to-all-done.4.x_ref), channel_id=1, source_target_pairs={{0,1},{1,0},{2,3},{3,2},{4,5},{5,4},{6,7},{7,6},{8,9},{9,8},{10,11... | collective-permute-start | bytes 1572872 | tf_op jit(solution)/shard_map/ppermute | solution.py:187
  116.0 3.4 %copy-start.2 = (bf16[1,1,256,128,128]{4,3,2,1,0:T(8,128)(2,1)S(1)}, bf16[1,1,256,128,128]{4,3,2,1,0:T(8,128)(2,1)}, u32[]{:S(2)}) copy-start(bf16[1,1,256,128,128]{4,3,2,1,0:T(8,128)(2,1)} %param.8) | copy-start | bytes 25165828
  123.6 16.3 %collective-permute-start.5 = (bf16[8,256,128]{2,1,0:T(8,128)(2,1)S(1)}, bf16[8,256,128]{2,1,0:T(8,128)(2,1)}, u32[]{:S(2)}, u32[]{:S(2)}) collective-permute-start(bf16[8,256,128]{2,1,0:T(8,128)(2,1)S(1)} %get-tuple-element.19), channel_id=1, source_target_pairs={{0,1},{1,0},{2,3},{3,2},{4,5},{5,4},{6,7},{7,6},{8,9},{9,8},{10,11... | collective-permute-start | bytes 1572872 | tf_op jit(solution)/shard_map/ppermute | solution.py:192
  126.0 3.4 %copy-start.3 = (bf16[1,1,256,128,128]{4,3,2,1,0:T(8,128)(2,1)S(1)}, bf16[1,1,256,128,128]{4,3,2,1,0:T(8,128)(2,1)}, u32[]{:S(2)}) copy-start(bf16[1,1,256,128,128]{4,3,2,1,0:T(8,128)(2,1)} %param.8) | copy-start | bytes 25165828
  134.4 13.7 %all-to-all-start.7 = ((bf16[8,2,128,128]{3,2,1,0:T(8,128)(2,1)}), bf16[8,2,128,128]{3,2,1,0:T(8,128)(2,1)S(1)}, u32[]{:S(2)}, u32[]{:S(2)}) async-start(bf16[8,2,128,128]{3,2,1,0:T(8,128)(2,1)} %mirror.3), calls=%async_computation.7 | async-start | bytes 1048576 | tf_op jit(solution)/shard_map/all_to_all | solution.py:181
  148.1 15.8 %all-to-all-start.6 = ((bf16[8,256,128]{2,1,0:T(8,128)(2,1)}), bf16[8,256,128]{2,1,0:T(8,128)(2,1)S(1)}, u32[]{:S(2)}, u32[]{:S(2)}) async-start(bf16[8,256,128]{2,1,0:T(8,128)(2,1)} %add_convert_fusion), calls=%async_computation.6 | async-start | bytes 1048576 | tf_op jit(solution)/shard_map/all_to_all | solution.py:181
  153.8 15.3 %collective-permute-start.7 = (bf16[256,128]{1,0:T(8,128)(2,1)S(1)}, bf16[256,128]{1,0:T(8,128)(2,1)S(1)}, u32[]{:S(2)}, u32[]{:S(2)}) collective-permute-start(bf16[256,128]{1,0:T(8,128)(2,1)S(1)} %bitcast.26), channel_id=1, source_target_pairs={{0,0},{16,1},{32,2},{48,3},{64,4},{80,5},{96,6},{112,7},{1,8},{17,... | collective-permute-start | bytes 196616 | tf_op jit(solution)/shard_map/ppermute | solution.py:195

commit v2 on v1

v2 whole, which is shorter than its diff:
```python
import functools

import jax
import jax.numpy as jnp
from jax import lax
from jax.experimental import pallas as pl
from jax.experimental.pallas import tpu as pltpu
from jax.sharding import Mesh
from jax.sharding import PartitionSpec as P

CENTER = 0.25
ATOM = 128
VECS = 128
AR = 32
AC = 16
SLOTS = 256
N_ROW = 8
N_COL = 16
BF = jnp.bfloat16
F32 = jnp.float32
ROWS = ("y", "xl")
COLS = ("xh", "z", "co")
ALL = ROWS + COLS
D_LEN = 9
M_LEN = 17


def tables(slot_rows, slot_cols, count, row, col):
    place = jnp.where(jnp.arange(SLOTS) < count, slot_rows * AC + slot_cols, -1)

    def pack(rows, cols, index, zero):
        want = (rows * AC + cols).reshape(-1, 1)
        entry = jnp.arange(SLOTS)[None, :] * 64 + index.reshape(-1, 1) - zero
        return zero + jnp.sum(jnp.where(place[None, :] == want, entry, 0), axis=1)

    a = jnp.arange(AR)[:, None]
    q = jnp.arange(D_LEN)[None, :]
    ga = row * AR + a
    gb = col * AC + 2 * q
    odd = ga % 2 == 1
    main = 2 * q + jnp.where(odd, ga <= gb + 1, ga > gb).astype(jnp.int32)
    extra = ga - 1 - col * AC
    extra = jnp.where(odd & (extra >= 0) & (extra < AC), extra, -AC * AR)
    b = jnp.where(q < 8, main, extra)
    direct = pack(a + 0 * b, b, b, AC)

    b = jnp.arange(AC)[:, None]
    q = jnp.arange(M_LEN)[None, :]
    gb = col * AC + b
    ga = row * AR + 2 * q
    odd = gb % 2 == 1
    main = 2 * q + jnp.where(odd, ga + 1 <= gb, ga > gb).astype(jnp.int32)
    extra = gb + 1 - row * AR
    extra = jnp.where((~odd) & (extra >= 0) & (extra < AR), extra, -AR)
    a = jnp.where(q < 16, main, extra)
    mirror = pack(a, b + 0 * a, a, AR)
    return direct, mirror


def keep_of(widths, shape, axis):
    place = lax.broadcasted_iota(jnp.int32, shape, axis)
    atom = lax.broadcasted_iota(jnp.int32, shape, 0)
    return (place < jnp.where(atom == 0, widths[0], widths[1])).astype(F32)


def send_forms(current, plain_ref, flip_ref):
    plain_ref[...] = current.reshape(2 * ATOM, VECS).astype(BF)
    flipped = jnp.swapaxes(current, 1, 2).astype(BF)
    for k in range(8):
        flip_ref[k] = flipped


def first_kernel(widths, vectors_ref, plain_ref, flip_ref):
    shape = (2, ATOM, VECS)
    first = vectors_ref[...].reshape(shape) * keep_of(widths, shape, 1)
    send_forms(first, plain_ref, flip_ref)


def applied(widths, own_ref, near_ref, far_ref):
    shape = (2, ATOM, VECS)
    total = near_ref[...] + far_ref[...]
    for k in range(8):
        total = total + own_ref[k].astype(F32)
    return total.reshape(shape) * keep_of(widths, shape, 1)


def second_kernel(widths, own_ref, near_ref, far_ref, vectors_ref, out_ref, plain_ref, flip_ref):
    shape = (2, ATOM, VECS)
    first = vectors_ref[...].reshape(shape) * keep_of(widths, shape, 1)
    second = applied(widths, own_ref, near_ref, far_ref) - CENTER * first
    out_ref[...] = second.reshape(2 * ATOM, VECS)
    send_forms(second, plain_ref, flip_ref)


def last_kernel(widths, own_ref, near_ref, far_ref, vectors_ref, second_ref, out_ref):
    shape = (2, ATOM, VECS)
    first = vectors_ref[...].reshape(shape) * keep_of(widths, shape, 1)
    third = applied(widths, own_ref, near_ref, far_ref)
    out = 2.0 * (third - CENTER * second_ref[...].reshape(shape)) - first
    out_ref[...] = out.reshape(2 * ATOM, VECS)


def load_kernel(src_ref, out_ref, sem):
    copy = pltpu.make_async_copy(src_ref, out_ref, sem)
    copy.start()
    copy.wait()


def direct_kernel(tab, place, x0_ref, x1_ref, x2_ref, x3_ref, t_ref, mine_ref, other_ref, held):
    co, y, xl = place[0], place[1], place[2]
    for s, ref in enumerate((x0_ref, x1_ref, x2_ref, x3_ref)):
        for rel in range(2):
            k = 2 * jnp.bitwise_and(y - s + 4, 3) + jnp.bitwise_xor(xl, rel)
            held[pl.ds(2 * k, 2)] = ref[rel].reshape(2, ATOM, VECS)
    held[AC] = jnp.zeros((ATOM, VECS), BF)

    def product(a, q, n):
        blocks, xs = [], []
        for k in range(n):
            e = tab[a * D_LEN + q + k]
            blocks.append(t_ref[lax.shift_right_logical(e, 6)])
            xs.append(held[jnp.bitwise_and(e, 63)])
        if n == 1:
            left, right = blocks[0], xs[0]
        else:
            left, right = jnp.concatenate(blocks, 1), jnp.concatenate(xs, 0)
        return jnp.dot(left, right, preferred_element_type=F32)

    def step(xz, carry):
        for which, out in ((0, mine_ref), (1, other_ref)):
            for t in range(2):
                a = 4 * xz + 2 * (co if which == 0 else 1 - co) + t
                total = product(a, 0, 8)
                if t:
                    total = total + product(a, 8, 1)
                out[xz, t * ATOM:(t + 1) * ATOM, :] = total.astype(out.dtype)
        return carry

    lax.fori_loop(0, 8, step, 0)


def mirror_kernel(tab, place, x_ref, y_ref, t_ref, o0_ref, o1_ref, o2_ref, o3_ref, held):
    co, y, xl = place[0], place[1], place[2]
    for xz in range(8):
        held[pl.ds(4 * xz + 2 * co, 2)] = x_ref[xz]
        held[pl.ds(4 * xz + 2 - 2 * co, 2)] = y_ref[xz]
    held[AR] = jnp.zeros((VECS, ATOM), BF)

    def product(b, q, n):
        blocks, xs = [], []
        for k in range(n):
            e = tab[b * M_LEN + q + k]
            blocks.append(t_ref[lax.shift_right_logical(e, 6)])
            xs.append(held[jnp.bitwise_and(e, 63)])
        if n == 1:
            left, right = xs[0], blocks[0]
        else:
            left, right = jnp.concatenate(xs, 1), jnp.concatenate(blocks, 0)
        return jnp.dot(left, right, preferred_element_type=F32)

    for s, out in enumerate((o0_ref, o1_ref, o2_ref, o3_ref)):

        def step(rel, carry, s=s, out=out):
            k = 2 * jnp.bitwise_and(y + s, 3) + jnp.bitwise_xor(xl, rel)
            for t in range(2):
                b = 2 * k + t
                total = product(b, 0, 8) + product(b, 8, 8)
                if not t:
                    total = total + product(b, 16, 1)
                out[rel, t] = total.astype(out.dtype)
            return carry

        lax.fori_loop(0, 2, step, 0)


def gathered_kernel(o0_ref, o1_ref, o2_ref, o3_ref, near_ref, far_ref):
    for rel, out in enumerate((near_ref, far_ref)):
        total = o0_ref[rel] + o1_ref[rel].astype(F32) + o2_ref[rel].astype(F32) + o3_ref[rel].astype(F32)
        out[...] = jnp.swapaxes(total, 1, 2).reshape(2 * ATOM, VECS)


def both_kernel(mine_ref, theirs_ref, out_ref):
    out_ref[...] = (mine_ref[...] + theirs_ref[...]).astype(BF)


SMEM = pl.BlockSpec(memory_space=pltpu.SMEM)
VMEM = pl.BlockSpec(memory_space=pltpu.VMEM)
PARAMS = pltpu.CompilerParams(vmem_limit_bytes=24 * 1024 * 1024)
PIECE = (2 * ATOM, VECS)
BLOCKS = (2, ATOM, VECS)


def like(shape, dtype):
    return jax.ShapeDtypeStruct(shape, dtype)


def call(kernel, out_shape, scalars, arrays, scratch=(), flops=0, size=2**20, name=None):
    single = not isinstance(out_shape, tuple)
    return pl.pallas_call(
        kernel,
        out_shape=out_shape,
        in_specs=[SMEM] * len(scalars) + [VMEM] * len(arrays),
        out_specs=VMEM if single else (VMEM,) * len(out_shape),
        scratch_shapes=list(scratch),
        compiler_params=PARAMS,
        cost_estimate=pl.CostEstimate(flops=flops, bytes_accessed=size, transcendentals=0),
        name=name,
    )(*scalars, *arrays)


def load(tiles):
    return pl.pallas_call(
        load_kernel,
        out_shape=pltpu.VMEM(tiles.shape, tiles.dtype),
        in_specs=[pl.BlockSpec(memory_space=pl.ANY)],
        scratch_shapes=[pltpu.SemaphoreType.DMA],
        compiler_params=pltpu.CompilerParams(vmem_limit_bytes=2**20),
        cost_estimate=pl.CostEstimate(flops=0, bytes_accessed=2**23, transcendentals=0),
        name="load",
    )(tiles)


def pairs(rel):
    return [
        (r * 16 + c, ((c % 8) ^ rel) * 16 + 2 * r + c // 8) for r in range(8) for c in range(16)
    ]


SWAP = [(0, 1), (1, 0)]


def turn(s):
    return [(k, (k + s) % 4) for k in range(4)]


def local(vectors, widths, tiles, block_rows, block_cols, block_count):
    row = lax.axis_index(ROWS)
    col = lax.axis_index(COLS)
    place = jnp.stack([lax.axis_index(n) for n in ("co", "y", "xl")]).astype(jnp.int32)
    tile_set = tiles[0, 0]
    direct_tab, mirror_tab = tables(
        block_rows[0, 0], block_cols[0, 0], block_count[0, 0], row, col
    )
    work = dict(flops=2 * SLOTS * ATOM**3, size=2**22)

    def exchange(x):
        return lax.all_to_all(x, ("xh", "z"), split_axis=0, concat_axis=0, tiled=True)

    def apply_matrix(plain, flipped):
        piece = jnp.stack([lax.ppermute(plain, ALL, pairs(rel)) for rel in range(2)])
        near = exchange(flipped)
        xs = [piece] + [lax.ppermute(piece, "y", turn(s)) for s in (1, 2, 3)]
        far = lax.ppermute(near, "co", SWAP)
        mine, other = call(
            direct_kernel,
            (like((8, *PIECE), F32), like((8, *PIECE), F32)),
            (direct_tab, place),
            (*xs, tile_set),
            [pltpu.VMEM((AC + 1, ATOM, VECS), BF)],
            name="direct",
            **work,
        )
        theirs = lax.ppermute(other, "co", SWAP)
        near, mine = lax.optimization_barrier((near, mine))
        outs = call(
            mirror_kernel,
            (like((2, *BLOCKS), F32),) + (like((2, *BLOCKS), BF),) * 3,
            (mirror_tab, place),
            (near, far, tile_set),
            [pltpu.VMEM((AR + 1, VECS, ATOM), BF)],
            name="mirror",
            **work,
        )
        both = call(both_kernel, like((8, *PIECE), BF), (), (mine, theirs), name="both")
        own = exchange(both)
        outs = [outs[0]] + [lax.ppermute(outs[s], "y", turn(s)) for s in (1, 2, 3)]
        sums = call(
            gathered_kernel, (like(PIECE, F32), like(PIECE, F32)), (), tuple(outs), name="gathered"
        )
        back = [
            lax.ppermute(sums[rel], ALL, [(d, s) for s, d in pairs(rel)]) for rel in range(2)
        ]
        return own, back[0], back[1]

    forms = (like(PIECE, BF), like((8, *BLOCKS), BF))
    plain, flipped = call(first_kernel, forms, (widths,), (vectors,), name="first")
    parts = apply_matrix(plain, flipped)
    second, plain, flipped = call(
        second_kernel, (like(PIECE, F32), *forms), (widths,), (*parts, vectors), name="second"
    )
    parts = apply_matrix(plain, flipped)
    return call(
        last_kernel, like(PIECE, F32), (widths,), (*parts, vectors, second), name="last"
    )

def solution(mesh):
    split = Mesh(mesh.devices.reshape(4, 2, 2, 4, 2), ALL)
    return jax.shard_map(
        local,
        mesh=split,
        in_specs=(
            P(ALL, None),
            P(ALL),
            P(ROWS, COLS, None, None, None),
            P(ROWS, COLS, None),
            P(ROWS, COLS, None),
            P(ROWS, COLS),
        ),
        out_specs=P(ALL, None),
        check_vma=False,
    )
```

time: 171 us -> 185 us (1.082)
  starting transfers between devices: 84.1 us -> 65.1 us
  waiting for transfers between devices: 43.4 us -> 60.8 us
  blocking collectives: 0 us -> 16 us
  other arithmetic: 8.25 us -> 1.57 us
  Pallas kernels: 18.5 us -> 24.1 us
    ppermute x4 -> x20, waiting for transfers between devices: 13.8 us -> 58.9 us  [the longest x4 18.3 us: apply_matrix(): lax.ppermute(sums[rel], ALL, [(d, s) for s, d in pairs(rel)])]
    all_to_all x8 -> x3, waiting for transfers between devices: 29.5 us -> 0.01 us  [exchange(): lax.all_to_all(x, ('xh', 'z'), split_axis=0, concat_axis=0, tiled=True)]
    all_to_all x8 -> x3, starting transfers between devices: 38 us -> 13.3 us  [exchange(): lax.all_to_all(x, ('xh', 'z'), split_axis=0, concat_axis=0, tiled=True)]
    all_to_all x0 -> x1, blocking collectives: none -> 16 us  [exchange(): lax.all_to_all(x, ('xh', 'z'), split_axis=0, concat_axis=0, tiled=True)]
    ppermute x4 -> x20, starting transfers between devices: 38.1 us -> 46.7 us  [the longest x4 24.1 us: apply_matrix(): lax.ppermute(sums[rel], ALL, [(d, s) for s, d in pairs(rel)])]
    convert_element_type x5 -> x0, other arithmetic: 5.72 us -> none  [the longest x2 3.9 us: apply_matrix(): both = (mine + theirs.astype(F32)).astype(BF)]
    pallas_call x4 -> x11, Pallas kernels: 18.5 us -> 24.1 us  [call(): pl.pallas_call(kernel, out_shape=out_shape, in_specs=[SMEM] * len(scalars...]
    unnamed x10 -> x16, local copies, waits for them, and re-layouts: 10.2 us -> 15.1 us
  transfers between devices with their start and end apart: 16 -> 27, of which waited for: 8 -> 20; matrix products, arithmetic and copies ran while one was open for 4% -> 1% of each run, Pallas kernels for 11% -> 9%
where the time goes in v2:
time: 185 us; the launch traced here: 184 us
  starting transfers between devices  65.1 us (35%)
  waiting for transfers between devices  60.8 us (33%)
  Pallas kernels  24.1 us (13%)
  blocking collectives  16 us (9%)
  local copies, waits for them, and re-layouts  15.5 us (8%)
    ppermute x4, starting transfers between devices, apply_matrix(): lax.ppermute(sums[rel], ALL, [(d, s) for s, d in pairs(rel)])  24.1 us
    pallas_call x11, Pallas kernels, call(): pl.pallas_call(kernel, out_shape=out_shape, in_specs=[SMEM] * len(scalars...  24.1 us
    ppermute x4, waiting for transfers between devices, apply_matrix(): lax.ppermute(sums[rel], ALL, [(d, s) for s, d in pairs(rel)])  18.3 us
    ppermute x6, waiting for transfers between devices, apply_matrix(): outs = [outs[0]] + [lax.ppermute(outs[s], 'y', turn(s)) for s in (1, 2, 3)]  17.5 us
    ppermute x4, starting transfers between devices, apply_matrix(): lax.ppermute(plain, ALL, pairs(rel))  16.1 us
    all_to_all x1, blocking collectives, exchange(): lax.all_to_all(x, ('xh', 'z'), split_axis=0, concat_axis=0, tiled=True)  16 us
    unnamed x16, local copies, waits for them, and re-layouts  15.1 us
    all_to_all x3, starting transfers between devices, exchange(): lax.all_to_all(x, ('xh', 'z'), split_axis=0, concat_axis=0, tiled=True)  13.3 us
  transfers between devices with their start and end apart: 27, of which 20 were waited for; matrix products, arithmetic and copies ran while one was open for 1% of the time, Pallas kernels for 9%

profile of v2, /device:TPU:25, one launch (start us, length us, event | category | flops | bytes accessed | tf_op | source)
XLA Modules:
  0.0 184.0 jit_solution(13250394476533926104)
XLA Ops:
  0.0 0.9 copy-done.4
  0.9 0.7 copy-done.6
  1.6 1.5 first.1
  3.0 6.3 %collective-permute-start.1 = (bf16[256,128]{1,0:T(8,128)(2,1)S(1)}, bf16[256,128]{1,0:T(8,128)(2,1)S(1)}, u32[]{:S(2)}, u32[]{:S(2)}) collective-permute-start(bf16[256,128]{1,0:T(8,128)(2,1)S(1)} %get-tuple-element.31), channel_id=1, source_target_pairs={{0,16},{1,0},{2,48},{3,32},{4,80},{5,64},{6,112},{7,96},{8,17},{9,... | collective-permute-start | bytes 196616 | tf_op jit(solution)/shard_map/ppermute | solution.py:250
  9.3 4.7 %collective-permute-start = (bf16[256,128]{1,0:T(8,128)(2,1)S(1)}, bf16[256,128]{1,0:T(8,128)(2,1)S(1)}, u32[]{:S(2)}, u32[]{:S(2)}) collective-permute-start(bf16[256,128]{1,0:T(8,128)(2,1)S(1)} %get-tuple-element.31), channel_id=1, source_target_pairs={{0,0},{1,16},{2,32},{3,48},{4,64},{5,80},{6,96},{7,112},{8,1},{9,1... | collective-permute-start | bytes 196616 | tf_op jit(solution)/shard_map/ppermute | solution.py:250
  14.0 3.5 %all-to-all-start = ((bf16[8,2,128,128]{3,2,1,0:T(8,128)(2,1)}), bf16[8,2,128,128]{3,2,1,0:T(8,128)(2,1)S(1)}, u32[]{:S(2)}, u32[]{:S(2)}) async-start(bf16[8,2,128,128]{3,2,1,0:T(8,128)(2,1)} %get-tuple-element.30), calls=%async_computation | async-start | bytes 1048576 | tf_op jit(solution)/shard_map/all_to_all | solution.py:247
  17.7 0.1 reshape.354
  18.5 0.1 add.246
  18.6 0.7 multiply_add_fusion.1
  19.3 0.3 select_reduce_fusion
  19.6 1.4 collective-permute-done
  21.1 1.1 collective-permute-start.3
  22.2 0.4 collective-permute-start.4
  22.6 2.6 %collective-permute-done.2.x1_ref = bf16[2,256,128]{2,1,0:T(8,128)(2,1)S(1)} collective-permute-done((bf16[2,256,128]{2,1,0:T(8,128)(2,1)S(1)}, bf16[2,256,128]{2,1,0:T(8,128)(2,1)S(1)}, u32[]{:S(2)}, u32[]{:S(2)}) %collective-permute-start.2) | collective-permute-done | bytes 131104 | tf_op jit(solution)/shard_map/ppermute | solution.py:252
  25.2 1.6 collective-permute-done.3.x2_ref
  26.8 1.9 %collective-permute-done.4.x3_ref = bf16[2,256,128]{2,1,0:T(8,128)(2,1)S(1)} collective-permute-done((bf16[2,256,128]{2,1,0:T(8,128)(2,1)S(1)}, bf16[2,256,128]{2,1,0:T(8,128)(2,1)S(1)}, u32[]{:S(2)}, u32[]{:S(2)}) %collective-permute-start.4) | collective-permute-done | bytes 131104 | tf_op jit(solution)/shard_map/ppermute | solution.py:252
  28.7 3.4 %copy-done = bf16[1,1,256,128,128]{4,3,2,1,0:T(8,128)(2,1)S(1)} copy-done((bf16[1,1,256,128,128]{4,3,2,1,0:T(8,128)(2,1)S(1)}, bf16[1,1,256,128,128]{4,3,2,1,0:T(8,128)(2,1)}, u32[]{:S(2)}) %copy-start) | copy-done | bytes 8388632
  32.1 5.2 %direct.2 = (f32[8,256,128]{2,1,0:T(8,128)S(1)}, f32[8,256,128]{2,1,0:T(8,128)}) custom-call(s32[288]{0:T(512)S(1)} %broadcast_add_fusion.1.tab, s32[3]{0:T(128)S(1)} %pad_add_fusion.place, bf16[2,256,128]{2,1,0:T(8,128)(2,1)S(1)} %pad_maximum_fusion.x0_ref, bf16[2,256,128]{2,1,0:T(8,128)(2,1)S(1)} %collective-permute-done.2.x1_ref, ...), custom_call_target="tpu_custom_call" | custom-call | flops 1073741824 | bytes 4194304 | tf_op jit(solution)/shard_map/direct/pallas_call | solution.py:199
  37.3 2.8 %collective-permute-start.5 = (f32[8,256,128]{2,1,0:T(8,128)}, f32[8,256,128]{2,1,0:T(8,128)S(1)}, u32[]{:S(2)}, u32[]{:S(2)}) collective-permute-start(f32[8,256,128]{2,1,0:T(8,128)} %get-tuple-element.34), channel_id=1, source_target_pairs={{0,1},{1,0},{2,3},{3,2},{4,5},{5,4},{6,7},{7,6},{8,9},{9,8},{10,11... | collective-permute-start | bytes 3145736 | tf_op jit(solution)/shard_map/ppermute | solution.py:263
  40.4 0.1 collective-permute-start.6
  40.5 0.2 select_reduce_fusion.1
  40.8 1.8 collective-permute-done.5.theirs_ref
  42.6 0.9 both.2
  43.5 6.2 %all-to-all-start.1 = ((bf16[8,256,128]{2,1,0:T(8,128)(2,1)}), bf16[8,256,128]{2,1,0:T(8,128)(2,1)S(1)}, u32[]{:S(2)}, u32[]{:S(2)}) async-start(bf16[8,256,128]{2,1,0:T(8,128)(2,1)} %both.2), calls=%async_computation.1 | async-start | bytes 1048576 | tf_op jit(solution)/shard_map/all_to_all | solution.py:247
  49.6 3.4 %copy-done.1 = bf16[1,1,256,128,128]{4,3,2,1,0:T(8,128)(2,1)S(1)} copy-done((bf16[1,1,256,128,128]{4,3,2,1,0:T(8,128)(2,1)S(1)}, bf16[1,1,256,128,128]{4,3,2,1,0:T(8,128)(2,1)}, u32[]{:S(2)}) %copy-start.1) | copy-done | bytes 8388632
  53.0 4.7 %mirror.2 = (f32[2,2,128,128]{3,2,1,0:T(8,128)S(1)}, bf16[2,2,128,128]{3,2,1,0:T(8,128)(2,1)S(1)}, bf16[2,2,128,128]{3,2,1,0:T(8,128)(2,1)S(1)}, bf16[2,2,128,128]{3,2,1,0:T(8,128)(2,1)S(1)}) custom-call(s32[272]{0:T(512)S(1)} %broadcast_add_fusion.tab, s32[3]{0:T(128)S(1)} %pad_add_fusion.place, bf16[8,2,128,128]{3,2,1,0:T(8,128)(2,1)S(1)} %all-to-all-done.x_ref, ...), custom_call_target="tpu_custom_call" | custom-call | flops 1073741824 | bytes 4194304 | tf_op jit(solution)/shard_map/mirror/pallas_call | solution.py:199
  57.7 1.2 collective-permute-start.7
  58.9 0.7 collective-permute-start.9
  59.6 2.6 %collective-permute-done.7.o1_ref = bf16[2,2,128,128]{3,2,1,0:T(8,128)(2,1)S(1)} collective-permute-done((bf16[2,2,128,128]{3,2,1,0:T(8,128)(2,1)S(1)}, bf16[2,2,128,128]{3,2,1,0:T(8,128)(2,1)S(1)}, u32[]{:S(2)}, u32[]{:S(2)}) %collective-permute-start.7) | collective-permute-done | bytes 131104 | tf_op jit(solution)/shard_map/ppermute | solution.py:276
  62.2 2.1 %collective-permute-done.8.o2_ref = bf16[2,2,128,128]{3,2,1,0:T(8,128)(2,1)S(1)} collective-permute-done((bf16[2,2,128,128]{3,2,1,0:T(8,128)(2,1)S(1)}, bf16[2,2,128,128]{3,2,1,0:T(8,128)(2,1)S(1)}, u32[]{:S(2)}, u32[]{:S(2)}) %collective-permute-start.8) | collective-permute-done | bytes 131104 | tf_op jit(solution)/shard_map/ppermute | solution.py:276
  64.3 3.9 %collective-permute-done.9.o3_ref = bf16[2,2,128,128]{3,2,1,0:T(8,128)(2,1)S(1)} collective-permute-done((bf16[2,2,128,128]{3,2,1,0:T(8,128)(2,1)S(1)}, bf16[2,2,128,128]{3,2,1,0:T(8,128)(2,1)S(1)}, u32[]{:S(2)}, u32[]{:S(2)}) %collective-permute-start.9) | collective-permute-done | bytes 131104 | tf_op jit(solution)/shard_map/ppermute | solution.py:276
  68.2 0.1 gathered.2
  68.4 7.8 %collective-permute-start.10 = (f32[256,128]{1,0:T(8,128)S(1)}, f32[256,128]{1,0:T(8,128)S(1)}, u32[]{:S(2)}, u32[]{:S(2)}) collective-permute-start(f32[256,128]{1,0:T(8,128)S(1)} %get-tuple-element.40), channel_id=1, source_target_pairs={{0,0},{16,1},{32,2},{48,3},{64,4},{80,5},{96,6},{112,7},{1,8},{17,... | collective-permute-start | bytes 393224 | tf_op jit(solution)/shard_map/ppermute | solution.py:281
  76.2 4.5 %collective-permute-start.11 = (f32[256,128]{1,0:T(8,128)S(1)}, f32[256,128]{1,0:T(8,128)S(1)}, u32[]{:S(2)}, u32[]{:S(2)}) collective-permute-start(f32[256,128]{1,0:T(8,128)S(1)} %get-tuple-element.41), channel_id=1, source_target_pairs={{16,0},{0,1},{48,2},{32,3},{80,4},{64,5},{112,6},{96,7},{17,8},{1,... | collective-permute-start | bytes 393224 | tf_op jit(solution)/shard_map/ppermute | solution.py:281
  80.7 4.1 %collective-permute-done.10.near_ref = f32[256,128]{1,0:T(8,128)S(1)} collective-permute-done((f32[256,128]{1,0:T(8,128)S(1)}, f32[256,128]{1,0:T(8,128)S(1)}, u32[]{:S(2)}, u32[]{:S(2)}) %collective-permute-start.10) | collective-permute-done | bytes 131104 | tf_op jit(solution)/shard_map/ppermute | solution.py:281
  84.9 5.0 %collective-permute-done.11.far_ref = f32[256,128]{1,0:T(8,128)S(1)} collective-permute-done((f32[256,128]{1,0:T(8,128)S(1)}, f32[256,128]{1,0:T(8,128)S(1)}, u32[]{:S(2)}, u32[]{:S(2)}) %collective-permute-start.11) | collective-permute-done | bytes 131104 | tf_op jit(solution)/shard_map/ppermute | solution.py:281
  89.9 0.7 second.1
  90.6 3.3 %collective-permute-start.13 = (bf16[256,128]{1,0:T(8,128)(2,1)S(1)}, bf16[256,128]{1,0:T(8,128)(2,1)S(1)}, u32[]{:S(2)}, u32[]{:S(2)}) collective-permute-start(bf16[256,128]{1,0:T(8,128)(2,1)S(1)} %get-tuple-element.43), channel_id=1, source_target_pairs={{0,16},{1,0},{2,48},{3,32},{4,80},{5,64},{6,112},{7,96},{8,17},{9,... | collective-permute-start | bytes 196616 | tf_op jit(solution)/shard_map/ppermute | solution.py:250
  93.9 1.9 %collective-permute-start.12 = (bf16[256,128]{1,0:T(8,128)(2,1)S(1)}, bf16[256,128]{1,0:T(8,128)(2,1)S(1)}, u32[]{:S(2)}, u32[]{:S(2)}) collective-permute-start(bf16[256,128]{1,0:T(8,128)(2,1)S(1)} %get-tuple-element.43), channel_id=1, source_target_pairs={{0,0},{1,16},{2,32},{3,48},{4,64},{5,80},{6,96},{7,112},{8,1},{9,1... | collective-permute-start | bytes 196616 | tf_op jit(solution)/shard_map/ppermute | solution.py:250
  95.8 4.5 %collective-permute-done.13 = bf16[256,128]{1,0:T(8,128)(2,1)S(1)} collective-permute-done((bf16[256,128]{1,0:T(8,128)(2,1)S(1)}, bf16[256,128]{1,0:T(8,128)(2,1)S(1)}, u32[]{:S(2)}, u32[]{:S(2)}) %collective-permute-start.13) | collective-permute-done | bytes 65568 | tf_op jit(solution)/shard_map/ppermute | solution.py:250
  100.4 4.9 %collective-permute-done.12 = bf16[256,128]{1,0:T(8,128)(2,1)S(1)} collective-permute-done((bf16[256,128]{1,0:T(8,128)(2,1)S(1)}, bf16[256,128]{1,0:T(8,128)(2,1)S(1)}, u32[]{:S(2)}, u32[]{:S(2)}) %collective-permute-start.12) | collective-permute-done | bytes 65568 | tf_op jit(solution)/shard_map/ppermute | solution.py:250
  105.4 1.4 collective-permute-start.16
  106.8 3.5 %collective-permute-done.14.x1_ref = bf16[2,256,128]{2,1,0:T(8,128)(2,1)S(1)} collective-permute-done((bf16[2,256,128]{2,1,0:T(8,128)(2,1)S(1)}, bf16[2,256,128]{2,1,0:T(8,128)(2,1)S(1)}, u32[]{:S(2)}, u32[]{:S(2)}) %collective-permute-start.14) | collective-permute-done | bytes 131104 | tf_op jit(solution)/shard_map/ppermute | solution.py:252
  110.3 1.3 collective-permute-done.15.x2_ref
  111.6 1.4 collective-permute-done.16.x3_ref
  113.0 3.4 %copy-done.2 = bf16[1,1,256,128,128]{4,3,2,1,0:T(8,128)(2,1)S(1)} copy-done((bf16[1,1,256,128,128]{4,3,2,1,0:T(8,128)(2,1)S(1)}, bf16[1,1,256,128,128]{4,3,2,1,0:T(8,128)(2,1)}, u32[]{:S(2)}) %copy-start.2) | copy-done | bytes 8388632
  116.4 4.2 %direct.3 = (f32[8,256,128]{2,1,0:T(8,128)S(1)}, f32[8,256,128]{2,1,0:T(8,128)S(1)}) custom-call(s32[288]{0:T(512)S(1)} %broadcast_add_fusion.1.tab, s32[3]{0:T(128)S(1)} %pad_add_fusion.place, bf16[2,256,128]{2,1,0:T(8,128)(2,1)S(1)} %pad_maximum_fusion.1.x0_ref, bf16[2,256,128]{2,1,0:T(8,128)(2,1)S(1)} %collective-permute-done.14.x1_ref, ...), custom_call_target="tpu_custom_call" | custom-call | flops 1073741824 | bytes 4194304 | tf_op jit(solution)/shard_map/direct/pallas_call | solution.py:199
  120.7 16.0 %all_to_all.20.x_ref = bf16[8,2,128,128]{3,2,1,0:T(8,128)(2,1)S(1)} all-to-all(bf16[8,2,128,128]{3,2,1,0:T(8,128)(2,1)S(1)} %get-tuple-element.42), channel_id=1, replica_groups=mesh['y'=4,'xl'=2,'xh'=2,'z'=4,'co'=2] {'xh','z'}, dimensions={0} | all-to-all | bytes 1048576 | tf_op jit(solution)/shard_map/all_to_all | solution.py:247
  136.7 2.2 %collective-permute-start.18 = (bf16[8,2,128,128]{3,2,1,0:T(8,128)(2,1)S(1)}, bf16[8,2,128,128]{3,2,1,0:T(8,128)(2,1)S(1)}, u32[]{:S(2)}, u32[]{:S(2)}) collective-permute-start(bf16[8,2,128,128]{3,2,1,0:T(8,128)(2,1)S(1)} %all_to_all.20.x_ref), channel_id=1, source_target_pairs={{0,1},{1,0},{2,3},{3,2},{4,5},{5,4},{6,7},{7,6},{8,9},{9,8},{10,11... | collective-permute-start | bytes 1572872 | tf_op jit(solution)/shard_map/ppermute | solution.py:253
  138.8 1.0 both.3
  139.8 3.7 %all-to-all-start.3 = ((bf16[8,256,128]{2,1,0:T(8,128)(2,1)}), bf16[8,256,128]{2,1,0:T(8,128)(2,1)S(1)}, u32[]{:S(2)}, u32[]{:S(2)}) async-start(bf16[8,256,128]{2,1,0:T(8,128)(2,1)} %both.3), calls=%async_computation.3 | async-start | bytes 1048576 | tf_op jit(solution)/shard_map/all_to_all | solution.py:247
  143.5 3.4 %copy-done.3 = bf16[1,1,256,128,128]{4,3,2,1,0:T(8,128)(2,1)S(1)} copy-done((bf16[1,1,256,128,128]{4,3,2,1,0:T(8,128)(2,1)S(1)}, bf16[1,1,256,128,128]{4,3,2,1,0:T(8,128)(2,1)}, u32[]{:S(2)}) %copy-start.3) | copy-done | bytes 8388632
  146.9 4.2 %mirror.3 = (f32[2,2,128,128]{3,2,1,0:T(8,128)S(1)}, bf16[2,2,128,128]{3,2,1,0:T(8,128)(2,1)S(1)}, bf16[2,2,128,128]{3,2,1,0:T(8,128)(2,1)S(1)}, bf16[2,2,128,128]{3,2,1,0:T(8,128)(2,1)S(1)}) custom-call(s32[272]{0:T(512)S(1)} %broadcast_add_fusion.tab, s32[3]{0:T(128)S(1)} %pad_add_fusion.place, bf16[8,2,128,128]{3,2,1,0:T(8,128)(2,1)S(1)} %all_to_all.20.x_ref, ...), custom_call_target="tpu_custom_call" | custom-call | flops 1073741824 | bytes 4194304 | tf_op jit(solution)/shard_map/mirror/pallas_call | solution.py:199
  151.1 0.7 collective-permute-start.19
  151.8 0.9 collective-permute-start.21
  152.6 3.7 %collective-permute-done.19.o1_ref = bf16[2,2,128,128]{3,2,1,0:T(8,128)(2,1)S(1)} collective-permute-done((bf16[2,2,128,128]{3,2,1,0:T(8,128)(2,1)S(1)}, bf16[2,2,128,128]{3,2,1,0:T(8,128)(2,1)S(1)}, u32[]{:S(2)}, u32[]{:S(2)}) %collective-permute-start.19) | collective-permute-done | bytes 131104 | tf_op jit(solution)/shard_map/ppermute | solution.py:276
  156.3 1.8 collective-permute-done.20.o2_ref
  158.1 3.4 %collective-permute-done.21.o3_ref = bf16[2,2,128,128]{3,2,1,0:T(8,128)(2,1)S(1)} collective-permute-done((bf16[2,2,128,128]{3,2,1,0:T(8,128)(2,1)S(1)}, bf16[2,2,128,128]{3,2,1,0:T(8,128)(2,1)S(1)}, u32[]{:S(2)}, u32[]{:S(2)}) %collective-permute-start.21) | collective-permute-done | bytes 131104 | tf_op jit(solution)/shard_map/ppermute | solution.py:276
  161.5 0.1 gathered.3
  161.7 7.1 %collective-permute-start.22 = (f32[256,128]{1,0:T(8,128)S(1)}, f32[256,128]{1,0:T(8,128)S(1)}, u32[]{:S(2)}, u32[]{:S(2)}) collective-permute-start(f32[256,128]{1,0:T(8,128)S(1)} %get-tuple-element.52), channel_id=1, source_target_pairs={{0,0},{16,1},{32,2},{48,3},{64,4},{80,5},{96,6},{112,7},{1,8},{17,... | collective-permute-start | bytes 393224 | tf_op jit(solution)/shard_map/ppermute | solution.py:281
  168.8 4.7 %collective-permute-start.23 = (f32[256,128]{1,0:T(8,128)S(1)}, f32[256,128]{1,0:T(8,128)S(1)}, u32[]{:S(2)}, u32[]{:S(2)}) collective-permute-start(f32[256,128]{1,0:T(8,128)S(1)} %get-tuple-element.53), channel_id=1, source_target_pairs={{16,0},{0,1},{48,2},{32,3},{80,4},{64,5},{112,6},{96,7},{17,8},{1,... | collective-permute-start | bytes 393224 | tf_op jit(solution)/shard_map/ppermute | solution.py:281
  173.5 5.1 %collective-permute-done.22.near_ref = f32[256,128]{1,0:T(8,128)S(1)} collective-permute-done((f32[256,128]{1,0:T(8,128)S(1)}, f32[256,128]{1,0:T(8,128)S(1)}, u32[]{:S(2)}, u32[]{:S(2)}) %collective-permute-start.22) | collective-permute-done | bytes 131104 | tf_op jit(solution)/shard_map/ppermute | solution.py:281
  178.6 4.1 %collective-permute-done.23.far_ref = f32[256,128]{1,0:T(8,128)S(1)} collective-permute-done((f32[256,128]{1,0:T(8,128)S(1)}, f32[256,128]{1,0:T(8,128)S(1)}, u32[]{:S(2)}, u32[]{:S(2)}) %collective-permute-start.23) | collective-permute-done | bytes 131104 | tf_op jit(solution)/shard_map/ppermute | solution.py:281
  182.7 1.3 last.1
  (48 shorter events, 1.0 us)
Async XLA Ops:
  0.0 0.9 copy-start.4
  0.9 0.7 copy-start.6
  3.0 16.5 %collective-permute-start.1 = (bf16[256,128]{1,0:T(8,128)(2,1)S(1)}, bf16[256,128]{1,0:T(8,128)(2,1)S(1)}, u32[]{:S(2)}, u32[]{:S(2)}) collective-permute-start(bf16[256,128]{1,0:T(8,128)(2,1)S(1)} %get-tuple-element.31), channel_id=1, source_target_pairs={{0,16},{1,0},{2,48},{3,32},{4,80},{5,64},{6,112},{7,96},{8,17},{9,... | collective-permute-start | bytes 196616 | tf_op jit(solution)/shard_map/ppermute | solution.py:250
  9.3 11.7 %collective-permute-start = (bf16[256,128]{1,0:T(8,128)(2,1)S(1)}, bf16[256,128]{1,0:T(8,128)(2,1)S(1)}, u32[]{:S(2)}, u32[]{:S(2)}) collective-permute-start(bf16[256,128]{1,0:T(8,128)(2,1)S(1)} %get-tuple-element.31), channel_id=1, source_target_pairs={{0,0},{1,16},{2,32},{3,48},{4,64},{5,80},{6,96},{7,112},{8,1},{9,1... | collective-permute-start | bytes 196616 | tf_op jit(solution)/shard_map/ppermute | solution.py:250
  14.0 26.4 %all-to-all-start = ((bf16[8,2,128,128]{3,2,1,0:T(8,128)(2,1)}), bf16[8,2,128,128]{3,2,1,0:T(8,128)(2,1)S(1)}, u32[]{:S(2)}, u32[]{:S(2)}) async-start(bf16[8,2,128,128]{3,2,1,0:T(8,128)(2,1)} %get-tuple-element.30), calls=%async_computation | async-start | bytes 1048576 | tf_op jit(solution)/shard_map/all_to_all | solution.py:247
  21.0 4.2 %collective-permute-start.2 = (bf16[2,256,128]{2,1,0:T(8,128)(2,1)S(1)}, bf16[2,256,128]{2,1,0:T(8,128)(2,1)S(1)}, u32[]{:S(2)}, u32[]{:S(2)}) collective-permute-start(bf16[2,256,128]{2,1,0:T(8,128)(2,1)S(1)} %pad_maximum_fusion.x0_ref), channel_id=1, source_target_pairs={{0,32},{32,64},{64,96},{96,0},{1,33},{33,65},{65,97},{97,1},{2,34}... | collective-permute-start | bytes 393224 | tf_op jit(solution)/shard_map/ppermute | solution.py:252
  21.1 5.7 %collective-permute-start.3 = (bf16[2,256,128]{2,1,0:T(8,128)(2,1)S(1)}, bf16[2,256,128]{2,1,0:T(8,128)(2,1)S(1)}, u32[]{:S(2)}, u32[]{:S(2)}) collective-permute-start(bf16[2,256,128]{2,1,0:T(8,128)(2,1)S(1)} %pad_maximum_fusion.x0_ref), channel_id=1, source_target_pairs={{0,64},{32,96},{64,0},{96,32},{1,65},{33,97},{65,1},{97,33},{2,66}... | collective-permute-start | bytes 393224 | tf_op jit(solution)/shard_map/ppermute | solution.py:252
  22.2 6.5 %collective-permute-start.4 = (bf16[2,256,128]{2,1,0:T(8,128)(2,1)S(1)}, bf16[2,256,128]{2,1,0:T(8,128)(2,1)S(1)}, u32[]{:S(2)}, u32[]{:S(2)}) collective-permute-start(bf16[2,256,128]{2,1,0:T(8,128)(2,1)S(1)} %pad_maximum_fusion.x0_ref), channel_id=1, source_target_pairs={{0,96},{32,0},{64,32},{96,64},{1,97},{33,1},{65,33},{97,65},{2,98}... | collective-permute-start | bytes 393224 | tf_op jit(solution)/shard_map/ppermute | solution.py:252
  28.7 3.4 %copy-start = (bf16[1,1,256,128,128]{4,3,2,1,0:T(8,128)(2,1)S(1)}, bf16[1,1,256,128,128]{4,3,2,1,0:T(8,128)(2,1)}, u32[]{:S(2)}) copy-start(bf16[1,1,256,128,128]{4,3,2,1,0:T(8,128)(2,1)} %param.8) | copy-start | bytes 25165828
  37.3 52.6 %copy-start.5 = (f32[256,128]{1,0:T(8,128)S(1)}, f32[256,128]{1,0:T(8,128)}, u32[]{:S(2)}) copy-start(f32[256,128]{1,0:T(8,128)} %vectors_ref.5) | copy-start | bytes 393220
  37.3 52.6 %copy-start.7 = (s32[2]{0:T(128)S(1)}, s32[2]{0:T(128)}, u32[]{:S(2)}) copy-start(s32[2]{0:T(128)} %widths.5) | copy-start | bytes 28
  37.3 5.3 %collective-permute-start.5 = (f32[8,256,128]{2,1,0:T(8,128)}, f32[8,256,128]{2,1,0:T(8,128)S(1)}, u32[]{:S(2)}, u32[]{:S(2)}) collective-permute-start(f32[8,256,128]{2,1,0:T(8,128)} %get-tuple-element.34), channel_id=1, source_target_pairs={{0,1},{1,0},{2,3},{3,2},{4,5},{5,4},{6,7},{7,6},{8,9},{9,8},{10,11... | collective-permute-start | bytes 3145736 | tf_op jit(solution)/shard_map/ppermute | solution.py:263
  40.4 9.2 %collective-permute-start.6 = (bf16[8,2,128,128]{3,2,1,0:T(8,128)(2,1)S(1)}, bf16[8,2,128,128]{3,2,1,0:T(8,128)(2,1)}, u32[]{:S(2)}, u32[]{:S(2)}) collective-permute-start(bf16[8,2,128,128]{3,2,1,0:T(8,128)(2,1)S(1)} %all-to-all-done.x_ref), channel_id=1, source_target_pairs={{0,1},{1,0},{2,3},{3,2},{4,5},{5,4},{6,7},{7,6},{8,9},{9,8},{10,11... | collective-permute-start | bytes 1572872 | tf_op jit(solution)/shard_map/ppermute | solution.py:253
  43.5 46.4 %all-to-all-start.1 = ((bf16[8,256,128]{2,1,0:T(8,128)(2,1)}), bf16[8,256,128]{2,1,0:T(8,128)(2,1)S(1)}, u32[]{:S(2)}, u32[]{:S(2)}) async-start(bf16[8,256,128]{2,1,0:T(8,128)(2,1)} %both.2), calls=%async_computation.1 | async-start | bytes 1048576 | tf_op jit(solution)/shard_map/all_to_all | solution.py:247
  49.6 3.4 %copy-start.1 = (bf16[1,1,256,128,128]{4,3,2,1,0:T(8,128)(2,1)S(1)}, bf16[1,1,256,128,128]{4,3,2,1,0:T(8,128)(2,1)}, u32[]{:S(2)}) copy-start(bf16[1,1,256,128,128]{4,3,2,1,0:T(8,128)(2,1)} %param.8) | copy-start | bytes 25165828
  57.7 4.5 %collective-permute-start.7 = (bf16[2,2,128,128]{3,2,1,0:T(8,128)(2,1)S(1)}, bf16[2,2,128,128]{3,2,1,0:T(8,128)(2,1)S(1)}, u32[]{:S(2)}, u32[]{:S(2)}) collective-permute-start(bf16[2,2,128,128]{3,2,1,0:T(8,128)(2,1)S(1)} %get-tuple-element.37), channel_id=1, source_target_pairs={{0,32},{32,64},{64,96},{96,0},{1,33},{33,65},{65,97},{97,1},{2,34}... | collective-permute-start | bytes 393224 | tf_op jit(solution)/shard_map/ppermute | solution.py:276
  58.9 5.4 %collective-permute-start.8 = (bf16[2,2,128,128]{3,2,1,0:T(8,128)(2,1)S(1)}, bf16[2,2,128,128]{3,2,1,0:T(8,128)(2,1)S(1)}, u32[]{:S(2)}, u32[]{:S(2)}) collective-permute-start(bf16[2,2,128,128]{3,2,1,0:T(8,128)(2,1)S(1)} %get-tuple-element.38), channel_id=1, source_target_pairs={{0,64},{32,96},{64,0},{96,32},{1,65},{33,97},{65,1},{97,33},{2,66}... | collective-permute-start | bytes 393224 | tf_op jit(solution)/shard_map/ppermute | solution.py:276
  58.9 9.3 %collective-permute-start.9 = (bf16[2,2,128,128]{3,2,1,0:T(8,128)(2,1)S(1)}, bf16[2,2,128,128]{3,2,1,0:T(8,128)(2,1)S(1)}, u32[]{:S(2)}, u32[]{:S(2)}) collective-permute-start(bf16[2,2,128,128]{3,2,1,0:T(8,128)(2,1)S(1)} %get-tuple-element.39), channel_id=1, source_target_pairs={{0,96},{32,0},{64,32},{96,64},{1,97},{33,1},{65,33},{97,65},{2,98}... | collective-permute-start | bytes 393224 | tf_op jit(solution)/shard_map/ppermute | solution.py:276
  68.4 16.5 %collective-permute-start.10 = (f32[256,128]{1,0:T(8,128)S(1)}, f32[256,128]{1,0:T(8,128)S(1)}, u32[]{:S(2)}, u32[]{:S(2)}) collective-permute-start(f32[256,128]{1,0:T(8,128)S(1)} %get-tuple-element.40), channel_id=1, source_target_pairs={{0,0},{16,1},{32,2},{48,3},{64,4},{80,5},{96,6},{112,7},{1,8},{17,... | collective-permute-start | bytes 393224 | tf_op jit(solution)/shard_map/ppermute | solution.py:281
  76.2 13.7 %collective-permute-start.11 = (f32[256,128]{1,0:T(8,128)S(1)}, f32[256,128]{1,0:T(8,128)S(1)}, u32[]{:S(2)}, u32[]{:S(2)}) collective-permute-start(f32[256,128]{1,0:T(8,128)S(1)} %get-tuple-element.41), channel_id=1, source_target_pairs={{16,0},{0,1},{48,2},{32,3},{80,4},{64,5},{112,6},{96,7},{17,8},{1,... | collective-permute-start | bytes 393224 | tf_op jit(solution)/shard_map/ppermute | solution.py:281
  90.6 9.7 %collective-permute-start.13 = (bf16[256,128]{1,0:T(8,128)(2,1)S(1)}, bf16[256,128]{1,0:T(8,128)(2,1)S(1)}, u32[]{:S(2)}, u32[]{:S(2)}) collective-permute-start(bf16[256,128]{1,0:T(8,128)(2,1)S(1)} %get-tuple-element.43), channel_id=1, source_target_pairs={{0,16},{1,0},{2,48},{3,32},{4,80},{5,64},{6,112},{7,96},{8,17},{9,... | collective-permute-start | bytes 196616 | tf_op jit(solution)/shard_map/ppermute | solution.py:250
  93.9 11.3 %collective-permute-start.12 = (bf16[256,128]{1,0:T(8,128)(2,1)S(1)}, bf16[256,128]{1,0:T(8,128)(2,1)S(1)}, u32[]{:S(2)}, u32[]{:S(2)}) collective-permute-start(bf16[256,128]{1,0:T(8,128)(2,1)S(1)} %get-tuple-element.43), channel_id=1, source_target_pairs={{0,0},{1,16},{2,32},{3,48},{4,64},{5,80},{6,96},{7,112},{8,1},{9,1... | collective-permute-start | bytes 196616 | tf_op jit(solution)/shard_map/ppermute | solution.py:250
  105.2 5.0 %collective-permute-start.14 = (bf16[2,256,128]{2,1,0:T(8,128)(2,1)S(1)}, bf16[2,256,128]{2,1,0:T(8,128)(2,1)S(1)}, u32[]{:S(2)}, u32[]{:S(2)}) collective-permute-start(bf16[2,256,128]{2,1,0:T(8,128)(2,1)S(1)} %pad_maximum_fusion.1.x0_ref), channel_id=1, source_target_pairs={{0,32},{32,64},{64,96},{96,0},{1,33},{33,65},{65,97},{97,1},{2,34}... | collective-permute-start | bytes 393224 | tf_op jit(solution)/shard_map/ppermute | solution.py:252
  105.3 6.3 %collective-permute-start.15 = (bf16[2,256,128]{2,1,0:T(8,128)(2,1)S(1)}, bf16[2,256,128]{2,1,0:T(8,128)(2,1)S(1)}, u32[]{:S(2)}, u32[]{:S(2)}) collective-permute-start(bf16[2,256,128]{2,1,0:T(8,128)(2,1)S(1)} %pad_maximum_fusion.1.x0_ref), channel_id=1, source_target_pairs={{0,64},{32,96},{64,0},{96,32},{1,65},{33,97},{65,1},{97,33},{2,66}... | collective-permute-start | bytes 393224 | tf_op jit(solution)/shard_map/ppermute | solution.py:252
  105.4 7.6 %collective-permute-start.16 = (bf16[2,256,128]{2,1,0:T(8,128)(2,1)S(1)}, bf16[2,256,128]{2,1,0:T(8,128)(2,1)S(1)}, u32[]{:S(2)}, u32[]{:S(2)}) collective-permute-start(bf16[2,256,128]{2,1,0:T(8,128)(2,1)S(1)} %pad_maximum_fusion.1.x0_ref), channel_id=1, source_target_pairs={{0,96},{32,0},{64,32},{96,64},{1,97},{33,1},{65,33},{97,65},{2,98}... | collective-permute-start | bytes 393224 | tf_op jit(solution)/shard_map/ppermute | solution.py:252
  113.0 3.4 %copy-start.2 = (bf16[1,1,256,128,128]{4,3,2,1,0:T(8,128)(2,1)S(1)}, bf16[1,1,256,128,128]{4,3,2,1,0:T(8,128)(2,1)}, u32[]{:S(2)}) copy-start(bf16[1,1,256,128,128]{4,3,2,1,0:T(8,128)(2,1)} %param.8) | copy-start | bytes 25165828
  120.6 18.2 %collective-permute-start.17 = (f32[8,256,128]{2,1,0:T(8,128)S(1)}, f32[8,256,128]{2,1,0:T(8,128)S(1)}, u32[]{:S(2)}, u32[]{:S(2)}) collective-permute-start(f32[8,256,128]{2,1,0:T(8,128)S(1)} %get-tuple-element.46), channel_id=1, source_target_pairs={{0,1},{1,0},{2,3},{3,2},{4,5},{5,4},{6,7},{7,6},{8,9},{9,8},{10,11... | collective-permute-start | bytes 3145736 | tf_op jit(solution)/shard_map/ppermute | solution.py:263
  136.7 6.8 %collective-permute-start.18 = (bf16[8,2,128,128]{3,2,1,0:T(8,128)(2,1)S(1)}, bf16[8,2,128,128]{3,2,1,0:T(8,128)(2,1)S(1)}, u32[]{:S(2)}, u32[]{:S(2)}) collective-permute-start(bf16[8,2,128,128]{3,2,1,0:T(8,128)(2,1)S(1)} %all_to_all.20.x_ref), channel_id=1, source_target_pairs={{0,1},{1,0},{2,3},{3,2},{4,5},{5,4},{6,7},{7,6},{8,9},{9,8},{10,11... | collective-permute-start | bytes 1572872 | tf_op jit(solution)/shard_map/ppermute | solution.py:253
  139.8 42.9 %all-to-all-start.3 = ((bf16[8,256,128]{2,1,0:T(8,128)(2,1)}), bf16[8,256,128]{2,1,0:T(8,128)(2,1)S(1)}, u32[]{:S(2)}, u32[]{:S(2)}) async-start(bf16[8,256,128]{2,1,0:T(8,128)(2,1)} %both.3), calls=%async_computation.3 | async-start | bytes 1048576 | tf_op jit(solution)/shard_map/all_to_all | solution.py:247
  143.5 3.4 %copy-start.3 = (bf16[1,1,256,128,128]{4,3,2,1,0:T(8,128)(2,1)S(1)}, bf16[1,1,256,128,128]{4,3,2,1,0:T(8,128)(2,1)}, u32[]{:S(2)}) copy-start(bf16[1,1,256,128,128]{4,3,2,1,0:T(8,128)(2,1)} %param.8) | copy-start | bytes 25165828
  151.1 5.2 %collective-permute-start.19 = (bf16[2,2,128,128]{3,2,1,0:T(8,128)(2,1)S(1)}, bf16[2,2,128,128]{3,2,1,0:T(8,128)(2,1)S(1)}, u32[]{:S(2)}, u32[]{:S(2)}) collective-permute-start(bf16[2,2,128,128]{3,2,1,0:T(8,128)(2,1)S(1)} %get-tuple-element.49), channel_id=1, source_target_pairs={{0,32},{32,64},{64,96},{96,0},{1,33},{33,65},{65,97},{97,1},{2,34}... | collective-permute-start | bytes 393224 | tf_op jit(solution)/shard_map/ppermute | solution.py:276
  151.8 6.4 %collective-permute-start.20 = (bf16[2,2,128,128]{3,2,1,0:T(8,128)(2,1)S(1)}, bf16[2,2,128,128]{3,2,1,0:T(8,128)(2,1)S(1)}, u32[]{:S(2)}, u32[]{:S(2)}) collective-permute-start(bf16[2,2,128,128]{3,2,1,0:T(8,128)(2,1)S(1)} %get-tuple-element.50), channel_id=1, source_target_pairs={{0,64},{32,96},{64,0},{96,32},{1,65},{33,97},{65,1},{97,33},{2,66}... | collective-permute-start | bytes 393224 | tf_op jit(solution)/shard_map/ppermute | solution.py:276
  151.8 9.8 %collective-permute-start.21 = (bf16[2,2,128,128]{3,2,1,0:T(8,128)(2,1)S(1)}, bf16[2,2,128,128]{3,2,1,0:T(8,128)(2,1)S(1)}, u32[]{:S(2)}, u32[]{:S(2)}) collective-permute-start(bf16[2,2,128,128]{3,2,1,0:T(8,128)(2,1)S(1)} %get-tuple-element.51), channel_id=1, source_target_pairs={{0,96},{32,0},{64,32},{96,64},{1,97},{33,1},{65,33},{97,65},{2,98}... | collective-permute-start | bytes 393224 | tf_op jit(solution)/shard_map/ppermute | solution.py:276
  161.7 16.9 %collective-permute-start.22 = (f32[256,128]{1,0:T(8,128)S(1)}, f32[256,128]{1,0:T(8,128)S(1)}, u32[]{:S(2)}, u32[]{:S(2)}) collective-permute-start(f32[256,128]{1,0:T(8,128)S(1)} %get-tuple-element.52), channel_id=1, source_target_pairs={{0,0},{16,1},{32,2},{48,3},{64,4},{80,5},{96,6},{112,7},{1,8},{17,... | collective-permute-start | bytes 393224 | tf_op jit(solution)/shard_map/ppermute | solution.py:281
  168.8 13.9 %collective-permute-start.23 = (f32[256,128]{1,0:T(8,128)S(1)}, f32[256,128]{1,0:T(8,128)S(1)}, u32[]{:S(2)}, u32[]{:S(2)}) collective-permute-start(f32[256,128]{1,0:T(8,128)S(1)} %get-tuple-element.53), channel_id=1, source_target_pairs={{16,0},{0,1},{48,2},{32,3},{80,4},{64,5},{112,6},{96,7},{17,8},{1,... | collective-permute-start | bytes 393224 | tf_op jit(solution)/shard_map/ppermute | solution.py:281

commit v3 on v2

--- a/solution.py
+++ b/solution.py
@@ -76,42 +76,39 @@
     send_forms(first, plain_ref, flip_ref)
 
 
-def applied(widths, own_ref, near_ref, far_ref):
-    shape = (2, ATOM, VECS)
-    total = near_ref[...] + far_ref[...]
+def applied(widths, own_ref, back_ref):
+    shape = (2, ATOM, VECS)
+    total = back_ref[...]
     for k in range(8):
         total = total + own_ref[k].astype(F32)
     return total.reshape(shape) * keep_of(widths, shape, 1)
 
 
-def second_kernel(widths, own_ref, near_ref, far_ref, vectors_ref, out_ref, plain_ref, flip_ref):
+def second_kernel(widths, own_ref, back_ref, vectors_ref, out_ref, plain_ref, flip_ref):
     shape = (2, ATOM, VECS)
     first = vectors_ref[...].reshape(shape) * keep_of(widths, shape, 1)
-    second = applied(widths, own_ref, near_ref, far_ref) - CENTER * first
+    second = applied(widths, own_ref, back_ref) - CENTER * first
     out_ref[...] = second.reshape(2 * ATOM, VECS)
     send_forms(second, plain_ref, flip_ref)
 
 
-def last_kernel(widths, own_ref, near_ref, far_ref, vectors_ref, second_ref, out_ref):
+def last_kernel(widths, own_ref, back_ref, vectors_ref, second_ref, out_ref):
     shape = (2, ATOM, VECS)
     first = vectors_ref[...].reshape(shape) * keep_of(widths, shape, 1)
-    third = applied(widths, own_ref, near_ref, far_ref)
+    third = applied(widths, own_ref, back_ref)
     out = 2.0 * (third - CENTER * second_ref[...].reshape(shape)) - first
     out_ref[...] = out.reshape(2 * ATOM, VECS)
 
 
-def load_kernel(src_ref, out_ref, sem):
-    copy = pltpu.make_async_copy(src_ref, out_ref, sem)
-    copy.start()
-    copy.wait()
-
-
-def direct_kernel(tab, place, x0_ref, x1_ref, x2_ref, x3_ref, t_ref, mine_ref, other_ref, held):
-    co, y, xl = place[0], place[1], place[2]
-    for s, ref in enumerate((x0_ref, x1_ref, x2_ref, x3_ref)):
-        for rel in range(2):
-            k = 2 * jnp.bitwise_and(y - s + 4, 3) + jnp.bitwise_xor(xl, rel)
-            held[pl.ds(2 * k, 2)] = ref[rel].reshape(2, ATOM, VECS)
+def piece_at(place, i):
+    y, xl = i // 2, i % 2
+    return 2 * jnp.bitwise_and(y - place[1] + 4, 3) + xl
+
+
+def direct_kernel(tab, place, x_ref, t_ref, mine_ref, other_ref, held):
+    co = place[0]
+    for i in range(8):
+        held[pl.ds(2 * piece_at(place, i), 2)] = x_ref[i].reshape(2, ATOM, VECS)
     held[AC] = jnp.zeros((ATOM, VECS), BF)
 
     def product(a, q, n):
@@ -139,8 +136,8 @@
     lax.fori_loop(0, 8, step, 0)
 
 
-def mirror_kernel(tab, place, x_ref, y_ref, t_ref, o0_ref, o1_ref, o2_ref, o3_ref, held):
-    co, y, xl = place[0], place[1], place[2]
+def mirror_kernel(tab, place, x_ref, y_ref, t_ref, out_ref, held):
+    co = place[0]
     for xz in range(8):
         held[pl.ds(4 * xz + 2 * co, 2)] = x_ref[xz]
         held[pl.ds(4 * xz + 2 - 2 * co, 2)] = y_ref[xz]
@@ -158,29 +155,28 @@
             left, right = jnp.concatenate(xs, 1), jnp.concatenate(blocks, 0)
         return jnp.dot(left, right, preferred_element_type=F32)
 
-    for s, out in enumerate((o0_ref, o1_ref, o2_ref, o3_ref)):
-
-        def step(rel, carry, s=s, out=out):
-            k = 2 * jnp.bitwise_and(y + s, 3) + jnp.bitwise_xor(xl, rel)
-            for t in range(2):
-                b = 2 * k + t
-                total = product(b, 0, 8) + product(b, 8, 8)
-                if not t:
-                    total = total + product(b, 16, 1)
-                out[rel, t] = total.astype(out.dtype)
-            return carry
-
-        lax.fori_loop(0, 2, step, 0)
-
-
-def gathered_kernel(o0_ref, o1_ref, o2_ref, o3_ref, near_ref, far_ref):
-    for rel, out in enumerate((near_ref, far_ref)):
-        total = o0_ref[rel] + o1_ref[rel].astype(F32) + o2_ref[rel].astype(F32) + o3_ref[rel].astype(F32)
-        out[...] = jnp.swapaxes(total, 1, 2).reshape(2 * ATOM, VECS)
+    def step(i, carry):
+        k = piece_at(place, i)
+        for t in range(2):
+            b = 2 * k + t
+            total = product(b, 0, 8) + product(b, 8, 8)
+            if not t:
+                total = total + product(b, 16, 1)
+            out_ref[i, t] = total.astype(out_ref.dtype)
+        return carry
+
+    lax.fori_loop(0, 8, step, 0)
+
+
+def gathered_kernel(got_ref, out_ref):
+    total = got_ref[0].astype(F32)
+    for i in range(1, 8):
+        total = total + got_ref[i].astype(F32)
+    out_ref[...] = jnp.swapaxes(total, 1, 2).reshape(2 * ATOM, VECS)
 
 
 def both_kernel(mine_ref, theirs_ref, out_ref):
-    out_ref[...] = (mine_ref[...] + theirs_ref[...]).astype(BF)
+    out_ref[...] = (mine_ref[...] + theirs_ref[...].astype(F32)).astype(BF)
 
 
 SMEM = pl.BlockSpec(memory_space=pltpu.SMEM)
@@ -208,79 +204,68 @@
     )(*scalars, *arrays)
 
 
-def load(tiles):
-    return pl.pallas_call(
-        load_kernel,
-        out_shape=pltpu.VMEM(tiles.shape, tiles.dtype),
-        in_specs=[pl.BlockSpec(memory_space=pl.ANY)],
-        scratch_shapes=[pltpu.SemaphoreType.DMA],
-        compiler_params=pltpu.CompilerParams(vmem_limit_bytes=2**20),
-        cost_estimate=pl.CostEstimate(flops=0, bytes_accessed=2**23, transcendentals=0),
-        name="load",
-    )(tiles)
-
-
-def pairs(rel):
-    return [
-        (r * 16 + c, ((c % 8) ^ rel) * 16 + 2 * r + c // 8) for r in range(8) for c in range(16)
-    ]
-
-
+def shift_of(column):
+    r = column // 2
+    return (r // 2 - r % 4 + 2 * (column % 2)) % 4
+
+
+def owners(r, c):
+    column = 2 * r + c // 8
+    y, xl = (c % 8 // 2 + shift_of(column)) % 4, c % 2
+    return (2 * y + xl) * 16 + column
+
+
+TO_COL = [(r * 16 + c, owners(r, c)) for r in range(8) for c in range(16)]
+TO_ROW = [(d, s) for s, d in TO_COL]
 SWAP = [(0, 1), (1, 0)]
-
-
-def turn(s):
-    return [(k, (k + s) % 4) for k in range(4)]
 
 
 def local(vectors, widths, tiles, block_rows, block_cols, block_count):
     row = lax.axis_index(ROWS)
     col = lax.axis_index(COLS)
-    place = jnp.stack([lax.axis_index(n) for n in ("co", "y", "xl")]).astype(jnp.int32)
+    place = jnp.stack([lax.axis_index("co"), shift_of(col)]).astype(jnp.int32)
     tile_set = tiles[0, 0]
     direct_tab, mirror_tab = tables(
         block_rows[0, 0], block_cols[0, 0], block_count[0, 0], row, col
     )
-    work = dict(flops=2 * SLOTS * ATOM**3, size=2**22)
-
-    def exchange(x):
-        return lax.all_to_all(x, ("xh", "z"), split_axis=0, concat_axis=0, tiled=True)
+    work = dict(flops=2 * SLOTS * ATOM**3, size=2**23)
+
+    def exchange(x, axes):
+        return lax.all_to_all(x, axes, split_axis=0, concat_axis=0, tiled=True)
 
     def apply_matrix(plain, flipped):
-        piece = jnp.stack([lax.ppermute(plain, ALL, pairs(rel)) for rel in range(2)])
-        near = exchange(flipped)
-        xs = [piece] + [lax.ppermute(piece, "y", turn(s)) for s in (1, 2, 3)]
+        piece = lax.ppermute(plain, ALL, TO_COL)
+        near = exchange(flipped, ("xh", "z"))
         far = lax.ppermute(near, "co", SWAP)
-        mine, other = call(
-            direct_kernel,
-            (like((8, *PIECE), F32), like((8, *PIECE), F32)),
-            (direct_tab, place),
-            (*xs, tile_set),
-            [pltpu.VMEM((AC + 1, ATOM, VECS), BF)],
-            name="direct",
-            **work,
-        )
-        theirs = lax.ppermute(other, "co", SWAP)
-        near, mine = lax.optimization_barrier((near, mine))
-        outs = call(
+        piece, near = lax.optimization_barrier((piece, near))
+        col_block = exchange(jnp.broadcast_to(piece[None], (8, *PIECE)), ROWS)
+        mirror = call(
             mirror_kernel,
-            (like((2, *BLOCKS), F32),) + (like((2, *BLOCKS), BF),) * 3,
+            like((8, *BLOCKS), BF),
             (mirror_tab, place),
             (near, far, tile_set),
             [pltpu.VMEM((AR + 1, VECS, ATOM), BF)],
             name="mirror",
             **work,
         )
+        col_block, mirror = lax.optimization_barrier((col_block, mirror))
+        got = exchange(mirror, ROWS)
+        mine, other = call(
+            direct_kernel,
+            (like((8, *PIECE), F32), like((8, *PIECE), BF)),
+            (direct_tab, place),
+            (col_block, tile_set),
+            [pltpu.VMEM((AC + 1, ATOM, VECS), BF)],
+            name="direct",
+            **work,
+        )
+        other, got = lax.optimization_barrier((other, got))
+        theirs = lax.ppermute(other, "co", SWAP)
         both = call(both_kernel, like((8, *PIECE), BF), (), (mine, theirs), name="both")
-        own = exchange(both)
-        outs = [outs[0]] + [lax.ppermute(outs[s], "y", turn(s)) for s in (1, 2, 3)]
-        sums = call(
-            gathered_kernel, (like(PIECE, F32), like(PIECE, F32)), (), tuple(outs), name="gathered"
-        )
-        back = [
-            lax.ppermute(sums[rel], ALL, [(d, s) for s, d in pairs(rel)]) for rel in range(2)
-        ]
-        return own, back[0], back[1]
+        own = exchange(both, ("xh", "z"))
+        gathered = call(gathered_kernel, like(PIECE, F32), (), (got,), name="gathered")
+        back = lax.ppermute(gathered, ALL, TO_ROW)
+        return own, back
 
     forms = (like(PIECE, BF), like((8, *BLOCKS), BF))
     plain, flipped = call(first_kernel, forms, (widths,), (vectors,), name="first")

time: 185 us -> 158 us (0.85)
  waiting for transfers between devices: 60.8 us -> 33 us
  blocking collectives: 16 us -> 13 us
  starting transfers between devices: 65.1 us -> 67 us
    ppermute x20 -> x4, waiting for transfers between devices: 58.9 us -> 29.9 us  [the longest x2 22.1 us: apply_matrix(): back = lax.ppermute(gathered, ALL, TO_ROW)]
    all_to_all x3 -> x7, starting transfers between devices: 13.3 us -> 35.7 us  [exchange(): return lax.all_to_all(x, axes, split_axis=0, concat_axis=0, tiled=True)]
    ppermute x20 -> x4, starting transfers between devices: 46.7 us -> 24.7 us  [the longest x2 13.7 us: apply_matrix(): back = lax.ppermute(gathered, ALL, TO_ROW)]
    all_to_all x1, blocking collectives: 16 us -> 13 us  [exchange(): return lax.all_to_all(x, axes, split_axis=0, concat_axis=0, tiled=True)]
  transfers between devices with their start and end apart: 27 -> 15, of which waited for: 20 -> 5; matrix products, arithmetic and copies ran while one was open for 1% -> 2% of each run, Pallas kernels for 9% -> 12%
where the time goes in v3:
time: 158 us; the launch traced here: 157 us
  starting transfers between devices  67 us (42%)
  waiting for transfers between devices  33 us (21%)
  Pallas kernels  24.1 us (15%)
  local copies, waits for them, and re-layouts  17.3 us (11%)
  blocking collectives  13 us (8%)
    all_to_all x7, starting transfers between devices, exchange(): return lax.all_to_all(x, axes, split_axis=0, concat_axis=0, tiled=True)  35.7 us
    pallas_call x11, Pallas kernels, call(): pl.pallas_call(kernel, out_shape=out_shape, in_specs=[SMEM] * len(scalars...  24.1 us
    ppermute x2, waiting for transfers between devices, apply_matrix(): back = lax.ppermute(gathered, ALL, TO_ROW)  22.1 us
    unnamed x16, local copies, waits for them, and re-layouts  15.1 us
    ppermute x2, starting transfers between devices, apply_matrix(): back = lax.ppermute(gathered, ALL, TO_ROW)  13.7 us
    all_to_all x1, blocking collectives, exchange(): return lax.all_to_all(x, axes, split_axis=0, concat_axis=0, tiled=True)  13 us
    ppermute x2, starting transfers between devices, apply_matrix(): piece = lax.ppermute(plain, ALL, TO_COL)  11.1 us
    ppermute x2, waiting for transfers between devices, apply_matrix(): piece = lax.ppermute(plain, ALL, TO_COL)  7.81 us
  transfers between devices with their start and end apart: 15, of which 5 were waited for; matrix products, arithmetic and copies ran while one was open for 2% of the time, Pallas kernels for 12%

profile of v3, /device:TPU:25, one launch (start us, length us, event | category | flops | bytes accessed | tf_op | source)
XLA Modules:
  0.0 156.8 jit_solution(14770796494986224030)
XLA Ops:
  0.0 0.9 copy-done.4
  0.9 0.7 copy-done.6
  1.6 1.5 first.1
  3.0 7.5 %all-to-all-start = ((bf16[8,2,128,128]{3,2,1,0:T(8,128)(2,1)}), bf16[8,2,128,128]{3,2,1,0:T(8,128)(2,1)S(1)}, u32[]{:S(2)}, u32[]{:S(2)}) async-start(bf16[8,2,128,128]{3,2,1,0:T(8,128)(2,1)} %get-tuple-element.27), calls=%async_computation | async-start | bytes 1048576 | tf_op jit(solution)/shard_map/all_to_all | solution.py:234
  10.5 8.8 %collective-permute-start = (bf16[256,128]{1,0:T(8,128)(2,1)S(1)}, bf16[256,128]{1,0:T(8,128)(2,1)S(1)}, u32[]{:S(2)}, u32[]{:S(2)}) collective-permute-start(bf16[256,128]{1,0:T(8,128)(2,1)S(1)} %get-tuple-element.26), channel_id=1, source_target_pairs={{0,0},{1,16},{2,32},{3,48},{4,64},{5,80},{6,96},{7,112},{8,65},{9,... | collective-permute-start | bytes 196616 | tf_op jit(solution)/shard_map/ppermute | solution.py:237
  20.1 0.1 add_select_fusion.1
  20.2 0.1 reshape.357
  20.3 0.1 add.295
  20.4 0.7 multiply_add_fusion.1
  21.1 0.2 select_reduce_fusion.1
  21.4 0.0 all-to-all-done.x_ref
  21.4 1.6 %collective-permute-start.1 = (bf16[8,2,128,128]{3,2,1,0:T(8,128)(2,1)S(1)}, bf16[8,2,128,128]{3,2,1,0:T(8,128)(2,1)S(1)}, u32[]{:S(2)}, u32[]{:S(2)}) collective-permute-start(bf16[8,2,128,128]{3,2,1,0:T(8,128)(2,1)S(1)} %all-to-all-done.x_ref), channel_id=1, source_target_pairs={{0,1},{1,0},{2,3},{3,2},{4,5},{5,4},{6,7},{7,6},{8,9},{9,8},{10,11... | collective-permute-start | bytes 1572872 | tf_op jit(solution)/shard_map/ppermute | solution.py:239
  23.1 0.0 collective-permute-done
  23.1 0.9 broadcast_in_dim.104
  23.9 4.2 %all-to-all-start.1 = ((bf16[8,256,128]{2,1,0:T(8,128)(2,1)}), bf16[8,256,128]{2,1,0:T(8,128)(2,1)S(1)}, u32[]{:S(2)}, u32[]{:S(2)}) async-start(bf16[8,256,128]{2,1,0:T(8,128)(2,1)} %broadcast_in_dim.104), calls=%async_computation.1 | async-start | bytes 1048576 | tf_op jit(solution)/shard_map/all_to_all | solution.py:234
  28.1 0.1 pad_add_fusion.place
  28.2 0.1 add_select_fusion
  28.3 0.0 collective-permute-done.1.y_ref
  28.3 0.0 copy-start
  28.3 3.4 %copy-done = bf16[1,1,256,128,128]{4,3,2,1,0:T(8,128)(2,1)S(1)} copy-done((bf16[1,1,256,128,128]{4,3,2,1,0:T(8,128)(2,1)S(1)}, bf16[1,1,256,128,128]{4,3,2,1,0:T(8,128)(2,1)}, u32[]{:S(2)}) %copy-start) | copy-done | bytes 8388632
  31.7 5.1 %mirror.2 = bf16[8,2,128,128]{3,2,1,0:T(8,128)(2,1)} custom-call(s32[272]{0:T(512)S(1)} %broadcast_add_fusion.tab, s32[2]{0:T(128)S(1)} %pad_add_fusion.place, bf16[8,2,128,128]{3,2,1,0:T(8,128)(2,1)S(1)} %all-to-all-done.x_ref, bf16[8,2,128,128]{3,2,1,0:T(8,128)(2,1)S(1)} %collective-permute-done.1.y_ref, bf16[256,128,128]{2,1,0:T(8,128)(2,1)S(1)} %bitcast.6), custom_call_target="tpu_custom_call" | custom-call | flops 1073741824 | bytes 8388608 | tf_op jit(solution)/shard_map/mirror/pallas_call | solution.py:195
  36.8 0.0 all-to-all-done.1.x_ref
  36.8 5.3 %all-to-all-start.2 = ((bf16[8,2,128,128]{3,2,1,0:T(8,128)(2,1)}), bf16[8,2,128,128]{3,2,1,0:T(8,128)(2,1)S(1)}, u32[]{:S(2)}, u32[]{:S(2)}) async-start(bf16[8,2,128,128]{3,2,1,0:T(8,128)(2,1)} %mirror.2), calls=%async_computation.2 | async-start | bytes 1048576 | tf_op jit(solution)/shard_map/all_to_all | solution.py:234
  42.0 0.1 reshape.356
  42.1 0.1 add.260
  42.2 0.1 add.261
  42.3 0.3 select_reduce_fusion
  42.6 0.0 copy-start.1
  42.6 3.4 %copy-done.1 = bf16[1,1,256,128,128]{4,3,2,1,0:T(8,128)(2,1)S(1)} copy-done((bf16[1,1,256,128,128]{4,3,2,1,0:T(8,128)(2,1)S(1)}, bf16[1,1,256,128,128]{4,3,2,1,0:T(8,128)(2,1)}, u32[]{:S(2)}) %copy-start.1) | copy-done | bytes 8388632
  46.0 4.2 %direct.2 = (f32[8,256,128]{2,1,0:T(8,128)S(1)}, bf16[8,256,128]{2,1,0:T(8,128)(2,1)S(1)}) custom-call(s32[288]{0:T(512)S(1)} %broadcast_add_fusion.1.tab, s32[2]{0:T(128)S(1)} %pad_add_fusion.place, bf16[8,256,128]{2,1,0:T(8,128)(2,1)S(1)} %all-to-all-done.1.x_ref, bf16[256,128,128]{2,1,0:T(8,128)(2,1)S(1)} %bitcast.7), custom_call_target="tpu_custom_call" | custom-call | flops 1073741824 | bytes 8388608 | tf_op jit(solution)/shard_map/direct/pallas_call | solution.py:195
  50.2 0.0 all-to-all-done.2.got_ref
  50.2 1.2 collective-permute-start.2
  51.4 1.5 collective-permute-done.2.theirs_ref
  53.0 0.9 both.2
  53.9 6.1 %all-to-all-start.3 = ((bf16[8,256,128]{2,1,0:T(8,128)(2,1)}), bf16[8,256,128]{2,1,0:T(8,128)(2,1)S(1)}, u32[]{:S(2)}, u32[]{:S(2)}) async-start(bf16[8,256,128]{2,1,0:T(8,128)(2,1)} %both.2), calls=%async_computation.3 | async-start | bytes 1048576 | tf_op jit(solution)/shard_map/all_to_all | solution.py:234
  60.0 0.1 gathered.2
  60.1 6.4 %collective-permute-start.3 = (f32[256,128]{1,0:T(8,128)S(1)}, f32[256,128]{1,0:T(8,128)S(1)}, u32[]{:S(2)}, u32[]{:S(2)}) collective-permute-start(f32[256,128]{1,0:T(8,128)S(1)} %gathered.2), channel_id=1, source_target_pairs={{0,0},{16,1},{32,2},{48,3},{64,4},{80,5},{96,6},{112,7},{65,8},{81... | collective-permute-start | bytes 393224 | tf_op jit(solution)/shard_map/ppermute | solution.py:267
  66.6 10.9 %collective-permute-done.3.back_ref = f32[256,128]{1,0:T(8,128)S(1)} collective-permute-done((f32[256,128]{1,0:T(8,128)S(1)}, f32[256,128]{1,0:T(8,128)S(1)}, u32[]{:S(2)}, u32[]{:S(2)}) %collective-permute-start.3) | collective-permute-done | bytes 131104 | tf_op jit(solution)/shard_map/ppermute | solution.py:267
  77.5 0.0 all-to-all-done.3.own_ref
  77.5 0.0 copy-done.5
  77.5 0.7 second.1
  78.2 13.0 %all_to_all.40.x_ref = bf16[8,2,128,128]{3,2,1,0:T(8,128)(2,1)S(1)} all-to-all(bf16[8,2,128,128]{3,2,1,0:T(8,128)(2,1)S(1)} %get-tuple-element.37), channel_id=1, replica_groups=mesh['y'=4,'xl'=2,'xh'=2,'z'=4,'co'=2] {'xh','z'}, dimensions={0} | all-to-all | bytes 1048576 | tf_op jit(solution)/shard_map/all_to_all | solution.py:234
  91.2 1.6 %collective-permute-start.5 = (bf16[8,2,128,128]{3,2,1,0:T(8,128)(2,1)S(1)}, bf16[8,2,128,128]{3,2,1,0:T(8,128)(2,1)S(1)}, u32[]{:S(2)}, u32[]{:S(2)}) collective-permute-start(bf16[8,2,128,128]{3,2,1,0:T(8,128)(2,1)S(1)} %all_to_all.40.x_ref), channel_id=1, source_target_pairs={{0,1},{1,0},{2,3},{3,2},{4,5},{5,4},{6,7},{7,6},{8,9},{9,8},{10,11... | collective-permute-start | bytes 1572872 | tf_op jit(solution)/shard_map/ppermute | solution.py:239
  92.8 2.3 %collective-permute-start.4 = (bf16[256,128]{1,0:T(8,128)(2,1)S(1)}, bf16[256,128]{1,0:T(8,128)(2,1)S(1)}, u32[]{:S(2)}, u32[]{:S(2)}) collective-permute-start(bf16[256,128]{1,0:T(8,128)(2,1)S(1)} %get-tuple-element.36), channel_id=1, source_target_pairs={{0,0},{1,16},{2,32},{3,48},{4,64},{5,80},{6,96},{7,112},{8,65},{9,... | collective-permute-start | bytes 196616 | tf_op jit(solution)/shard_map/ppermute | solution.py:237
  95.1 7.8 %collective-permute-done.4 = bf16[256,128]{1,0:T(8,128)(2,1)S(1)} collective-permute-done((bf16[256,128]{1,0:T(8,128)(2,1)S(1)}, bf16[256,128]{1,0:T(8,128)(2,1)S(1)}, u32[]{:S(2)}, u32[]{:S(2)}) %collective-permute-start.4) | collective-permute-done | bytes 65568 | tf_op jit(solution)/shard_map/ppermute | solution.py:237
  102.9 0.9 broadcast_in_dim.112
  103.8 4.0 %all-to-all-start.5 = ((bf16[8,256,128]{2,1,0:T(8,128)(2,1)}), bf16[8,256,128]{2,1,0:T(8,128)(2,1)S(1)}, u32[]{:S(2)}, u32[]{:S(2)}) async-start(bf16[8,256,128]{2,1,0:T(8,128)(2,1)} %broadcast_in_dim.112), calls=%async_computation.5 | async-start | bytes 1048576 | tf_op jit(solution)/shard_map/all_to_all | solution.py:234
  107.7 0.0 collective-permute-done.5.y_ref
  107.8 3.4 %copy-done.2 = bf16[1,1,256,128,128]{4,3,2,1,0:T(8,128)(2,1)S(1)} copy-done((bf16[1,1,256,128,128]{4,3,2,1,0:T(8,128)(2,1)S(1)}, bf16[1,1,256,128,128]{4,3,2,1,0:T(8,128)(2,1)}, u32[]{:S(2)}) %copy-start.2) | copy-done | bytes 8388632
  111.1 5.1 %mirror.3 = bf16[8,2,128,128]{3,2,1,0:T(8,128)(2,1)} custom-call(s32[272]{0:T(512)S(1)} %broadcast_add_fusion.tab, s32[2]{0:T(128)S(1)} %pad_add_fusion.place, bf16[8,2,128,128]{3,2,1,0:T(8,128)(2,1)S(1)} %all_to_all.40.x_ref, bf16[8,2,128,128]{3,2,1,0:T(8,128)(2,1)S(1)} %collective-permute-done.5.y_ref, bf16[256,128,128]{2,1,0:T(8,128)(2,1)S(1)} %bitcast.8), custom_call_target="tpu_custom_call" | custom-call | flops 1073741824 | bytes 8388608 | tf_op jit(solution)/shard_map/mirror/pallas_call | solution.py:195
  116.2 0.0 all-to-all-done.5.x_ref
  116.2 5.1 %all-to-all-start.6 = ((bf16[8,2,128,128]{3,2,1,0:T(8,128)(2,1)}), bf16[8,2,128,128]{3,2,1,0:T(8,128)(2,1)S(1)}, u32[]{:S(2)}, u32[]{:S(2)}) async-start(bf16[8,2,128,128]{3,2,1,0:T(8,128)(2,1)} %mirror.3), calls=%async_computation.6 | async-start | bytes 1048576 | tf_op jit(solution)/shard_map/all_to_all | solution.py:234
  121.4 3.4 %copy-done.3 = bf16[1,1,256,128,128]{4,3,2,1,0:T(8,128)(2,1)S(1)} copy-done((bf16[1,1,256,128,128]{4,3,2,1,0:T(8,128)(2,1)S(1)}, bf16[1,1,256,128,128]{4,3,2,1,0:T(8,128)(2,1)}, u32[]{:S(2)}) %copy-start.3) | copy-done | bytes 8388632
  124.7 4.2 %direct.3 = (f32[8,256,128]{2,1,0:T(8,128)S(1)}, bf16[8,256,128]{2,1,0:T(8,128)(2,1)S(1)}) custom-call(s32[288]{0:T(512)S(1)} %broadcast_add_fusion.1.tab, s32[2]{0:T(128)S(1)} %pad_add_fusion.place, bf16[8,256,128]{2,1,0:T(8,128)(2,1)S(1)} %all-to-all-done.5.x_ref, bf16[256,128,128]{2,1,0:T(8,128)(2,1)S(1)} %bitcast.9), custom_call_target="tpu_custom_call" | custom-call | flops 1073741824 | bytes 8388608 | tf_op jit(solution)/shard_map/direct/pallas_call | solution.py:195
  129.0 0.0 all-to-all-done.6.got_ref
  129.0 2.2 %collective-permute-start.6 = (bf16[8,256,128]{2,1,0:T(8,128)(2,1)S(1)}, bf16[8,256,128]{2,1,0:T(8,128)(2,1)S(1)}, u32[]{:S(2)}, u32[]{:S(2)}) collective-permute-start(bf16[8,256,128]{2,1,0:T(8,128)(2,1)S(1)} %get-tuple-element.44), channel_id=1, source_target_pairs={{0,1},{1,0},{2,3},{3,2},{4,5},{5,4},{6,7},{7,6},{8,9},{9,8},{10,11... | collective-permute-start | bytes 1572872 | tf_op jit(solution)/shard_map/ppermute | solution.py:263
  131.1 1.5 collective-permute-done.6.theirs_ref
  132.7 0.9 both.3
  133.5 3.5 %all-to-all-start.7 = ((bf16[8,256,128]{2,1,0:T(8,128)(2,1)}), bf16[8,256,128]{2,1,0:T(8,128)(2,1)S(1)}, u32[]{:S(2)}, u32[]{:S(2)}) async-start(bf16[8,256,128]{2,1,0:T(8,128)(2,1)} %both.3), calls=%async_computation.7 | async-start | bytes 1048576 | tf_op jit(solution)/shard_map/all_to_all | solution.py:234
  137.0 0.1 gathered.3
  137.2 7.2 %collective-permute-start.7 = (f32[256,128]{1,0:T(8,128)S(1)}, f32[256,128]{1,0:T(8,128)S(1)}, u32[]{:S(2)}, u32[]{:S(2)}) collective-permute-start(f32[256,128]{1,0:T(8,128)S(1)} %gathered.3), channel_id=1, source_target_pairs={{0,0},{16,1},{32,2},{48,3},{64,4},{80,5},{96,6},{112,7},{65,8},{81... | collective-permute-start | bytes 393224 | tf_op jit(solution)/shard_map/ppermute | solution.py:267
  144.4 11.1 %collective-permute-done.7.back_ref = f32[256,128]{1,0:T(8,128)S(1)} collective-permute-done((f32[256,128]{1,0:T(8,128)S(1)}, f32[256,128]{1,0:T(8,128)S(1)}, u32[]{:S(2)}, u32[]{:S(2)}) %collective-permute-start.7) | collective-permute-done | bytes 131104 | tf_op jit(solution)/shard_map/ppermute | solution.py:267
  155.5 0.0 all-to-all-done.7.own_ref
  155.5 1.3 last.1
  (24 shorter events, 0.1 us)
Async XLA Ops:
  0.0 0.9 copy-start.4
  0.9 0.7 copy-start.6
  3.0 18.4 %all-to-all-start = ((bf16[8,2,128,128]{3,2,1,0:T(8,128)(2,1)}), bf16[8,2,128,128]{3,2,1,0:T(8,128)(2,1)S(1)}, u32[]{:S(2)}, u32[]{:S(2)}) async-start(bf16[8,2,128,128]{3,2,1,0:T(8,128)(2,1)} %get-tuple-element.27), calls=%async_computation | async-start | bytes 1048576 | tf_op jit(solution)/shard_map/all_to_all | solution.py:234
  10.5 12.5 %collective-permute-start = (bf16[256,128]{1,0:T(8,128)(2,1)S(1)}, bf16[256,128]{1,0:T(8,128)(2,1)S(1)}, u32[]{:S(2)}, u32[]{:S(2)}) collective-permute-start(bf16[256,128]{1,0:T(8,128)(2,1)S(1)} %get-tuple-element.26), channel_id=1, source_target_pairs={{0,0},{1,16},{2,32},{3,48},{4,64},{5,80},{6,96},{7,112},{8,65},{9,... | collective-permute-start | bytes 196616 | tf_op jit(solution)/shard_map/ppermute | solution.py:237
  21.4 6.9 %collective-permute-start.1 = (bf16[8,2,128,128]{3,2,1,0:T(8,128)(2,1)S(1)}, bf16[8,2,128,128]{3,2,1,0:T(8,128)(2,1)S(1)}, u32[]{:S(2)}, u32[]{:S(2)}) collective-permute-start(bf16[8,2,128,128]{3,2,1,0:T(8,128)(2,1)S(1)} %all-to-all-done.x_ref), channel_id=1, source_target_pairs={{0,1},{1,0},{2,3},{3,2},{4,5},{5,4},{6,7},{7,6},{8,9},{9,8},{10,11... | collective-permute-start | bytes 1572872 | tf_op jit(solution)/shard_map/ppermute | solution.py:239
  23.9 12.8 %all-to-all-start.1 = ((bf16[8,256,128]{2,1,0:T(8,128)(2,1)}), bf16[8,256,128]{2,1,0:T(8,128)(2,1)S(1)}, u32[]{:S(2)}, u32[]{:S(2)}) async-start(bf16[8,256,128]{2,1,0:T(8,128)(2,1)} %broadcast_in_dim.104), calls=%async_computation.1 | async-start | bytes 1048576 | tf_op jit(solution)/shard_map/all_to_all | solution.py:234
  28.3 3.4 %copy-start = (bf16[1,1,256,128,128]{4,3,2,1,0:T(8,128)(2,1)S(1)}, bf16[1,1,256,128,128]{4,3,2,1,0:T(8,128)(2,1)}, u32[]{:S(2)}) copy-start(bf16[1,1,256,128,128]{4,3,2,1,0:T(8,128)(2,1)} %param.8) | copy-start | bytes 25165828
  36.7 40.7 %copy-start.5 = (f32[256,128]{1,0:T(8,128)S(1)}, f32[256,128]{1,0:T(8,128)}, u32[]{:S(2)}) copy-start(f32[256,128]{1,0:T(8,128)} %vectors_ref.5) | copy-start | bytes 393220
  36.7 40.7 %copy-start.7 = (s32[2]{0:T(128)S(1)}, s32[2]{0:T(128)}, u32[]{:S(2)}) copy-start(s32[2]{0:T(128)} %widths.5) | copy-start | bytes 28
  36.8 13.5 %all-to-all-start.2 = ((bf16[8,2,128,128]{3,2,1,0:T(8,128)(2,1)}), bf16[8,2,128,128]{3,2,1,0:T(8,128)(2,1)S(1)}, u32[]{:S(2)}, u32[]{:S(2)}) async-start(bf16[8,2,128,128]{3,2,1,0:T(8,128)(2,1)} %mirror.2), calls=%async_computation.2 | async-start | bytes 1048576 | tf_op jit(solution)/shard_map/all_to_all | solution.py:234
  42.6 3.4 %copy-start.1 = (bf16[1,1,256,128,128]{4,3,2,1,0:T(8,128)(2,1)S(1)}, bf16[1,1,256,128,128]{4,3,2,1,0:T(8,128)(2,1)}, u32[]{:S(2)}) copy-start(bf16[1,1,256,128,128]{4,3,2,1,0:T(8,128)(2,1)} %param.8) | copy-start | bytes 25165828
  50.2 2.7 %collective-permute-start.2 = (bf16[8,256,128]{2,1,0:T(8,128)(2,1)S(1)}, bf16[8,256,128]{2,1,0:T(8,128)(2,1)S(1)}, u32[]{:S(2)}, u32[]{:S(2)}) collective-permute-start(bf16[8,256,128]{2,1,0:T(8,128)(2,1)S(1)} %get-tuple-element.34), channel_id=1, source_target_pairs={{0,1},{1,0},{2,3},{3,2},{4,5},{5,4},{6,7},{7,6},{8,9},{9,8},{10,11... | collective-permute-start | bytes 1572872 | tf_op jit(solution)/shard_map/ppermute | solution.py:263
  53.9 23.6 %all-to-all-start.3 = ((bf16[8,256,128]{2,1,0:T(8,128)(2,1)}), bf16[8,256,128]{2,1,0:T(8,128)(2,1)S(1)}, u32[]{:S(2)}, u32[]{:S(2)}) async-start(bf16[8,256,128]{2,1,0:T(8,128)(2,1)} %both.2), calls=%async_computation.3 | async-start | bytes 1048576 | tf_op jit(solution)/shard_map/all_to_all | solution.py:234
  60.1 17.4 %collective-permute-start.3 = (f32[256,128]{1,0:T(8,128)S(1)}, f32[256,128]{1,0:T(8,128)S(1)}, u32[]{:S(2)}, u32[]{:S(2)}) collective-permute-start(f32[256,128]{1,0:T(8,128)S(1)} %gathered.2), channel_id=1, source_target_pairs={{0,0},{16,1},{32,2},{48,3},{64,4},{80,5},{96,6},{112,7},{65,8},{81... | collective-permute-start | bytes 393224 | tf_op jit(solution)/shard_map/ppermute | solution.py:267
  91.2 16.5 %collective-permute-start.5 = (bf16[8,2,128,128]{3,2,1,0:T(8,128)(2,1)S(1)}, bf16[8,2,128,128]{3,2,1,0:T(8,128)(2,1)S(1)}, u32[]{:S(2)}, u32[]{:S(2)}) collective-permute-start(bf16[8,2,128,128]{3,2,1,0:T(8,128)(2,1)S(1)} %all_to_all.40.x_ref), channel_id=1, source_target_pairs={{0,1},{1,0},{2,3},{3,2},{4,5},{5,4},{6,7},{7,6},{8,9},{9,8},{10,11... | collective-permute-start | bytes 1572872 | tf_op jit(solution)/shard_map/ppermute | solution.py:239
  92.8 10.1 %collective-permute-start.4 = (bf16[256,128]{1,0:T(8,128)(2,1)S(1)}, bf16[256,128]{1,0:T(8,128)(2,1)S(1)}, u32[]{:S(2)}, u32[]{:S(2)}) collective-permute-start(bf16[256,128]{1,0:T(8,128)(2,1)S(1)} %get-tuple-element.36), channel_id=1, source_target_pairs={{0,0},{1,16},{2,32},{3,48},{4,64},{5,80},{6,96},{7,112},{8,65},{9,... | collective-permute-start | bytes 196616 | tf_op jit(solution)/shard_map/ppermute | solution.py:237
  103.8 12.4 %all-to-all-start.5 = ((bf16[8,256,128]{2,1,0:T(8,128)(2,1)}), bf16[8,256,128]{2,1,0:T(8,128)(2,1)S(1)}, u32[]{:S(2)}, u32[]{:S(2)}) async-start(bf16[8,256,128]{2,1,0:T(8,128)(2,1)} %broadcast_in_dim.112), calls=%async_computation.5 | async-start | bytes 1048576 | tf_op jit(solution)/shard_map/all_to_all | solution.py:234
  107.7 3.4 %copy-start.2 = (bf16[1,1,256,128,128]{4,3,2,1,0:T(8,128)(2,1)S(1)}, bf16[1,1,256,128,128]{4,3,2,1,0:T(8,128)(2,1)}, u32[]{:S(2)}) copy-start(bf16[1,1,256,128,128]{4,3,2,1,0:T(8,128)(2,1)} %param.8) | copy-start | bytes 25165828
  116.2 12.8 %all-to-all-start.6 = ((bf16[8,2,128,128]{3,2,1,0:T(8,128)(2,1)}), bf16[8,2,128,128]{3,2,1,0:T(8,128)(2,1)S(1)}, u32[]{:S(2)}, u32[]{:S(2)}) async-start(bf16[8,2,128,128]{3,2,1,0:T(8,128)(2,1)} %mirror.3), calls=%async_computation.6 | async-start | bytes 1048576 | tf_op jit(solution)/shard_map/all_to_all | solution.py:234
  121.3 3.4 %copy-start.3 = (bf16[1,1,256,128,128]{4,3,2,1,0:T(8,128)(2,1)S(1)}, bf16[1,1,256,128,128]{4,3,2,1,0:T(8,128)(2,1)}, u32[]{:S(2)}) copy-start(bf16[1,1,256,128,128]{4,3,2,1,0:T(8,128)(2,1)} %param.8) | copy-start | bytes 25165828
  129.0 3.7 %collective-permute-start.6 = (bf16[8,256,128]{2,1,0:T(8,128)(2,1)S(1)}, bf16[8,256,128]{2,1,0:T(8,128)(2,1)S(1)}, u32[]{:S(2)}, u32[]{:S(2)}) collective-permute-start(bf16[8,256,128]{2,1,0:T(8,128)(2,1)S(1)} %get-tuple-element.44), channel_id=1, source_target_pairs={{0,1},{1,0},{2,3},{3,2},{4,5},{5,4},{6,7},{7,6},{8,9},{9,8},{10,11... | collective-permute-start | bytes 1572872 | tf_op jit(solution)/shard_map/ppermute | solution.py:263
  133.5 22.0 %all-to-all-start.7 = ((bf16[8,256,128]{2,1,0:T(8,128)(2,1)}), bf16[8,256,128]{2,1,0:T(8,128)(2,1)S(1)}, u32[]{:S(2)}, u32[]{:S(2)}) async-start(bf16[8,256,128]{2,1,0:T(8,128)(2,1)} %both.3), calls=%async_computation.7 | async-start | bytes 1048576 | tf_op jit(solution)/shard_map/all_to_all | solution.py:234
  137.2 18.4 %collective-permute-start.7 = (f32[256,128]{1,0:T(8,128)S(1)}, f32[256,128]{1,0:T(8,128)S(1)}, u32[]{:S(2)}, u32[]{:S(2)}) collective-permute-start(f32[256,128]{1,0:T(8,128)S(1)} %gathered.3), channel_id=1, source_target_pairs={{0,0},{16,1},{32,2},{48,3},{64,4},{80,5},{96,6},{112,7},{65,8},{81... | collective-permute-start | bytes 393224 | tf_op jit(solution)/shard_map/ppermute | solution.py:267

commit v4 on v3

--- a/solution.py
+++ b/solution.py
@@ -105,67 +105,77 @@
     return 2 * jnp.bitwise_and(y - place[1] + 4, 3) + xl
 
 
-def direct_kernel(tab, place, x_ref, t_ref, mine_ref, other_ref, held):
-    co = place[0]
+def streamed(steps, fetch, wait, compute):
+    fetch(0)
+    fetch(1)
+
+    def step(n, carry):
+        fetch(n + 2)
+        wait(n)
+        compute(n)
+        return carry
+
+    lax.fori_loop(0, steps - 2, step, 0)
+    for n in (steps - 2, steps - 1):
+        wait(n)
+        compute(n)
+
+
+def direct_kernel(far, tab, place, x_ref, t_ref, out_ref, held, blocks, sem):
     for i in range(8):
         held[pl.ds(2 * piece_at(place, i), 2)] = x_ref[i].reshape(2, ATOM, VECS)
     held[AC] = jnp.zeros((ATOM, VECS), BF)
-
-    def product(a, q, n):
-        blocks, xs = [], []
-        for k in range(n):
-            e = tab[a * D_LEN + q + k]
-            blocks.append(t_ref[lax.shift_right_logical(e, 6)])
-            xs.append(held[jnp.bitwise_and(e, 63)])
-        if n == 1:
-            left, right = blocks[0], xs[0]
-        else:
-            left, right = jnp.concatenate(blocks, 1), jnp.concatenate(xs, 0)
-        return jnp.dot(left, right, preferred_element_type=F32)
-
-    def step(xz, carry):
-        for which, out in ((0, mine_ref), (1, other_ref)):
-            for t in range(2):
-                a = 4 * xz + 2 * (co if which == 0 else 1 - co) + t
-                total = product(a, 0, 8)
-                if t:
-                    total = total + product(a, 8, 1)
-                out[xz, t * ATOM:(t + 1) * ATOM, :] = total.astype(out.dtype)
-        return carry
-
-    lax.fori_loop(0, 8, step, 0)
-
-
-def mirror_kernel(tab, place, x_ref, y_ref, t_ref, out_ref, held):
+    core = 1 - place[0] if far else place[0]
+
+    def entry(n, q):
+        return tab[(4 * n + 2 * core) * D_LEN + q + (1 if q >= 8 else 0)]
+
+    def fetch(n):
+        for q in range(17):
+            source = t_ref.at[lax.shift_right_logical(entry(n, q), 6)]
+            pltpu.make_async_copy(source, blocks.at[n, q], sem.at[n]).start()
+
+    def wait(n):
+        pltpu.make_async_copy(t_ref.at[pl.ds(0, 17)], blocks.at[n], sem.at[n]).wait()
+
+    def compute(n):
+        for t, (low, high) in enumerate(((0, 8), (8, 17))):
+            left = jnp.concatenate([blocks[n, q] for q in range(low, high)], 1)
+            right = [held[jnp.bitwise_and(entry(n, q), 63)] for q in range(low, high)]
+            right = jnp.concatenate(right, 0)
+            total = jnp.dot(left, right, preferred_element_type=F32)
+            out_ref[n, t * ATOM:(t + 1) * ATOM, :] = total.astype(out_ref.dtype)
+
+    streamed(8, fetch, wait, compute)
+
+
+def mirror_kernel(tab, place, x_ref, y_ref, t_ref, out_ref, held, blocks, sem):
     co = place[0]
     for xz in range(8):
         held[pl.ds(4 * xz + 2 * co, 2)] = x_ref[xz]
         held[pl.ds(4 * xz + 2 - 2 * co, 2)] = y_ref[xz]
     held[AR] = jnp.zeros((VECS, ATOM), BF)
 
-    def product(b, q, n):
-        blocks, xs = [], []
-        for k in range(n):
-            e = tab[b * M_LEN + q + k]
-            blocks.append(t_ref[lax.shift_right_logical(e, 6)])
-            xs.append(held[jnp.bitwise_and(e, 63)])
-        if n == 1:
-            left, right = xs[0], blocks[0]
-        else:
-            left, right = jnp.concatenate(xs, 1), jnp.concatenate(blocks, 0)
-        return jnp.dot(left, right, preferred_element_type=F32)
-
-    def step(i, carry):
-        k = piece_at(place, i)
-        for t in range(2):
-            b = 2 * k + t
-            total = product(b, 0, 8) + product(b, 8, 8)
-            if not t:
-                total = total + product(b, 16, 1)
-            out_ref[i, t] = total.astype(out_ref.dtype)
-        return carry
-
-    lax.fori_loop(0, 8, step, 0)
+    def entry(n, q):
+        return tab[2 * piece_at(place, n) * M_LEN + q]
+
+    def fetch(n):
+        for q in range(33):
+            source = t_ref.at[lax.shift_right_logical(entry(n, q), 6)]
+            pltpu.make_async_copy(source, blocks.at[n, q], sem.at[n]).start()
+
+    def wait(n):
+        pltpu.make_async_copy(t_ref.at[pl.ds(0, 33)], blocks.at[n], sem.at[n]).wait()
+
+    def compute(n):
+        for t, (low, high) in enumerate(((0, 17), (17, 33))):
+            left = [held[jnp.bitwise_and(entry(n, q), 63)] for q in range(low, high)]
+            left = jnp.concatenate(left, 1)
+            right = jnp.concatenate([blocks[n, q] for q in range(low, high)], 0)
+            total = jnp.dot(left, right, preferred_element_type=F32)
+            out_ref[n, t] = total.astype(out_ref.dtype)
+
+    streamed(8, fetch, wait, compute)
 
 
 def gathered_kernel(got_ref, out_ref):
@@ -181,6 +191,7 @@
 
 SMEM = pl.BlockSpec(memory_space=pltpu.SMEM)
 VMEM = pl.BlockSpec(memory_space=pltpu.VMEM)
+ANY = pl.BlockSpec(memory_space=pl.ANY)
 PARAMS = pltpu.CompilerParams(vmem_limit_bytes=24 * 1024 * 1024)
 PIECE = (2 * ATOM, VECS)
 BLOCKS = (2, ATOM, VECS)
@@ -190,18 +201,18 @@
     return jax.ShapeDtypeStruct(shape, dtype)
 
 
-def call(kernel, out_shape, scalars, arrays, scratch=(), flops=0, size=2**20, name=None):
+def call(kernel, out_shape, scalars, arrays, scratch=(), blocks=(), flops=0, size=2**20, name=None):
     single = not isinstance(out_shape, tuple)
     return pl.pallas_call(
         kernel,
         out_shape=out_shape,
-        in_specs=[SMEM] * len(scalars) + [VMEM] * len(arrays),
+        in_specs=[SMEM] * len(scalars) + [VMEM] * len(arrays) + [ANY] * len(blocks),
         out_specs=VMEM if single else (VMEM,) * len(out_shape),
         scratch_shapes=list(scratch),
         compiler_params=PARAMS,
         cost_estimate=pl.CostEstimate(flops=flops, bytes_accessed=size, transcendentals=0),
         name=name,
-    )(*scalars, *arrays)
+    )(*scalars, *arrays, *blocks)
 
 
 def shift_of(column):
@@ -228,7 +239,22 @@
     direct_tab, mirror_tab = tables(
         block_rows[0, 0], block_cols[0, 0], block_count[0, 0], row, col
     )
-    work = dict(flops=2 * SLOTS * ATOM**3, size=2**23)
+    work = dict(blocks=(tile_set,), flops=2 * SLOTS * ATOM**3, size=2**23)
+
+    def direct(far, tab, col_block):
+        return call(
+            functools.partial(direct_kernel, far),
+            like((8, *PIECE), BF if far else F32),
+            (tab, place),
+            (col_block,),
+            [
+                pltpu.VMEM((AC + 1, ATOM, VECS), BF),
+                pltpu.VMEM((8, 17, ATOM, ATOM), BF),
+                pltpu.SemaphoreType.DMA((8,)),
+            ],
+            name="direct_far" if far else "direct_own",
+            **work,
+        )
 
     def exchange(x, axes):
         return lax.all_to_all(x, axes, split_axis=0, concat_axis=0, tiled=True)
@@ -236,35 +262,33 @@
     def apply_matrix(plain, flipped):
         piece = lax.ppermute(plain, ALL, TO_COL)
         near = exchange(flipped, ("xh", "z"))
+        piece, near = lax.optimization_barrier((piece, near))
         far = lax.ppermute(near, "co", SWAP)
-        piece, near = lax.optimization_barrier((piece, near))
         col_block = exchange(jnp.broadcast_to(piece[None], (8, *PIECE)), ROWS)
         mirror = call(
             mirror_kernel,
             like((8, *BLOCKS), BF),
             (mirror_tab, place),
-            (near, far, tile_set),
-            [pltpu.VMEM((AR + 1, VECS, ATOM), BF)],
+            (near, far),
+            [
+                pltpu.VMEM((AR + 1, VECS, ATOM), BF),
+                pltpu.VMEM((8, 33, ATOM, ATOM), BF),
+                pltpu.SemaphoreType.DMA((8,)),
+            ],
             name="mirror",
             **work,
         )
         col_block, mirror = lax.optimization_barrier((col_block, mirror))
         got = exchange(mirror, ROWS)
-        mine, other = call(
-            direct_kernel,
-            (like((8, *PIECE), F32), like((8, *PIECE), BF)),
-            (direct_tab, place),
-            (col_block, tile_set),
-            [pltpu.VMEM((AC + 1, ATOM, VECS), BF)],
-            name="direct",
-            **work,
-        )
+        other = direct(1, direct_tab, col_block)
         other, got = lax.optimization_barrier((other, got))
         theirs = lax.ppermute(other, "co", SWAP)
+        gathered = call(gathered_kernel, like(PIECE, F32), (), (got,), name="gathered")
+        back = lax.ppermute(gathered, ALL, TO_ROW)
+        col_block, gathered = lax.optimization_barrier((col_block, gathered))
+        mine = direct(0, direct_tab, col_block)
         both = call(both_kernel, like((8, *PIECE), BF), (), (mine, theirs), name="both")
         own = exchange(both, ("xh", "z"))
-        gathered = call(gathered_kernel, like(PIECE, F32), (), (got,), name="gathered")
-        back = lax.ppermute(gathered, ALL, TO_ROW)
         return own, back
 
     forms = (like(PIECE, BF), like((8, *BLOCKS), BF))

time: 158 us -> 212 us (1.34)
  Pallas kernels: 24.1 us -> 82.4 us
  blocking collectives: 13 us -> 0 us
  starting transfers between devices: 67 us -> 75.9 us
  waiting for transfers between devices: 33 us -> 25.7 us
  local copies, waits for them, and re-layouts: 17.3 us -> 24 us
    pallas_call x11 -> x13, Pallas kernels: 24.1 us -> 82.4 us  [call(): pl.pallas_call(kernel, out_shape=out_shape, in_specs=[SMEM] * len(scalars...]
    all_to_all x1 -> x0, blocking collectives: 13 us -> none  [exchange(): return lax.all_to_all(x, axes, split_axis=0, concat_axis=0, tiled=True)]
    all_to_all x7 -> x8, starting transfers between devices: 35.7 us -> 42.5 us  [exchange(): return lax.all_to_all(x, axes, split_axis=0, concat_axis=0, tiled=True)]
    unnamed x16 -> x20, local copies, waits for them, and re-layouts: 15.1 us -> 21.8 us
    ppermute x2, starting transfers between devices: 11.1 us -> 17.3 us  [apply_matrix(): piece = lax.ppermute(plain, ALL, TO_COL)]
    ppermute x2, waiting for transfers between devices: 7.81 us -> 2.1 us  [apply_matrix(): piece = lax.ppermute(plain, ALL, TO_COL)]
    ppermute x2, waiting for transfers between devices: 3.07 us -> 0.01 us  [apply_matrix(): theirs = lax.ppermute(other, 'co', SWAP)]
    ppermute x2, starting transfers between devices: 13.7 us -> 11.3 us  [apply_matrix(): back = lax.ppermute(gathered, ALL, TO_ROW)]
  transfers between devices with their start and end apart: 15 -> 16, of which waited for: 5 -> 5; matrix products, arithmetic and copies ran while one was open for 2% -> 2% of each run, Pallas kernels for 12% -> 36%
where the time goes in v4:
time: 212 us; the launch traced here: 211 us
  Pallas kernels  82.4 us (39%)
  starting transfers between devices  75.9 us (36%)
  waiting for transfers between devices  25.7 us (12%)
  local copies, waits for them, and re-layouts  24 us (11%)
    pallas_call x13, Pallas kernels, call(): pl.pallas_call(kernel, out_shape=out_shape, in_specs=[SMEM] * len(scalars...  82.4 us
    all_to_all x8, starting transfers between devices, exchange(): return lax.all_to_all(x, axes, split_axis=0, concat_axis=0, tiled=True)  42.5 us
    ppermute x2, waiting for transfers between devices, apply_matrix(): back = lax.ppermute(gathered, ALL, TO_ROW)  22.9 us
    unnamed x20, local copies, waits for them, and re-layouts  21.8 us
    ppermute x2, starting transfers between devices, apply_matrix(): piece = lax.ppermute(plain, ALL, TO_COL)  17.3 us
    ppermute x2, starting transfers between devices, apply_matrix(): back = lax.ppermute(gathered, ALL, TO_ROW)  11.3 us
  transfers between devices with their start and end apart: 16, of which 5 were waited for; matrix products, arithmetic and copies ran while one was open for 2% of the time, Pallas kernels for 36%

profile of v4, /device:TPU:25, one launch (start us, length us, event | category | flops | bytes accessed | tf_op | source)
XLA Modules:
  0.0 210.5 jit_solution(6660756160067675726)
XLA Ops:
  0.0 0.9 copy-done.6
  0.9 0.7 copy-done.8
  1.6 1.5 first.1
  3.0 7.5 %all-to-all-start = ((bf16[8,2,128,128]{3,2,1,0:T(8,128)(2,1)}), bf16[8,2,128,128]{3,2,1,0:T(8,128)(2,1)S(1)}, u32[]{:S(2)}, u32[]{:S(2)}) async-start(bf16[8,2,128,128]{3,2,1,0:T(8,128)(2,1)} %get-tuple-element.25), calls=%async_computation | async-start | bytes 1048576 | tf_op jit(solution)/shard_map/all_to_all | solution.py:260
  10.5 8.8 %collective-permute-start = (bf16[256,128]{1,0:T(8,128)(2,1)S(1)}, bf16[256,128]{1,0:T(8,128)(2,1)S(1)}, u32[]{:S(2)}, u32[]{:S(2)}) collective-permute-start(bf16[256,128]{1,0:T(8,128)(2,1)S(1)} %get-tuple-element.24), channel_id=1, source_target_pairs={{0,0},{1,16},{2,32},{3,48},{4,64},{5,80},{6,96},{7,112},{8,65},{9,... | collective-permute-start | bytes 196616 | tf_op jit(solution)/shard_map/ppermute | solution.py:263
  20.1 0.1 add_select_fusion.1
  20.2 0.1 reshape.357
  20.3 0.1 add.295
  20.4 0.7 multiply_add_fusion.1
  21.1 0.3 select_reduce_fusion.1
  21.4 0.2 collective-permute-done
  21.6 0.0 all-to-all-done.x_ref
  21.6 1.4 collective-permute-start.1
  23.1 0.9 broadcast_in_dim.104
  23.9 4.2 %all-to-all-start.1 = ((bf16[8,256,128]{2,1,0:T(8,128)(2,1)}), bf16[8,256,128]{2,1,0:T(8,128)(2,1)S(1)}, u32[]{:S(2)}, u32[]{:S(2)}) async-start(bf16[8,256,128]{2,1,0:T(8,128)(2,1)} %broadcast_in_dim.104), calls=%async_computation.1 | async-start | bytes 1048576 | tf_op jit(solution)/shard_map/all_to_all | solution.py:260
  28.1 0.1 pad_add_fusion.place
  28.2 0.1 add_select_fusion
  28.3 0.0 collective-permute-done.1.y_ref
  28.3 0.0 copy-start
  28.3 3.4 %copy-done = bf16[1,1,256,128,128]{4,3,2,1,0:T(8,128)(2,1)S(1)} copy-done((bf16[1,1,256,128,128]{4,3,2,1,0:T(8,128)(2,1)S(1)}, bf16[1,1,256,128,128]{4,3,2,1,0:T(8,128)(2,1)}, u32[]{:S(2)}) %copy-start) | copy-done | bytes 8388632
  31.7 19.1 %mirror.2 = bf16[8,2,128,128]{3,2,1,0:T(8,128)(2,1)} custom-call(s32[272]{0:T(512)S(1)} %broadcast_add_fusion.tab, s32[2]{0:T(128)S(1)} %pad_add_fusion.place, bf16[8,2,128,128]{3,2,1,0:T(8,128)(2,1)S(1)} %all-to-all-done.x_ref, bf16[8,2,128,128]{3,2,1,0:T(8,128)(2,1)S(1)} %collective-permute-done.1.y_ref, bf16[256,128,128]{2,1,0:T(8,128)(2,1)S(1)} %bitcast.6), custom_call_target="tpu_custom_call" | custom-call | flops 1073741824 | bytes 8388608 | tf_op jit(solution)/shard_map/mirror/pallas_call | solution.py:206
  50.8 5.2 %all-to-all-start.2 = ((bf16[8,2,128,128]{3,2,1,0:T(8,128)(2,1)}), bf16[8,2,128,128]{3,2,1,0:T(8,128)(2,1)S(1)}, u32[]{:S(2)}, u32[]{:S(2)}) async-start(bf16[8,2,128,128]{3,2,1,0:T(8,128)(2,1)} %mirror.2), calls=%async_computation.2 | async-start | bytes 1048576 | tf_op jit(solution)/shard_map/all_to_all | solution.py:260
  55.9 0.1 reshape.356
  56.0 0.1 add.260
  56.1 0.1 add.261
  56.2 0.3 select_reduce_fusion
  56.5 0.0 copy-start.1
  56.5 3.4 %copy-done.1 = bf16[1,1,256,128,128]{4,3,2,1,0:T(8,128)(2,1)S(1)} copy-done((bf16[1,1,256,128,128]{4,3,2,1,0:T(8,128)(2,1)S(1)}, bf16[1,1,256,128,128]{4,3,2,1,0:T(8,128)(2,1)}, u32[]{:S(2)}) %copy-start.1) | copy-done | bytes 8388632
  59.9 9.5 %direct_far.2 = bf16[8,256,128]{2,1,0:T(8,128)(2,1)S(1)} custom-call(s32[288]{0:T(512)S(1)} %broadcast_add_fusion.1.tab, s32[2]{0:T(128)S(1)} %pad_add_fusion.place, bf16[8,256,128]{2,1,0:T(8,128)(2,1)S(1)} %all-to-all-done.1.x_ref, bf16[256,128,128]{2,1,0:T(8,128)(2,1)S(1)} %bitcast.7), custom_call_target="tpu_custom_call" | custom-call | flops 1073741824 | bytes 8388608 | tf_op jit(solution)/shard_map/direct_far/pallas_call | solution.py:206
  69.4 0.0 copy-start.7
  69.4 0.0 copy-start.9
  69.4 0.0 all-to-all-done.2.got_ref
  69.4 1.2 collective-permute-start.2
  70.6 0.1 gathered.2
  70.7 0.0 copy-start.2
  70.8 3.4 %copy-done.2 = bf16[1,1,256,128,128]{4,3,2,1,0:T(8,128)(2,1)S(1)} copy-done((bf16[1,1,256,128,128]{4,3,2,1,0:T(8,128)(2,1)S(1)}, bf16[1,1,256,128,128]{4,3,2,1,0:T(8,128)(2,1)}, u32[]{:S(2)}) %copy-start.2) | copy-done | bytes 8388632
  74.1 9.5 %direct_own.2.mine_ref = f32[8,256,128]{2,1,0:T(8,128)S(1)} custom-call(s32[288]{0:T(512)S(1)} %broadcast_add_fusion.1.tab, s32[2]{0:T(128)S(1)} %pad_add_fusion.place, bf16[8,256,128]{2,1,0:T(8,128)(2,1)S(1)} %all-to-all-done.1.x_ref, bf16[256,128,128]{2,1,0:T(8,128)(2,1)S(1)} %bitcast.8), custom_call_target="tpu_custom_call" | custom-call | flops 1073741824 | bytes 8388608 | tf_op jit(solution)/shard_map/direct_own/pallas_call | solution.py:206
  83.6 0.9 both.2
  84.5 6.1 %all-to-all-start.3 = ((bf16[8,256,128]{2,1,0:T(8,128)(2,1)}), bf16[8,256,128]{2,1,0:T(8,128)(2,1)S(1)}, u32[]{:S(2)}, u32[]{:S(2)}) async-start(bf16[8,256,128]{2,1,0:T(8,128)(2,1)} %both.2), calls=%async_computation.3 | async-start | bytes 1048576 | tf_op jit(solution)/shard_map/all_to_all | solution.py:260
  90.6 5.7 %collective-permute-start.3 = (f32[256,128]{1,0:T(8,128)S(1)}, f32[256,128]{1,0:T(8,128)S(1)}, u32[]{:S(2)}, u32[]{:S(2)}) collective-permute-start(f32[256,128]{1,0:T(8,128)S(1)} %gathered.2), channel_id=1, source_target_pairs={{0,0},{16,1},{32,2},{48,3},{64,4},{80,5},{96,6},{112,7},{65,8},{81... | collective-permute-start | bytes 393224 | tf_op jit(solution)/shard_map/ppermute | solution.py:287
  96.3 11.5 %collective-permute-done.3.back_ref = f32[256,128]{1,0:T(8,128)S(1)} collective-permute-done((f32[256,128]{1,0:T(8,128)S(1)}, f32[256,128]{1,0:T(8,128)S(1)}, u32[]{:S(2)}, u32[]{:S(2)}) %collective-permute-start.3) | collective-permute-done | bytes 131104 | tf_op jit(solution)/shard_map/ppermute | solution.py:287
  107.8 1.5 second.1
  109.3 3.5 %all-to-all-start.4 = ((bf16[8,2,128,128]{3,2,1,0:T(8,128)(2,1)}), bf16[8,2,128,128]{3,2,1,0:T(8,128)(2,1)S(1)}, u32[]{:S(2)}, u32[]{:S(2)}) async-start(bf16[8,2,128,128]{3,2,1,0:T(8,128)(2,1)} %get-tuple-element.34), calls=%async_computation.4 | async-start | bytes 1048576 | tf_op jit(solution)/shard_map/all_to_all | solution.py:260
  112.8 8.5 %collective-permute-start.4 = (bf16[256,128]{1,0:T(8,128)(2,1)S(1)}, bf16[256,128]{1,0:T(8,128)(2,1)S(1)}, u32[]{:S(2)}, u32[]{:S(2)}) collective-permute-start(bf16[256,128]{1,0:T(8,128)(2,1)S(1)} %get-tuple-element.33), channel_id=1, source_target_pairs={{0,0},{1,16},{2,32},{3,48},{4,64},{5,80},{6,96},{7,112},{8,65},{9,... | collective-permute-start | bytes 196616 | tf_op jit(solution)/shard_map/ppermute | solution.py:263
  121.3 1.9 collective-permute-done.4
  123.2 0.6 all-to-all-done.4.x_ref
  123.8 0.9 collective-permute-start.5
  124.7 0.9 broadcast_in_dim.112
  125.5 4.2 %all-to-all-start.5 = ((bf16[8,256,128]{2,1,0:T(8,128)(2,1)}), bf16[8,256,128]{2,1,0:T(8,128)(2,1)S(1)}, u32[]{:S(2)}, u32[]{:S(2)}) async-start(bf16[8,256,128]{2,1,0:T(8,128)(2,1)} %broadcast_in_dim.112), calls=%async_computation.5 | async-start | bytes 1048576 | tf_op jit(solution)/shard_map/all_to_all | solution.py:260
  129.8 3.4 %copy-done.3 = bf16[1,1,256,128,128]{4,3,2,1,0:T(8,128)(2,1)S(1)} copy-done((bf16[1,1,256,128,128]{4,3,2,1,0:T(8,128)(2,1)S(1)}, bf16[1,1,256,128,128]{4,3,2,1,0:T(8,128)(2,1)}, u32[]{:S(2)}) %copy-start.3) | copy-done | bytes 8388632
  133.1 19.1 %mirror.3 = bf16[8,2,128,128]{3,2,1,0:T(8,128)(2,1)} custom-call(s32[272]{0:T(512)S(1)} %broadcast_add_fusion.tab, s32[2]{0:T(128)S(1)} %pad_add_fusion.place, bf16[8,2,128,128]{3,2,1,0:T(8,128)(2,1)S(1)} %all-to-all-done.4.x_ref, bf16[8,2,128,128]{3,2,1,0:T(8,128)(2,1)S(1)} %collective-permute-done.5.y_ref, bf16[256,128,128]{2,1,0:T(8,128)(2,1)S(1)} %bitcast.9), custom_call_target="tpu_custom_call" | custom-call | flops 1073741824 | bytes 8388608 | tf_op jit(solution)/shard_map/mirror/pallas_call | solution.py:206
  152.3 5.2 %all-to-all-start.6 = ((bf16[8,2,128,128]{3,2,1,0:T(8,128)(2,1)}), bf16[8,2,128,128]{3,2,1,0:T(8,128)(2,1)S(1)}, u32[]{:S(2)}, u32[]{:S(2)}) async-start(bf16[8,2,128,128]{3,2,1,0:T(8,128)(2,1)} %mirror.3), calls=%async_computation.6 | async-start | bytes 1048576 | tf_op jit(solution)/shard_map/all_to_all | solution.py:260
  157.4 3.4 %copy-done.4 = bf16[1,1,256,128,128]{4,3,2,1,0:T(8,128)(2,1)S(1)} copy-done((bf16[1,1,256,128,128]{4,3,2,1,0:T(8,128)(2,1)S(1)}, bf16[1,1,256,128,128]{4,3,2,1,0:T(8,128)(2,1)}, u32[]{:S(2)}) %copy-start.4) | copy-done | bytes 8388632
  160.8 9.5 %direct_far.3 = bf16[8,256,128]{2,1,0:T(8,128)(2,1)S(1)} custom-call(s32[288]{0:T(512)S(1)} %broadcast_add_fusion.1.tab, s32[2]{0:T(128)S(1)} %pad_add_fusion.place, bf16[8,256,128]{2,1,0:T(8,128)(2,1)S(1)} %all-to-all-done.5.x_ref, bf16[256,128,128]{2,1,0:T(8,128)(2,1)S(1)} %bitcast.10), custom_call_target="tpu_custom_call" | custom-call | flops 1073741824 | bytes 8388608 | tf_op jit(solution)/shard_map/direct_far/pallas_call | solution.py:206
  170.3 1.2 collective-permute-start.6
  171.5 0.1 gathered.3
  171.6 0.0 copy-start.5
  171.6 3.4 %copy-done.5 = bf16[1,1,256,128,128]{4,3,2,1,0:T(8,128)(2,1)S(1)} copy-done((bf16[1,1,256,128,128]{4,3,2,1,0:T(8,128)(2,1)S(1)}, bf16[1,1,256,128,128]{4,3,2,1,0:T(8,128)(2,1)}, u32[]{:S(2)}) %copy-start.5) | copy-done | bytes 8388632
  175.0 9.5 %direct_own.3.mine_ref = f32[8,256,128]{2,1,0:T(8,128)S(1)} custom-call(s32[288]{0:T(512)S(1)} %broadcast_add_fusion.1.tab, s32[2]{0:T(128)S(1)} %pad_add_fusion.place, bf16[8,256,128]{2,1,0:T(8,128)(2,1)S(1)} %all-to-all-done.5.x_ref, bf16[256,128,128]{2,1,0:T(8,128)(2,1)S(1)} %bitcast.11), custom_call_target="tpu_custom_call" | custom-call | flops 1073741824 | bytes 8388608 | tf_op jit(solution)/shard_map/direct_own/pallas_call | solution.py:206
  184.5 0.9 both.3
  185.4 6.7 %all-to-all-start.7 = ((bf16[8,256,128]{2,1,0:T(8,128)(2,1)}), bf16[8,256,128]{2,1,0:T(8,128)(2,1)S(1)}, u32[]{:S(2)}, u32[]{:S(2)}) async-start(bf16[8,256,128]{2,1,0:T(8,128)(2,1)} %both.3), calls=%async_computation.7 | async-start | bytes 1048576 | tf_op jit(solution)/shard_map/all_to_all | solution.py:260
  192.1 5.7 %collective-permute-start.7 = (f32[256,128]{1,0:T(8,128)S(1)}, f32[256,128]{1,0:T(8,128)S(1)}, u32[]{:S(2)}, u32[]{:S(2)}) collective-permute-start(f32[256,128]{1,0:T(8,128)S(1)} %gathered.3), channel_id=1, source_target_pairs={{0,0},{16,1},{32,2},{48,3},{64,4},{80,5},{96,6},{112,7},{65,8},{81... | collective-permute-start | bytes 393224 | tf_op jit(solution)/shard_map/ppermute | solution.py:287
  197.7 11.5 %collective-permute-done.7.back_ref = f32[256,128]{1,0:T(8,128)S(1)} collective-permute-done((f32[256,128]{1,0:T(8,128)S(1)}, f32[256,128]{1,0:T(8,128)S(1)}, u32[]{:S(2)}, u32[]{:S(2)}) %collective-permute-start.7) | collective-permute-done | bytes 131104 | tf_op jit(solution)/shard_map/ppermute | solution.py:287
  209.2 1.3 last.1
  (31 shorter events, 0.2 us)
Async XLA Ops:
  0.0 0.9 copy-start.6
  0.9 0.7 copy-start.8
  3.0 18.6 %all-to-all-start = ((bf16[8,2,128,128]{3,2,1,0:T(8,128)(2,1)}), bf16[8,2,128,128]{3,2,1,0:T(8,128)(2,1)S(1)}, u32[]{:S(2)}, u32[]{:S(2)}) async-start(bf16[8,2,128,128]{3,2,1,0:T(8,128)(2,1)} %get-tuple-element.25), calls=%async_computation | async-start | bytes 1048576 | tf_op jit(solution)/shard_map/all_to_all | solution.py:260
  10.5 11.1 %collective-permute-start = (bf16[256,128]{1,0:T(8,128)(2,1)S(1)}, bf16[256,128]{1,0:T(8,128)(2,1)S(1)}, u32[]{:S(2)}, u32[]{:S(2)}) collective-permute-start(bf16[256,128]{1,0:T(8,128)(2,1)S(1)} %get-tuple-element.24), channel_id=1, source_target_pairs={{0,0},{1,16},{2,32},{3,48},{4,64},{5,80},{6,96},{7,112},{8,65},{9,... | collective-permute-start | bytes 196616 | tf_op jit(solution)/shard_map/ppermute | solution.py:263
  21.6 6.7 %collective-permute-start.1 = (bf16[8,2,128,128]{3,2,1,0:T(8,128)(2,1)S(1)}, bf16[8,2,128,128]{3,2,1,0:T(8,128)(2,1)S(1)}, u32[]{:S(2)}, u32[]{:S(2)}) collective-permute-start(bf16[8,2,128,128]{3,2,1,0:T(8,128)(2,1)S(1)} %all-to-all-done.x_ref), channel_id=1, source_target_pairs={{0,1},{1,0},{2,3},{3,2},{4,5},{5,4},{6,7},{7,6},{8,9},{9,8},{10,11... | collective-permute-start | bytes 1572872 | tf_op jit(solution)/shard_map/ppermute | solution.py:266
  23.9 26.9 %all-to-all-start.1 = ((bf16[8,256,128]{2,1,0:T(8,128)(2,1)}), bf16[8,256,128]{2,1,0:T(8,128)(2,1)S(1)}, u32[]{:S(2)}, u32[]{:S(2)}) async-start(bf16[8,256,128]{2,1,0:T(8,128)(2,1)} %broadcast_in_dim.104), calls=%async_computation.1 | async-start | bytes 1048576 | tf_op jit(solution)/shard_map/all_to_all | solution.py:260
  28.3 3.4 %copy-start = (bf16[1,1,256,128,128]{4,3,2,1,0:T(8,128)(2,1)S(1)}, bf16[1,1,256,128,128]{4,3,2,1,0:T(8,128)(2,1)}, u32[]{:S(2)}) copy-start(bf16[1,1,256,128,128]{4,3,2,1,0:T(8,128)(2,1)} %param.8) | copy-start | bytes 25165828
  50.8 18.6 %all-to-all-start.2 = ((bf16[8,2,128,128]{3,2,1,0:T(8,128)(2,1)}), bf16[8,2,128,128]{3,2,1,0:T(8,128)(2,1)S(1)}, u32[]{:S(2)}, u32[]{:S(2)}) async-start(bf16[8,2,128,128]{3,2,1,0:T(8,128)(2,1)} %mirror.2), calls=%async_computation.2 | async-start | bytes 1048576 | tf_op jit(solution)/shard_map/all_to_all | solution.py:260
  56.5 3.4 %copy-start.1 = (bf16[1,1,256,128,128]{4,3,2,1,0:T(8,128)(2,1)S(1)}, bf16[1,1,256,128,128]{4,3,2,1,0:T(8,128)(2,1)}, u32[]{:S(2)}) copy-start(bf16[1,1,256,128,128]{4,3,2,1,0:T(8,128)(2,1)} %param.8) | copy-start | bytes 25165828
  69.4 38.4 %copy-start.7 = (f32[256,128]{1,0:T(8,128)S(1)}, f32[256,128]{1,0:T(8,128)}, u32[]{:S(2)}) copy-start(f32[256,128]{1,0:T(8,128)} %vectors_ref.5) | copy-start | bytes 393220
  69.4 38.4 %copy-start.9 = (s32[2]{0:T(128)S(1)}, s32[2]{0:T(128)}, u32[]{:S(2)}) copy-start(s32[2]{0:T(128)} %widths.5) | copy-start | bytes 28
  69.4 14.2 %collective-permute-start.2 = (bf16[8,256,128]{2,1,0:T(8,128)(2,1)S(1)}, bf16[8,256,128]{2,1,0:T(8,128)(2,1)S(1)}, u32[]{:S(2)}, u32[]{:S(2)}) collective-permute-start(bf16[8,256,128]{2,1,0:T(8,128)(2,1)S(1)} %direct_far.2), channel_id=1, source_target_pairs={{0,1},{1,0},{2,3},{3,2},{4,5},{5,4},{6,7},{7,6},{8,9},{9,8},{10,11... | collective-permute-start | bytes 1572872 | tf_op jit(solution)/shard_map/ppermute | solution.py:285
  70.7 3.4 %copy-start.2 = (bf16[1,1,256,128,128]{4,3,2,1,0:T(8,128)(2,1)S(1)}, bf16[1,1,256,128,128]{4,3,2,1,0:T(8,128)(2,1)}, u32[]{:S(2)}) copy-start(bf16[1,1,256,128,128]{4,3,2,1,0:T(8,128)(2,1)} %param.8) | copy-start | bytes 25165828
  84.5 23.3 %all-to-all-start.3 = ((bf16[8,256,128]{2,1,0:T(8,128)(2,1)}), bf16[8,256,128]{2,1,0:T(8,128)(2,1)S(1)}, u32[]{:S(2)}, u32[]{:S(2)}) async-start(bf16[8,256,128]{2,1,0:T(8,128)(2,1)} %both.2), calls=%async_computation.3 | async-start | bytes 1048576 | tf_op jit(solution)/shard_map/all_to_all | solution.py:260
  90.6 17.1 %collective-permute-start.3 = (f32[256,128]{1,0:T(8,128)S(1)}, f32[256,128]{1,0:T(8,128)S(1)}, u32[]{:S(2)}, u32[]{:S(2)}) collective-permute-start(f32[256,128]{1,0:T(8,128)S(1)} %gathered.2), channel_id=1, source_target_pairs={{0,0},{16,1},{32,2},{48,3},{64,4},{80,5},{96,6},{112,7},{65,8},{81... | collective-permute-start | bytes 393224 | tf_op jit(solution)/shard_map/ppermute | solution.py:287
  109.3 14.5 %all-to-all-start.4 = ((bf16[8,2,128,128]{3,2,1,0:T(8,128)(2,1)}), bf16[8,2,128,128]{3,2,1,0:T(8,128)(2,1)S(1)}, u32[]{:S(2)}, u32[]{:S(2)}) async-start(bf16[8,2,128,128]{3,2,1,0:T(8,128)(2,1)} %get-tuple-element.34), calls=%async_computation.4 | async-start | bytes 1048576 | tf_op jit(solution)/shard_map/all_to_all | solution.py:260
  112.8 10.4 %collective-permute-start.4 = (bf16[256,128]{1,0:T(8,128)(2,1)S(1)}, bf16[256,128]{1,0:T(8,128)(2,1)S(1)}, u32[]{:S(2)}, u32[]{:S(2)}) collective-permute-start(bf16[256,128]{1,0:T(8,128)(2,1)S(1)} %get-tuple-element.33), channel_id=1, source_target_pairs={{0,0},{1,16},{2,32},{3,48},{4,64},{5,80},{6,96},{7,112},{8,65},{9,... | collective-permute-start | bytes 196616 | tf_op jit(solution)/shard_map/ppermute | solution.py:263
  123.8 5.9 %collective-permute-start.5 = (bf16[8,2,128,128]{3,2,1,0:T(8,128)(2,1)S(1)}, bf16[8,2,128,128]{3,2,1,0:T(8,128)(2,1)S(1)}, u32[]{:S(2)}, u32[]{:S(2)}) collective-permute-start(bf16[8,2,128,128]{3,2,1,0:T(8,128)(2,1)S(1)} %all-to-all-done.4.x_ref), channel_id=1, source_target_pairs={{0,1},{1,0},{2,3},{3,2},{4,5},{5,4},{6,7},{7,6},{8,9},{9,8},{10,11... | collective-permute-start | bytes 1572872 | tf_op jit(solution)/shard_map/ppermute | solution.py:266
  125.5 26.7 %all-to-all-start.5 = ((bf16[8,256,128]{2,1,0:T(8,128)(2,1)}), bf16[8,256,128]{2,1,0:T(8,128)(2,1)S(1)}, u32[]{:S(2)}, u32[]{:S(2)}) async-start(bf16[8,256,128]{2,1,0:T(8,128)(2,1)} %broadcast_in_dim.112), calls=%async_computation.5 | async-start | bytes 1048576 | tf_op jit(solution)/shard_map/all_to_all | solution.py:260
  129.8 3.4 %copy-start.3 = (bf16[1,1,256,128,128]{4,3,2,1,0:T(8,128)(2,1)S(1)}, bf16[1,1,256,128,128]{4,3,2,1,0:T(8,128)(2,1)}, u32[]{:S(2)}) copy-start(bf16[1,1,256,128,128]{4,3,2,1,0:T(8,128)(2,1)} %param.8) | copy-start | bytes 25165828
  152.3 18.0 %all-to-all-start.6 = ((bf16[8,2,128,128]{3,2,1,0:T(8,128)(2,1)}), bf16[8,2,128,128]{3,2,1,0:T(8,128)(2,1)S(1)}, u32[]{:S(2)}, u32[]{:S(2)}) async-start(bf16[8,2,128,128]{3,2,1,0:T(8,128)(2,1)} %mirror.3), calls=%async_computation.6 | async-start | bytes 1048576 | tf_op jit(solution)/shard_map/all_to_all | solution.py:260
  157.4 3.4 %copy-start.4 = (bf16[1,1,256,128,128]{4,3,2,1,0:T(8,128)(2,1)S(1)}, bf16[1,1,256,128,128]{4,3,2,1,0:T(8,128)(2,1)}, u32[]{:S(2)}) copy-start(bf16[1,1,256,128,128]{4,3,2,1,0:T(8,128)(2,1)} %param.8) | copy-start | bytes 25165828
  170.3 14.2 %collective-permute-start.6 = (bf16[8,256,128]{2,1,0:T(8,128)(2,1)S(1)}, bf16[8,256,128]{2,1,0:T(8,128)(2,1)S(1)}, u32[]{:S(2)}, u32[]{:S(2)}) collective-permute-start(bf16[8,256,128]{2,1,0:T(8,128)(2,1)S(1)} %direct_far.3), channel_id=1, source_target_pairs={{0,1},{1,0},{2,3},{3,2},{4,5},{5,4},{6,7},{7,6},{8,9},{9,8},{10,11... | collective-permute-start | bytes 1572872 | tf_op jit(solution)/shard_map/ppermute | solution.py:285
  171.6 3.4 %copy-start.5 = (bf16[1,1,256,128,128]{4,3,2,1,0:T(8,128)(2,1)S(1)}, bf16[1,1,256,128,128]{4,3,2,1,0:T(8,128)(2,1)}, u32[]{:S(2)}) copy-start(bf16[1,1,256,128,128]{4,3,2,1,0:T(8,128)(2,1)} %param.8) | copy-start | bytes 25165828
  185.4 23.8 %all-to-all-start.7 = ((bf16[8,256,128]{2,1,0:T(8,128)(2,1)}), bf16[8,256,128]{2,1,0:T(8,128)(2,1)S(1)}, u32[]{:S(2)}, u32[]{:S(2)}) async-start(bf16[8,256,128]{2,1,0:T(8,128)(2,1)} %both.3), calls=%async_computation.7 | async-start | bytes 1048576 | tf_op jit(solution)/shard_map/all_to_all | solution.py:260
  192.1 17.1 %collective-permute-start.7 = (f32[256,128]{1,0:T(8,128)S(1)}, f32[256,128]{1,0:T(8,128)S(1)}, u32[]{:S(2)}, u32[]{:S(2)}) collective-permute-start(f32[256,128]{1,0:T(8,128)S(1)} %gathered.3), channel_id=1, source_target_pairs={{0,0},{16,1},{32,2},{48,3},{64,4},{80,5},{96,6},{112,7},{65,8},{81... | collective-permute-start | bytes 393224 | tf_op jit(solution)/shard_map/ppermute | solution.py:287

commit v5 on v3

--- a/solution.py
+++ b/solution.py
@@ -133,7 +133,7 @@
                 out[xz, t * ATOM:(t + 1) * ATOM, :] = total.astype(out.dtype)
         return carry
 
-    lax.fori_loop(0, 8, step, 0)
+    lax.fori_loop(0, 8, step, 0, unroll=True)
 
 
 def mirror_kernel(tab, place, x_ref, y_ref, t_ref, out_ref, held):
@@ -165,14 +165,18 @@
             out_ref[i, t] = total.astype(out_ref.dtype)
         return carry
 
-    lax.fori_loop(0, 8, step, 0)
+    lax.fori_loop(0, 8, step, 0, unroll=True)
 
 
 def gathered_kernel(got_ref, out_ref):
     total = got_ref[0].astype(F32)
     for i in range(1, 8):
         total = total + got_ref[i].astype(F32)
-    out_ref[...] = jnp.swapaxes(total, 1, 2).reshape(2 * ATOM, VECS)
+    out_ref[...] = total.astype(out_ref.dtype)
+
+
+def turned_kernel(sum_ref, out_ref):
+    out_ref[...] = jnp.swapaxes(sum_ref[...].astype(F32), 1, 2).reshape(2 * ATOM, VECS)
 
 
 def both_kernel(mine_ref, theirs_ref, out_ref):
@@ -233,11 +237,11 @@
     def exchange(x, axes):
         return lax.all_to_all(x, axes, split_axis=0, concat_axis=0, tiled=True)
 
-    def apply_matrix(plain, flipped):
+    def apply_matrix(plain, flipped, sent):
         piece = lax.ppermute(plain, ALL, TO_COL)
         near = exchange(flipped, ("xh", "z"))
+        piece, near = lax.optimization_barrier((piece, near))
         far = lax.ppermute(near, "co", SWAP)
-        piece, near = lax.optimization_barrier((piece, near))
         col_block = exchange(jnp.broadcast_to(piece[None], (8, *PIECE)), ROWS)
         mirror = call(
             mirror_kernel,
@@ -263,17 +267,18 @@
         theirs = lax.ppermute(other, "co", SWAP)
         both = call(both_kernel, like((8, *PIECE), BF), (), (mine, theirs), name="both")
         own = exchange(both, ("xh", "z"))
-        gathered = call(gathered_kernel, like(PIECE, F32), (), (got,), name="gathered")
+        gathered = call(gathered_kernel, like(BLOCKS, sent), (), (got,), name="gathered")
         back = lax.ppermute(gathered, ALL, TO_ROW)
-        return own, back
+        turned = call(turned_kernel, like(PIECE, F32), (), (back,), name="turned")
+        return own, turned
 
     forms = (like(PIECE, BF), like((8, *BLOCKS), BF))
     plain, flipped = call(first_kernel, forms, (widths,), (vectors,), name="first")
-    parts = apply_matrix(plain, flipped)
+    parts = apply_matrix(plain, flipped, F32)
     second, plain, flipped = call(
         second_kernel, (like(PIECE, F32), *forms), (widths,), (*parts, vectors), name="second"
     )
-    parts = apply_matrix(plain, flipped)
+    parts = apply_matrix(plain, flipped, BF)
     return call(
         last_kernel, like(PIECE, F32), (widths,), (*parts, vectors, second), name="last"
     )

time: 158 us -> 147 us (0.930)
  starting transfers between devices: 67 us -> 80.9 us
  blocking collectives: 13 us -> 0 us
  waiting for transfers between devices: 33 us -> 25.1 us
  Pallas kernels: 24.1 us -> 20.6 us
    all_to_all x1 -> x0, blocking collectives: 13 us -> none  [exchange(): return lax.all_to_all(x, axes, split_axis=0, concat_axis=0, tiled=True)]
    all_to_all x7 -> x8, starting transfers between devices: 35.7 us -> 42.7 us  [exchange(): return lax.all_to_all(x, axes, split_axis=0, concat_axis=0, tiled=True)]
    ppermute x2, starting transfers between devices: 11.1 us -> 15.8 us  [apply_matrix(): piece = lax.ppermute(plain, ALL, TO_COL)]
    ppermute x2, waiting for transfers between devices: 7.81 us -> 3.24 us  [apply_matrix(): piece = lax.ppermute(plain, ALL, TO_COL)]
    ppermute x2, waiting for transfers between devices: 22.1 us -> 17.9 us  [apply_matrix(): back = lax.ppermute(gathered, ALL, TO_ROW)]
    pallas_call x11 -> x13, Pallas kernels: 24.1 us -> 20.6 us  [call(): pl.pallas_call(kernel, out_shape=out_shape, in_specs=[SMEM] * len(scalars...]
    ppermute x2, starting transfers between devices: 13.7 us -> 16.8 us  [apply_matrix(): back = lax.ppermute(gathered, ALL, TO_ROW)]
    ppermute x2, starting transfers between devices: 3.25 us -> 1.44 us  [apply_matrix(): far = lax.ppermute(near, 'co', SWAP)]
  transfers between devices with their start and end apart: 15 -> 16, of which waited for: 5 -> 8; matrix products, arithmetic and copies ran while one was open for 2% -> 3% of each run, Pallas kernels for 12% -> 10%
where the time goes in v5:
time: 147 us; the launch traced here: 146 us
  starting transfers between devices  80.9 us (55%)
  waiting for transfers between devices  25.1 us (17%)
  Pallas kernels  20.6 us (14%)
  local copies, waits for them, and re-layouts  17.2 us (12%)
  other arithmetic  1.55 us (1%)
    all_to_all x8, starting transfers between devices, exchange(): return lax.all_to_all(x, axes, split_axis=0, concat_axis=0, tiled=True)  42.7 us
    pallas_call x13, Pallas kernels, call(): pl.pallas_call(kernel, out_shape=out_shape, in_specs=[SMEM] * len(scalars...  20.6 us
    ppermute x2, waiting for transfers between devices, apply_matrix(): back = lax.ppermute(gathered, ALL, TO_ROW)  17.9 us
    ppermute x2, starting transfers between devices, apply_matrix(): back = lax.ppermute(gathered, ALL, TO_ROW)  16.8 us
    ppermute x2, starting transfers between devices, apply_matrix(): piece = lax.ppermute(plain, ALL, TO_COL)  15.8 us
    unnamed x16, local copies, waits for them, and re-layouts  15.1 us
    ppermute x2, starting transfers between devices, apply_matrix(): theirs = lax.ppermute(other, 'co', SWAP)  4.11 us
    ppermute x2, waiting for transfers between devices, apply_matrix(): piece = lax.ppermute(plain, ALL, TO_COL)  3.24 us
  transfers between devices with their start and end apart: 16, of which 8 were waited for; matrix products, arithmetic and copies ran while one was open for 3% of the time, Pallas kernels for 10%

profile of v5, /device:TPU:25, one launch (start us, length us, event | category | flops | bytes accessed | tf_op | source)
XLA Modules:
  0.0 146.3 jit_solution(13092546117230483292)
XLA Ops:
  0.0 0.9 copy-done.4
  0.9 0.7 copy-done.6
  1.6 1.5 first.1
  3.0 7.5 %all-to-all-start = ((bf16[8,2,128,128]{3,2,1,0:T(8,128)(2,1)}), bf16[8,2,128,128]{3,2,1,0:T(8,128)(2,1)S(1)}, u32[]{:S(2)}, u32[]{:S(2)}) async-start(bf16[8,2,128,128]{3,2,1,0:T(8,128)(2,1)} %get-tuple-element.27), calls=%async_computation | async-start | bytes 1048576 | tf_op jit(solution)/shard_map/all_to_all | solution.py:238
  10.5 8.8 %collective-permute-start = (bf16[256,128]{1,0:T(8,128)(2,1)S(1)}, bf16[256,128]{1,0:T(8,128)(2,1)S(1)}, u32[]{:S(2)}, u32[]{:S(2)}) collective-permute-start(bf16[256,128]{1,0:T(8,128)(2,1)S(1)} %get-tuple-element.26), channel_id=1, source_target_pairs={{0,0},{1,16},{2,32},{3,48},{4,64},{5,80},{6,96},{7,112},{8,65},{9,... | collective-permute-start | bytes 196616 | tf_op jit(solution)/shard_map/ppermute | solution.py:241
  20.1 0.1 add_select_fusion.1
  20.2 0.1 reshape.357
  20.3 0.1 add.295
  20.4 0.7 multiply_add_fusion.1
  21.1 0.3 select_reduce_fusion.1
  21.4 0.2 collective-permute-done
  21.6 0.0 all-to-all-done.x_ref
  21.6 1.4 collective-permute-start.1
  23.1 0.9 broadcast_in_dim.104
  23.9 4.2 %all-to-all-start.1 = ((bf16[8,256,128]{2,1,0:T(8,128)(2,1)}), bf16[8,256,128]{2,1,0:T(8,128)(2,1)S(1)}, u32[]{:S(2)}, u32[]{:S(2)}) async-start(bf16[8,256,128]{2,1,0:T(8,128)(2,1)} %broadcast_in_dim.104), calls=%async_computation.1 | async-start | bytes 1048576 | tf_op jit(solution)/shard_map/all_to_all | solution.py:238
  28.1 0.1 pad_add_fusion.place
  28.2 0.1 add_select_fusion
  28.3 0.0 copy-start
  28.3 3.4 %copy-done = bf16[1,1,256,128,128]{4,3,2,1,0:T(8,128)(2,1)S(1)} copy-done((bf16[1,1,256,128,128]{4,3,2,1,0:T(8,128)(2,1)S(1)}, bf16[1,1,256,128,128]{4,3,2,1,0:T(8,128)(2,1)}, u32[]{:S(2)}) %copy-start) | copy-done | bytes 8388632
  31.7 3.9 %mirror.2 = bf16[8,2,128,128]{3,2,1,0:T(8,128)(2,1)} custom-call(s32[272]{0:T(512)S(1)} %broadcast_add_fusion.tab, s32[2]{0:T(128)S(1)} %pad_add_fusion.place, bf16[8,2,128,128]{3,2,1,0:T(8,128)(2,1)S(1)} %all-to-all-done.x_ref, bf16[8,2,128,128]{3,2,1,0:T(8,128)(2,1)S(1)} %collective-permute-done.1.y_ref, bf16[256,128,128]{2,1,0:T(8,128)(2,1)S(1)} %bitcast.6), custom_call_target="tpu_custom_call" | custom-call | flops 1073741824 | bytes 8388608 | tf_op jit(solution)/shard_map/mirror/pallas_call | solution.py:199
  35.6 0.3 all-to-all-done.1.x_ref
  35.9 5.2 %all-to-all-start.2 = ((bf16[8,2,128,128]{3,2,1,0:T(8,128)(2,1)}), bf16[8,2,128,128]{3,2,1,0:T(8,128)(2,1)S(1)}, u32[]{:S(2)}, u32[]{:S(2)}) async-start(bf16[8,2,128,128]{3,2,1,0:T(8,128)(2,1)} %mirror.2), calls=%async_computation.2 | async-start | bytes 1048576 | tf_op jit(solution)/shard_map/all_to_all | solution.py:238
  41.2 0.1 reshape.356
  41.3 0.1 add.260
  41.3 0.1 add.261
  41.5 0.3 select_reduce_fusion
  41.7 0.0 copy-start.1
  41.7 3.4 %copy-done.1 = bf16[1,1,256,128,128]{4,3,2,1,0:T(8,128)(2,1)S(1)} copy-done((bf16[1,1,256,128,128]{4,3,2,1,0:T(8,128)(2,1)S(1)}, bf16[1,1,256,128,128]{4,3,2,1,0:T(8,128)(2,1)}, u32[]{:S(2)}) %copy-start.1) | copy-done | bytes 8388632
  45.1 3.2 %direct.2 = (f32[8,256,128]{2,1,0:T(8,128)S(1)}, bf16[8,256,128]{2,1,0:T(8,128)(2,1)S(1)}) custom-call(s32[288]{0:T(512)S(1)} %broadcast_add_fusion.1.tab, s32[2]{0:T(128)S(1)} %pad_add_fusion.place, bf16[8,256,128]{2,1,0:T(8,128)(2,1)S(1)} %all-to-all-done.1.x_ref, bf16[256,128,128]{2,1,0:T(8,128)(2,1)S(1)} %bitcast.7), custom_call_target="tpu_custom_call" | custom-call | flops 1073741824 | bytes 8388608 | tf_op jit(solution)/shard_map/direct/pallas_call | solution.py:199
  48.3 0.0 all-to-all-done.2.got_ref
  48.3 1.8 %collective-permute-start.2 = (bf16[8,256,128]{2,1,0:T(8,128)(2,1)S(1)}, bf16[8,256,128]{2,1,0:T(8,128)(2,1)S(1)}, u32[]{:S(2)}, u32[]{:S(2)}) collective-permute-start(bf16[8,256,128]{2,1,0:T(8,128)(2,1)S(1)} %get-tuple-element.34), channel_id=1, source_target_pairs={{0,1},{1,0},{2,3},{3,2},{4,5},{5,4},{6,7},{7,6},{8,9},{9,8},{10,11... | collective-permute-start | bytes 1572872 | tf_op jit(solution)/shard_map/ppermute | solution.py:267
  50.1 1.5 %collective-permute-done.2.theirs_ref = bf16[8,256,128]{2,1,0:T(8,128)(2,1)S(1)} collective-permute-done((bf16[8,256,128]{2,1,0:T(8,128)(2,1)S(1)}, bf16[8,256,128]{2,1,0:T(8,128)(2,1)S(1)}, u32[]{:S(2)}, u32[]{:S(2)}) %collective-permute-start.2) | collective-permute-done | bytes 524320 | tf_op jit(solution)/shard_map/ppermute | solution.py:267
  51.6 0.9 both.2
  52.5 6.1 %all-to-all-start.3 = ((bf16[8,256,128]{2,1,0:T(8,128)(2,1)}), bf16[8,256,128]{2,1,0:T(8,128)(2,1)S(1)}, u32[]{:S(2)}, u32[]{:S(2)}) async-start(bf16[8,256,128]{2,1,0:T(8,128)(2,1)} %both.2), calls=%async_computation.3 | async-start | bytes 1048576 | tf_op jit(solution)/shard_map/all_to_all | solution.py:238
  58.6 0.1 gathered.2
  58.7 8.4 %collective-permute-start.3 = (f32[2,128,128]{2,1,0:T(8,128)S(1)}, f32[2,128,128]{2,1,0:T(8,128)S(1)}, u32[]{:S(2)}, u32[]{:S(2)}) collective-permute-start(f32[2,128,128]{2,1,0:T(8,128)S(1)} %gathered.2), channel_id=1, source_target_pairs={{0,0},{16,1},{32,2},{48,3},{64,4},{80,5},{96,6},{112,7},{65,8},{81... | collective-permute-start | bytes 393224 | tf_op jit(solution)/shard_map/ppermute | solution.py:271
  67.1 10.5 %collective-permute-done.3.sum_ref = f32[2,128,128]{2,1,0:T(8,128)S(1)} collective-permute-done((f32[2,128,128]{2,1,0:T(8,128)S(1)}, f32[2,128,128]{2,1,0:T(8,128)S(1)}, u32[]{:S(2)}, u32[]{:S(2)}) %collective-permute-start.3) | collective-permute-done | bytes 131104 | tf_op jit(solution)/shard_map/ppermute | solution.py:271
  77.6 0.1 turned.2.back_ref
  77.7 0.0 all-to-all-done.3.own_ref
  77.8 1.5 %second.1 = (f32[256,128]{1,0:T(8,128)S(1)}, bf16[256,128]{1,0:T(8,128)(2,1)S(1)}, bf16[8,2,128,128]{3,2,1,0:T(8,128)(2,1)}) custom-call(s32[2]{0:T(128)S(1)} %copy-done.7, bf16[8,256,128]{2,1,0:T(8,128)(2,1)S(1)} %all-to-all-done.3.own_ref, f32[256,128]{1,0:T(8,128)S(1)} %turned.2.back_ref, f32[256,128]{1,0:T(8,128)S(1)} %copy-done.5), custom_call_target="tpu_custom_call" | custom-call | bytes 1048576 | tf_op jit(solution)/shard_map/second/pallas_call | solution.py:199
  79.3 3.5 %all-to-all-start.4 = ((bf16[8,2,128,128]{3,2,1,0:T(8,128)(2,1)}), bf16[8,2,128,128]{3,2,1,0:T(8,128)(2,1)S(1)}, u32[]{:S(2)}, u32[]{:S(2)}) async-start(bf16[8,2,128,128]{3,2,1,0:T(8,128)(2,1)} %get-tuple-element.37), calls=%async_computation.4 | async-start | bytes 1048576 | tf_op jit(solution)/shard_map/all_to_all | solution.py:238
  82.8 7.0 %collective-permute-start.4 = (bf16[256,128]{1,0:T(8,128)(2,1)S(1)}, bf16[256,128]{1,0:T(8,128)(2,1)S(1)}, u32[]{:S(2)}, u32[]{:S(2)}) collective-permute-start(bf16[256,128]{1,0:T(8,128)(2,1)S(1)} %get-tuple-element.36), channel_id=1, source_target_pairs={{0,0},{1,16},{2,32},{3,48},{4,64},{5,80},{6,96},{7,112},{8,65},{9,... | collective-permute-start | bytes 196616 | tf_op jit(solution)/shard_map/ppermute | solution.py:241
  89.8 3.0 %collective-permute-done.4 = bf16[256,128]{1,0:T(8,128)(2,1)S(1)} collective-permute-done((bf16[256,128]{1,0:T(8,128)(2,1)S(1)}, bf16[256,128]{1,0:T(8,128)(2,1)S(1)}, u32[]{:S(2)}, u32[]{:S(2)}) %collective-permute-start.4) | collective-permute-done | bytes 65568 | tf_op jit(solution)/shard_map/ppermute | solution.py:241
  92.9 0.0 all-to-all-done.4.x_ref
  92.9 0.0 collective-permute-start.5
  92.9 0.9 broadcast_in_dim.112
  93.7 4.9 %all-to-all-start.5 = ((bf16[8,256,128]{2,1,0:T(8,128)(2,1)}), bf16[8,256,128]{2,1,0:T(8,128)(2,1)S(1)}, u32[]{:S(2)}, u32[]{:S(2)}) async-start(bf16[8,256,128]{2,1,0:T(8,128)(2,1)} %broadcast_in_dim.112), calls=%async_computation.5 | async-start | bytes 1048576 | tf_op jit(solution)/shard_map/all_to_all | solution.py:238
  98.6 0.0 collective-permute-done.5.y_ref
  98.6 3.4 %copy-done.2 = bf16[1,1,256,128,128]{4,3,2,1,0:T(8,128)(2,1)S(1)} copy-done((bf16[1,1,256,128,128]{4,3,2,1,0:T(8,128)(2,1)S(1)}, bf16[1,1,256,128,128]{4,3,2,1,0:T(8,128)(2,1)}, u32[]{:S(2)}) %copy-start.2) | copy-done | bytes 8388632
  102.0 3.9 %mirror.3 = bf16[8,2,128,128]{3,2,1,0:T(8,128)(2,1)} custom-call(s32[272]{0:T(512)S(1)} %broadcast_add_fusion.tab, s32[2]{0:T(128)S(1)} %pad_add_fusion.place, bf16[8,2,128,128]{3,2,1,0:T(8,128)(2,1)S(1)} %all-to-all-done.4.x_ref, bf16[8,2,128,128]{3,2,1,0:T(8,128)(2,1)S(1)} %collective-permute-done.5.y_ref, bf16[256,128,128]{2,1,0:T(8,128)(2,1)S(1)} %bitcast.8), custom_call_target="tpu_custom_call" | custom-call | flops 1073741824 | bytes 8388608 | tf_op jit(solution)/shard_map/mirror/pallas_call | solution.py:199
  105.9 0.5 all-to-all-done.5.x_ref
  106.5 5.2 %all-to-all-start.6 = ((bf16[8,2,128,128]{3,2,1,0:T(8,128)(2,1)}), bf16[8,2,128,128]{3,2,1,0:T(8,128)(2,1)S(1)}, u32[]{:S(2)}, u32[]{:S(2)}) async-start(bf16[8,2,128,128]{3,2,1,0:T(8,128)(2,1)} %mirror.3), calls=%async_computation.6 | async-start | bytes 1048576 | tf_op jit(solution)/shard_map/all_to_all | solution.py:238
  111.7 3.4 %copy-done.3 = bf16[1,1,256,128,128]{4,3,2,1,0:T(8,128)(2,1)S(1)} copy-done((bf16[1,1,256,128,128]{4,3,2,1,0:T(8,128)(2,1)S(1)}, bf16[1,1,256,128,128]{4,3,2,1,0:T(8,128)(2,1)}, u32[]{:S(2)}) %copy-start.3) | copy-done | bytes 8388632
  115.1 3.2 %direct.3 = (f32[8,256,128]{2,1,0:T(8,128)S(1)}, bf16[8,256,128]{2,1,0:T(8,128)(2,1)S(1)}) custom-call(s32[288]{0:T(512)S(1)} %broadcast_add_fusion.1.tab, s32[2]{0:T(128)S(1)} %pad_add_fusion.place, bf16[8,256,128]{2,1,0:T(8,128)(2,1)S(1)} %all-to-all-done.5.x_ref, bf16[256,128,128]{2,1,0:T(8,128)(2,1)S(1)} %bitcast.9), custom_call_target="tpu_custom_call" | custom-call | flops 1073741824 | bytes 8388608 | tf_op jit(solution)/shard_map/direct/pallas_call | solution.py:199
  118.3 0.0 all-to-all-done.6.got_ref
  118.3 2.3 %collective-permute-start.6 = (bf16[8,256,128]{2,1,0:T(8,128)(2,1)S(1)}, bf16[8,256,128]{2,1,0:T(8,128)(2,1)S(1)}, u32[]{:S(2)}, u32[]{:S(2)}) collective-permute-start(bf16[8,256,128]{2,1,0:T(8,128)(2,1)S(1)} %get-tuple-element.44), channel_id=1, source_target_pairs={{0,1},{1,0},{2,3},{3,2},{4,5},{5,4},{6,7},{7,6},{8,9},{9,8},{10,11... | collective-permute-start | bytes 1572872 | tf_op jit(solution)/shard_map/ppermute | solution.py:267
  120.6 1.5 %collective-permute-done.6.theirs_ref = bf16[8,256,128]{2,1,0:T(8,128)(2,1)S(1)} collective-permute-done((bf16[8,256,128]{2,1,0:T(8,128)(2,1)S(1)}, bf16[8,256,128]{2,1,0:T(8,128)(2,1)S(1)}, u32[]{:S(2)}, u32[]{:S(2)}) %collective-permute-start.6) | collective-permute-done | bytes 524320 | tf_op jit(solution)/shard_map/ppermute | solution.py:267
  122.2 0.9 both.3
  123.0 6.0 %all-to-all-start.7 = ((bf16[8,256,128]{2,1,0:T(8,128)(2,1)}), bf16[8,256,128]{2,1,0:T(8,128)(2,1)S(1)}, u32[]{:S(2)}, u32[]{:S(2)}) async-start(bf16[8,256,128]{2,1,0:T(8,128)(2,1)} %both.3), calls=%async_computation.7 | async-start | bytes 1048576 | tf_op jit(solution)/shard_map/all_to_all | solution.py:238
  129.0 0.1 gathered.3
  129.1 8.4 %collective-permute-start.7 = (bf16[2,128,128]{2,1,0:T(8,128)(2,1)S(1)}, bf16[2,128,128]{2,1,0:T(8,128)(2,1)S(1)}, u32[]{:S(2)}, u32[]{:S(2)}) collective-permute-start(bf16[2,128,128]{2,1,0:T(8,128)(2,1)S(1)} %gathered.3), channel_id=1, source_target_pairs={{0,0},{16,1},{32,2},{48,3},{64,4},{80,5},{96,6},{112,7},{65,8},{81... | collective-permute-start | bytes 196616 | tf_op jit(solution)/shard_map/ppermute | solution.py:271
  137.5 7.4 %collective-permute-done.7.sum_ref = bf16[2,128,128]{2,1,0:T(8,128)(2,1)S(1)} collective-permute-done((bf16[2,128,128]{2,1,0:T(8,128)(2,1)S(1)}, bf16[2,128,128]{2,1,0:T(8,128)(2,1)S(1)}, u32[]{:S(2)}, u32[]{:S(2)}) %collective-permute-start.7) | collective-permute-done | bytes 65568 | tf_op jit(solution)/shard_map/ppermute | solution.py:271
  144.9 0.1 turned.3.back_ref
  145.0 1.3 last.1
  (27 shorter events, 0.1 us)
Async XLA Ops:
  0.0 0.9 copy-start.4
  0.9 0.7 copy-start.6
  3.0 18.6 %all-to-all-start = ((bf16[8,2,128,128]{3,2,1,0:T(8,128)(2,1)}), bf16[8,2,128,128]{3,2,1,0:T(8,128)(2,1)S(1)}, u32[]{:S(2)}, u32[]{:S(2)}) async-start(bf16[8,2,128,128]{3,2,1,0:T(8,128)(2,1)} %get-tuple-element.27), calls=%async_computation | async-start | bytes 1048576 | tf_op jit(solution)/shard_map/all_to_all | solution.py:238
  10.5 11.1 %collective-permute-start = (bf16[256,128]{1,0:T(8,128)(2,1)S(1)}, bf16[256,128]{1,0:T(8,128)(2,1)S(1)}, u32[]{:S(2)}, u32[]{:S(2)}) collective-permute-start(bf16[256,128]{1,0:T(8,128)(2,1)S(1)} %get-tuple-element.26), channel_id=1, source_target_pairs={{0,0},{1,16},{2,32},{3,48},{4,64},{5,80},{6,96},{7,112},{8,65},{9,... | collective-permute-start | bytes 196616 | tf_op jit(solution)/shard_map/ppermute | solution.py:241
  21.6 6.7 %collective-permute-start.1 = (bf16[8,2,128,128]{3,2,1,0:T(8,128)(2,1)S(1)}, bf16[8,2,128,128]{3,2,1,0:T(8,128)(2,1)S(1)}, u32[]{:S(2)}, u32[]{:S(2)}) collective-permute-start(bf16[8,2,128,128]{3,2,1,0:T(8,128)(2,1)S(1)} %all-to-all-done.x_ref), channel_id=1, source_target_pairs={{0,1},{1,0},{2,3},{3,2},{4,5},{5,4},{6,7},{7,6},{8,9},{9,8},{10,11... | collective-permute-start | bytes 1572872 | tf_op jit(solution)/shard_map/ppermute | solution.py:244
  23.9 12.0 %all-to-all-start.1 = ((bf16[8,256,128]{2,1,0:T(8,128)(2,1)}), bf16[8,256,128]{2,1,0:T(8,128)(2,1)S(1)}, u32[]{:S(2)}, u32[]{:S(2)}) async-start(bf16[8,256,128]{2,1,0:T(8,128)(2,1)} %broadcast_in_dim.104), calls=%async_computation.1 | async-start | bytes 1048576 | tf_op jit(solution)/shard_map/all_to_all | solution.py:238
  28.3 3.4 %copy-start = (bf16[1,1,256,128,128]{4,3,2,1,0:T(8,128)(2,1)S(1)}, bf16[1,1,256,128,128]{4,3,2,1,0:T(8,128)(2,1)}, u32[]{:S(2)}) copy-start(bf16[1,1,256,128,128]{4,3,2,1,0:T(8,128)(2,1)} %param.8) | copy-start | bytes 25165828
  35.6 42.1 %copy-start.5 = (f32[256,128]{1,0:T(8,128)S(1)}, f32[256,128]{1,0:T(8,128)}, u32[]{:S(2)}) copy-start(f32[256,128]{1,0:T(8,128)} %vectors_ref.5) | copy-start | bytes 393220
  35.6 42.2 %copy-start.7 = (s32[2]{0:T(128)S(1)}, s32[2]{0:T(128)}, u32[]{:S(2)}) copy-start(s32[2]{0:T(128)} %widths.5) | copy-start | bytes 28
  35.9 12.4 %all-to-all-start.2 = ((bf16[8,2,128,128]{3,2,1,0:T(8,128)(2,1)}), bf16[8,2,128,128]{3,2,1,0:T(8,128)(2,1)S(1)}, u32[]{:S(2)}, u32[]{:S(2)}) async-start(bf16[8,2,128,128]{3,2,1,0:T(8,128)(2,1)} %mirror.2), calls=%async_computation.2 | async-start | bytes 1048576 | tf_op jit(solution)/shard_map/all_to_all | solution.py:238
  41.7 3.4 %copy-start.1 = (bf16[1,1,256,128,128]{4,3,2,1,0:T(8,128)(2,1)S(1)}, bf16[1,1,256,128,128]{4,3,2,1,0:T(8,128)(2,1)}, u32[]{:S(2)}) copy-start(bf16[1,1,256,128,128]{4,3,2,1,0:T(8,128)(2,1)} %param.8) | copy-start | bytes 25165828
  48.3 3.3 %collective-permute-start.2 = (bf16[8,256,128]{2,1,0:T(8,128)(2,1)S(1)}, bf16[8,256,128]{2,1,0:T(8,128)(2,1)S(1)}, u32[]{:S(2)}, u32[]{:S(2)}) collective-permute-start(bf16[8,256,128]{2,1,0:T(8,128)(2,1)S(1)} %get-tuple-element.34), channel_id=1, source_target_pairs={{0,1},{1,0},{2,3},{3,2},{4,5},{5,4},{6,7},{7,6},{8,9},{9,8},{10,11... | collective-permute-start | bytes 1572872 | tf_op jit(solution)/shard_map/ppermute | solution.py:267
  52.5 25.2 %all-to-all-start.3 = ((bf16[8,256,128]{2,1,0:T(8,128)(2,1)}), bf16[8,256,128]{2,1,0:T(8,128)(2,1)S(1)}, u32[]{:S(2)}, u32[]{:S(2)}) async-start(bf16[8,256,128]{2,1,0:T(8,128)(2,1)} %both.2), calls=%async_computation.3 | async-start | bytes 1048576 | tf_op jit(solution)/shard_map/all_to_all | solution.py:238
  58.7 18.9 %collective-permute-start.3 = (f32[2,128,128]{2,1,0:T(8,128)S(1)}, f32[2,128,128]{2,1,0:T(8,128)S(1)}, u32[]{:S(2)}, u32[]{:S(2)}) collective-permute-start(f32[2,128,128]{2,1,0:T(8,128)S(1)} %gathered.2), channel_id=1, source_target_pairs={{0,0},{16,1},{32,2},{48,3},{64,4},{80,5},{96,6},{112,7},{65,8},{81... | collective-permute-start | bytes 393224 | tf_op jit(solution)/shard_map/ppermute | solution.py:271
  79.3 13.6 %all-to-all-start.4 = ((bf16[8,2,128,128]{3,2,1,0:T(8,128)(2,1)}), bf16[8,2,128,128]{3,2,1,0:T(8,128)(2,1)S(1)}, u32[]{:S(2)}, u32[]{:S(2)}) async-start(bf16[8,2,128,128]{3,2,1,0:T(8,128)(2,1)} %get-tuple-element.37), calls=%async_computation.4 | async-start | bytes 1048576 | tf_op jit(solution)/shard_map/all_to_all | solution.py:238
  82.8 10.1 %collective-permute-start.4 = (bf16[256,128]{1,0:T(8,128)(2,1)S(1)}, bf16[256,128]{1,0:T(8,128)(2,1)S(1)}, u32[]{:S(2)}, u32[]{:S(2)}) collective-permute-start(bf16[256,128]{1,0:T(8,128)(2,1)S(1)} %get-tuple-element.36), channel_id=1, source_target_pairs={{0,0},{1,16},{2,32},{3,48},{4,64},{5,80},{6,96},{7,112},{8,65},{9,... | collective-permute-start | bytes 196616 | tf_op jit(solution)/shard_map/ppermute | solution.py:241
  92.9 5.7 %collective-permute-start.5 = (bf16[8,2,128,128]{3,2,1,0:T(8,128)(2,1)S(1)}, bf16[8,2,128,128]{3,2,1,0:T(8,128)(2,1)S(1)}, u32[]{:S(2)}, u32[]{:S(2)}) collective-permute-start(bf16[8,2,128,128]{3,2,1,0:T(8,128)(2,1)S(1)} %all-to-all-done.4.x_ref), channel_id=1, source_target_pairs={{0,1},{1,0},{2,3},{3,2},{4,5},{5,4},{6,7},{7,6},{8,9},{9,8},{10,11... | collective-permute-start | bytes 1572872 | tf_op jit(solution)/shard_map/ppermute | solution.py:244
  93.7 12.7 %all-to-all-start.5 = ((bf16[8,256,128]{2,1,0:T(8,128)(2,1)}), bf16[8,256,128]{2,1,0:T(8,128)(2,1)S(1)}, u32[]{:S(2)}, u32[]{:S(2)}) async-start(bf16[8,256,128]{2,1,0:T(8,128)(2,1)} %broadcast_in_dim.112), calls=%async_computation.5 | async-start | bytes 1048576 | tf_op jit(solution)/shard_map/all_to_all | solution.py:238
  98.6 3.4 %copy-start.2 = (bf16[1,1,256,128,128]{4,3,2,1,0:T(8,128)(2,1)S(1)}, bf16[1,1,256,128,128]{4,3,2,1,0:T(8,128)(2,1)}, u32[]{:S(2)}) copy-start(bf16[1,1,256,128,128]{4,3,2,1,0:T(8,128)(2,1)} %param.8) | copy-start | bytes 25165828
  106.5 11.8 %all-to-all-start.6 = ((bf16[8,2,128,128]{3,2,1,0:T(8,128)(2,1)}), bf16[8,2,128,128]{3,2,1,0:T(8,128)(2,1)S(1)}, u32[]{:S(2)}, u32[]{:S(2)}) async-start(bf16[8,2,128,128]{3,2,1,0:T(8,128)(2,1)} %mirror.3), calls=%async_computation.6 | async-start | bytes 1048576 | tf_op jit(solution)/shard_map/all_to_all | solution.py:238
  111.7 3.4 %copy-start.3 = (bf16[1,1,256,128,128]{4,3,2,1,0:T(8,128)(2,1)S(1)}, bf16[1,1,256,128,128]{4,3,2,1,0:T(8,128)(2,1)}, u32[]{:S(2)}) copy-start(bf16[1,1,256,128,128]{4,3,2,1,0:T(8,128)(2,1)} %param.8) | copy-start | bytes 25165828
  118.3 3.9 %collective-permute-start.6 = (bf16[8,256,128]{2,1,0:T(8,128)(2,1)S(1)}, bf16[8,256,128]{2,1,0:T(8,128)(2,1)S(1)}, u32[]{:S(2)}, u32[]{:S(2)}) collective-permute-start(bf16[8,256,128]{2,1,0:T(8,128)(2,1)S(1)} %get-tuple-element.44), channel_id=1, source_target_pairs={{0,1},{1,0},{2,3},{3,2},{4,5},{5,4},{6,7},{7,6},{8,9},{9,8},{10,11... | collective-permute-start | bytes 1572872 | tf_op jit(solution)/shard_map/ppermute | solution.py:267
  123.0 22.0 %all-to-all-start.7 = ((bf16[8,256,128]{2,1,0:T(8,128)(2,1)}), bf16[8,256,128]{2,1,0:T(8,128)(2,1)S(1)}, u32[]{:S(2)}, u32[]{:S(2)}) async-start(bf16[8,256,128]{2,1,0:T(8,128)(2,1)} %both.3), calls=%async_computation.7 | async-start | bytes 1048576 | tf_op jit(solution)/shard_map/all_to_all | solution.py:238
  129.1 15.8 %collective-permute-start.7 = (bf16[2,128,128]{2,1,0:T(8,128)(2,1)S(1)}, bf16[2,128,128]{2,1,0:T(8,128)(2,1)S(1)}, u32[]{:S(2)}, u32[]{:S(2)}) collective-permute-start(bf16[2,128,128]{2,1,0:T(8,128)(2,1)S(1)} %gathered.3), channel_id=1, source_target_pairs={{0,0},{16,1},{32,2},{48,3},{64,4},{80,5},{96,6},{112,7},{65,8},{81... | collective-permute-start | bytes 196616 | tf_op jit(solution)/shard_map/ppermute | solution.py:271

commit v6 on v5

--- a/solution.py
+++ b/solution.py
@@ -23,6 +23,8 @@
 ALL = ROWS + COLS
 D_LEN = 9
 M_LEN = 17
+PIECE = (2 * ATOM, VECS)
+BLOCKS = (2, ATOM, VECS)
 
 
 def tables(slot_rows, slot_cols, count, row, col):
@@ -63,41 +65,66 @@
     return (place < jnp.where(atom == 0, widths[0], widths[1])).astype(F32)
 
 
-def send_forms(current, plain_ref, flip_ref):
-    plain_ref[...] = current.reshape(2 * ATOM, VECS).astype(BF)
-    flipped = jnp.swapaxes(current, 1, 2).astype(BF)
-    for k in range(8):
-        flip_ref[k] = flipped
+def flip(current):
+    return jnp.swapaxes(current, 1, 2)
 
 
 def first_kernel(widths, vectors_ref, plain_ref, flip_ref):
-    shape = (2, ATOM, VECS)
-    first = vectors_ref[...].reshape(shape) * keep_of(widths, shape, 1)
-    send_forms(first, plain_ref, flip_ref)
-
-
-def applied(widths, own_ref, back_ref):
-    shape = (2, ATOM, VECS)
-    total = back_ref[...]
-    for k in range(8):
+    first = vectors_ref[...].reshape(BLOCKS) * keep_of(widths, BLOCKS, 1)
+    plain_ref[...] = first.reshape(PIECE).astype(BF)
+    flip_ref[...] = flip(first).astype(BF)
+
+
+def own_sum(own_ref):
+    total = own_ref[0].astype(F32)
+    for k in range(1, 8):
         total = total + own_ref[k].astype(F32)
-    return total.reshape(shape) * keep_of(widths, shape, 1)
-
-
-def second_kernel(widths, own_ref, back_ref, vectors_ref, out_ref, plain_ref, flip_ref):
-    shape = (2, ATOM, VECS)
-    first = vectors_ref[...].reshape(shape) * keep_of(widths, shape, 1)
-    second = applied(widths, own_ref, back_ref) - CENTER * first
-    out_ref[...] = second.reshape(2 * ATOM, VECS)
-    send_forms(second, plain_ref, flip_ref)
-
-
-def last_kernel(widths, own_ref, back_ref, vectors_ref, second_ref, out_ref):
-    shape = (2, ATOM, VECS)
-    first = vectors_ref[...].reshape(shape) * keep_of(widths, shape, 1)
-    third = applied(widths, own_ref, back_ref)
-    out = 2.0 * (third - CENTER * second_ref[...].reshape(shape)) - first
-    out_ref[...] = out.reshape(2 * ATOM, VECS)
+    return total.reshape(BLOCKS)
+
+
+def second_part_kernel(widths, own_ref, vectors_ref, out_ref):
+    keep = keep_of(widths, BLOCKS, 1)
+    part = own_sum(own_ref) * keep - CENTER * (vectors_ref[...].reshape(BLOCKS) * keep)
+    out_ref[...] = part.reshape(PIECE)
+
+
+def second_col_kernel(widths, got_ref, part_ref, back_ref, copies_ref):
+    total = got_ref[0].astype(F32)
+    for i in range(1, 8):
+        total = total + got_ref[i].astype(F32)
+    total = flip(total)
+    back_ref[...] = total.reshape(PIECE)
+    second = total * keep_of(widths, BLOCKS, 1) + part_ref[...].reshape(BLOCKS)
+    second = second.reshape(PIECE).astype(BF)
+    for i in range(8):
+        copies_ref[i] = second
+
+
+def second_row_kernel(widths, back_ref, part_ref, out_ref, flip_ref):
+    second = back_ref[...].reshape(BLOCKS) * keep_of(widths, BLOCKS, 1)
+    second = second + part_ref[...].reshape(BLOCKS)
+    out_ref[...] = second.reshape(PIECE)
+    flip_ref[...] = flip(second).astype(BF)
+
+
+def last_part_kernel(widths, own_ref, vectors_ref, second_ref, out_ref):
+    keep = keep_of(widths, BLOCKS, 1)
+    first = vectors_ref[...].reshape(BLOCKS) * keep
+    third = own_sum(own_ref) * keep
+    part = 2.0 * (third - CENTER * second_ref[...].reshape(BLOCKS)) - first
+    out_ref[...] = part.reshape(PIECE)
+
+
+def gathered_kernel(got_ref, out_ref):
+    total = got_ref[0].astype(F32)
+    for i in range(1, 8):
+        total = total + got_ref[i].astype(F32)
+    out_ref[...] = flip(total).reshape(PIECE).astype(out_ref.dtype)
+
+
+def last_kernel(widths, back_ref, part_ref, out_ref):
+    back = back_ref[...].astype(F32).reshape(BLOCKS) * keep_of(widths, BLOCKS, 1)
+    out_ref[...] = part_ref[...] + 2.0 * back.reshape(PIECE)
 
 
 def piece_at(place, i):
@@ -136,11 +163,17 @@
     lax.fori_loop(0, 8, step, 0, unroll=True)
 
 
-def mirror_kernel(tab, place, x_ref, y_ref, t_ref, out_ref, held):
-    co = place[0]
-    for xz in range(8):
-        held[pl.ds(4 * xz + 2 * co, 2)] = x_ref[xz]
-        held[pl.ds(4 * xz + 2 - 2 * co, 2)] = y_ref[xz]
+def mirror_kernel(tab, place, z0_ref, z1_ref, z2_ref, z3_ref, c0_ref, c1_ref, c2_ref, c3_ref,
+                  t_ref, out_ref, held):
+    co, z, xh = place[0], place[2], place[3]
+    for core, refs in (
+        (co, (z0_ref, z1_ref, z2_ref, z3_ref)),
+        (1 - co, (c0_ref, c1_ref, c2_ref, c3_ref)),
+    ):
+        for s, ref in enumerate(refs):
+            for rel in range(2):
+                c = 8 * jnp.bitwise_xor(xh, rel) + 2 * jnp.bitwise_and(z - s + 4, 3) + core
+                held[pl.ds(2 * c, 2)] = ref[rel]
     held[AR] = jnp.zeros((VECS, ATOM), BF)
 
     def product(b, q, n):
@@ -168,17 +201,6 @@
     lax.fori_loop(0, 8, step, 0, unroll=True)
 
 
-def gathered_kernel(got_ref, out_ref):
-    total = got_ref[0].astype(F32)
-    for i in range(1, 8):
-        total = total + got_ref[i].astype(F32)
-    out_ref[...] = total.astype(out_ref.dtype)
-
-
-def turned_kernel(sum_ref, out_ref):
-    out_ref[...] = jnp.swapaxes(sum_ref[...].astype(F32), 1, 2).reshape(2 * ATOM, VECS)
-
-
 def both_kernel(mine_ref, theirs_ref, out_ref):
     out_ref[...] = (mine_ref[...] + theirs_ref[...].astype(F32)).astype(BF)
 
@@ -186,10 +208,6 @@
 SMEM = pl.BlockSpec(memory_space=pltpu.SMEM)
 VMEM = pl.BlockSpec(memory_space=pltpu.VMEM)
 PARAMS = pltpu.CompilerParams(vmem_limit_bytes=24 * 1024 * 1024)
-PIECE = (2 * ATOM, VECS)
-BLOCKS = (2, ATOM, VECS)
-
-
 def like(shape, dtype):
     return jax.ShapeDtypeStruct(shape, dtype)
 
@@ -224,10 +242,16 @@
 SWAP = [(0, 1), (1, 0)]
 
 
+def turn(s):
+    return [(k, (k + s) % 4) for k in range(4)]
+
+
 def local(vectors, widths, tiles, block_rows, block_cols, block_count):
     row = lax.axis_index(ROWS)
     col = lax.axis_index(COLS)
-    place = jnp.stack([lax.axis_index("co"), shift_of(col)]).astype(jnp.int32)
+    place = jnp.stack(
+        [lax.axis_index("co"), shift_of(col), lax.axis_index("z"), lax.axis_index("xh")]
+    ).astype(jnp.int32)
     tile_set = tiles[0, 0]
     direct_tab, mirror_tab = tables(
         block_rows[0, 0], block_cols[0, 0], block_count[0, 0], row, col
@@ -237,23 +261,13 @@
     def exchange(x, axes):
         return lax.all_to_all(x, axes, split_axis=0, concat_axis=0, tiled=True)
 
-    def apply_matrix(plain, flipped, sent):
-        piece = lax.ppermute(plain, ALL, TO_COL)
-        near = exchange(flipped, ("xh", "z"))
-        piece, near = lax.optimization_barrier((piece, near))
-        far = lax.ppermute(near, "co", SWAP)
-        col_block = exchange(jnp.broadcast_to(piece[None], (8, *PIECE)), ROWS)
-        mirror = call(
-            mirror_kernel,
-            like((8, *BLOCKS), BF),
-            (mirror_tab, place),
-            (near, far, tile_set),
-            [pltpu.VMEM((AR + 1, VECS, ATOM), BF)],
-            name="mirror",
-            **work,
-        )
-        col_block, mirror = lax.optimization_barrier((col_block, mirror))
-        got = exchange(mirror, ROWS)
+    def row_block(flipped):
+        far = lax.ppermute(flipped, "xh", SWAP)
+        pair = jnp.stack([flipped, far])
+        turned = [pair] + [lax.ppermute(pair, "z", turn(s)) for s in (1, 2, 3)]
+        return (*turned, *(lax.ppermute(t, "co", SWAP) for t in turned))
+
+    def products(col_block, flipped):
         mine, other = call(
             direct_kernel,
             (like((8, *PIECE), F32), like((8, *PIECE), BF)),
@@ -263,25 +277,56 @@
             name="direct",
             **work,
         )
-        other, got = lax.optimization_barrier((other, got))
         theirs = lax.ppermute(other, "co", SWAP)
         both = call(both_kernel, like((8, *PIECE), BF), (), (mine, theirs), name="both")
         own = exchange(both, ("xh", "z"))
-        gathered = call(gathered_kernel, like(BLOCKS, sent), (), (got,), name="gathered")
-        back = lax.ppermute(gathered, ALL, TO_ROW)
-        turned = call(turned_kernel, like(PIECE, F32), (), (back,), name="turned")
-        return own, turned
-
-    forms = (like(PIECE, BF), like((8, *BLOCKS), BF))
-    plain, flipped = call(first_kernel, forms, (widths,), (vectors,), name="first")
-    parts = apply_matrix(plain, flipped, F32)
-    second, plain, flipped = call(
-        second_kernel, (like(PIECE, F32), *forms), (widths,), (*parts, vectors), name="second"
-    )
-    parts = apply_matrix(plain, flipped, BF)
-    return call(
-        last_kernel, like(PIECE, F32), (widths,), (*parts, vectors, second), name="last"
-    )
+        mirror = call(
+            mirror_kernel,
+            like((8, *BLOCKS), BF),
+            (mirror_tab, place),
+            (*row_block(flipped), tile_set),
+            [pltpu.VMEM((AR + 1, VECS, ATOM), BF)],
+            name="mirror",
+            **work,
+        )
+        own, mirror = lax.optimization_barrier((own, mirror))
+        return own, exchange(mirror, ROWS)
+
+    plain, flipped = call(
+        first_kernel, (like(PIECE, BF), like(BLOCKS, BF)), (widths,), (vectors,), name="first"
+    )
+    piece = lax.ppermute(plain, ALL, TO_COL)
+    col_widths = lax.ppermute(
+        jnp.broadcast_to(widths.astype(F32)[:, None], (2, VECS)), ALL, TO_COL
+    )[:, 0].astype(jnp.int32)
+    col_block = exchange(jnp.broadcast_to(piece[None], (8, *PIECE)), ROWS)
+    own, got = products(col_block, flipped)
+    part = call(second_part_kernel, like(PIECE, F32), (widths,), (own, vectors), name="part")
+    col_part = lax.ppermute(part, ALL, TO_COL)
+    back, copies = call(
+        second_col_kernel,
+        (like(PIECE, F32), like((8, *PIECE), BF)),
+        (col_widths,),
+        (got, col_part),
+        name="second_col",
+    )
+    back = lax.ppermute(back, ALL, TO_ROW)
+    col_block = exchange(copies, ROWS)
+    second, flipped = call(
+        second_row_kernel,
+        (like(PIECE, F32), like(BLOCKS, BF)),
+        (widths,),
+        (back, part),
+        name="second_row",
+    )
+    own, got = products(col_block, flipped)
+    part = call(
+        last_part_kernel, like(PIECE, F32), (widths,), (own, vectors, second), name="last_part"
+    )
+    back = call(gathered_kernel, like(PIECE, BF), (), (got,), name="gathered")
+    back = lax.ppermute(back, ALL, TO_ROW)
+    return call(last_kernel, like(PIECE, F32), (widths,), (back, part), name="last")
+
 
 def solution(mesh):
     split = Mesh(mesh.devices.reshape(4, 2, 2, 4, 2), ALL)

time: 147 us -> 172 us (1.17)
  blocking collectives: 0 us -> 22.8 us
  waiting for transfers between devices: 25.1 us -> 41.9 us
  starting transfers between devices: 80.9 us -> 66.9 us
    all_to_all x8 -> x4, starting transfers between devices: 42.7 us -> 18.4 us  [exchange(): return lax.all_to_all(x, axes, split_axis=0, concat_axis=0, tiled=True)]
    all_to_all x0 -> x2, blocking collectives: none -> 22.8 us  [exchange(): return lax.all_to_all(x, axes, split_axis=0, concat_axis=0, tiled=True)]
    ppermute x8 -> x23, waiting for transfers between devices: 24.2 us -> 35.3 us  [the longest x2 16.5 us: local(): back = lax.ppermute(back, ALL, TO_ROW)]
    ppermute x8 -> x23, starting transfers between devices: 38.2 us -> 48.5 us  [the longest x2 9.21 us: local(): back = lax.ppermute(back, ALL, TO_ROW)]
    all_to_all x8 -> x4, waiting for transfers between devices: 0.88 us -> 6.64 us  [exchange(): return lax.all_to_all(x, axes, split_axis=0, concat_axis=0, tiled=True)]
  transfers between devices with their start and end apart: 16 -> 27, of which waited for: 8 -> 14; matrix products, arithmetic and copies ran while one was open for 3% -> 2% of each run, Pallas kernels for 10% -> 8%
where the time goes in v6:
time: 172 us; the launch traced here: 171 us
  starting transfers between devices  66.9 us (39%)
  waiting for transfers between devices  41.9 us (24%)
  blocking collectives  22.8 us (13%)
  Pallas kernels  19.8 us (12%)
  local copies, waits for them, and re-layouts  16.4 us (10%)
    all_to_all x2, blocking collectives, exchange(): return lax.all_to_all(x, axes, split_axis=0, concat_axis=0, tiled=True)  22.8 us
    pallas_call x13, Pallas kernels, call(): pl.pallas_call(kernel, out_shape=out_shape, in_specs=[SMEM] * len(scalars...  19.8 us
    all_to_all x4, starting transfers between devices, exchange(): return lax.all_to_all(x, axes, split_axis=0, concat_axis=0, tiled=True)  18.4 us
    ppermute x2, waiting for transfers between devices, local(): back = lax.ppermute(back, ALL, TO_ROW)  16.5 us
    unnamed x16, local copies, waits for them, and re-layouts  15.1 us
    ppermute x2, starting transfers between devices, local(): back = lax.ppermute(back, ALL, TO_ROW)  9.21 us
    ppermute x6, starting transfers between devices, row_block(): turned = [pair] + [lax.ppermute(pair, 'z', turn(s)) for s in (1, 2, 3)]  9.04 us
    ppermute x1, starting transfers between devices, local(): piece = lax.ppermute(plain, ALL, TO_COL)  8.93 us
  transfers between devices with their start and end apart: 27, of which 14 were waited for; matrix products, arithmetic and copies ran while one was open for 2% of the time, Pallas kernels for 8%

profile of v6, /device:TPU:25, one launch (start us, length us, event | category | flops | bytes accessed | tf_op | source)
XLA Modules:
  0.0 170.5 jit_solution(18002733928928364274)
XLA Ops:
  0.0 0.9 copy-done.4
  0.9 0.7 copy-done.6
  1.6 0.6 first.1
  2.2 8.9 %collective-permute-start.1 = (bf16[256,128]{1,0:T(8,128)(2,1)S(1)}, bf16[256,128]{1,0:T(8,128)(2,1)S(1)}, u32[]{:S(2)}, u32[]{:S(2)}) collective-permute-start(bf16[256,128]{1,0:T(8,128)(2,1)S(1)} %get-tuple-element.19), channel_id=1, source_target_pairs={{0,0},{1,16},{2,32},{3,48},{4,64},{5,80},{6,96},{7,112},{8,65},{9,... | collective-permute-start | bytes 196616 | tf_op jit(solution)/shard_map/ppermute | solution.py:298
  11.5 0.1 reshape.357
  12.4 0.1 add.261
  12.5 0.7 multiply_add_fusion.1
  13.2 0.7 collective-permute-done.1
  13.9 0.8 broadcast_in_dim.105
  14.7 4.0 %all-to-all-start = ((bf16[8,256,128]{2,1,0:T(8,128)(2,1)}), bf16[8,256,128]{2,1,0:T(8,128)(2,1)S(1)}, u32[]{:S(2)}, u32[]{:S(2)}) async-start(bf16[8,256,128]{2,1,0:T(8,128)(2,1)} %broadcast_in_dim.105), calls=%async_computation | async-start | bytes 1048576 | tf_op jit(solution)/shard_map/all_to_all | solution.py:262
  18.8 0.3 select_reduce_fusion
  19.0 6.6 %all-to-all-done.x_ref = bf16[8,256,128]{2,1,0:T(8,128)(2,1)S(1)} async-done(((bf16[8,256,128]{2,1,0:T(8,128)(2,1)}), bf16[8,256,128]{2,1,0:T(8,128)(2,1)S(1)}, u32[]{:S(2)}, u32[]{:S(2)}) %all-to-all-start) | async-done | bytes 524320 | tf_op jit(solution)/shard_map/all_to_all | solution.py:262
  25.7 3.4 %copy-done = bf16[1,1,256,128,128]{4,3,2,1,0:T(8,128)(2,1)S(1)} copy-done((bf16[1,1,256,128,128]{4,3,2,1,0:T(8,128)(2,1)S(1)}, bf16[1,1,256,128,128]{4,3,2,1,0:T(8,128)(2,1)}, u32[]{:S(2)}) %copy-start) | copy-done | bytes 8388632
  29.0 3.1 %direct.2 = (f32[8,256,128]{2,1,0:T(8,128)S(1)}, bf16[8,256,128]{2,1,0:T(8,128)(2,1)S(1)}) custom-call(s32[288]{0:T(512)S(1)} %broadcast_add_fusion.1.tab, s32[4]{0:T(128)S(1)} %pad_add_fusion.place, bf16[8,256,128]{2,1,0:T(8,128)(2,1)S(1)} %all-to-all-done.x_ref, bf16[256,128,128]{2,1,0:T(8,128)(2,1)S(1)} %bitcast.14), custom_call_target="tpu_custom_call" | custom-call | flops 1073741824 | bytes 8388608 | tf_op jit(solution)/shard_map/direct/pallas_call | solution.py:217
  32.2 2.0 %collective-permute-start.2 = (bf16[8,256,128]{2,1,0:T(8,128)(2,1)S(1)}, bf16[8,256,128]{2,1,0:T(8,128)(2,1)S(1)}, u32[]{:S(2)}, u32[]{:S(2)}) collective-permute-start(bf16[8,256,128]{2,1,0:T(8,128)(2,1)S(1)} %get-tuple-element.21), channel_id=1, source_target_pairs={{0,1},{1,0},{2,3},{3,2},{4,5},{5,4},{6,7},{7,6},{8,9},{9,8},{10,11... | collective-permute-start | bytes 1572872 | tf_op jit(solution)/shard_map/ppermute | solution.py:280
  34.6 1.3 collective-permute-start.4
  35.9 2.7 %collective-permute-start.5 = (bf16[2,2,128,128]{3,2,1,0:T(8,128)(2,1)S(1)}, bf16[2,2,128,128]{3,2,1,0:T(8,128)(2,1)S(1)}, u32[]{:S(2)}, u32[]{:S(2)}) collective-permute-start(bf16[2,2,128,128]{3,2,1,0:T(8,128)(2,1)S(1)} %pad_maximum_fusion.z0_ref), channel_id=1, source_target_pairs={{0,4},{2,6},{4,0},{6,2},{1,5},{3,7},{5,1},{7,3},{8,12},{10,14},{12... | collective-permute-start | bytes 393224 | tf_op jit(solution)/shard_map/ppermute | solution.py:267
  38.6 0.3 collective-permute-start.6
  38.9 0.9 both.2
  39.8 4.7 %all-to-all-start.1 = ((bf16[8,256,128]{2,1,0:T(8,128)(2,1)}), bf16[8,256,128]{2,1,0:T(8,128)(2,1)S(1)}, u32[]{:S(2)}, u32[]{:S(2)}) async-start(bf16[8,256,128]{2,1,0:T(8,128)(2,1)} %both.2), calls=%async_computation.1 | async-start | bytes 1048576 | tf_op jit(solution)/shard_map/all_to_all | solution.py:262
  44.5 0.2 select_reduce_fusion.1
  44.8 1.2 collective-permute-start.7
  46.0 0.1 collective-permute-start.8
  46.1 0.4 collective-permute-start.9
  46.6 0.4 collective-permute-done.7.c0_ref
  47.0 0.4 collective-permute-done.8.c1_ref
  47.3 0.2 collective-permute-done.9.c2_ref
  47.5 0.3 collective-permute-done.10.c3_ref
  47.9 3.4 %copy-done.1 = bf16[1,1,256,128,128]{4,3,2,1,0:T(8,128)(2,1)S(1)} copy-done((bf16[1,1,256,128,128]{4,3,2,1,0:T(8,128)(2,1)S(1)}, bf16[1,1,256,128,128]{4,3,2,1,0:T(8,128)(2,1)}, u32[]{:S(2)}) %copy-start.1) | copy-done | bytes 8388632
  51.2 3.9 %mirror.2 = bf16[8,2,128,128]{3,2,1,0:T(8,128)(2,1)} custom-call(s32[272]{0:T(512)S(1)} %broadcast_add_fusion.tab, s32[4]{0:T(128)S(1)} %pad_add_fusion.place, bf16[2,2,128,128]{3,2,1,0:T(8,128)(2,1)S(1)} %pad_maximum_fusion.z0_ref, bf16[2,2,128,128]{3,2,1,0:T(8,128)(2,1)S(1)} %collective-permute-done.4.z1_ref, ...), custom_call_target="tpu_custom_call" | custom-call | flops 1073741824 | bytes 8388608 | tf_op jit(solution)/shard_map/mirror/pallas_call | solution.py:217
  55.2 5.5 %all-to-all-start.2 = ((bf16[8,2,128,128]{3,2,1,0:T(8,128)(2,1)}), bf16[8,2,128,128]{3,2,1,0:T(8,128)(2,1)S(1)}, u32[]{:S(2)}, u32[]{:S(2)}) async-start(bf16[8,2,128,128]{3,2,1,0:T(8,128)(2,1)} %mirror.2), calls=%async_computation.2 | async-start | bytes 1048576 | tf_op jit(solution)/shard_map/all_to_all | solution.py:262
  60.7 8.8 %collective-permute-start = (f32[2,128]{0,1:T(8,128)S(1)}, f32[2,128]{0,1:T(8,128)S(1)}, u32[]{:S(2)}, u32[]{:S(2)}) collective-permute-start(f32[2,128]{0,1:T(8,128)S(1)} %broadcast_in_dim.104), channel_id=1, source_target_pairs={{0,0},{1,16},{2,32},{3,48},{4,64},{5,80},{6,96},{7,112},{8,65},{9,... | collective-permute-start | bytes 3080 | tf_op jit(solution)/shard_map/ppermute | solution.py:299
  69.5 0.6 part.1.part_ref
  70.2 3.3 %collective-permute-start.11 = (f32[256,128]{1,0:T(8,128)S(1)}, f32[256,128]{1,0:T(8,128)S(1)}, u32[]{:S(2)}, u32[]{:S(2)}) collective-permute-start(f32[256,128]{1,0:T(8,128)S(1)} %part.1.part_ref), channel_id=1, source_target_pairs={{0,0},{1,16},{2,32},{3,48},{4,64},{5,80},{6,96},{7,112},{8,65},{9,... | collective-permute-start | bytes 393224 | tf_op jit(solution)/shard_map/ppermute | solution.py:305
  73.5 7.4 %collective-permute-done.11.part_ref = f32[256,128]{1,0:T(8,128)S(1)} collective-permute-done((f32[256,128]{1,0:T(8,128)S(1)}, f32[256,128]{1,0:T(8,128)S(1)}, u32[]{:S(2)}, u32[]{:S(2)}) %collective-permute-start.11) | collective-permute-done | bytes 131104 | tf_op jit(solution)/shard_map/ppermute | solution.py:305
  81.0 0.7 second_col.1
  81.7 10.9 %all_to_all.30.x_ref = bf16[8,256,128]{2,1,0:T(8,128)(2,1)S(1)} all-to-all(bf16[8,256,128]{2,1,0:T(8,128)(2,1)S(1)} %get-tuple-element.25), channel_id=1, replica_groups=mesh['y'=4,'xl'=2,'xh'=2,'z'=4,'co'=2] {'y','xl'}, dimensions={0} | all-to-all | bytes 1048576 | tf_op jit(solution)/shard_map/all_to_all | solution.py:262
  92.5 3.4 %copy-done.2 = bf16[1,1,256,128,128]{4,3,2,1,0:T(8,128)(2,1)S(1)} copy-done((bf16[1,1,256,128,128]{4,3,2,1,0:T(8,128)(2,1)S(1)}, bf16[1,1,256,128,128]{4,3,2,1,0:T(8,128)(2,1)}, u32[]{:S(2)}) %copy-start.2) | copy-done | bytes 8388632
  95.9 3.1 %direct.3 = (f32[8,256,128]{2,1,0:T(8,128)S(1)}, bf16[8,256,128]{2,1,0:T(8,128)(2,1)S(1)}) custom-call(s32[288]{0:T(512)S(1)} %broadcast_add_fusion.1.tab, s32[4]{0:T(128)S(1)} %pad_add_fusion.place, bf16[8,256,128]{2,1,0:T(8,128)(2,1)S(1)} %all_to_all.30.x_ref, bf16[256,128,128]{2,1,0:T(8,128)(2,1)S(1)} %bitcast.16), custom_call_target="tpu_custom_call" | custom-call | flops 1073741824 | bytes 8388608 | tf_op jit(solution)/shard_map/direct/pallas_call | solution.py:217
  99.1 1.9 %collective-permute-start.12 = (bf16[8,256,128]{2,1,0:T(8,128)(2,1)S(1)}, bf16[8,256,128]{2,1,0:T(8,128)(2,1)S(1)}, u32[]{:S(2)}, u32[]{:S(2)}) collective-permute-start(bf16[8,256,128]{2,1,0:T(8,128)(2,1)S(1)} %get-tuple-element.27), channel_id=1, source_target_pairs={{0,1},{1,0},{2,3},{3,2},{4,5},{5,4},{6,7},{7,6},{8,9},{9,8},{10,11... | collective-permute-start | bytes 1572872 | tf_op jit(solution)/shard_map/ppermute | solution.py:280
  101.0 2.6 %collective-permute-start.13 = (f32[256,128]{1,0:T(8,128)S(1)}, f32[256,128]{1,0:T(8,128)S(1)}, u32[]{:S(2)}, u32[]{:S(2)}) collective-permute-start(f32[256,128]{1,0:T(8,128)S(1)} %get-tuple-element.28), channel_id=1, source_target_pairs={{0,0},{16,1},{32,2},{48,3},{64,4},{80,5},{96,6},{112,7},{65,8},{81... | collective-permute-start | bytes 393224 | tf_op jit(solution)/shard_map/ppermute | solution.py:313
  103.6 11.8 %collective-permute-done.13.back_ref = f32[256,128]{1,0:T(8,128)S(1)} collective-permute-done((f32[256,128]{1,0:T(8,128)S(1)}, f32[256,128]{1,0:T(8,128)S(1)}, u32[]{:S(2)}, u32[]{:S(2)}) %collective-permute-start.13) | collective-permute-done | bytes 131104 | tf_op jit(solution)/shard_map/ppermute | solution.py:313
  115.4 0.6 second_row.1
  116.1 0.9 both.3
  117.0 4.2 %all-to-all-start.4 = ((bf16[8,256,128]{2,1,0:T(8,128)(2,1)}), bf16[8,256,128]{2,1,0:T(8,128)(2,1)S(1)}, u32[]{:S(2)}, u32[]{:S(2)}) async-start(bf16[8,256,128]{2,1,0:T(8,128)(2,1)} %both.3), calls=%async_computation.4 | async-start | bytes 1048576 | tf_op jit(solution)/shard_map/all_to_all | solution.py:262
  121.2 0.4 collective-permute-done.14
  121.7 1.1 collective-permute-start.15
  122.8 2.4 %collective-permute-start.16 = (bf16[2,2,128,128]{3,2,1,0:T(8,128)(2,1)S(1)}, bf16[2,2,128,128]{3,2,1,0:T(8,128)(2,1)S(1)}, u32[]{:S(2)}, u32[]{:S(2)}) collective-permute-start(bf16[2,2,128,128]{3,2,1,0:T(8,128)(2,1)S(1)} %pad_maximum_fusion.1.z0_ref), channel_id=1, source_target_pairs={{0,4},{2,6},{4,0},{6,2},{1,5},{3,7},{5,1},{7,3},{8,12},{10,14},{12... | collective-permute-start | bytes 393224 | tf_op jit(solution)/shard_map/ppermute | solution.py:267
  125.2 1.2 collective-permute-start.17
  126.4 1.3 collective-permute-start.18
  127.7 5.8 %collective-permute-done.15.z1_ref = bf16[2,2,128,128]{3,2,1,0:T(8,128)(2,1)S(1)} collective-permute-done((bf16[2,2,128,128]{3,2,1,0:T(8,128)(2,1)S(1)}, bf16[2,2,128,128]{3,2,1,0:T(8,128)(2,1)S(1)}, u32[]{:S(2)}, u32[]{:S(2)}) %collective-permute-start.15) | collective-permute-done | bytes 131104 | tf_op jit(solution)/shard_map/ppermute | solution.py:267
  133.5 1.0 collective-permute-start.19
  134.5 1.9 %collective-permute-done.16.z2_ref = bf16[2,2,128,128]{3,2,1,0:T(8,128)(2,1)S(1)} collective-permute-done((bf16[2,2,128,128]{3,2,1,0:T(8,128)(2,1)S(1)}, bf16[2,2,128,128]{3,2,1,0:T(8,128)(2,1)S(1)}, u32[]{:S(2)}, u32[]{:S(2)}) %collective-permute-start.16) | collective-permute-done | bytes 131104 | tf_op jit(solution)/shard_map/ppermute | solution.py:267
  136.3 1.0 collective-permute-start.20
  137.3 1.0 collective-permute-done.20.c2_ref
  138.3 0.4 collective-permute-done.21.c3_ref
  138.6 3.4 %copy-done.3 = bf16[1,1,256,128,128]{4,3,2,1,0:T(8,128)(2,1)S(1)} copy-done((bf16[1,1,256,128,128]{4,3,2,1,0:T(8,128)(2,1)S(1)}, bf16[1,1,256,128,128]{4,3,2,1,0:T(8,128)(2,1)}, u32[]{:S(2)}) %copy-start.3) | copy-done | bytes 8388632
  142.0 3.1 %mirror.3 = bf16[8,2,128,128]{3,2,1,0:T(8,128)(2,1)S(1)} custom-call(s32[272]{0:T(512)S(1)} %broadcast_add_fusion.tab, s32[4]{0:T(128)S(1)} %pad_add_fusion.place, bf16[2,2,128,128]{3,2,1,0:T(8,128)(2,1)S(1)} %pad_maximum_fusion.1.z0_ref, bf16[2,2,128,128]{3,2,1,0:T(8,128)(2,1)S(1)} %collective-permute-done.15.z1_ref, ...), custom_call_target="tpu_custom_call" | custom-call | flops 1073741824 | bytes 8388608 | tf_op jit(solution)/shard_map/mirror/pallas_call | solution.py:217
  145.2 12.0 %all_to_all.31.got_ref = bf16[8,2,128,128]{3,2,1,0:T(8,128)(2,1)S(1)} all-to-all(bf16[8,2,128,128]{3,2,1,0:T(8,128)(2,1)S(1)} %mirror.3), channel_id=1, replica_groups=mesh['y'=4,'xl'=2,'xh'=2,'z'=4,'co'=2] {'y','xl'}, dimensions={0} | all-to-all | bytes 1048576 | tf_op jit(solution)/shard_map/all_to_all | solution.py:262
  157.1 0.1 gathered.1
  157.3 6.6 %collective-permute-start.22 = (bf16[256,128]{1,0:T(8,128)(2,1)S(1)}, bf16[256,128]{1,0:T(8,128)(2,1)S(1)}, u32[]{:S(2)}, u32[]{:S(2)}) collective-permute-start(bf16[256,128]{1,0:T(8,128)(2,1)S(1)} %gathered.1), channel_id=1, source_target_pairs={{0,0},{16,1},{32,2},{48,3},{64,4},{80,5},{96,6},{112,7},{65,8},{81... | collective-permute-start | bytes 196616 | tf_op jit(solution)/shard_map/ppermute | solution.py:327
  163.9 0.6 last_part.1.part_ref
  164.6 4.7 %collective-permute-done.22.back_ref = bf16[256,128]{1,0:T(8,128)(2,1)S(1)} collective-permute-done((bf16[256,128]{1,0:T(8,128)(2,1)S(1)}, bf16[256,128]{1,0:T(8,128)(2,1)S(1)}, u32[]{:S(2)}, u32[]{:S(2)}) %collective-permute-start.22) | collective-permute-done | bytes 65568 | tf_op jit(solution)/shard_map/ppermute | solution.py:327
  169.3 1.2 last.1
  (55 shorter events, 1.0 us)
Async XLA Ops:
  0.0 0.9 copy-start.4
  0.9 0.7 copy-start.6
  2.2 11.7 %collective-permute-start.1 = (bf16[256,128]{1,0:T(8,128)(2,1)S(1)}, bf16[256,128]{1,0:T(8,128)(2,1)S(1)}, u32[]{:S(2)}, u32[]{:S(2)}) collective-permute-start(bf16[256,128]{1,0:T(8,128)(2,1)S(1)} %get-tuple-element.19), channel_id=1, source_target_pairs={{0,0},{1,16},{2,32},{3,48},{4,64},{5,80},{6,96},{7,112},{8,65},{9,... | collective-permute-start | bytes 196616 | tf_op jit(solution)/shard_map/ppermute | solution.py:298
  11.1 23.4 %collective-permute-start.3 = (bf16[2,128,128]{2,1,0:T(8,128)(2,1)S(1)}, bf16[2,128,128]{2,1,0:T(8,128)(2,1)S(1)}, u32[]{:S(2)}, u32[]{:S(2)}) collective-permute-start(bf16[2,128,128]{2,1,0:T(8,128)(2,1)S(1)} %get-tuple-element.22), channel_id=1, source_target_pairs={{0,8},{8,0},{1,9},{9,1},{2,10},{10,2},{3,11},{11,3},{4,12},{12,4},... | collective-permute-start | bytes 196616 | tf_op jit(solution)/shard_map/ppermute | solution.py:265
  14.7 10.9 %all-to-all-start = ((bf16[8,256,128]{2,1,0:T(8,128)(2,1)}), bf16[8,256,128]{2,1,0:T(8,128)(2,1)S(1)}, u32[]{:S(2)}, u32[]{:S(2)}) async-start(bf16[8,256,128]{2,1,0:T(8,128)(2,1)} %broadcast_in_dim.105), calls=%async_computation | async-start | bytes 1048576 | tf_op jit(solution)/shard_map/all_to_all | solution.py:262
  25.7 3.4 %copy-start = (bf16[1,1,256,128,128]{4,3,2,1,0:T(8,128)(2,1)S(1)}, bf16[1,1,256,128,128]{4,3,2,1,0:T(8,128)(2,1)}, u32[]{:S(2)}) copy-start(bf16[1,1,256,128,128]{4,3,2,1,0:T(8,128)(2,1)} %param.8) | copy-start | bytes 25165828
  32.2 28.5 %copy-start.7 = (s32[2]{0:T(128)S(1)}, s32[2]{0:T(128)}, u32[]{:S(2)}) copy-start(s32[2]{0:T(128)} %widths.9) | copy-start | bytes 28
  32.2 37.3 %copy-start.5 = (f32[256,128]{1,0:T(8,128)S(1)}, f32[256,128]{1,0:T(8,128)}, u32[]{:S(2)}) copy-start(f32[256,128]{1,0:T(8,128)} %vectors_ref.5) | copy-start | bytes 393220
  32.2 6.7 %collective-permute-start.2 = (bf16[8,256,128]{2,1,0:T(8,128)(2,1)S(1)}, bf16[8,256,128]{2,1,0:T(8,128)(2,1)S(1)}, u32[]{:S(2)}, u32[]{:S(2)}) collective-permute-start(bf16[8,256,128]{2,1,0:T(8,128)(2,1)S(1)} %get-tuple-element.21), channel_id=1, source_target_pairs={{0,1},{1,0},{2,3},{3,2},{4,5},{5,4},{6,7},{7,6},{8,9},{9,8},{10,11... | collective-permute-start | bytes 1572872 | tf_op jit(solution)/shard_map/ppermute | solution.py:280
  34.6 11.4 %collective-permute-start.4 = (bf16[2,2,128,128]{3,2,1,0:T(8,128)(2,1)S(1)}, bf16[2,2,128,128]{3,2,1,0:T(8,128)(2,1)S(1)}, u32[]{:S(2)}, u32[]{:S(2)}) collective-permute-start(bf16[2,2,128,128]{3,2,1,0:T(8,128)(2,1)S(1)} %pad_maximum_fusion.z0_ref), channel_id=1, source_target_pairs={{0,2},{2,4},{4,6},{6,0},{1,3},{3,5},{5,7},{7,1},{8,10},{10,12},{12... | collective-permute-start | bytes 393224 | tf_op jit(solution)/shard_map/ppermute | solution.py:267
  35.9 10.2 %collective-permute-start.5 = (bf16[2,2,128,128]{3,2,1,0:T(8,128)(2,1)S(1)}, bf16[2,2,128,128]{3,2,1,0:T(8,128)(2,1)S(1)}, u32[]{:S(2)}, u32[]{:S(2)}) collective-permute-start(bf16[2,2,128,128]{3,2,1,0:T(8,128)(2,1)S(1)} %pad_maximum_fusion.z0_ref), channel_id=1, source_target_pairs={{0,4},{2,6},{4,0},{6,2},{1,5},{3,7},{5,1},{7,3},{8,12},{10,14},{12... | collective-permute-start | bytes 393224 | tf_op jit(solution)/shard_map/ppermute | solution.py:267
  38.6 7.9 %collective-permute-start.6 = (bf16[2,2,128,128]{3,2,1,0:T(8,128)(2,1)S(1)}, bf16[2,2,128,128]{3,2,1,0:T(8,128)(2,1)S(1)}, u32[]{:S(2)}, u32[]{:S(2)}) collective-permute-start(bf16[2,2,128,128]{3,2,1,0:T(8,128)(2,1)S(1)} %pad_maximum_fusion.z0_ref), channel_id=1, source_target_pairs={{0,6},{2,0},{4,2},{6,4},{1,7},{3,1},{5,3},{7,5},{8,14},{10,8},{12,... | collective-permute-start | bytes 393224 | tf_op jit(solution)/shard_map/ppermute | solution.py:267
  39.8 15.3 %all-to-all-start.1 = ((bf16[8,256,128]{2,1,0:T(8,128)(2,1)}), bf16[8,256,128]{2,1,0:T(8,128)(2,1)S(1)}, u32[]{:S(2)}, u32[]{:S(2)}) async-start(bf16[8,256,128]{2,1,0:T(8,128)(2,1)} %both.2), calls=%async_computation.1 | async-start | bytes 1048576 | tf_op jit(solution)/shard_map/all_to_all | solution.py:262
  44.8 2.2 %collective-permute-start.7 = (bf16[2,2,128,128]{3,2,1,0:T(8,128)(2,1)S(1)}, bf16[2,2,128,128]{3,2,1,0:T(8,128)(2,1)S(1)}, u32[]{:S(2)}, u32[]{:S(2)}) collective-permute-start(bf16[2,2,128,128]{3,2,1,0:T(8,128)(2,1)S(1)} %pad_maximum_fusion.z0_ref), channel_id=1, source_target_pairs={{0,1},{1,0},{2,3},{3,2},{4,5},{5,4},{6,7},{7,6},{8,9},{9,8},{10,11... | collective-permute-start | bytes 393224 | tf_op jit(solution)/shard_map/ppermute | solution.py:268
  46.0 1.3 collective-permute-start.8
  46.1 1.4 collective-permute-start.9
  46.5 1.3 collective-permute-start.10
  47.9 3.4 %copy-start.1 = (bf16[1,1,256,128,128]{4,3,2,1,0:T(8,128)(2,1)S(1)}, bf16[1,1,256,128,128]{4,3,2,1,0:T(8,128)(2,1)}, u32[]{:S(2)}) copy-start(bf16[1,1,256,128,128]{4,3,2,1,0:T(8,128)(2,1)} %param.8) | copy-start | bytes 25165828
  55.2 25.8 %all-to-all-start.2 = ((bf16[8,2,128,128]{3,2,1,0:T(8,128)(2,1)}), bf16[8,2,128,128]{3,2,1,0:T(8,128)(2,1)S(1)}, u32[]{:S(2)}, u32[]{:S(2)}) async-start(bf16[8,2,128,128]{3,2,1,0:T(8,128)(2,1)} %mirror.2), calls=%async_computation.2 | async-start | bytes 1048576 | tf_op jit(solution)/shard_map/all_to_all | solution.py:262
  60.7 12.8 %collective-permute-start = (f32[2,128]{0,1:T(8,128)S(1)}, f32[2,128]{0,1:T(8,128)S(1)}, u32[]{:S(2)}, u32[]{:S(2)}) collective-permute-start(f32[2,128]{0,1:T(8,128)S(1)} %broadcast_in_dim.104), channel_id=1, source_target_pairs={{0,0},{1,16},{2,32},{3,48},{4,64},{5,80},{6,96},{7,112},{8,65},{9,... | collective-permute-start | bytes 3080 | tf_op jit(solution)/shard_map/ppermute | solution.py:299
  70.2 10.8 %collective-permute-start.11 = (f32[256,128]{1,0:T(8,128)S(1)}, f32[256,128]{1,0:T(8,128)S(1)}, u32[]{:S(2)}, u32[]{:S(2)}) collective-permute-start(f32[256,128]{1,0:T(8,128)S(1)} %part.1.part_ref), channel_id=1, source_target_pairs={{0,0},{1,16},{2,32},{3,48},{4,64},{5,80},{6,96},{7,112},{8,65},{9,... | collective-permute-start | bytes 393224 | tf_op jit(solution)/shard_map/ppermute | solution.py:305
  92.5 3.4 %copy-start.2 = (bf16[1,1,256,128,128]{4,3,2,1,0:T(8,128)(2,1)S(1)}, bf16[1,1,256,128,128]{4,3,2,1,0:T(8,128)(2,1)}, u32[]{:S(2)}) copy-start(bf16[1,1,256,128,128]{4,3,2,1,0:T(8,128)(2,1)} %param.8) | copy-start | bytes 25165828
  99.1 17.0 %collective-permute-start.12 = (bf16[8,256,128]{2,1,0:T(8,128)(2,1)S(1)}, bf16[8,256,128]{2,1,0:T(8,128)(2,1)S(1)}, u32[]{:S(2)}, u32[]{:S(2)}) collective-permute-start(bf16[8,256,128]{2,1,0:T(8,128)(2,1)S(1)} %get-tuple-element.27), channel_id=1, source_target_pairs={{0,1},{1,0},{2,3},{3,2},{4,5},{5,4},{6,7},{7,6},{8,9},{9,8},{10,11... | collective-permute-start | bytes 1572872 | tf_op jit(solution)/shard_map/ppermute | solution.py:280
  101.0 14.4 %collective-permute-start.13 = (f32[256,128]{1,0:T(8,128)S(1)}, f32[256,128]{1,0:T(8,128)S(1)}, u32[]{:S(2)}, u32[]{:S(2)}) collective-permute-start(f32[256,128]{1,0:T(8,128)S(1)} %get-tuple-element.28), channel_id=1, source_target_pairs={{0,0},{16,1},{32,2},{48,3},{64,4},{80,5},{96,6},{112,7},{65,8},{81... | collective-permute-start | bytes 393224 | tf_op jit(solution)/shard_map/ppermute | solution.py:313
  116.0 5.6 %collective-permute-start.14 = (bf16[2,128,128]{2,1,0:T(8,128)(2,1)S(1)}, bf16[2,128,128]{2,1,0:T(8,128)(2,1)S(1)}, u32[]{:S(2)}, u32[]{:S(2)}) collective-permute-start(bf16[2,128,128]{2,1,0:T(8,128)(2,1)S(1)} %get-tuple-element.29), channel_id=1, source_target_pairs={{0,8},{8,0},{1,9},{9,1},{2,10},{10,2},{3,11},{11,3},{4,12},{12,4},... | collective-permute-start | bytes 196616 | tf_op jit(solution)/shard_map/ppermute | solution.py:265
  117.0 28.1 %all-to-all-start.4 = ((bf16[8,256,128]{2,1,0:T(8,128)(2,1)}), bf16[8,256,128]{2,1,0:T(8,128)(2,1)S(1)}, u32[]{:S(2)}, u32[]{:S(2)}) async-start(bf16[8,256,128]{2,1,0:T(8,128)(2,1)} %both.3), calls=%async_computation.4 | async-start | bytes 1048576 | tf_op jit(solution)/shard_map/all_to_all | solution.py:262
  121.7 11.8 %collective-permute-start.15 = (bf16[2,2,128,128]{3,2,1,0:T(8,128)(2,1)S(1)}, bf16[2,2,128,128]{3,2,1,0:T(8,128)(2,1)S(1)}, u32[]{:S(2)}, u32[]{:S(2)}) collective-permute-start(bf16[2,2,128,128]{3,2,1,0:T(8,128)(2,1)S(1)} %pad_maximum_fusion.1.z0_ref), channel_id=1, source_target_pairs={{0,2},{2,4},{4,6},{6,0},{1,3},{3,5},{5,7},{7,1},{8,10},{10,12},{12... | collective-permute-start | bytes 393224 | tf_op jit(solution)/shard_map/ppermute | solution.py:267
  122.8 13.5 %collective-permute-start.16 = (bf16[2,2,128,128]{3,2,1,0:T(8,128)(2,1)S(1)}, bf16[2,2,128,128]{3,2,1,0:T(8,128)(2,1)S(1)}, u32[]{:S(2)}, u32[]{:S(2)}) collective-permute-start(bf16[2,2,128,128]{3,2,1,0:T(8,128)(2,1)S(1)} %pad_maximum_fusion.1.z0_ref), channel_id=1, source_target_pairs={{0,4},{2,6},{4,0},{6,2},{1,5},{3,7},{5,1},{7,3},{8,12},{10,14},{12... | collective-permute-start | bytes 393224 | tf_op jit(solution)/shard_map/ppermute | solution.py:267
  125.2 12.1 %collective-permute-start.17 = (bf16[2,2,128,128]{3,2,1,0:T(8,128)(2,1)S(1)}, bf16[2,2,128,128]{3,2,1,0:T(8,128)(2,1)S(1)}, u32[]{:S(2)}, u32[]{:S(2)}) collective-permute-start(bf16[2,2,128,128]{3,2,1,0:T(8,128)(2,1)S(1)} %pad_maximum_fusion.1.z0_ref), channel_id=1, source_target_pairs={{0,6},{2,0},{4,2},{6,4},{1,7},{3,1},{5,3},{7,5},{8,14},{10,8},{12,... | collective-permute-start | bytes 393224 | tf_op jit(solution)/shard_map/ppermute | solution.py:267
  126.4 10.9 %collective-permute-start.18 = (bf16[2,2,128,128]{3,2,1,0:T(8,128)(2,1)S(1)}, bf16[2,2,128,128]{3,2,1,0:T(8,128)(2,1)S(1)}, u32[]{:S(2)}, u32[]{:S(2)}) collective-permute-start(bf16[2,2,128,128]{3,2,1,0:T(8,128)(2,1)S(1)} %pad_maximum_fusion.1.z0_ref), channel_id=1, source_target_pairs={{0,1},{1,0},{2,3},{3,2},{4,5},{5,4},{6,7},{7,6},{8,9},{9,8},{10,11... | collective-permute-start | bytes 393224 | tf_op jit(solution)/shard_map/ppermute | solution.py:268
  133.5 3.9 %collective-permute-start.19 = (bf16[2,2,128,128]{3,2,1,0:T(8,128)(2,1)S(1)}, bf16[2,2,128,128]{3,2,1,0:T(8,128)(2,1)S(1)}, u32[]{:S(2)}, u32[]{:S(2)}) collective-permute-start(bf16[2,2,128,128]{3,2,1,0:T(8,128)(2,1)S(1)} %collective-permute-done.15.z1_ref), channel_id=1, source_target_pairs={{0,1},{1,0},{2,3},{3,2},{4,5},{5,4},{6,7},{7,6},{8,9},{9,8},{10,11... | collective-permute-start | bytes 393224 | tf_op jit(solution)/shard_map/ppermute | solution.py:268
  136.3 2.0 %collective-permute-start.20 = (bf16[2,2,128,128]{3,2,1,0:T(8,128)(2,1)S(1)}, bf16[2,2,128,128]{3,2,1,0:T(8,128)(2,1)S(1)}, u32[]{:S(2)}, u32[]{:S(2)}) collective-permute-start(bf16[2,2,128,128]{3,2,1,0:T(8,128)(2,1)S(1)} %collective-permute-done.16.z2_ref), channel_id=1, source_target_pairs={{0,1},{1,0},{2,3},{3,2},{4,5},{5,4},{6,7},{7,6},{8,9},{9,8},{10,11... | collective-permute-start | bytes 393224 | tf_op jit(solution)/shard_map/ppermute | solution.py:268
  137.3 1.3 collective-permute-start.21
  138.6 3.4 %copy-start.3 = (bf16[1,1,256,128,128]{4,3,2,1,0:T(8,128)(2,1)S(1)}, bf16[1,1,256,128,128]{4,3,2,1,0:T(8,128)(2,1)}, u32[]{:S(2)}) copy-start(bf16[1,1,256,128,128]{4,3,2,1,0:T(8,128)(2,1)} %param.8) | copy-start | bytes 25165828
  157.3 12.0 %collective-permute-start.22 = (bf16[256,128]{1,0:T(8,128)(2,1)S(1)}, bf16[256,128]{1,0:T(8,128)(2,1)S(1)}, u32[]{:S(2)}, u32[]{:S(2)}) collective-permute-start(bf16[256,128]{1,0:T(8,128)(2,1)S(1)} %gathered.1), channel_id=1, source_target_pairs={{0,0},{16,1},{32,2},{48,3},{64,4},{80,5},{96,6},{112,7},{65,8},{81... | collective-permute-start | bytes 196616 | tf_op jit(solution)/shard_map/ppermute | solution.py:327

commit v7 on v6

--- a/solution.py
+++ b/solution.py
@@ -71,7 +71,10 @@
 
 def first_kernel(widths, vectors_ref, plain_ref, flip_ref):
     first = vectors_ref[...].reshape(BLOCKS) * keep_of(widths, BLOCKS, 1)
-    plain_ref[...] = first.reshape(PIECE).astype(BF)
+    plain_ref[: 2 * ATOM] = first.reshape(PIECE).astype(BF)
+    atom = lax.broadcasted_iota(jnp.int32, (16, VECS), 0) // 8
+    width = jnp.where(atom == 0, widths[0], widths[1])
+    plain_ref[2 * ATOM:] = width.astype(F32).astype(BF)
     flip_ref[...] = flip(first).astype(BF)
 
 
@@ -88,16 +91,20 @@
     out_ref[...] = part.reshape(PIECE)
 
 
-def second_col_kernel(widths, got_ref, part_ref, back_ref, copies_ref):
+def second_col_kernel(got_ref, part_ref, widths_ref, back_ref, copies_ref):
     total = got_ref[0].astype(F32)
     for i in range(1, 8):
         total = total + got_ref[i].astype(F32)
     total = flip(total)
     back_ref[...] = total.reshape(PIECE)
-    second = total * keep_of(widths, BLOCKS, 1) + part_ref[...].reshape(BLOCKS)
-    second = second.reshape(PIECE).astype(BF)
-    for i in range(8):
-        copies_ref[i] = second
+    place = lax.broadcasted_iota(jnp.int32, (ATOM, VECS), 0).astype(F32)
+    for atom in range(2):
+        width = widths_ref[pl.ds(2 * ATOM, 16)].astype(F32)[8 * atom:8 * atom + 1]
+        keep = (place < width).astype(F32)
+        rows = pl.ds(atom * ATOM, ATOM)
+        second = (total[atom] * keep + part_ref[rows]).astype(BF)
+        for i in range(8):
+            copies_ref[i, rows] = second
 
 
 def second_row_kernel(widths, back_ref, part_ref, out_ref, flip_ref):
@@ -264,10 +271,10 @@
     def row_block(flipped):
         far = lax.ppermute(flipped, "xh", SWAP)
         pair = jnp.stack([flipped, far])
-        turned = [pair] + [lax.ppermute(pair, "z", turn(s)) for s in (1, 2, 3)]
-        return (*turned, *(lax.ppermute(t, "co", SWAP) for t in turned))
-
-    def products(col_block, flipped):
+        return [pair] + [lax.ppermute(pair, "z", turn(s)) for s in (1, 2, 3)]
+
+    def products(col_block, turned):
+        crossed = [lax.ppermute(t, "co", SWAP) for t in turned]
         mine, other = call(
             direct_kernel,
             (like((8, *PIECE), F32), like((8, *PIECE), BF)),
@@ -284,7 +291,7 @@
             mirror_kernel,
             like((8, *BLOCKS), BF),
             (mirror_tab, place),
-            (*row_block(flipped), tile_set),
+            (*turned, *crossed, tile_set),
             [pltpu.VMEM((AR + 1, VECS, ATOM), BF)],
             name="mirror",
             **work,
@@ -293,21 +300,25 @@
         return own, exchange(mirror, ROWS)
 
     plain, flipped = call(
-        first_kernel, (like(PIECE, BF), like(BLOCKS, BF)), (widths,), (vectors,), name="first"
+        first_kernel,
+        (like((2 * ATOM + 16, VECS), BF), like(BLOCKS, BF)),
+        (widths,),
+        (vectors,),
+        name="first",
     )
     piece = lax.ppermute(plain, ALL, TO_COL)
-    col_widths = lax.ppermute(
-        jnp.broadcast_to(widths.astype(F32)[:, None], (2, VECS)), ALL, TO_COL
-    )[:, 0].astype(jnp.int32)
-    col_block = exchange(jnp.broadcast_to(piece[None], (8, *PIECE)), ROWS)
-    own, got = products(col_block, flipped)
+    turned, col_block = row_block(flipped), exchange(
+        jnp.broadcast_to(piece[None, : 2 * ATOM], (8, *PIECE)), ROWS
+    )
+    turned, col_block = lax.optimization_barrier((turned, col_block))
+    own, got = products(col_block, turned)
     part = call(second_part_kernel, like(PIECE, F32), (widths,), (own, vectors), name="part")
     col_part = lax.ppermute(part, ALL, TO_COL)
     back, copies = call(
         second_col_kernel,
         (like(PIECE, F32), like((8, *PIECE), BF)),
-        (col_widths,),
-        (got, col_part),
+        (),
+        (got, col_part, piece),
         name="second_col",
     )
     back = lax.ppermute(back, ALL, TO_ROW)
@@ -319,7 +330,8 @@
         (back, part),
         name="second_row",
     )
-    own, got = products(col_block, flipped)
+    col_block, flipped = lax.optimization_barrier((col_block, flipped))
+    own, got = products(col_block, row_block(flipped))
     part = call(
         last_part_kernel, like(PIECE, F32), (widths,), (own, vectors, second), name="last_part"
     )

time: 172 us -> 161 us (0.936)
  waiting for transfers between devices: 41.9 us -> 31.3 us
  blocking collectives: 22.8 us -> 12.3 us
  starting transfers between devices: 66.9 us -> 76.9 us
    all_to_all x2 -> x1, blocking collectives: 22.8 us -> 12.3 us  [exchange(): return lax.all_to_all(x, axes, split_axis=0, concat_axis=0, tiled=True)]
    ppermute x15 -> x14, starting transfers between devices: 22.9 us -> 15.4 us  [the longest x6 10.3 us: row_block(): return [pair] + [lax.ppermute(pair, 'z', turn(s)) for s in (1, 2, 3)]]
    all_to_all x4 -> x5, waiting for transfers between devices: 6.64 us -> 0.01 us  [exchange(): return lax.all_to_all(x, axes, split_axis=0, concat_axis=0, tiled=True)]
    ppermute x1, starting transfers between devices: 3.34 us -> 9.7 us  [local(): col_part = lax.ppermute(part, ALL, TO_COL)]
    ppermute x2, waiting for transfers between devices: 16.5 us -> 10.7 us  [local(): back = lax.ppermute(back, ALL, TO_ROW)]
    ppermute x2, starting transfers between devices: 9.21 us -> 13.9 us  [local(): back = lax.ppermute(back, ALL, TO_ROW)]
    ppermute x1, waiting for transfers between devices: 7.43 us -> 3.57 us  [local(): col_part = lax.ppermute(part, ALL, TO_COL)]
    ppermute x15 -> x14, waiting for transfers between devices: 10.2 us -> 13.8 us  [the longest x6 11.2 us: row_block(): return [pair] + [lax.ppermute(pair, 'z', turn(s)) for s in (1, 2, 3)]]
  transfers between devices with their start and end apart: 27 -> 27, of which waited for: 14 -> 17; matrix products, arithmetic and copies ran while one was open for 2% -> 2% of each run, Pallas kernels for 8% -> 6%
where the time goes in v7:
time: 161 us; the launch traced here: 160 us
  starting transfers between devices  76.9 us (48%)
  waiting for transfers between devices  31.3 us (19%)
  Pallas kernels  20.1 us (12%)
  local copies, waits for them, and re-layouts  16.4 us (10%)
  blocking collectives  12.3 us (8%)
    all_to_all x5, starting transfers between devices, exchange(): return lax.all_to_all(x, axes, split_axis=0, concat_axis=0, tiled=True)  20.5 us
    pallas_call x13, Pallas kernels, call(): pl.pallas_call(kernel, out_shape=out_shape, in_specs=[SMEM] * len(scalars...  20.1 us
    unnamed x16, local copies, waits for them, and re-layouts  15.1 us
    ppermute x2, starting transfers between devices, local(): back = lax.ppermute(back, ALL, TO_ROW)  13.9 us
    all_to_all x1, blocking collectives, exchange(): return lax.all_to_all(x, axes, split_axis=0, concat_axis=0, tiled=True)  12.3 us
    ppermute x6, waiting for transfers between devices, row_block(): return [pair] + [lax.ppermute(pair, 'z', turn(s)) for s in (1, 2, 3)]  11.2 us
    ppermute x2, waiting for transfers between devices, local(): back = lax.ppermute(back, ALL, TO_ROW)  10.7 us
    ppermute x6, starting transfers between devices, row_block(): return [pair] + [lax.ppermute(pair, 'z', turn(s)) for s in (1, 2, 3)]  10.3 us
  transfers between devices with their start and end apart: 27, of which 17 were waited for; matrix products, arithmetic and copies ran while one was open for 2% of the time, Pallas kernels for 6%

profile of v7, /device:TPU:25, one launch (start us, length us, event | category | flops | bytes accessed | tf_op | source)
XLA Modules:
  0.0 159.5 jit_solution(11347174303664426291)
XLA Ops:
  0.0 0.9 copy-done.4
  0.9 0.7 copy-done.6
  1.6 0.6 first.1
  2.2 2.8 %collective-permute-start = (bf16[2,128,128]{2,1,0:T(8,128)(2,1)S(1)}, bf16[2,128,128]{2,1,0:T(8,128)(2,1)S(1)}, u32[]{:S(2)}, u32[]{:S(2)}) collective-permute-start(bf16[2,128,128]{2,1,0:T(8,128)(2,1)S(1)} %get-tuple-element.26), channel_id=1, source_target_pairs={{0,8},{8,0},{1,9},{9,1},{2,10},{10,2},{3,11},{11,3},{4,12},{12,4},... | collective-permute-start | bytes 196616 | tf_op jit(solution)/shard_map/ppermute | solution.py:272
  5.0 7.6 %collective-permute-start.4 = (bf16[272,128]{1,0:T(8,128)(2,1)S(1)}, bf16[272,128]{1,0:T(8,128)(2,1)S(1)}, u32[]{:S(2)}, u32[]{:S(2)}) collective-permute-start(bf16[272,128]{1,0:T(8,128)(2,1)S(1)} %get-tuple-element.27), channel_id=1, source_target_pairs={{0,0},{1,16},{2,32},{3,48},{4,64},{5,80},{6,96},{7,112},{8,65},{9,... | collective-permute-start | bytes 208904 | tf_op jit(solution)/shard_map/ppermute | solution.py:309
  13.8 0.7 multiply_add_fusion.1
  14.5 0.3 select_reduce_fusion
  14.7 0.5 collective-permute-done.4.widths_ref
  15.2 0.9 broadcast_in_dim.98
  16.1 4.0 %all-to-all-start = ((bf16[8,256,128]{2,1,0:T(8,128)(2,1)}), bf16[8,256,128]{2,1,0:T(8,128)(2,1)S(1)}, u32[]{:S(2)}, u32[]{:S(2)}) async-start(bf16[8,256,128]{2,1,0:T(8,128)(2,1)} %broadcast_in_dim.98), calls=%async_computation | async-start | bytes 1048576 | tf_op jit(solution)/shard_map/all_to_all | solution.py:269
  20.1 1.9 %collective-permute-start.1 = (bf16[2,2,128,128]{3,2,1,0:T(8,128)(2,1)S(1)}, bf16[2,2,128,128]{3,2,1,0:T(8,128)(2,1)S(1)}, u32[]{:S(2)}, u32[]{:S(2)}) collective-permute-start(bf16[2,2,128,128]{3,2,1,0:T(8,128)(2,1)S(1)} %pad_maximum_fusion.z0_ref), channel_id=1, source_target_pairs={{0,2},{2,4},{4,6},{6,0},{1,3},{3,5},{5,7},{7,1},{8,10},{10,12},{12... | collective-permute-start | bytes 393224 | tf_op jit(solution)/shard_map/ppermute | solution.py:274
  22.0 3.0 %collective-permute-start.2 = (bf16[2,2,128,128]{3,2,1,0:T(8,128)(2,1)S(1)}, bf16[2,2,128,128]{3,2,1,0:T(8,128)(2,1)S(1)}, u32[]{:S(2)}, u32[]{:S(2)}) collective-permute-start(bf16[2,2,128,128]{3,2,1,0:T(8,128)(2,1)S(1)} %pad_maximum_fusion.z0_ref), channel_id=1, source_target_pairs={{0,4},{2,6},{4,0},{6,2},{1,5},{3,7},{5,1},{7,3},{8,12},{10,14},{12... | collective-permute-start | bytes 393224 | tf_op jit(solution)/shard_map/ppermute | solution.py:274
  25.0 0.4 collective-permute-start.3
  25.5 0.9 collective-permute-done.1.z1_ref
  26.4 2.4 %collective-permute-done.2.z2_ref = bf16[2,2,128,128]{3,2,1,0:T(8,128)(2,1)S(1)} collective-permute-done((bf16[2,2,128,128]{3,2,1,0:T(8,128)(2,1)S(1)}, bf16[2,2,128,128]{3,2,1,0:T(8,128)(2,1)S(1)}, u32[]{:S(2)}, u32[]{:S(2)}) %collective-permute-start.2) | collective-permute-done | bytes 131104 | tf_op jit(solution)/shard_map/ppermute | solution.py:274
  28.8 0.7 collective-permute-done.3.z3_ref
  29.6 3.4 %copy-done = bf16[1,1,256,128,128]{4,3,2,1,0:T(8,128)(2,1)S(1)} copy-done((bf16[1,1,256,128,128]{4,3,2,1,0:T(8,128)(2,1)S(1)}, bf16[1,1,256,128,128]{4,3,2,1,0:T(8,128)(2,1)}, u32[]{:S(2)}) %copy-start) | copy-done | bytes 8388632
  33.0 3.1 %direct.2 = (f32[8,256,128]{2,1,0:T(8,128)S(1)}, bf16[8,256,128]{2,1,0:T(8,128)(2,1)S(1)}) custom-call(s32[288]{0:T(512)S(1)} %broadcast_add_fusion.1.tab, s32[4]{0:T(128)S(1)} %pad_add_fusion.place, bf16[8,256,128]{2,1,0:T(8,128)(2,1)S(1)} %all-to-all-done.x_ref, bf16[256,128,128]{2,1,0:T(8,128)(2,1)S(1)} %bitcast.12), custom_call_target="tpu_custom_call" | custom-call | flops 1073741824 | bytes 8388608 | tf_op jit(solution)/shard_map/direct/pallas_call | solution.py:224
  36.1 3.4 %collective-permute-start.5 = (bf16[8,256,128]{2,1,0:T(8,128)(2,1)S(1)}, bf16[8,256,128]{2,1,0:T(8,128)(2,1)S(1)}, u32[]{:S(2)}, u32[]{:S(2)}) collective-permute-start(bf16[8,256,128]{2,1,0:T(8,128)(2,1)S(1)} %get-tuple-element.30), channel_id=1, source_target_pairs={{0,1},{1,0},{2,3},{3,2},{4,5},{5,4},{6,7},{7,6},{8,9},{9,8},{10,11... | collective-permute-start | bytes 1572872 | tf_op jit(solution)/shard_map/ppermute | solution.py:287
  39.9 1.2 collective-permute-done.5.theirs_ref
  41.1 0.9 both.2
  42.0 4.1 %all-to-all-start.1 = ((bf16[8,256,128]{2,1,0:T(8,128)(2,1)}), bf16[8,256,128]{2,1,0:T(8,128)(2,1)S(1)}, u32[]{:S(2)}, u32[]{:S(2)}) async-start(bf16[8,256,128]{2,1,0:T(8,128)(2,1)} %both.2), calls=%async_computation.1 | async-start | bytes 1048576 | tf_op jit(solution)/shard_map/all_to_all | solution.py:269
  46.1 0.2 select_reduce_fusion.1
  46.3 0.7 collective-permute-start.6
  47.2 0.4 collective-permute-start.8
  47.7 0.4 collective-permute-done.6.c0_ref
  48.1 0.4 collective-permute-done.7.c1_ref
  48.4 0.2 collective-permute-done.8.c2_ref
  48.6 0.3 collective-permute-done.9.c3_ref
  48.9 3.4 %copy-done.1 = bf16[1,1,256,128,128]{4,3,2,1,0:T(8,128)(2,1)S(1)} copy-done((bf16[1,1,256,128,128]{4,3,2,1,0:T(8,128)(2,1)S(1)}, bf16[1,1,256,128,128]{4,3,2,1,0:T(8,128)(2,1)}, u32[]{:S(2)}) %copy-start.1) | copy-done | bytes 8388632
  52.3 3.9 %mirror.2 = bf16[8,2,128,128]{3,2,1,0:T(8,128)(2,1)} custom-call(s32[272]{0:T(512)S(1)} %broadcast_add_fusion.tab, s32[4]{0:T(128)S(1)} %pad_add_fusion.place, bf16[2,2,128,128]{3,2,1,0:T(8,128)(2,1)S(1)} %pad_maximum_fusion.z0_ref, bf16[2,2,128,128]{3,2,1,0:T(8,128)(2,1)S(1)} %collective-permute-done.1.z1_ref, ...), custom_call_target="tpu_custom_call" | custom-call | flops 1073741824 | bytes 8388608 | tf_op jit(solution)/shard_map/mirror/pallas_call | solution.py:224
  56.3 4.5 %all-to-all-start.2 = ((bf16[8,2,128,128]{3,2,1,0:T(8,128)(2,1)}), bf16[8,2,128,128]{3,2,1,0:T(8,128)(2,1)S(1)}, u32[]{:S(2)}, u32[]{:S(2)}) async-start(bf16[8,2,128,128]{3,2,1,0:T(8,128)(2,1)} %mirror.2), calls=%async_computation.2 | async-start | bytes 1048576 | tf_op jit(solution)/shard_map/all_to_all | solution.py:269
  60.8 0.6 part.1.part_ref
  61.5 9.7 %collective-permute-start.10 = (f32[256,128]{1,0:T(8,128)S(1)}, f32[256,128]{1,0:T(8,128)S(1)}, u32[]{:S(2)}, u32[]{:S(2)}) collective-permute-start(f32[256,128]{1,0:T(8,128)S(1)} %part.1.part_ref), channel_id=1, source_target_pairs={{0,0},{1,16},{2,32},{3,48},{4,64},{5,80},{6,96},{7,112},{8,65},{9,... | collective-permute-start | bytes 393224 | tf_op jit(solution)/shard_map/ppermute | solution.py:316
  71.2 3.6 %collective-permute-done.10.part_ref = f32[256,128]{1,0:T(8,128)S(1)} collective-permute-done((f32[256,128]{1,0:T(8,128)S(1)}, f32[256,128]{1,0:T(8,128)S(1)}, u32[]{:S(2)}, u32[]{:S(2)}) %collective-permute-start.10) | collective-permute-done | bytes 131104 | tf_op jit(solution)/shard_map/ppermute | solution.py:316
  74.7 1.0 second_col.1
  75.7 4.4 %all-to-all-start.3 = ((bf16[8,256,128]{2,1,0:T(8,128)(2,1)}), bf16[8,256,128]{2,1,0:T(8,128)(2,1)S(1)}, u32[]{:S(2)}, u32[]{:S(2)}) async-start(bf16[8,256,128]{2,1,0:T(8,128)(2,1)} %get-tuple-element.37), calls=%async_computation.3 | async-start | bytes 1048576 | tf_op jit(solution)/shard_map/all_to_all | solution.py:269
  80.1 6.7 %collective-permute-start.11 = (f32[256,128]{1,0:T(8,128)S(1)}, f32[256,128]{1,0:T(8,128)S(1)}, u32[]{:S(2)}, u32[]{:S(2)}) collective-permute-start(f32[256,128]{1,0:T(8,128)S(1)} %get-tuple-element.38), channel_id=1, source_target_pairs={{0,0},{16,1},{32,2},{48,3},{64,4},{80,5},{96,6},{112,7},{65,8},{81... | collective-permute-start | bytes 393224 | tf_op jit(solution)/shard_map/ppermute | solution.py:324
  86.8 6.6 %collective-permute-done.11.back_ref = f32[256,128]{1,0:T(8,128)S(1)} collective-permute-done((f32[256,128]{1,0:T(8,128)S(1)}, f32[256,128]{1,0:T(8,128)S(1)}, u32[]{:S(2)}, u32[]{:S(2)}) %collective-permute-start.11) | collective-permute-done | bytes 131104 | tf_op jit(solution)/shard_map/ppermute | solution.py:324
  93.4 0.6 second_row.1
  94.1 3.4 %copy-done.2 = bf16[1,1,256,128,128]{4,3,2,1,0:T(8,128)(2,1)S(1)} copy-done((bf16[1,1,256,128,128]{4,3,2,1,0:T(8,128)(2,1)S(1)}, bf16[1,1,256,128,128]{4,3,2,1,0:T(8,128)(2,1)}, u32[]{:S(2)}) %copy-start.2) | copy-done | bytes 8388632
  97.4 3.1 %direct.3 = (f32[8,256,128]{2,1,0:T(8,128)S(1)}, bf16[8,256,128]{2,1,0:T(8,128)(2,1)S(1)}) custom-call(s32[288]{0:T(512)S(1)} %broadcast_add_fusion.1.tab, s32[4]{0:T(128)S(1)} %pad_add_fusion.place, bf16[8,256,128]{2,1,0:T(8,128)(2,1)S(1)} %all-to-all-done.3.x_ref, bf16[256,128,128]{2,1,0:T(8,128)(2,1)S(1)} %bitcast.14), custom_call_target="tpu_custom_call" | custom-call | flops 1073741824 | bytes 8388608 | tf_op jit(solution)/shard_map/direct/pallas_call | solution.py:224
  100.6 3.5 %collective-permute-start.12 = (bf16[8,256,128]{2,1,0:T(8,128)(2,1)S(1)}, bf16[8,256,128]{2,1,0:T(8,128)(2,1)S(1)}, u32[]{:S(2)}, u32[]{:S(2)}) collective-permute-start(bf16[8,256,128]{2,1,0:T(8,128)(2,1)S(1)} %get-tuple-element.42), channel_id=1, source_target_pairs={{0,1},{1,0},{2,3},{3,2},{4,5},{5,4},{6,7},{7,6},{8,9},{9,8},{10,11... | collective-permute-start | bytes 1572872 | tf_op jit(solution)/shard_map/ppermute | solution.py:287
  104.1 1.5 collective-permute-done.12.theirs_ref
  105.7 0.9 both.3
  106.6 3.5 %all-to-all-start.4 = ((bf16[8,256,128]{2,1,0:T(8,128)(2,1)}), bf16[8,256,128]{2,1,0:T(8,128)(2,1)S(1)}, u32[]{:S(2)}, u32[]{:S(2)}) async-start(bf16[8,256,128]{2,1,0:T(8,128)(2,1)} %both.3), calls=%async_computation.4 | async-start | bytes 1048576 | tf_op jit(solution)/shard_map/all_to_all | solution.py:269
  110.1 1.4 collective-permute-start.14
  111.5 2.4 %collective-permute-start.15 = (bf16[2,2,128,128]{3,2,1,0:T(8,128)(2,1)S(1)}, bf16[2,2,128,128]{3,2,1,0:T(8,128)(2,1)S(1)}, u32[]{:S(2)}, u32[]{:S(2)}) collective-permute-start(bf16[2,2,128,128]{3,2,1,0:T(8,128)(2,1)S(1)} %pad_maximum_fusion.1.z0_ref), channel_id=1, source_target_pairs={{0,4},{2,6},{4,0},{6,2},{1,5},{3,7},{5,1},{7,3},{8,12},{10,14},{12... | collective-permute-start | bytes 393224 | tf_op jit(solution)/shard_map/ppermute | solution.py:274
  113.9 1.2 collective-permute-start.16
  115.1 1.5 collective-permute-start.17
  116.6 5.7 %collective-permute-done.14.z1_ref = bf16[2,2,128,128]{3,2,1,0:T(8,128)(2,1)S(1)} collective-permute-done((bf16[2,2,128,128]{3,2,1,0:T(8,128)(2,1)S(1)}, bf16[2,2,128,128]{3,2,1,0:T(8,128)(2,1)S(1)}, u32[]{:S(2)}, u32[]{:S(2)}) %collective-permute-start.14) | collective-permute-done | bytes 131104 | tf_op jit(solution)/shard_map/ppermute | solution.py:274
  122.3 1.1 collective-permute-start.18
  123.4 1.4 collective-permute-done.15.z2_ref
  124.8 1.2 collective-permute-start.19
  126.0 1.0 collective-permute-done.19.c2_ref
  127.0 0.4 collective-permute-done.20.c3_ref
  127.4 3.4 %copy-done.3 = bf16[1,1,256,128,128]{4,3,2,1,0:T(8,128)(2,1)S(1)} copy-done((bf16[1,1,256,128,128]{4,3,2,1,0:T(8,128)(2,1)S(1)}, bf16[1,1,256,128,128]{4,3,2,1,0:T(8,128)(2,1)}, u32[]{:S(2)}) %copy-start.3) | copy-done | bytes 8388632
  130.8 3.1 %mirror.3 = bf16[8,2,128,128]{3,2,1,0:T(8,128)(2,1)S(1)} custom-call(s32[272]{0:T(512)S(1)} %broadcast_add_fusion.tab, s32[4]{0:T(128)S(1)} %pad_add_fusion.place, bf16[2,2,128,128]{3,2,1,0:T(8,128)(2,1)S(1)} %pad_maximum_fusion.1.z0_ref, bf16[2,2,128,128]{3,2,1,0:T(8,128)(2,1)S(1)} %collective-permute-done.14.z1_ref, ...), custom_call_target="tpu_custom_call" | custom-call | flops 1073741824 | bytes 8388608 | tf_op jit(solution)/shard_map/mirror/pallas_call | solution.py:224
  133.9 12.3 %all_to_all.30.got_ref = bf16[8,2,128,128]{3,2,1,0:T(8,128)(2,1)S(1)} all-to-all(bf16[8,2,128,128]{3,2,1,0:T(8,128)(2,1)S(1)} %mirror.3), channel_id=1, replica_groups=mesh['y'=4,'xl'=2,'xh'=2,'z'=4,'co'=2] {'y','xl'}, dimensions={0} | all-to-all | bytes 1048576 | tf_op jit(solution)/shard_map/all_to_all | solution.py:269
  146.2 0.1 gathered.1
  146.3 7.2 %collective-permute-start.21 = (bf16[256,128]{1,0:T(8,128)(2,1)S(1)}, bf16[256,128]{1,0:T(8,128)(2,1)S(1)}, u32[]{:S(2)}, u32[]{:S(2)}) collective-permute-start(bf16[256,128]{1,0:T(8,128)(2,1)S(1)} %gathered.1), channel_id=1, source_target_pairs={{0,0},{16,1},{32,2},{48,3},{64,4},{80,5},{96,6},{112,7},{65,8},{81... | collective-permute-start | bytes 196616 | tf_op jit(solution)/shard_map/ppermute | solution.py:339
  153.6 0.6 last_part.1.part_ref
  154.2 4.0 %collective-permute-done.21.back_ref = bf16[256,128]{1,0:T(8,128)(2,1)S(1)} collective-permute-done((bf16[256,128]{1,0:T(8,128)(2,1)S(1)}, bf16[256,128]{1,0:T(8,128)(2,1)S(1)}, u32[]{:S(2)}, u32[]{:S(2)}) %collective-permute-start.21) | collective-permute-done | bytes 65568 | tf_op jit(solution)/shard_map/ppermute | solution.py:339
  158.3 1.2 last.1
  (52 shorter events, 1.1 us)
Async XLA Ops:
  0.0 0.9 copy-start.4
  0.9 0.7 copy-start.6
  2.2 17.8 %collective-permute-start = (bf16[2,128,128]{2,1,0:T(8,128)(2,1)S(1)}, bf16[2,128,128]{2,1,0:T(8,128)(2,1)S(1)}, u32[]{:S(2)}, u32[]{:S(2)}) collective-permute-start(bf16[2,128,128]{2,1,0:T(8,128)(2,1)S(1)} %get-tuple-element.26), channel_id=1, source_target_pairs={{0,8},{8,0},{1,9},{9,1},{2,10},{10,2},{3,11},{11,3},{4,12},{12,4},... | collective-permute-start | bytes 196616 | tf_op jit(solution)/shard_map/ppermute | solution.py:272
  5.0 10.2 %collective-permute-start.4 = (bf16[272,128]{1,0:T(8,128)(2,1)S(1)}, bf16[272,128]{1,0:T(8,128)(2,1)S(1)}, u32[]{:S(2)}, u32[]{:S(2)}) collective-permute-start(bf16[272,128]{1,0:T(8,128)(2,1)S(1)} %get-tuple-element.27), channel_id=1, source_target_pairs={{0,0},{1,16},{2,32},{3,48},{4,64},{5,80},{6,96},{7,112},{8,65},{9,... | collective-permute-start | bytes 208904 | tf_op jit(solution)/shard_map/ppermute | solution.py:309
  16.1 13.5 %all-to-all-start = ((bf16[8,256,128]{2,1,0:T(8,128)(2,1)}), bf16[8,256,128]{2,1,0:T(8,128)(2,1)S(1)}, u32[]{:S(2)}, u32[]{:S(2)}) async-start(bf16[8,256,128]{2,1,0:T(8,128)(2,1)} %broadcast_in_dim.98), calls=%async_computation | async-start | bytes 1048576 | tf_op jit(solution)/shard_map/all_to_all | solution.py:269
  20.1 6.4 %collective-permute-start.1 = (bf16[2,2,128,128]{3,2,1,0:T(8,128)(2,1)S(1)}, bf16[2,2,128,128]{3,2,1,0:T(8,128)(2,1)S(1)}, u32[]{:S(2)}, u32[]{:S(2)}) collective-permute-start(bf16[2,2,128,128]{3,2,1,0:T(8,128)(2,1)S(1)} %pad_maximum_fusion.z0_ref), channel_id=1, source_target_pairs={{0,2},{2,4},{4,6},{6,0},{1,3},{3,5},{5,7},{7,1},{8,10},{10,12},{12... | collective-permute-start | bytes 393224 | tf_op jit(solution)/shard_map/ppermute | solution.py:274
  22.0 6.9 %collective-permute-start.2 = (bf16[2,2,128,128]{3,2,1,0:T(8,128)(2,1)S(1)}, bf16[2,2,128,128]{3,2,1,0:T(8,128)(2,1)S(1)}, u32[]{:S(2)}, u32[]{:S(2)}) collective-permute-start(bf16[2,2,128,128]{3,2,1,0:T(8,128)(2,1)S(1)} %pad_maximum_fusion.z0_ref), channel_id=1, source_target_pairs={{0,4},{2,6},{4,0},{6,2},{1,5},{3,7},{5,1},{7,3},{8,12},{10,14},{12... | collective-permute-start | bytes 393224 | tf_op jit(solution)/shard_map/ppermute | solution.py:274
  25.0 4.6 %collective-permute-start.3 = (bf16[2,2,128,128]{3,2,1,0:T(8,128)(2,1)S(1)}, bf16[2,2,128,128]{3,2,1,0:T(8,128)(2,1)S(1)}, u32[]{:S(2)}, u32[]{:S(2)}) collective-permute-start(bf16[2,2,128,128]{3,2,1,0:T(8,128)(2,1)S(1)} %pad_maximum_fusion.z0_ref), channel_id=1, source_target_pairs={{0,6},{2,0},{4,2},{6,4},{1,7},{3,1},{5,3},{7,5},{8,14},{10,8},{12,... | collective-permute-start | bytes 393224 | tf_op jit(solution)/shard_map/ppermute | solution.py:274
  29.6 3.4 %copy-start = (bf16[1,1,256,128,128]{4,3,2,1,0:T(8,128)(2,1)S(1)}, bf16[1,1,256,128,128]{4,3,2,1,0:T(8,128)(2,1)}, u32[]{:S(2)}) copy-start(bf16[1,1,256,128,128]{4,3,2,1,0:T(8,128)(2,1)} %param.8) | copy-start | bytes 25165828
  36.1 24.7 %copy-start.5 = (f32[256,128]{1,0:T(8,128)S(1)}, f32[256,128]{1,0:T(8,128)}, u32[]{:S(2)}) copy-start(f32[256,128]{1,0:T(8,128)} %vectors_ref.5) | copy-start | bytes 393220
  36.1 24.7 %copy-start.7 = (s32[2]{0:T(128)S(1)}, s32[2]{0:T(128)}, u32[]{:S(2)}) copy-start(s32[2]{0:T(128)} %widths.9) | copy-start | bytes 28
  36.1 5.0 %collective-permute-start.5 = (bf16[8,256,128]{2,1,0:T(8,128)(2,1)S(1)}, bf16[8,256,128]{2,1,0:T(8,128)(2,1)S(1)}, u32[]{:S(2)}, u32[]{:S(2)}) collective-permute-start(bf16[8,256,128]{2,1,0:T(8,128)(2,1)S(1)} %get-tuple-element.30), channel_id=1, source_target_pairs={{0,1},{1,0},{2,3},{3,2},{4,5},{5,4},{6,7},{7,6},{8,9},{9,8},{10,11... | collective-permute-start | bytes 1572872 | tf_op jit(solution)/shard_map/ppermute | solution.py:287
  42.0 14.2 %all-to-all-start.1 = ((bf16[8,256,128]{2,1,0:T(8,128)(2,1)}), bf16[8,256,128]{2,1,0:T(8,128)(2,1)S(1)}, u32[]{:S(2)}, u32[]{:S(2)}) async-start(bf16[8,256,128]{2,1,0:T(8,128)(2,1)} %both.2), calls=%async_computation.1 | async-start | bytes 1048576 | tf_op jit(solution)/shard_map/all_to_all | solution.py:269
  46.3 1.7 %collective-permute-start.6 = (bf16[2,2,128,128]{3,2,1,0:T(8,128)(2,1)S(1)}, bf16[2,2,128,128]{3,2,1,0:T(8,128)(2,1)S(1)}, u32[]{:S(2)}, u32[]{:S(2)}) collective-permute-start(bf16[2,2,128,128]{3,2,1,0:T(8,128)(2,1)S(1)} %pad_maximum_fusion.z0_ref), channel_id=1, source_target_pairs={{0,1},{1,0},{2,3},{3,2},{4,5},{5,4},{6,7},{7,6},{8,9},{9,8},{10,11... | collective-permute-start | bytes 393224 | tf_op jit(solution)/shard_map/ppermute | solution.py:277
  47.1 1.3 collective-permute-start.7
  47.2 1.4 collective-permute-start.8
  47.6 1.3 collective-permute-start.9
  48.9 3.4 %copy-start.1 = (bf16[1,1,256,128,128]{4,3,2,1,0:T(8,128)(2,1)S(1)}, bf16[1,1,256,128,128]{4,3,2,1,0:T(8,128)(2,1)}, u32[]{:S(2)}) copy-start(bf16[1,1,256,128,128]{4,3,2,1,0:T(8,128)(2,1)} %param.8) | copy-start | bytes 25165828
  56.3 18.5 %all-to-all-start.2 = ((bf16[8,2,128,128]{3,2,1,0:T(8,128)(2,1)}), bf16[8,2,128,128]{3,2,1,0:T(8,128)(2,1)S(1)}, u32[]{:S(2)}, u32[]{:S(2)}) async-start(bf16[8,2,128,128]{3,2,1,0:T(8,128)(2,1)} %mirror.2), calls=%async_computation.2 | async-start | bytes 1048576 | tf_op jit(solution)/shard_map/all_to_all | solution.py:269
  61.5 13.3 %collective-permute-start.10 = (f32[256,128]{1,0:T(8,128)S(1)}, f32[256,128]{1,0:T(8,128)S(1)}, u32[]{:S(2)}, u32[]{:S(2)}) collective-permute-start(f32[256,128]{1,0:T(8,128)S(1)} %part.1.part_ref), channel_id=1, source_target_pairs={{0,0},{1,16},{2,32},{3,48},{4,64},{5,80},{6,96},{7,112},{8,65},{9,... | collective-permute-start | bytes 393224 | tf_op jit(solution)/shard_map/ppermute | solution.py:316
  75.7 18.4 %all-to-all-start.3 = ((bf16[8,256,128]{2,1,0:T(8,128)(2,1)}), bf16[8,256,128]{2,1,0:T(8,128)(2,1)S(1)}, u32[]{:S(2)}, u32[]{:S(2)}) async-start(bf16[8,256,128]{2,1,0:T(8,128)(2,1)} %get-tuple-element.37), calls=%async_computation.3 | async-start | bytes 1048576 | tf_op jit(solution)/shard_map/all_to_all | solution.py:269
  80.1 13.3 %collective-permute-start.11 = (f32[256,128]{1,0:T(8,128)S(1)}, f32[256,128]{1,0:T(8,128)S(1)}, u32[]{:S(2)}, u32[]{:S(2)}) collective-permute-start(f32[256,128]{1,0:T(8,128)S(1)} %get-tuple-element.38), channel_id=1, source_target_pairs={{0,0},{16,1},{32,2},{48,3},{64,4},{80,5},{96,6},{112,7},{65,8},{81... | collective-permute-start | bytes 393224 | tf_op jit(solution)/shard_map/ppermute | solution.py:324
  94.1 3.4 %copy-start.2 = (bf16[1,1,256,128,128]{4,3,2,1,0:T(8,128)(2,1)S(1)}, bf16[1,1,256,128,128]{4,3,2,1,0:T(8,128)(2,1)}, u32[]{:S(2)}) copy-start(bf16[1,1,256,128,128]{4,3,2,1,0:T(8,128)(2,1)} %param.8) | copy-start | bytes 25165828
  100.6 5.1 %collective-permute-start.12 = (bf16[8,256,128]{2,1,0:T(8,128)(2,1)S(1)}, bf16[8,256,128]{2,1,0:T(8,128)(2,1)S(1)}, u32[]{:S(2)}, u32[]{:S(2)}) collective-permute-start(bf16[8,256,128]{2,1,0:T(8,128)(2,1)S(1)} %get-tuple-element.42), channel_id=1, source_target_pairs={{0,1},{1,0},{2,3},{3,2},{4,5},{5,4},{6,7},{7,6},{8,9},{9,8},{10,11... | collective-permute-start | bytes 1572872 | tf_op jit(solution)/shard_map/ppermute | solution.py:287
  104.1 6.0 %collective-permute-start.13 = (bf16[2,128,128]{2,1,0:T(8,128)(2,1)S(1)}, bf16[2,128,128]{2,1,0:T(8,128)(2,1)S(1)}, u32[]{:S(2)}, u32[]{:S(2)}) collective-permute-start(bf16[2,128,128]{2,1,0:T(8,128)(2,1)S(1)} %get-tuple-element.43), channel_id=1, source_target_pairs={{0,8},{8,0},{1,9},{9,1},{2,10},{10,2},{3,11},{11,3},{4,12},{12,4},... | collective-permute-start | bytes 196616 | tf_op jit(solution)/shard_map/ppermute | solution.py:272
  106.6 27.3 %all-to-all-start.4 = ((bf16[8,256,128]{2,1,0:T(8,128)(2,1)}), bf16[8,256,128]{2,1,0:T(8,128)(2,1)S(1)}, u32[]{:S(2)}, u32[]{:S(2)}) async-start(bf16[8,256,128]{2,1,0:T(8,128)(2,1)} %both.3), calls=%async_computation.4 | async-start | bytes 1048576 | tf_op jit(solution)/shard_map/all_to_all | solution.py:269
  110.1 12.2 %collective-permute-start.14 = (bf16[2,2,128,128]{3,2,1,0:T(8,128)(2,1)S(1)}, bf16[2,2,128,128]{3,2,1,0:T(8,128)(2,1)S(1)}, u32[]{:S(2)}, u32[]{:S(2)}) collective-permute-start(bf16[2,2,128,128]{3,2,1,0:T(8,128)(2,1)S(1)} %pad_maximum_fusion.1.z0_ref), channel_id=1, source_target_pairs={{0,2},{2,4},{4,6},{6,0},{1,3},{3,5},{5,7},{7,1},{8,10},{10,12},{12... | collective-permute-start | bytes 393224 | tf_op jit(solution)/shard_map/ppermute | solution.py:274
  111.5 13.3 %collective-permute-start.15 = (bf16[2,2,128,128]{3,2,1,0:T(8,128)(2,1)S(1)}, bf16[2,2,128,128]{3,2,1,0:T(8,128)(2,1)S(1)}, u32[]{:S(2)}, u32[]{:S(2)}) collective-permute-start(bf16[2,2,128,128]{3,2,1,0:T(8,128)(2,1)S(1)} %pad_maximum_fusion.1.z0_ref), channel_id=1, source_target_pairs={{0,4},{2,6},{4,0},{6,2},{1,5},{3,7},{5,1},{7,3},{8,12},{10,14},{12... | collective-permute-start | bytes 393224 | tf_op jit(solution)/shard_map/ppermute | solution.py:274
  113.9 12.1 %collective-permute-start.16 = (bf16[2,2,128,128]{3,2,1,0:T(8,128)(2,1)S(1)}, bf16[2,2,128,128]{3,2,1,0:T(8,128)(2,1)S(1)}, u32[]{:S(2)}, u32[]{:S(2)}) collective-permute-start(bf16[2,2,128,128]{3,2,1,0:T(8,128)(2,1)S(1)} %pad_maximum_fusion.1.z0_ref), channel_id=1, source_target_pairs={{0,6},{2,0},{4,2},{6,4},{1,7},{3,1},{5,3},{7,5},{8,14},{10,8},{12,... | collective-permute-start | bytes 393224 | tf_op jit(solution)/shard_map/ppermute | solution.py:274
  115.1 10.9 %collective-permute-start.17 = (bf16[2,2,128,128]{3,2,1,0:T(8,128)(2,1)S(1)}, bf16[2,2,128,128]{3,2,1,0:T(8,128)(2,1)S(1)}, u32[]{:S(2)}, u32[]{:S(2)}) collective-permute-start(bf16[2,2,128,128]{3,2,1,0:T(8,128)(2,1)S(1)} %pad_maximum_fusion.1.z0_ref), channel_id=1, source_target_pairs={{0,1},{1,0},{2,3},{3,2},{4,5},{5,4},{6,7},{7,6},{8,9},{9,8},{10,11... | collective-permute-start | bytes 393224 | tf_op jit(solution)/shard_map/ppermute | solution.py:277
  122.3 3.7 %collective-permute-start.18 = (bf16[2,2,128,128]{3,2,1,0:T(8,128)(2,1)S(1)}, bf16[2,2,128,128]{3,2,1,0:T(8,128)(2,1)S(1)}, u32[]{:S(2)}, u32[]{:S(2)}) collective-permute-start(bf16[2,2,128,128]{3,2,1,0:T(8,128)(2,1)S(1)} %collective-permute-done.14.z1_ref), channel_id=1, source_target_pairs={{0,1},{1,0},{2,3},{3,2},{4,5},{5,4},{6,7},{7,6},{8,9},{9,8},{10,11... | collective-permute-start | bytes 393224 | tf_op jit(solution)/shard_map/ppermute | solution.py:277
  124.8 2.2 %collective-permute-start.19 = (bf16[2,2,128,128]{3,2,1,0:T(8,128)(2,1)S(1)}, bf16[2,2,128,128]{3,2,1,0:T(8,128)(2,1)S(1)}, u32[]{:S(2)}, u32[]{:S(2)}) collective-permute-start(bf16[2,2,128,128]{3,2,1,0:T(8,128)(2,1)S(1)} %collective-permute-done.15.z2_ref), channel_id=1, source_target_pairs={{0,1},{1,0},{2,3},{3,2},{4,5},{5,4},{6,7},{7,6},{8,9},{9,8},{10,11... | collective-permute-start | bytes 393224 | tf_op jit(solution)/shard_map/ppermute | solution.py:277
  126.0 1.3 collective-permute-start.20
  127.4 3.4 %copy-start.3 = (bf16[1,1,256,128,128]{4,3,2,1,0:T(8,128)(2,1)S(1)}, bf16[1,1,256,128,128]{4,3,2,1,0:T(8,128)(2,1)}, u32[]{:S(2)}) copy-start(bf16[1,1,256,128,128]{4,3,2,1,0:T(8,128)(2,1)} %param.8) | copy-start | bytes 25165828
  146.3 11.9 %collective-permute-start.21 = (bf16[256,128]{1,0:T(8,128)(2,1)S(1)}, bf16[256,128]{1,0:T(8,128)(2,1)S(1)}, u32[]{:S(2)}, u32[]{:S(2)}) collective-permute-start(bf16[256,128]{1,0:T(8,128)(2,1)S(1)} %gathered.1), channel_id=1, source_target_pairs={{0,0},{16,1},{32,2},{48,3},{64,4},{80,5},{96,6},{112,7},{65,8},{81... | collective-permute-start | bytes 196616 | tf_op jit(solution)/shard_map/ppermute | solution.py:339

commit v8 on v5

--- a/solution.py
+++ b/solution.py
@@ -21,40 +21,52 @@
 ROWS = ("y", "xl")
 COLS = ("xh", "z", "co")
 ALL = ROWS + COLS
-D_LEN = 9
-M_LEN = 17
+D_LEN = 10
+M_LEN = 18
+
+
+def row_lists(row, col):
+    t = jnp.arange(2)[None, :, None]
+    q = jnp.arange(D_LEN)[None, None, :]
+    ga = row * AR + 4 * jnp.arange(8)[:, None, None] + t
+    m = jnp.minimum(q, 7)
+    gb = col * AC + 2 * m
+    main = 2 * m + jnp.where(t == 1, ga <= gb + 1, ga > gb).astype(jnp.int32)
+    near = ga - t - col * AC + jnp.where(t == 1, 0, 1)
+    extra = jnp.where(q == 8, near, jnp.where(t == 1, near + 2, -1))
+    extra = jnp.where((extra >= 0) & (extra < AC), extra, -1)
+    return jnp.where(q < 8, main, extra)
+
+
+def col_lists(row, col):
+    t = jnp.arange(2)[None, :, None]
+    q = jnp.arange(M_LEN)[None, None, :]
+    gb = col * AC + 4 * jnp.arange(4)[:, None, None] + t
+    m = jnp.minimum(q, 15)
+    ga = row * AR + 2 * m
+    main = 2 * m + jnp.where(t == 1, ga + 1 <= gb + 2, ga > gb + 2).astype(jnp.int32)
+    near = gb + 1 - row * AR
+    extra = jnp.where(q == 16, near, jnp.where(t == 0, near + 2, -1))
+    extra = jnp.where((extra >= 0) & (extra < AR), extra, -1)
+    return jnp.where(q < 16, main, extra)
 
 
 def tables(slot_rows, slot_cols, count, row, col):
-    place = jnp.where(jnp.arange(SLOTS) < count, slot_rows * AC + slot_cols, -1)
-
-    def pack(rows, cols, index, zero):
-        want = (rows * AC + cols).reshape(-1, 1)
-        entry = jnp.arange(SLOTS)[None, :] * 64 + index.reshape(-1, 1) - zero
-        return zero + jnp.sum(jnp.where(place[None, :] == want, entry, 0), axis=1)
-
-    a = jnp.arange(AR)[:, None]
-    q = jnp.arange(D_LEN)[None, :]
-    ga = row * AR + a
-    gb = col * AC + 2 * q
-    odd = ga % 2 == 1
-    main = 2 * q + jnp.where(odd, ga <= gb + 1, ga > gb).astype(jnp.int32)
-    extra = ga - 1 - col * AC
-    extra = jnp.where(odd & (extra >= 0) & (extra < AC), extra, -AC * AR)
-    b = jnp.where(q < 8, main, extra)
-    direct = pack(a + 0 * b, b, b, AC)
-
-    b = jnp.arange(AC)[:, None]
-    q = jnp.arange(M_LEN)[None, :]
-    gb = col * AC + b
-    ga = row * AR + 2 * q
-    odd = gb % 2 == 1
-    main = 2 * q + jnp.where(odd, ga + 1 <= gb, ga > gb).astype(jnp.int32)
-    extra = gb + 1 - row * AR
-    extra = jnp.where((~odd) & (extra >= 0) & (extra < AR), extra, -AR)
-    a = jnp.where(q < 16, main, extra)
-    mirror = pack(a, b + 0 * a, a, AR)
-    return direct, mirror
+    place = jnp.where(jnp.arange(SLOTS) < count, slot_rows * AC + slot_cols, -AC * AR)
+
+    def slots(rows, cols, index):
+        want = jnp.where(index < 0, -1, rows * AC + cols).reshape(-1, 1)
+        entry = jnp.arange(SLOTS)[None, :] + 1
+        return jnp.sum(jnp.where(place[None, :] == want, entry, 0), axis=1) - 1
+
+    b = row_lists(row, col)[:, None]
+    a = jnp.arange(AR).reshape(8, 2, 2, 1)
+    direct = slots(a + 0 * b, b + 0 * a, b + 0 * a)
+    a = col_lists(row, col)[:, None]
+    c = jnp.arange(AC).reshape(4, 2, 2, 1)
+    mirror = slots(a + 0 * c, c + 0 * a, a + 0 * c)
+    lists = [jnp.maximum(x, 0).reshape(-1) for x in (b, a)]
+    return lists[0], direct, lists[1], mirror
 
 
 def keep_of(widths, shape, axis):
@@ -105,67 +117,66 @@
     return 2 * jnp.bitwise_and(y - place[1] + 4, 3) + xl
 
 
-def direct_kernel(tab, place, x_ref, t_ref, mine_ref, other_ref, held):
+def device_of(place, k):
+    return 2 * jnp.bitwise_and(k // 2 + place[1], 3) + k % 2
+
+
+def stored(t_ref, e):
+    block = t_ref[jnp.maximum(e, 0)]
+    return jnp.where(e >= 0, block, jnp.zeros_like(block))
+
+
+def direct_kernel(lists, slots, place, x_ref, t_ref, mine_ref, other_ref, held):
     co = place[0]
     for i in range(8):
         held[pl.ds(2 * piece_at(place, i), 2)] = x_ref[i].reshape(2, ATOM, VECS)
-    held[AC] = jnp.zeros((ATOM, VECS), BF)
-
-    def product(a, q, n):
-        blocks, xs = [], []
-        for k in range(n):
-            e = tab[a * D_LEN + q + k]
-            blocks.append(t_ref[lax.shift_right_logical(e, 6)])
-            xs.append(held[jnp.bitwise_and(e, 63)])
-        if n == 1:
-            left, right = blocks[0], xs[0]
-        else:
-            left, right = jnp.concatenate(blocks, 1), jnp.concatenate(xs, 0)
-        return jnp.dot(left, right, preferred_element_type=F32)
 
     def step(xz, carry):
-        for which, out in ((0, mine_ref), (1, other_ref)):
-            for t in range(2):
-                a = 4 * xz + 2 * (co if which == 0 else 1 - co) + t
-                total = product(a, 0, 8)
-                if t:
-                    total = total + product(a, 8, 1)
-                out[xz, t * ATOM:(t + 1) * ATOM, :] = total.astype(out.dtype)
+        for t in range(2):
+            length = 9 + t
+            left = []
+            for core in (co, 1 - co):
+                at = (4 * xz + 2 * core + t) * D_LEN
+                blocks = [stored(t_ref, slots[at + q]) for q in range(length)]
+                left.append(jnp.concatenate(blocks, 1))
+            right = [held[lists[(2 * xz + t) * D_LEN + q]] for q in range(length)]
+            total = jnp.dot(
+                jnp.concatenate(left, 0),
+                jnp.concatenate(right, 0),
+                preferred_element_type=F32,
+            )
+            rows = slice(t * ATOM, (t + 1) * ATOM)
+            mine_ref[xz, rows, :] = total[:ATOM]
+            other_ref[xz, rows, :] = total[ATOM:].astype(BF)
         return carry
 
     lax.fori_loop(0, 8, step, 0, unroll=True)
 
 
-def mirror_kernel(tab, place, x_ref, y_ref, t_ref, out_ref, held):
+def mirror_kernel(lists, slots, place, x_ref, y_ref, t_ref, out_ref, held):
     co = place[0]
     for xz in range(8):
         held[pl.ds(4 * xz + 2 * co, 2)] = x_ref[xz]
         held[pl.ds(4 * xz + 2 - 2 * co, 2)] = y_ref[xz]
-    held[AR] = jnp.zeros((VECS, ATOM), BF)
-
-    def product(b, q, n):
-        blocks, xs = [], []
-        for k in range(n):
-            e = tab[b * M_LEN + q + k]
-            blocks.append(t_ref[lax.shift_right_logical(e, 6)])
-            xs.append(held[jnp.bitwise_and(e, 63)])
-        if n == 1:
-            left, right = xs[0], blocks[0]
-        else:
-            left, right = jnp.concatenate(xs, 1), jnp.concatenate(blocks, 0)
-        return jnp.dot(left, right, preferred_element_type=F32)
-
-    def step(i, carry):
-        k = piece_at(place, i)
+
+    def step(k, carry):
         for t in range(2):
-            b = 2 * k + t
-            total = product(b, 0, 8) + product(b, 8, 8)
-            if not t:
-                total = total + product(b, 16, 1)
-            out_ref[i, t] = total.astype(out_ref.dtype)
+            length = 18 - t
+            left = [held[lists[(2 * k + t) * M_LEN + q]] for q in range(length)]
+            right = []
+            for b in (4 * k + t, 4 * k + 2 + t):
+                blocks = [stored(t_ref, slots[b * M_LEN + q]) for q in range(length)]
+                right.append(jnp.concatenate(blocks, 0))
+            total = jnp.dot(
+                jnp.concatenate(left, 1),
+                jnp.concatenate(right, 1),
+                preferred_element_type=F32,
+            ).astype(BF)
+            out_ref[device_of(place, 2 * k), t] = total[:, :ATOM]
+            out_ref[device_of(place, 2 * k + 1), t] = total[:, ATOM:]
         return carry
 
-    lax.fori_loop(0, 8, step, 0, unroll=True)
+    lax.fori_loop(0, 4, step, 0, unroll=True)
 
 
 def gathered_kernel(got_ref, out_ref):
@@ -229,7 +240,7 @@
     col = lax.axis_index(COLS)
     place = jnp.stack([lax.axis_index("co"), shift_of(col)]).astype(jnp.int32)
     tile_set = tiles[0, 0]
-    direct_tab, mirror_tab = tables(
+    direct_lists, direct_slots, mirror_lists, mirror_slots = tables(
         block_rows[0, 0], block_cols[0, 0], block_count[0, 0], row, col
     )
     work = dict(flops=2 * SLOTS * ATOM**3, size=2**23)
@@ -246,9 +257,9 @@
         mirror = call(
             mirror_kernel,
             like((8, *BLOCKS), BF),
-            (mirror_tab, place),
+            (mirror_lists, mirror_slots, place),
             (near, far, tile_set),
-            [pltpu.VMEM((AR + 1, VECS, ATOM), BF)],
+            [pltpu.VMEM((AR, VECS, ATOM), BF)],
             name="mirror",
             **work,
         )
@@ -257,9 +268,9 @@
         mine, other = call(
             direct_kernel,
             (like((8, *PIECE), F32), like((8, *PIECE), BF)),
-            (direct_tab, place),
+            (direct_lists, direct_slots, place),
             (col_block, tile_set),
-            [pltpu.VMEM((AC + 1, ATOM, VECS), BF)],
+            [pltpu.VMEM((AC, ATOM, VECS), BF)],
             name="direct",
             **work,
         )

time: 147 us -> 147 us (level)
  transfers between devices with their start and end apart: 16 -> 16, of which waited for: 8 -> 7; matrix products, arithmetic and copies ran while one was open for 3% -> 3% of each run, Pallas kernels for 10% -> 10%
where the time goes in v8:
time: 147 us; the launch traced here: 146 us
  starting transfers between devices  79.9 us (54%)
  waiting for transfers between devices  25.4 us (17%)
  Pallas kernels  20.4 us (14%)
  local copies, waits for them, and re-layouts  17.6 us (12%)
  other arithmetic  2.2 us (1%)
    all_to_all x8, starting transfers between devices, exchange(): return lax.all_to_all(x, axes, split_axis=0, concat_axis=0, tiled=True)  42.7 us
    pallas_call x13, Pallas kernels, call(): pl.pallas_call(kernel, out_shape=out_shape, in_specs=[SMEM] * len(scalars...  20.4 us
    ppermute x2, waiting for transfers between devices, apply_matrix(): back = lax.ppermute(gathered, ALL, TO_ROW)  17.9 us
    ppermute x2, starting transfers between devices, apply_matrix(): back = lax.ppermute(gathered, ALL, TO_ROW)  16.7 us
    ppermute x2, starting transfers between devices, apply_matrix(): piece = lax.ppermute(plain, ALL, TO_COL)  15.8 us
    unnamed x16, local copies, waits for them, and re-layouts  15.1 us
    ppermute x2, starting transfers between devices, apply_matrix(): theirs = lax.ppermute(other, 'co', SWAP)  3.87 us
    ppermute x2, waiting for transfers between devices, apply_matrix(): theirs = lax.ppermute(other, 'co', SWAP)  3.07 us
  transfers between devices with their start and end apart: 16, of which 7 were waited for; matrix products, arithmetic and copies ran while one was open for 3% of the time, Pallas kernels for 10%

profile of v8, /device:TPU:25, one launch (start us, length us, event | category | flops | bytes accessed | tf_op | source)
XLA Modules:
  0.0 146.4 jit_solution(12291881015002767014)
XLA Ops:
  0.0 0.9 copy-done.4
  0.9 0.7 copy-done.6
  1.6 1.5 %first.1 = (bf16[256,128]{1,0:T(8,128)(2,1)S(1)}, bf16[8,2,128,128]{3,2,1,0:T(8,128)(2,1)}) custom-call(s32[2]{0:T(128)S(1)} %copy-done.6, f32[256,128]{1,0:T(8,128)S(1)} %copy-done.4), custom_call_target="tpu_custom_call" | custom-call | bytes 1048576 | tf_op jit(solution)/shard_map/first/pallas_call | solution.py:210
  3.0 7.5 %all-to-all-start = ((bf16[8,2,128,128]{3,2,1,0:T(8,128)(2,1)}), bf16[8,2,128,128]{3,2,1,0:T(8,128)(2,1)S(1)}, u32[]{:S(2)}, u32[]{:S(2)}) async-start(bf16[8,2,128,128]{3,2,1,0:T(8,128)(2,1)} %get-tuple-element.27), calls=%async_computation | async-start | bytes 1048576 | tf_op jit(solution)/shard_map/all_to_all | solution.py:249
  10.5 8.8 %collective-permute-start = (bf16[256,128]{1,0:T(8,128)(2,1)S(1)}, bf16[256,128]{1,0:T(8,128)(2,1)S(1)}, u32[]{:S(2)}, u32[]{:S(2)}) collective-permute-start(bf16[256,128]{1,0:T(8,128)(2,1)S(1)} %get-tuple-element.26), channel_id=1, source_target_pairs={{0,0},{1,16},{2,32},{3,48},{4,64},{5,80},{6,96},{7,112},{8,65},{9,... | collective-permute-start | bytes 196616 | tf_op jit(solution)/shard_map/ppermute | solution.py:252
  20.1 0.1 iota_add_fusion
  20.2 0.1 add_subtract_fusion
  20.3 0.1 broadcast_select_fusion.1
  20.4 0.1 fusion.3
  20.4 0.1 broadcast_multiply_fusion
  20.5 0.1 add_select_fusion.1
  20.6 0.1 select_n.222
  20.7 0.7 multiply_add_fusion.1
  21.4 0.1 broadcast_add_fusion
  21.5 0.1 broadcast_select_fusion
  21.6 0.1 fusion
  21.7 0.2 select_reduce_fusion.1
  21.9 0.1 broadcast_compare_fusion
  22.0 0.1 broadcast_in_dim.233
  22.1 0.1 select_n.214
  22.2 0.1 add.363
  22.3 0.8 collective-permute-start.1
  23.1 0.9 broadcast_in_dim.231
  23.9 4.2 %all-to-all-start.1 = ((bf16[8,256,128]{2,1,0:T(8,128)(2,1)}), bf16[8,256,128]{2,1,0:T(8,128)(2,1)S(1)}, u32[]{:S(2)}, u32[]{:S(2)}) async-start(bf16[8,256,128]{2,1,0:T(8,128)(2,1)} %broadcast_in_dim.231), calls=%async_computation.1 | async-start | bytes 1048576 | tf_op jit(solution)/shard_map/all_to_all | solution.py:249
  28.1 0.1 pad_add_fusion.place
  28.2 0.1 broadcast_in_dim.211
  28.3 0.1 select_n.195
  28.4 0.1 add.334
  28.5 0.1 add_select_fusion
  28.6 3.4 %copy-done = bf16[1,1,256,128,128]{4,3,2,1,0:T(8,128)(2,1)S(1)} copy-done((bf16[1,1,256,128,128]{4,3,2,1,0:T(8,128)(2,1)S(1)}, bf16[1,1,256,128,128]{4,3,2,1,0:T(8,128)(2,1)}, u32[]{:S(2)}) %copy-start) | copy-done | bytes 8388632
  32.0 3.5 %mirror.2 = bf16[8,2,128,128]{3,2,1,0:T(8,128)(2,1)} custom-call(s32[144]{0:T(256)S(1)} %fusion.9.lists, s32[288]{0:T(512)S(1)} %broadcast_add_fusion.1.slots, s32[2]{0:T(128)S(1)} %pad_add_fusion.place, bf16[8,2,128,128]{3,2,1,0:T(8,128)(2,1)S(1)} %all-to-all-done.x_ref, bf16[8,2,128,128]{3,2,1,0:T(8,128)(2,1)S(1)} %collective-permute-done.1.y_ref, ...), custom_call_target="tpu_custom_call" | custom-call | flops 1073741824 | bytes 8388608 | tf_op jit(solution)/shard_map/mirror/pallas_call | solution.py:210
  35.5 0.4 all-to-all-done.1.x_ref
  35.9 5.2 %all-to-all-start.2 = ((bf16[8,2,128,128]{3,2,1,0:T(8,128)(2,1)}), bf16[8,2,128,128]{3,2,1,0:T(8,128)(2,1)S(1)}, u32[]{:S(2)}, u32[]{:S(2)}) async-start(bf16[8,2,128,128]{3,2,1,0:T(8,128)(2,1)} %mirror.2), calls=%async_computation.2 | async-start | bytes 1048576 | tf_op jit(solution)/shard_map/all_to_all | solution.py:249
  41.1 0.1 select_n.204
  41.2 0.2 select_reduce_fusion
  41.5 3.4 %copy-done.1 = bf16[1,1,256,128,128]{4,3,2,1,0:T(8,128)(2,1)S(1)} copy-done((bf16[1,1,256,128,128]{4,3,2,1,0:T(8,128)(2,1)S(1)}, bf16[1,1,256,128,128]{4,3,2,1,0:T(8,128)(2,1)}, u32[]{:S(2)}) %copy-start.1) | copy-done | bytes 8388632
  44.9 3.5 %direct.2 = (f32[8,256,128]{2,1,0:T(8,128)S(1)}, bf16[8,256,128]{2,1,0:T(8,128)(2,1)S(1)}) custom-call(s32[160]{0:T(256)S(1)} %fusion.10.lists, s32[320]{0:T(512)S(1)} %broadcast_add_fusion.2.slots, s32[2]{0:T(128)S(1)} %pad_add_fusion.place, bf16[8,256,128]{2,1,0:T(8,128)(2,1)S(1)} %all-to-all-done.1.x_ref, bf16[256,128,128]{2,1,0:T(8,128)(2,1)S(1)} %bitcast.11), custom_call_target="tpu_custom_call" | custom-call | flops 1073741824 | bytes 8388608 | tf_op jit(solution)/shard_map/direct/pallas_call | solution.py:210
  48.4 1.8 %collective-permute-start.2 = (bf16[8,256,128]{2,1,0:T(8,128)(2,1)S(1)}, bf16[8,256,128]{2,1,0:T(8,128)(2,1)S(1)}, u32[]{:S(2)}, u32[]{:S(2)}) collective-permute-start(bf16[8,256,128]{2,1,0:T(8,128)(2,1)S(1)} %get-tuple-element.34), channel_id=1, source_target_pairs={{0,1},{1,0},{2,3},{3,2},{4,5},{5,4},{6,7},{7,6},{8,9},{9,8},{10,11... | collective-permute-start | bytes 1572872 | tf_op jit(solution)/shard_map/ppermute | solution.py:278
  50.2 1.5 %collective-permute-done.2.theirs_ref = bf16[8,256,128]{2,1,0:T(8,128)(2,1)S(1)} collective-permute-done((bf16[8,256,128]{2,1,0:T(8,128)(2,1)S(1)}, bf16[8,256,128]{2,1,0:T(8,128)(2,1)S(1)}, u32[]{:S(2)}, u32[]{:S(2)}) %collective-permute-start.2) | collective-permute-done | bytes 524320 | tf_op jit(solution)/shard_map/ppermute | solution.py:278
  51.7 0.9 both.2
  52.6 6.1 %all-to-all-start.3 = ((bf16[8,256,128]{2,1,0:T(8,128)(2,1)}), bf16[8,256,128]{2,1,0:T(8,128)(2,1)S(1)}, u32[]{:S(2)}, u32[]{:S(2)}) async-start(bf16[8,256,128]{2,1,0:T(8,128)(2,1)} %both.2), calls=%async_computation.3 | async-start | bytes 1048576 | tf_op jit(solution)/shard_map/all_to_all | solution.py:249
  58.8 8.3 %collective-permute-start.3 = (f32[2,128,128]{2,1,0:T(8,128)S(1)}, f32[2,128,128]{2,1,0:T(8,128)S(1)}, u32[]{:S(2)}, u32[]{:S(2)}) collective-permute-start(f32[2,128,128]{2,1,0:T(8,128)S(1)} %gathered.2), channel_id=1, source_target_pairs={{0,0},{16,1},{32,2},{48,3},{64,4},{80,5},{96,6},{112,7},{65,8},{81... | collective-permute-start | bytes 393224 | tf_op jit(solution)/shard_map/ppermute | solution.py:282
  67.1 10.5 %collective-permute-done.3.sum_ref = f32[2,128,128]{2,1,0:T(8,128)S(1)} collective-permute-done((f32[2,128,128]{2,1,0:T(8,128)S(1)}, f32[2,128,128]{2,1,0:T(8,128)S(1)}, u32[]{:S(2)}, u32[]{:S(2)}) %collective-permute-start.3) | collective-permute-done | bytes 131104 | tf_op jit(solution)/shard_map/ppermute | solution.py:282
  77.6 0.1 turned.2.back_ref
  77.7 1.5 %second.1 = (f32[256,128]{1,0:T(8,128)S(1)}, bf16[256,128]{1,0:T(8,128)(2,1)S(1)}, bf16[8,2,128,128]{3,2,1,0:T(8,128)(2,1)}) custom-call(s32[2]{0:T(128)S(1)} %copy-done.7, bf16[8,256,128]{2,1,0:T(8,128)(2,1)S(1)} %all-to-all-done.3.own_ref, f32[256,128]{1,0:T(8,128)S(1)} %turned.2.back_ref, f32[256,128]{1,0:T(8,128)S(1)} %copy-done.5), custom_call_target="tpu_custom_call" | custom-call | bytes 1048576 | tf_op jit(solution)/shard_map/second/pallas_call | solution.py:210
  79.3 3.5 %all-to-all-start.4 = ((bf16[8,2,128,128]{3,2,1,0:T(8,128)(2,1)}), bf16[8,2,128,128]{3,2,1,0:T(8,128)(2,1)S(1)}, u32[]{:S(2)}, u32[]{:S(2)}) async-start(bf16[8,2,128,128]{3,2,1,0:T(8,128)(2,1)} %get-tuple-element.37), calls=%async_computation.4 | async-start | bytes 1048576 | tf_op jit(solution)/shard_map/all_to_all | solution.py:249
  82.8 7.0 %collective-permute-start.4 = (bf16[256,128]{1,0:T(8,128)(2,1)S(1)}, bf16[256,128]{1,0:T(8,128)(2,1)S(1)}, u32[]{:S(2)}, u32[]{:S(2)}) collective-permute-start(bf16[256,128]{1,0:T(8,128)(2,1)S(1)} %get-tuple-element.36), channel_id=1, source_target_pairs={{0,0},{1,16},{2,32},{3,48},{4,64},{5,80},{6,96},{7,112},{8,65},{9,... | collective-permute-start | bytes 196616 | tf_op jit(solution)/shard_map/ppermute | solution.py:252
  89.8 3.0 %collective-permute-done.4 = bf16[256,128]{1,0:T(8,128)(2,1)S(1)} collective-permute-done((bf16[256,128]{1,0:T(8,128)(2,1)S(1)}, bf16[256,128]{1,0:T(8,128)(2,1)S(1)}, u32[]{:S(2)}, u32[]{:S(2)}) %collective-permute-start.4) | collective-permute-done | bytes 65568 | tf_op jit(solution)/shard_map/ppermute | solution.py:252
  92.9 0.9 broadcast_in_dim.251
  93.7 4.9 %all-to-all-start.5 = ((bf16[8,256,128]{2,1,0:T(8,128)(2,1)}), bf16[8,256,128]{2,1,0:T(8,128)(2,1)S(1)}, u32[]{:S(2)}, u32[]{:S(2)}) async-start(bf16[8,256,128]{2,1,0:T(8,128)(2,1)} %broadcast_in_dim.251), calls=%async_computation.5 | async-start | bytes 1048576 | tf_op jit(solution)/shard_map/all_to_all | solution.py:249
  98.6 3.4 %copy-done.2 = bf16[1,1,256,128,128]{4,3,2,1,0:T(8,128)(2,1)S(1)} copy-done((bf16[1,1,256,128,128]{4,3,2,1,0:T(8,128)(2,1)S(1)}, bf16[1,1,256,128,128]{4,3,2,1,0:T(8,128)(2,1)}, u32[]{:S(2)}) %copy-start.2) | copy-done | bytes 8388632
  102.0 3.5 %mirror.3 = bf16[8,2,128,128]{3,2,1,0:T(8,128)(2,1)} custom-call(s32[144]{0:T(256)S(1)} %fusion.9.lists, s32[288]{0:T(512)S(1)} %broadcast_add_fusion.1.slots, s32[2]{0:T(128)S(1)} %pad_add_fusion.place, bf16[8,2,128,128]{3,2,1,0:T(8,128)(2,1)S(1)} %all-to-all-done.4.x_ref, bf16[8,2,128,128]{3,2,1,0:T(8,128)(2,1)S(1)} %collective-permute-done.5.y_ref, ...), custom_call_target="tpu_custom_call" | custom-call | flops 1073741824 | bytes 8388608 | tf_op jit(solution)/shard_map/mirror/pallas_call | solution.py:210
  105.5 1.0 all-to-all-done.5.x_ref
  106.5 5.2 %all-to-all-start.6 = ((bf16[8,2,128,128]{3,2,1,0:T(8,128)(2,1)}), bf16[8,2,128,128]{3,2,1,0:T(8,128)(2,1)S(1)}, u32[]{:S(2)}, u32[]{:S(2)}) async-start(bf16[8,2,128,128]{3,2,1,0:T(8,128)(2,1)} %mirror.3), calls=%async_computation.6 | async-start | bytes 1048576 | tf_op jit(solution)/shard_map/all_to_all | solution.py:249
  111.7 3.4 %copy-done.3 = bf16[1,1,256,128,128]{4,3,2,1,0:T(8,128)(2,1)S(1)} copy-done((bf16[1,1,256,128,128]{4,3,2,1,0:T(8,128)(2,1)S(1)}, bf16[1,1,256,128,128]{4,3,2,1,0:T(8,128)(2,1)}, u32[]{:S(2)}) %copy-start.3) | copy-done | bytes 8388632
  115.1 3.5 %direct.3 = (f32[8,256,128]{2,1,0:T(8,128)S(1)}, bf16[8,256,128]{2,1,0:T(8,128)(2,1)S(1)}) custom-call(s32[160]{0:T(256)S(1)} %fusion.10.lists, s32[320]{0:T(512)S(1)} %broadcast_add_fusion.2.slots, s32[2]{0:T(128)S(1)} %pad_add_fusion.place, bf16[8,256,128]{2,1,0:T(8,128)(2,1)S(1)} %all-to-all-done.5.x_ref, bf16[256,128,128]{2,1,0:T(8,128)(2,1)S(1)} %bitcast.13), custom_call_target="tpu_custom_call" | custom-call | flops 1073741824 | bytes 8388608 | tf_op jit(solution)/shard_map/direct/pallas_call | solution.py:210
  118.6 2.0 %collective-permute-start.6 = (bf16[8,256,128]{2,1,0:T(8,128)(2,1)S(1)}, bf16[8,256,128]{2,1,0:T(8,128)(2,1)S(1)}, u32[]{:S(2)}, u32[]{:S(2)}) collective-permute-start(bf16[8,256,128]{2,1,0:T(8,128)(2,1)S(1)} %get-tuple-element.44), channel_id=1, source_target_pairs={{0,1},{1,0},{2,3},{3,2},{4,5},{5,4},{6,7},{7,6},{8,9},{9,8},{10,11... | collective-permute-start | bytes 1572872 | tf_op jit(solution)/shard_map/ppermute | solution.py:278
  120.6 1.5 %collective-permute-done.6.theirs_ref = bf16[8,256,128]{2,1,0:T(8,128)(2,1)S(1)} collective-permute-done((bf16[8,256,128]{2,1,0:T(8,128)(2,1)S(1)}, bf16[8,256,128]{2,1,0:T(8,128)(2,1)S(1)}, u32[]{:S(2)}, u32[]{:S(2)}) %collective-permute-start.6) | collective-permute-done | bytes 524320 | tf_op jit(solution)/shard_map/ppermute | solution.py:278
  122.2 0.9 both.3
  123.0 6.0 %all-to-all-start.7 = ((bf16[8,256,128]{2,1,0:T(8,128)(2,1)}), bf16[8,256,128]{2,1,0:T(8,128)(2,1)S(1)}, u32[]{:S(2)}, u32[]{:S(2)}) async-start(bf16[8,256,128]{2,1,0:T(8,128)(2,1)} %both.3), calls=%async_computation.7 | async-start | bytes 1048576 | tf_op jit(solution)/shard_map/all_to_all | solution.py:249
  129.2 8.4 %collective-permute-start.7 = (bf16[2,128,128]{2,1,0:T(8,128)(2,1)S(1)}, bf16[2,128,128]{2,1,0:T(8,128)(2,1)S(1)}, u32[]{:S(2)}, u32[]{:S(2)}) collective-permute-start(bf16[2,128,128]{2,1,0:T(8,128)(2,1)S(1)} %gathered.3), channel_id=1, source_target_pairs={{0,0},{16,1},{32,2},{48,3},{64,4},{80,5},{96,6},{112,7},{65,8},{81... | collective-permute-start | bytes 196616 | tf_op jit(solution)/shard_map/ppermute | solution.py:282
  137.6 7.4 %collective-permute-done.7.sum_ref = bf16[2,128,128]{2,1,0:T(8,128)(2,1)S(1)} collective-permute-done((bf16[2,128,128]{2,1,0:T(8,128)(2,1)S(1)}, bf16[2,128,128]{2,1,0:T(8,128)(2,1)S(1)}, u32[]{:S(2)}, u32[]{:S(2)}) %collective-permute-start.7) | collective-permute-done | bytes 65568 | tf_op jit(solution)/shard_map/ppermute | solution.py:282
  145.0 0.1 turned.3.back_ref
  145.1 1.3 last.1
  (43 shorter events, 0.3 us)
Async XLA Ops:
  0.0 0.9 copy-start.4
  0.9 0.7 copy-start.6
  3.0 19.3 %all-to-all-start = ((bf16[8,2,128,128]{3,2,1,0:T(8,128)(2,1)}), bf16[8,2,128,128]{3,2,1,0:T(8,128)(2,1)S(1)}, u32[]{:S(2)}, u32[]{:S(2)}) async-start(bf16[8,2,128,128]{3,2,1,0:T(8,128)(2,1)} %get-tuple-element.27), calls=%async_computation | async-start | bytes 1048576 | tf_op jit(solution)/shard_map/all_to_all | solution.py:249
  10.5 11.8 %collective-permute-start = (bf16[256,128]{1,0:T(8,128)(2,1)S(1)}, bf16[256,128]{1,0:T(8,128)(2,1)S(1)}, u32[]{:S(2)}, u32[]{:S(2)}) collective-permute-start(bf16[256,128]{1,0:T(8,128)(2,1)S(1)} %get-tuple-element.26), channel_id=1, source_target_pairs={{0,0},{1,16},{2,32},{3,48},{4,64},{5,80},{6,96},{7,112},{8,65},{9,... | collective-permute-start | bytes 196616 | tf_op jit(solution)/shard_map/ppermute | solution.py:252
  22.3 6.3 %collective-permute-start.1 = (bf16[8,2,128,128]{3,2,1,0:T(8,128)(2,1)S(1)}, bf16[8,2,128,128]{3,2,1,0:T(8,128)(2,1)S(1)}, u32[]{:S(2)}, u32[]{:S(2)}) collective-permute-start(bf16[8,2,128,128]{3,2,1,0:T(8,128)(2,1)S(1)} %all-to-all-done.x_ref), channel_id=1, source_target_pairs={{0,1},{1,0},{2,3},{3,2},{4,5},{5,4},{6,7},{7,6},{8,9},{9,8},{10,11... | collective-permute-start | bytes 1572872 | tf_op jit(solution)/shard_map/ppermute | solution.py:255
  23.9 11.9 %all-to-all-start.1 = ((bf16[8,256,128]{2,1,0:T(8,128)(2,1)}), bf16[8,256,128]{2,1,0:T(8,128)(2,1)S(1)}, u32[]{:S(2)}, u32[]{:S(2)}) async-start(bf16[8,256,128]{2,1,0:T(8,128)(2,1)} %broadcast_in_dim.231), calls=%async_computation.1 | async-start | bytes 1048576 | tf_op jit(solution)/shard_map/all_to_all | solution.py:249
  28.6 3.4 %copy-start = (bf16[1,1,256,128,128]{4,3,2,1,0:T(8,128)(2,1)S(1)}, bf16[1,1,256,128,128]{4,3,2,1,0:T(8,128)(2,1)}, u32[]{:S(2)}) copy-start(bf16[1,1,256,128,128]{4,3,2,1,0:T(8,128)(2,1)} %param.8) | copy-start | bytes 25165828
  35.5 42.2 %copy-start.5 = (f32[256,128]{1,0:T(8,128)S(1)}, f32[256,128]{1,0:T(8,128)}, u32[]{:S(2)}) copy-start(f32[256,128]{1,0:T(8,128)} %vectors_ref.5) | copy-start | bytes 393220
  35.5 42.3 %copy-start.7 = (s32[2]{0:T(128)S(1)}, s32[2]{0:T(128)}, u32[]{:S(2)}) copy-start(s32[2]{0:T(128)} %widths.5) | copy-start | bytes 28
  35.9 12.5 %all-to-all-start.2 = ((bf16[8,2,128,128]{3,2,1,0:T(8,128)(2,1)}), bf16[8,2,128,128]{3,2,1,0:T(8,128)(2,1)S(1)}, u32[]{:S(2)}, u32[]{:S(2)}) async-start(bf16[8,2,128,128]{3,2,1,0:T(8,128)(2,1)} %mirror.2), calls=%async_computation.2 | async-start | bytes 1048576 | tf_op jit(solution)/shard_map/all_to_all | solution.py:249
  41.5 3.4 %copy-start.1 = (bf16[1,1,256,128,128]{4,3,2,1,0:T(8,128)(2,1)S(1)}, bf16[1,1,256,128,128]{4,3,2,1,0:T(8,128)(2,1)}, u32[]{:S(2)}) copy-start(bf16[1,1,256,128,128]{4,3,2,1,0:T(8,128)(2,1)} %param.8) | copy-start | bytes 25165828
  48.4 3.4 %collective-permute-start.2 = (bf16[8,256,128]{2,1,0:T(8,128)(2,1)S(1)}, bf16[8,256,128]{2,1,0:T(8,128)(2,1)S(1)}, u32[]{:S(2)}, u32[]{:S(2)}) collective-permute-start(bf16[8,256,128]{2,1,0:T(8,128)(2,1)S(1)} %get-tuple-element.34), channel_id=1, source_target_pairs={{0,1},{1,0},{2,3},{3,2},{4,5},{5,4},{6,7},{7,6},{8,9},{9,8},{10,11... | collective-permute-start | bytes 1572872 | tf_op jit(solution)/shard_map/ppermute | solution.py:278
  52.6 25.1 %all-to-all-start.3 = ((bf16[8,256,128]{2,1,0:T(8,128)(2,1)}), bf16[8,256,128]{2,1,0:T(8,128)(2,1)S(1)}, u32[]{:S(2)}, u32[]{:S(2)}) async-start(bf16[8,256,128]{2,1,0:T(8,128)(2,1)} %both.2), calls=%async_computation.3 | async-start | bytes 1048576 | tf_op jit(solution)/shard_map/all_to_all | solution.py:249
  58.8 18.8 %collective-permute-start.3 = (f32[2,128,128]{2,1,0:T(8,128)S(1)}, f32[2,128,128]{2,1,0:T(8,128)S(1)}, u32[]{:S(2)}, u32[]{:S(2)}) collective-permute-start(f32[2,128,128]{2,1,0:T(8,128)S(1)} %gathered.2), channel_id=1, source_target_pairs={{0,0},{16,1},{32,2},{48,3},{64,4},{80,5},{96,6},{112,7},{65,8},{81... | collective-permute-start | bytes 393224 | tf_op jit(solution)/shard_map/ppermute | solution.py:282
  79.3 13.6 %all-to-all-start.4 = ((bf16[8,2,128,128]{3,2,1,0:T(8,128)(2,1)}), bf16[8,2,128,128]{3,2,1,0:T(8,128)(2,1)S(1)}, u32[]{:S(2)}, u32[]{:S(2)}) async-start(bf16[8,2,128,128]{3,2,1,0:T(8,128)(2,1)} %get-tuple-element.37), calls=%async_computation.4 | async-start | bytes 1048576 | tf_op jit(solution)/shard_map/all_to_all | solution.py:249
  82.8 10.1 %collective-permute-start.4 = (bf16[256,128]{1,0:T(8,128)(2,1)S(1)}, bf16[256,128]{1,0:T(8,128)(2,1)S(1)}, u32[]{:S(2)}, u32[]{:S(2)}) collective-permute-start(bf16[256,128]{1,0:T(8,128)(2,1)S(1)} %get-tuple-element.36), channel_id=1, source_target_pairs={{0,0},{1,16},{2,32},{3,48},{4,64},{5,80},{6,96},{7,112},{8,65},{9,... | collective-permute-start | bytes 196616 | tf_op jit(solution)/shard_map/ppermute | solution.py:252
  92.9 5.8 %collective-permute-start.5 = (bf16[8,2,128,128]{3,2,1,0:T(8,128)(2,1)S(1)}, bf16[8,2,128,128]{3,2,1,0:T(8,128)(2,1)S(1)}, u32[]{:S(2)}, u32[]{:S(2)}) collective-permute-start(bf16[8,2,128,128]{3,2,1,0:T(8,128)(2,1)S(1)} %all-to-all-done.4.x_ref), channel_id=1, source_target_pairs={{0,1},{1,0},{2,3},{3,2},{4,5},{5,4},{6,7},{7,6},{8,9},{9,8},{10,11... | collective-permute-start | bytes 1572872 | tf_op jit(solution)/shard_map/ppermute | solution.py:255
  93.7 12.7 %all-to-all-start.5 = ((bf16[8,256,128]{2,1,0:T(8,128)(2,1)}), bf16[8,256,128]{2,1,0:T(8,128)(2,1)S(1)}, u32[]{:S(2)}, u32[]{:S(2)}) async-start(bf16[8,256,128]{2,1,0:T(8,128)(2,1)} %broadcast_in_dim.251), calls=%async_computation.5 | async-start | bytes 1048576 | tf_op jit(solution)/shard_map/all_to_all | solution.py:249
  98.6 3.4 %copy-start.2 = (bf16[1,1,256,128,128]{4,3,2,1,0:T(8,128)(2,1)S(1)}, bf16[1,1,256,128,128]{4,3,2,1,0:T(8,128)(2,1)}, u32[]{:S(2)}) copy-start(bf16[1,1,256,128,128]{4,3,2,1,0:T(8,128)(2,1)} %param.8) | copy-start | bytes 25165828
  106.5 12.1 %all-to-all-start.6 = ((bf16[8,2,128,128]{3,2,1,0:T(8,128)(2,1)}), bf16[8,2,128,128]{3,2,1,0:T(8,128)(2,1)S(1)}, u32[]{:S(2)}, u32[]{:S(2)}) async-start(bf16[8,2,128,128]{3,2,1,0:T(8,128)(2,1)} %mirror.3), calls=%async_computation.6 | async-start | bytes 1048576 | tf_op jit(solution)/shard_map/all_to_all | solution.py:249
  111.7 3.4 %copy-start.3 = (bf16[1,1,256,128,128]{4,3,2,1,0:T(8,128)(2,1)S(1)}, bf16[1,1,256,128,128]{4,3,2,1,0:T(8,128)(2,1)}, u32[]{:S(2)}) copy-start(bf16[1,1,256,128,128]{4,3,2,1,0:T(8,128)(2,1)} %param.8) | copy-start | bytes 25165828
  118.6 3.6 %collective-permute-start.6 = (bf16[8,256,128]{2,1,0:T(8,128)(2,1)S(1)}, bf16[8,256,128]{2,1,0:T(8,128)(2,1)S(1)}, u32[]{:S(2)}, u32[]{:S(2)}) collective-permute-start(bf16[8,256,128]{2,1,0:T(8,128)(2,1)S(1)} %get-tuple-element.44), channel_id=1, source_target_pairs={{0,1},{1,0},{2,3},{3,2},{4,5},{5,4},{6,7},{7,6},{8,9},{9,8},{10,11... | collective-permute-start | bytes 1572872 | tf_op jit(solution)/shard_map/ppermute | solution.py:278
  123.0 22.0 %all-to-all-start.7 = ((bf16[8,256,128]{2,1,0:T(8,128)(2,1)}), bf16[8,256,128]{2,1,0:T(8,128)(2,1)S(1)}, u32[]{:S(2)}, u32[]{:S(2)}) async-start(bf16[8,256,128]{2,1,0:T(8,128)(2,1)} %both.3), calls=%async_computation.7 | async-start | bytes 1048576 | tf_op jit(solution)/shard_map/all_to_all | solution.py:249
  129.2 15.8 %collective-permute-start.7 = (bf16[2,128,128]{2,1,0:T(8,128)(2,1)S(1)}, bf16[2,128,128]{2,1,0:T(8,128)(2,1)S(1)}, u32[]{:S(2)}, u32[]{:S(2)}) collective-permute-start(bf16[2,128,128]{2,1,0:T(8,128)(2,1)S(1)} %gathered.3), channel_id=1, source_target_pairs={{0,0},{16,1},{32,2},{48,3},{64,4},{80,5},{96,6},{112,7},{65,8},{81... | collective-permute-start | bytes 196616 | tf_op jit(solution)/shard_map/ppermute | solution.py:282

commit v9 on v5

--- a/solution.py
+++ b/solution.py
@@ -65,9 +65,7 @@
 
 def send_forms(current, plain_ref, flip_ref):
     plain_ref[...] = current.reshape(2 * ATOM, VECS).astype(BF)
-    flipped = jnp.swapaxes(current, 1, 2).astype(BF)
-    for k in range(8):
-        flip_ref[k] = flipped
+    flip_ref[...] = jnp.swapaxes(current, 1, 2).astype(BF)
 
 
 def first_kernel(widths, vectors_ref, plain_ref, flip_ref):
@@ -136,11 +134,17 @@
     lax.fori_loop(0, 8, step, 0, unroll=True)
 
 
-def mirror_kernel(tab, place, x_ref, y_ref, t_ref, out_ref, held):
-    co = place[0]
-    for xz in range(8):
-        held[pl.ds(4 * xz + 2 * co, 2)] = x_ref[xz]
-        held[pl.ds(4 * xz + 2 - 2 * co, 2)] = y_ref[xz]
+def mirror_kernel(tab, place, z0_ref, z1_ref, z2_ref, z3_ref, c0_ref, c1_ref, c2_ref, c3_ref,
+                  t_ref, out_ref, held):
+    co, z, xh = place[0], place[2], place[3]
+    for core, refs in (
+        (co, (z0_ref, z1_ref, z2_ref, z3_ref)),
+        (1 - co, (c0_ref, c1_ref, c2_ref, c3_ref)),
+    ):
+        for s, ref in enumerate(refs):
+            for rel in range(2):
+                c = 8 * jnp.bitwise_xor(xh, rel) + 2 * jnp.bitwise_and(z - s + 4, 3) + core
+                held[pl.ds(2 * c, 2)] = ref[rel]
     held[AR] = jnp.zeros((VECS, ATOM), BF)
 
     def product(b, q, n):
@@ -224,10 +228,16 @@
 SWAP = [(0, 1), (1, 0)]
 
 
+def turn(s):
+    return [(k, (k + s) % 4) for k in range(4)]
+
+
 def local(vectors, widths, tiles, block_rows, block_cols, block_count):
     row = lax.axis_index(ROWS)
     col = lax.axis_index(COLS)
-    place = jnp.stack([lax.axis_index("co"), shift_of(col)]).astype(jnp.int32)
+    place = jnp.stack(
+        [lax.axis_index("co"), shift_of(col), lax.axis_index("z"), lax.axis_index("xh")]
+    ).astype(jnp.int32)
     tile_set = tiles[0, 0]
     direct_tab, mirror_tab = tables(
         block_rows[0, 0], block_cols[0, 0], block_count[0, 0], row, col
@@ -239,15 +249,17 @@
 
     def apply_matrix(plain, flipped, sent):
         piece = lax.ppermute(plain, ALL, TO_COL)
-        near = exchange(flipped, ("xh", "z"))
-        piece, near = lax.optimization_barrier((piece, near))
-        far = lax.ppermute(near, "co", SWAP)
+        pair = jnp.stack([flipped, lax.ppermute(flipped, "xh", SWAP)])
+        turns = [lax.ppermute(pair, "z", turn(s)) for s in (1, 2, 3)]
+        piece, *turns = lax.optimization_barrier((piece, *turns))
+        turns = [pair, *turns]
+        crossed = [lax.ppermute(t, "co", SWAP) for t in turns]
         col_block = exchange(jnp.broadcast_to(piece[None], (8, *PIECE)), ROWS)
         mirror = call(
             mirror_kernel,
             like((8, *BLOCKS), BF),
             (mirror_tab, place),
-            (near, far, tile_set),
+            (*turns, *crossed, tile_set),
             [pltpu.VMEM((AR + 1, VECS, ATOM), BF)],
             name="mirror",
             **work,
@@ -272,7 +284,7 @@
         turned = call(turned_kernel, like(PIECE, F32), (), (back,), name="turned")
         return own, turned
 
-    forms = (like(PIECE, BF), like((8, *BLOCKS), BF))
+    forms = (like(PIECE, BF), like(BLOCKS, BF))
     plain, flipped = call(first_kernel, forms, (widths,), (vectors,), name="first")
     parts = apply_matrix(plain, flipped, F32)
     second, plain, flipped = call(

time: 147 us -> 156 us (1.061)
  waiting for transfers between devices: 25.1 us -> 41 us
  starting transfers between devices: 80.9 us -> 74.9 us
    ppermute x2 -> x16, waiting for transfers between devices: 0.01 us -> 16 us  [the longest x2 7.33 us: apply_matrix(): pair = jnp.stack([flipped, lax.ppermute(flipped, 'xh', SWAP)])]
    all_to_all x8 -> x6, starting transfers between devices: 42.7 us -> 29.5 us  [exchange(): return lax.all_to_all(x, axes, split_axis=0, concat_axis=0, tiled=True)]
    ppermute x2 -> x16, starting transfers between devices: 1.44 us -> 9.92 us  [the longest x8 6.68 us: apply_matrix(): crossed = [lax.ppermute(t, 'co', SWAP) for t in turns]]
  transfers between devices with their start and end apart: 16 -> 28, of which waited for: 8 -> 20; matrix products, arithmetic and copies ran while one was open for 3% -> 1% of each run, Pallas kernels for 10% -> 9%
where the time goes in v9:
time: 156 us; the launch traced here: 155 us
  starting transfers between devices  74.9 us (48%)
  waiting for transfers between devices  41 us (26%)
  Pallas kernels  19.1 us (12%)
  local copies, waits for them, and re-layouts  17.3 us (11%)
  other arithmetic  1.58 us (1%)
    all_to_all x6, starting transfers between devices, exchange(): return lax.all_to_all(x, axes, split_axis=0, concat_axis=0, tiled=True)  29.5 us
    pallas_call x13, Pallas kernels, call(): pl.pallas_call(kernel, out_shape=out_shape, in_specs=[SMEM] * len(scalars...  19.1 us
    ppermute x2, waiting for transfers between devices, apply_matrix(): back = lax.ppermute(gathered, ALL, TO_ROW)  17.1 us
    ppermute x2, starting transfers between devices, apply_matrix(): back = lax.ppermute(gathered, ALL, TO_ROW)  16.5 us
    ppermute x2, starting transfers between devices, apply_matrix(): piece = lax.ppermute(plain, ALL, TO_COL)  16.3 us
    unnamed x16, local copies, waits for them, and re-layouts  15.1 us
    ppermute x2, waiting for transfers between devices, apply_matrix(): pair = jnp.stack([flipped, lax.ppermute(flipped, 'xh', SWAP)])  7.33 us
    ppermute x8, starting transfers between devices, apply_matrix(): crossed = [lax.ppermute(t, 'co', SWAP) for t in turns]  6.68 us
  transfers between devices with their start and end apart: 28, of which 20 were waited for; matrix products, arithmetic and copies ran while one was open for 1% of the time, Pallas kernels for 9%

profile of v9, /device:TPU:25, one launch (start us, length us, event | category | flops | bytes accessed | tf_op | source)
XLA Modules:
  0.0 154.8 jit_solution(17015905626609212373)
XLA Ops:
  0.0 0.9 copy-done.4
  0.9 0.7 copy-done.6
  1.6 0.6 first.1
  2.2 8.9 %collective-permute-start = (bf16[256,128]{1,0:T(8,128)(2,1)S(1)}, bf16[256,128]{1,0:T(8,128)(2,1)S(1)}, u32[]{:S(2)}, u32[]{:S(2)}) collective-permute-start(bf16[256,128]{1,0:T(8,128)(2,1)S(1)} %get-tuple-element.30), channel_id=1, source_target_pairs={{0,0},{1,16},{2,32},{3,48},{4,64},{5,80},{6,96},{7,112},{8,65},{9,... | collective-permute-start | bytes 196616 | tf_op jit(solution)/shard_map/ppermute | solution.py:251
  11.8 0.7 multiply_add_fusion.1
  13.1 2.7 %collective-permute-done.1 = bf16[2,128,128]{2,1,0:T(8,128)(2,1)S(1)} collective-permute-done((bf16[2,128,128]{2,1,0:T(8,128)(2,1)S(1)}, bf16[2,128,128]{2,1,0:T(8,128)(2,1)S(1)}, u32[]{:S(2)}, u32[]{:S(2)}) %collective-permute-start.1) | collective-permute-done | bytes 65568 | tf_op jit(solution)/shard_map/ppermute | solution.py:252
  15.9 1.0 collective-permute-start.3
  16.9 0.5 collective-permute-start.2
  17.4 2.3 %collective-permute-done.4.z3_ref = bf16[2,2,128,128]{3,2,1,0:T(8,128)(2,1)S(1)} collective-permute-done((bf16[2,2,128,128]{3,2,1,0:T(8,128)(2,1)S(1)}, bf16[2,2,128,128]{3,2,1,0:T(8,128)(2,1)S(1)}, u32[]{:S(2)}, u32[]{:S(2)}) %collective-permute-start.4) | collective-permute-done | bytes 131104 | tf_op jit(solution)/shard_map/ppermute | solution.py:253
  19.8 1.7 %collective-permute-done.3.z2_ref = bf16[2,2,128,128]{3,2,1,0:T(8,128)(2,1)S(1)} collective-permute-done((bf16[2,2,128,128]{3,2,1,0:T(8,128)(2,1)S(1)}, bf16[2,2,128,128]{3,2,1,0:T(8,128)(2,1)S(1)}, u32[]{:S(2)}, u32[]{:S(2)}) %collective-permute-start.3) | collective-permute-done | bytes 131104 | tf_op jit(solution)/shard_map/ppermute | solution.py:253
  21.4 2.2 %collective-permute-done.2.z1_ref = bf16[2,2,128,128]{3,2,1,0:T(8,128)(2,1)S(1)} collective-permute-done((bf16[2,2,128,128]{3,2,1,0:T(8,128)(2,1)S(1)}, bf16[2,2,128,128]{3,2,1,0:T(8,128)(2,1)S(1)}, u32[]{:S(2)}, u32[]{:S(2)}) %collective-permute-start.2) | collective-permute-done | bytes 131104 | tf_op jit(solution)/shard_map/ppermute | solution.py:253
  23.6 0.9 broadcast_in_dim.104
  24.4 6.8 %all-to-all-start = ((bf16[8,256,128]{2,1,0:T(8,128)(2,1)}), bf16[8,256,128]{2,1,0:T(8,128)(2,1)S(1)}, u32[]{:S(2)}, u32[]{:S(2)}) async-start(bf16[8,256,128]{2,1,0:T(8,128)(2,1)} %broadcast_in_dim.104), calls=%async_computation | async-start | bytes 1048576 | tf_op jit(solution)/shard_map/all_to_all | solution.py:248
  31.3 0.2 select_reduce_fusion.1
  31.5 1.6 %collective-permute-start.5 = (bf16[2,2,128,128]{3,2,1,0:T(8,128)(2,1)S(1)}, bf16[2,2,128,128]{3,2,1,0:T(8,128)(2,1)S(1)}, u32[]{:S(2)}, u32[]{:S(2)}) collective-permute-start(bf16[2,2,128,128]{3,2,1,0:T(8,128)(2,1)S(1)} %pad_maximum_fusion.z0_ref), channel_id=1, source_target_pairs={{0,1},{1,0},{2,3},{3,2},{4,5},{5,4},{6,7},{7,6},{8,9},{9,8},{10,11... | collective-permute-start | bytes 393224 | tf_op jit(solution)/shard_map/ppermute | solution.py:256
  33.2 0.4 collective-permute-start.7
  33.8 0.3 collective-permute-done.5.c0_ref
  34.1 0.4 collective-permute-done.6.c1_ref
  34.4 0.2 collective-permute-done.7.c2_ref
  34.6 0.3 collective-permute-done.8.c3_ref
  34.9 3.4 %copy-done = bf16[1,1,256,128,128]{4,3,2,1,0:T(8,128)(2,1)S(1)} copy-done((bf16[1,1,256,128,128]{4,3,2,1,0:T(8,128)(2,1)S(1)}, bf16[1,1,256,128,128]{4,3,2,1,0:T(8,128)(2,1)}, u32[]{:S(2)}) %copy-start) | copy-done | bytes 8388632
  38.3 4.0 %mirror.2 = bf16[8,2,128,128]{3,2,1,0:T(8,128)(2,1)} custom-call(s32[272]{0:T(512)S(1)} %broadcast_add_fusion.tab, s32[4]{0:T(128)S(1)} %pad_add_fusion.place, bf16[2,2,128,128]{3,2,1,0:T(8,128)(2,1)S(1)} %pad_maximum_fusion.z0_ref, bf16[2,2,128,128]{3,2,1,0:T(8,128)(2,1)S(1)} %collective-permute-done.2.z1_ref, ...), custom_call_target="tpu_custom_call" | custom-call | flops 1073741824 | bytes 8388608 | tf_op jit(solution)/shard_map/mirror/pallas_call | solution.py:203
  42.3 5.3 %all-to-all-start.1 = ((bf16[8,2,128,128]{3,2,1,0:T(8,128)(2,1)}), bf16[8,2,128,128]{3,2,1,0:T(8,128)(2,1)S(1)}, u32[]{:S(2)}, u32[]{:S(2)}) async-start(bf16[8,2,128,128]{3,2,1,0:T(8,128)(2,1)} %mirror.2), calls=%async_computation.1 | async-start | bytes 1048576 | tf_op jit(solution)/shard_map/all_to_all | solution.py:248
  47.6 0.1 reshape.356
  47.8 0.1 add.261
  47.9 0.3 select_reduce_fusion
  48.2 3.4 %copy-done.1 = bf16[1,1,256,128,128]{4,3,2,1,0:T(8,128)(2,1)S(1)} copy-done((bf16[1,1,256,128,128]{4,3,2,1,0:T(8,128)(2,1)S(1)}, bf16[1,1,256,128,128]{4,3,2,1,0:T(8,128)(2,1)}, u32[]{:S(2)}) %copy-start.1) | copy-done | bytes 8388632
  51.6 3.2 %direct.2 = (f32[8,256,128]{2,1,0:T(8,128)S(1)}, bf16[8,256,128]{2,1,0:T(8,128)(2,1)S(1)}) custom-call(s32[288]{0:T(512)S(1)} %broadcast_add_fusion.1.tab, s32[4]{0:T(128)S(1)} %pad_add_fusion.place, bf16[8,256,128]{2,1,0:T(8,128)(2,1)S(1)} %all-to-all-done.x_ref, bf16[256,128,128]{2,1,0:T(8,128)(2,1)S(1)} %bitcast.13), custom_call_target="tpu_custom_call" | custom-call | flops 1073741824 | bytes 8388608 | tf_op jit(solution)/shard_map/direct/pallas_call | solution.py:203
  54.7 0.5 all-to-all-done.1.got_ref
  55.2 1.3 collective-permute-start.9
  56.5 1.5 collective-permute-done.9.theirs_ref
  58.1 0.9 both.2
  59.0 3.5 %all-to-all-start.2 = ((bf16[8,256,128]{2,1,0:T(8,128)(2,1)}), bf16[8,256,128]{2,1,0:T(8,128)(2,1)S(1)}, u32[]{:S(2)}, u32[]{:S(2)}) async-start(bf16[8,256,128]{2,1,0:T(8,128)(2,1)} %both.2), calls=%async_computation.2 | async-start | bytes 1048576 | tf_op jit(solution)/shard_map/all_to_all | solution.py:248
  62.5 8.0 %collective-permute-start.10 = (f32[2,128,128]{2,1,0:T(8,128)S(1)}, f32[2,128,128]{2,1,0:T(8,128)S(1)}, u32[]{:S(2)}, u32[]{:S(2)}) collective-permute-start(f32[2,128,128]{2,1,0:T(8,128)S(1)} %gathered.2), channel_id=1, source_target_pairs={{0,0},{16,1},{32,2},{48,3},{64,4},{80,5},{96,6},{112,7},{65,8},{81... | collective-permute-start | bytes 393224 | tf_op jit(solution)/shard_map/ppermute | solution.py:283
  70.6 10.3 %collective-permute-done.10.sum_ref = f32[2,128,128]{2,1,0:T(8,128)S(1)} collective-permute-done((f32[2,128,128]{2,1,0:T(8,128)S(1)}, f32[2,128,128]{2,1,0:T(8,128)S(1)}, u32[]{:S(2)}, u32[]{:S(2)}) %collective-permute-start.10) | collective-permute-done | bytes 131104 | tf_op jit(solution)/shard_map/ppermute | solution.py:283
  80.9 0.1 turned.2.back_ref
  81.0 0.7 second.1
  81.8 4.6 %collective-permute-done.12 = bf16[2,128,128]{2,1,0:T(8,128)(2,1)S(1)} collective-permute-done((bf16[2,128,128]{2,1,0:T(8,128)(2,1)S(1)}, bf16[2,128,128]{2,1,0:T(8,128)(2,1)S(1)}, u32[]{:S(2)}, u32[]{:S(2)}) %collective-permute-start.12) | collective-permute-done | bytes 65568 | tf_op jit(solution)/shard_map/ppermute | solution.py:252
  86.4 0.7 collective-permute-start.15
  87.1 0.9 collective-permute-start.13
  88.0 7.4 %collective-permute-start.11 = (bf16[256,128]{1,0:T(8,128)(2,1)S(1)}, bf16[256,128]{1,0:T(8,128)(2,1)S(1)}, u32[]{:S(2)}, u32[]{:S(2)}) collective-permute-start(bf16[256,128]{1,0:T(8,128)(2,1)S(1)} %get-tuple-element.42), channel_id=1, source_target_pairs={{0,0},{1,16},{2,32},{3,48},{4,64},{5,80},{6,96},{7,112},{8,65},{9,... | collective-permute-start | bytes 196616 | tf_op jit(solution)/shard_map/ppermute | solution.py:251
  95.4 3.3 %collective-permute-done.11 = bf16[256,128]{1,0:T(8,128)(2,1)S(1)} collective-permute-done((bf16[256,128]{1,0:T(8,128)(2,1)S(1)}, bf16[256,128]{1,0:T(8,128)(2,1)S(1)}, u32[]{:S(2)}, u32[]{:S(2)}) %collective-permute-start.11) | collective-permute-done | bytes 65568 | tf_op jit(solution)/shard_map/ppermute | solution.py:251
  98.7 0.9 broadcast_in_dim.112
  99.6 4.0 %all-to-all-start.3 = ((bf16[8,256,128]{2,1,0:T(8,128)(2,1)}), bf16[8,256,128]{2,1,0:T(8,128)(2,1)S(1)}, u32[]{:S(2)}, u32[]{:S(2)}) async-start(bf16[8,256,128]{2,1,0:T(8,128)(2,1)} %broadcast_in_dim.112), calls=%async_computation.3 | async-start | bytes 1048576 | tf_op jit(solution)/shard_map/all_to_all | solution.py:248
  103.5 4.0 %collective-permute-start.16 = (bf16[2,2,128,128]{3,2,1,0:T(8,128)(2,1)S(1)}, bf16[2,2,128,128]{3,2,1,0:T(8,128)(2,1)S(1)}, u32[]{:S(2)}, u32[]{:S(2)}) collective-permute-start(bf16[2,2,128,128]{3,2,1,0:T(8,128)(2,1)S(1)} %pad_maximum_fusion.1.z0_ref), channel_id=1, source_target_pairs={{0,1},{1,0},{2,3},{3,2},{4,5},{5,4},{6,7},{7,6},{8,9},{9,8},{10,11... | collective-permute-start | bytes 393224 | tf_op jit(solution)/shard_map/ppermute | solution.py:256
  107.5 0.5 collective-permute-start.18
  108.0 0.5 collective-permute-done.16.c0_ref
  108.5 0.4 collective-permute-done.17.c1_ref
  108.8 0.2 collective-permute-done.18.c2_ref
  109.0 0.3 collective-permute-done.19.c3_ref
  109.3 3.4 %copy-done.2 = bf16[1,1,256,128,128]{4,3,2,1,0:T(8,128)(2,1)S(1)} copy-done((bf16[1,1,256,128,128]{4,3,2,1,0:T(8,128)(2,1)S(1)}, bf16[1,1,256,128,128]{4,3,2,1,0:T(8,128)(2,1)}, u32[]{:S(2)}) %copy-start.2) | copy-done | bytes 8388632
  112.7 4.0 %mirror.3 = bf16[8,2,128,128]{3,2,1,0:T(8,128)(2,1)} custom-call(s32[272]{0:T(512)S(1)} %broadcast_add_fusion.tab, s32[4]{0:T(128)S(1)} %pad_add_fusion.place, bf16[2,2,128,128]{3,2,1,0:T(8,128)(2,1)S(1)} %pad_maximum_fusion.1.z0_ref, bf16[2,2,128,128]{3,2,1,0:T(8,128)(2,1)S(1)} %collective-permute-done.13.z1_ref, ...), custom_call_target="tpu_custom_call" | custom-call | flops 1073741824 | bytes 8388608 | tf_op jit(solution)/shard_map/mirror/pallas_call | solution.py:203
  116.7 5.1 %all-to-all-start.4 = ((bf16[8,2,128,128]{3,2,1,0:T(8,128)(2,1)}), bf16[8,2,128,128]{3,2,1,0:T(8,128)(2,1)S(1)}, u32[]{:S(2)}, u32[]{:S(2)}) async-start(bf16[8,2,128,128]{3,2,1,0:T(8,128)(2,1)} %mirror.3), calls=%async_computation.4 | async-start | bytes 1048576 | tf_op jit(solution)/shard_map/all_to_all | solution.py:248
  121.9 3.4 %copy-done.3 = bf16[1,1,256,128,128]{4,3,2,1,0:T(8,128)(2,1)S(1)} copy-done((bf16[1,1,256,128,128]{4,3,2,1,0:T(8,128)(2,1)S(1)}, bf16[1,1,256,128,128]{4,3,2,1,0:T(8,128)(2,1)}, u32[]{:S(2)}) %copy-start.3) | copy-done | bytes 8388632
  125.2 3.2 %direct.3 = (f32[8,256,128]{2,1,0:T(8,128)S(1)}, bf16[8,256,128]{2,1,0:T(8,128)(2,1)S(1)}) custom-call(s32[288]{0:T(512)S(1)} %broadcast_add_fusion.1.tab, s32[4]{0:T(128)S(1)} %pad_add_fusion.place, bf16[8,256,128]{2,1,0:T(8,128)(2,1)S(1)} %all-to-all-done.3.x_ref, bf16[256,128,128]{2,1,0:T(8,128)(2,1)S(1)} %bitcast.15), custom_call_target="tpu_custom_call" | custom-call | flops 1073741824 | bytes 8388608 | tf_op jit(solution)/shard_map/direct/pallas_call | solution.py:203
  128.4 1.1 all-to-all-done.4.got_ref
  129.5 1.3 collective-permute-start.20
  130.8 1.5 collective-permute-done.20.theirs_ref
  132.3 0.9 both.3
  133.2 4.8 %all-to-all-start.5 = ((bf16[8,256,128]{2,1,0:T(8,128)(2,1)}), bf16[8,256,128]{2,1,0:T(8,128)(2,1)S(1)}, u32[]{:S(2)}, u32[]{:S(2)}) async-start(bf16[8,256,128]{2,1,0:T(8,128)(2,1)} %both.3), calls=%async_computation.5 | async-start | bytes 1048576 | tf_op jit(solution)/shard_map/all_to_all | solution.py:248
  138.1 8.4 %collective-permute-start.21 = (bf16[2,128,128]{2,1,0:T(8,128)(2,1)S(1)}, bf16[2,128,128]{2,1,0:T(8,128)(2,1)S(1)}, u32[]{:S(2)}, u32[]{:S(2)}) collective-permute-start(bf16[2,128,128]{2,1,0:T(8,128)(2,1)S(1)} %gathered.3), channel_id=1, source_target_pairs={{0,0},{16,1},{32,2},{48,3},{64,4},{80,5},{96,6},{112,7},{65,8},{81... | collective-permute-start | bytes 196616 | tf_op jit(solution)/shard_map/ppermute | solution.py:283
  146.5 6.8 %collective-permute-done.21.sum_ref = bf16[2,128,128]{2,1,0:T(8,128)(2,1)S(1)} collective-permute-done((bf16[2,128,128]{2,1,0:T(8,128)(2,1)S(1)}, bf16[2,128,128]{2,1,0:T(8,128)(2,1)S(1)}, u32[]{:S(2)}, u32[]{:S(2)}) %collective-permute-start.21) | collective-permute-done | bytes 65568 | tf_op jit(solution)/shard_map/ppermute | solution.py:283
  153.4 0.1 turned.3.back_ref
  153.5 1.3 last.1
  (53 shorter events, 1.2 us)
Async XLA Ops:
  0.0 0.9 copy-start.4
  0.9 0.7 copy-start.6
  2.2 15.2 %collective-permute-start = (bf16[256,128]{1,0:T(8,128)(2,1)S(1)}, bf16[256,128]{1,0:T(8,128)(2,1)S(1)}, u32[]{:S(2)}, u32[]{:S(2)}) collective-permute-start(bf16[256,128]{1,0:T(8,128)(2,1)S(1)} %get-tuple-element.30), channel_id=1, source_target_pairs={{0,0},{1,16},{2,32},{3,48},{4,64},{5,80},{6,96},{7,112},{8,65},{9,... | collective-permute-start | bytes 196616 | tf_op jit(solution)/shard_map/ppermute | solution.py:251
  11.1 4.7 %collective-permute-start.1 = (bf16[2,128,128]{2,1,0:T(8,128)(2,1)S(1)}, bf16[2,128,128]{2,1,0:T(8,128)(2,1)S(1)}, u32[]{:S(2)}, u32[]{:S(2)}) collective-permute-start(bf16[2,128,128]{2,1,0:T(8,128)(2,1)S(1)} %get-tuple-element.31), channel_id=1, source_target_pairs={{0,8},{8,0},{1,9},{9,1},{2,10},{10,2},{3,11},{11,3},{4,12},{12,4},... | collective-permute-start | bytes 196616 | tf_op jit(solution)/shard_map/ppermute | solution.py:252
  15.9 3.9 %collective-permute-start.4 = (bf16[2,2,128,128]{3,2,1,0:T(8,128)(2,1)S(1)}, bf16[2,2,128,128]{3,2,1,0:T(8,128)(2,1)S(1)}, u32[]{:S(2)}, u32[]{:S(2)}) collective-permute-start(bf16[2,2,128,128]{3,2,1,0:T(8,128)(2,1)S(1)} %pad_maximum_fusion.z0_ref), channel_id=1, source_target_pairs={{0,6},{2,0},{4,2},{6,4},{1,7},{3,1},{5,3},{7,5},{8,14},{10,8},{12,... | collective-permute-start | bytes 393224 | tf_op jit(solution)/shard_map/ppermute | solution.py:253
  15.9 5.5 %collective-permute-start.3 = (bf16[2,2,128,128]{3,2,1,0:T(8,128)(2,1)S(1)}, bf16[2,2,128,128]{3,2,1,0:T(8,128)(2,1)S(1)}, u32[]{:S(2)}, u32[]{:S(2)}) collective-permute-start(bf16[2,2,128,128]{3,2,1,0:T(8,128)(2,1)S(1)} %pad_maximum_fusion.z0_ref), channel_id=1, source_target_pairs={{0,4},{2,6},{4,0},{6,2},{1,5},{3,7},{5,1},{7,3},{8,12},{10,14},{12... | collective-permute-start | bytes 393224 | tf_op jit(solution)/shard_map/ppermute | solution.py:253
  16.9 6.7 %collective-permute-start.2 = (bf16[2,2,128,128]{3,2,1,0:T(8,128)(2,1)S(1)}, bf16[2,2,128,128]{3,2,1,0:T(8,128)(2,1)S(1)}, u32[]{:S(2)}, u32[]{:S(2)}) collective-permute-start(bf16[2,2,128,128]{3,2,1,0:T(8,128)(2,1)S(1)} %pad_maximum_fusion.z0_ref), channel_id=1, source_target_pairs={{0,2},{2,4},{4,6},{6,0},{1,3},{3,5},{5,7},{7,1},{8,10},{10,12},{12... | collective-permute-start | bytes 393224 | tf_op jit(solution)/shard_map/ppermute | solution.py:253
  24.4 17.9 %all-to-all-start = ((bf16[8,256,128]{2,1,0:T(8,128)(2,1)}), bf16[8,256,128]{2,1,0:T(8,128)(2,1)S(1)}, u32[]{:S(2)}, u32[]{:S(2)}) async-start(bf16[8,256,128]{2,1,0:T(8,128)(2,1)} %broadcast_in_dim.104), calls=%async_computation | async-start | bytes 1048576 | tf_op jit(solution)/shard_map/all_to_all | solution.py:248
  31.5 2.6 %collective-permute-start.5 = (bf16[2,2,128,128]{3,2,1,0:T(8,128)(2,1)S(1)}, bf16[2,2,128,128]{3,2,1,0:T(8,128)(2,1)S(1)}, u32[]{:S(2)}, u32[]{:S(2)}) collective-permute-start(bf16[2,2,128,128]{3,2,1,0:T(8,128)(2,1)S(1)} %pad_maximum_fusion.z0_ref), channel_id=1, source_target_pairs={{0,1},{1,0},{2,3},{3,2},{4,5},{5,4},{6,7},{7,6},{8,9},{9,8},{10,11... | collective-permute-start | bytes 393224 | tf_op jit(solution)/shard_map/ppermute | solution.py:256
  33.1 1.3 collective-permute-start.6
  33.2 1.4 collective-permute-start.7
  33.6 1.3 collective-permute-start.8
  34.9 3.4 %copy-start = (bf16[1,1,256,128,128]{4,3,2,1,0:T(8,128)(2,1)S(1)}, bf16[1,1,256,128,128]{4,3,2,1,0:T(8,128)(2,1)}, u32[]{:S(2)}) copy-start(bf16[1,1,256,128,128]{4,3,2,1,0:T(8,128)(2,1)} %param.8) | copy-start | bytes 25165828
  42.3 38.7 %copy-start.5 = (f32[256,128]{1,0:T(8,128)S(1)}, f32[256,128]{1,0:T(8,128)}, u32[]{:S(2)}) copy-start(f32[256,128]{1,0:T(8,128)} %vectors_ref.5) | copy-start | bytes 393220
  42.3 38.7 %copy-start.7 = (s32[2]{0:T(128)S(1)}, s32[2]{0:T(128)}, u32[]{:S(2)}) copy-start(s32[2]{0:T(128)} %widths.5) | copy-start | bytes 28
  42.3 12.9 %all-to-all-start.1 = ((bf16[8,2,128,128]{3,2,1,0:T(8,128)(2,1)}), bf16[8,2,128,128]{3,2,1,0:T(8,128)(2,1)S(1)}, u32[]{:S(2)}, u32[]{:S(2)}) async-start(bf16[8,2,128,128]{3,2,1,0:T(8,128)(2,1)} %mirror.2), calls=%async_computation.1 | async-start | bytes 1048576 | tf_op jit(solution)/shard_map/all_to_all | solution.py:248
  48.2 3.4 %copy-start.1 = (bf16[1,1,256,128,128]{4,3,2,1,0:T(8,128)(2,1)S(1)}, bf16[1,1,256,128,128]{4,3,2,1,0:T(8,128)(2,1)}, u32[]{:S(2)}) copy-start(bf16[1,1,256,128,128]{4,3,2,1,0:T(8,128)(2,1)} %param.8) | copy-start | bytes 25165828
  55.2 2.9 %collective-permute-start.9 = (bf16[8,256,128]{2,1,0:T(8,128)(2,1)S(1)}, bf16[8,256,128]{2,1,0:T(8,128)(2,1)S(1)}, u32[]{:S(2)}, u32[]{:S(2)}) collective-permute-start(bf16[8,256,128]{2,1,0:T(8,128)(2,1)S(1)} %get-tuple-element.40), channel_id=1, source_target_pairs={{0,1},{1,0},{2,3},{3,2},{4,5},{5,4},{6,7},{7,6},{8,9},{9,8},{10,11... | collective-permute-start | bytes 1572872 | tf_op jit(solution)/shard_map/ppermute | solution.py:279
  59.0 22.0 %all-to-all-start.2 = ((bf16[8,256,128]{2,1,0:T(8,128)(2,1)}), bf16[8,256,128]{2,1,0:T(8,128)(2,1)S(1)}, u32[]{:S(2)}, u32[]{:S(2)}) async-start(bf16[8,256,128]{2,1,0:T(8,128)(2,1)} %both.2), calls=%async_computation.2 | async-start | bytes 1048576 | tf_op jit(solution)/shard_map/all_to_all | solution.py:248
  62.5 18.3 %collective-permute-start.10 = (f32[2,128,128]{2,1,0:T(8,128)S(1)}, f32[2,128,128]{2,1,0:T(8,128)S(1)}, u32[]{:S(2)}, u32[]{:S(2)}) collective-permute-start(f32[2,128,128]{2,1,0:T(8,128)S(1)} %gathered.2), channel_id=1, source_target_pairs={{0,0},{16,1},{32,2},{48,3},{64,4},{80,5},{96,6},{112,7},{65,8},{81... | collective-permute-start | bytes 393224 | tf_op jit(solution)/shard_map/ppermute | solution.py:283
  81.7 4.7 %collective-permute-start.12 = (bf16[2,128,128]{2,1,0:T(8,128)(2,1)S(1)}, bf16[2,128,128]{2,1,0:T(8,128)(2,1)S(1)}, u32[]{:S(2)}, u32[]{:S(2)}) collective-permute-start(bf16[2,128,128]{2,1,0:T(8,128)(2,1)S(1)} %get-tuple-element.43), channel_id=1, source_target_pairs={{0,8},{8,0},{1,9},{9,1},{2,10},{10,2},{3,11},{11,3},{4,12},{12,4},... | collective-permute-start | bytes 196616 | tf_op jit(solution)/shard_map/ppermute | solution.py:252
  86.4 12.3 %collective-permute-start.15 = (bf16[2,2,128,128]{3,2,1,0:T(8,128)(2,1)S(1)}, bf16[2,2,128,128]{3,2,1,0:T(8,128)(2,1)S(1)}, u32[]{:S(2)}, u32[]{:S(2)}) collective-permute-start(bf16[2,2,128,128]{3,2,1,0:T(8,128)(2,1)S(1)} %pad_maximum_fusion.1.z0_ref), channel_id=1, source_target_pairs={{0,6},{2,0},{4,2},{6,4},{1,7},{3,1},{5,3},{7,5},{8,14},{10,8},{12,... | collective-permute-start | bytes 393224 | tf_op jit(solution)/shard_map/ppermute | solution.py:253
  87.1 11.6 %collective-permute-start.14 = (bf16[2,2,128,128]{3,2,1,0:T(8,128)(2,1)S(1)}, bf16[2,2,128,128]{3,2,1,0:T(8,128)(2,1)S(1)}, u32[]{:S(2)}, u32[]{:S(2)}) collective-permute-start(bf16[2,2,128,128]{3,2,1,0:T(8,128)(2,1)S(1)} %pad_maximum_fusion.1.z0_ref), channel_id=1, source_target_pairs={{0,4},{2,6},{4,0},{6,2},{1,5},{3,7},{5,1},{7,3},{8,12},{10,14},{12... | collective-permute-start | bytes 393224 | tf_op jit(solution)/shard_map/ppermute | solution.py:253
  87.1 11.6 %collective-permute-start.13 = (bf16[2,2,128,128]{3,2,1,0:T(8,128)(2,1)S(1)}, bf16[2,2,128,128]{3,2,1,0:T(8,128)(2,1)S(1)}, u32[]{:S(2)}, u32[]{:S(2)}) collective-permute-start(bf16[2,2,128,128]{3,2,1,0:T(8,128)(2,1)S(1)} %pad_maximum_fusion.1.z0_ref), channel_id=1, source_target_pairs={{0,2},{2,4},{4,6},{6,0},{1,3},{3,5},{5,7},{7,1},{8,10},{10,12},{12... | collective-permute-start | bytes 393224 | tf_op jit(solution)/shard_map/ppermute | solution.py:253
  88.0 10.7 %collective-permute-start.11 = (bf16[256,128]{1,0:T(8,128)(2,1)S(1)}, bf16[256,128]{1,0:T(8,128)(2,1)S(1)}, u32[]{:S(2)}, u32[]{:S(2)}) collective-permute-start(bf16[256,128]{1,0:T(8,128)(2,1)S(1)} %get-tuple-element.42), channel_id=1, source_target_pairs={{0,0},{1,16},{2,32},{3,48},{4,64},{5,80},{6,96},{7,112},{8,65},{9,... | collective-permute-start | bytes 196616 | tf_op jit(solution)/shard_map/ppermute | solution.py:251
  99.6 17.2 %all-to-all-start.3 = ((bf16[8,256,128]{2,1,0:T(8,128)(2,1)}), bf16[8,256,128]{2,1,0:T(8,128)(2,1)S(1)}, u32[]{:S(2)}, u32[]{:S(2)}) async-start(bf16[8,256,128]{2,1,0:T(8,128)(2,1)} %broadcast_in_dim.112), calls=%async_computation.3 | async-start | bytes 1048576 | tf_op jit(solution)/shard_map/all_to_all | solution.py:248
  103.5 5.0 %collective-permute-start.16 = (bf16[2,2,128,128]{3,2,1,0:T(8,128)(2,1)S(1)}, bf16[2,2,128,128]{3,2,1,0:T(8,128)(2,1)S(1)}, u32[]{:S(2)}, u32[]{:S(2)}) collective-permute-start(bf16[2,2,128,128]{3,2,1,0:T(8,128)(2,1)S(1)} %pad_maximum_fusion.1.z0_ref), channel_id=1, source_target_pairs={{0,1},{1,0},{2,3},{3,2},{4,5},{5,4},{6,7},{7,6},{8,9},{9,8},{10,11... | collective-permute-start | bytes 393224 | tf_op jit(solution)/shard_map/ppermute | solution.py:256
  107.5 1.3 collective-permute-start.17
  107.5 1.5 collective-permute-start.18
  108.0 1.3 collective-permute-start.19
  109.3 3.4 %copy-start.2 = (bf16[1,1,256,128,128]{4,3,2,1,0:T(8,128)(2,1)S(1)}, bf16[1,1,256,128,128]{4,3,2,1,0:T(8,128)(2,1)}, u32[]{:S(2)}) copy-start(bf16[1,1,256,128,128]{4,3,2,1,0:T(8,128)(2,1)} %param.8) | copy-start | bytes 25165828
  116.7 12.8 %all-to-all-start.4 = ((bf16[8,2,128,128]{3,2,1,0:T(8,128)(2,1)}), bf16[8,2,128,128]{3,2,1,0:T(8,128)(2,1)S(1)}, u32[]{:S(2)}, u32[]{:S(2)}) async-start(bf16[8,2,128,128]{3,2,1,0:T(8,128)(2,1)} %mirror.3), calls=%async_computation.4 | async-start | bytes 1048576 | tf_op jit(solution)/shard_map/all_to_all | solution.py:248
  121.9 3.4 %copy-start.3 = (bf16[1,1,256,128,128]{4,3,2,1,0:T(8,128)(2,1)S(1)}, bf16[1,1,256,128,128]{4,3,2,1,0:T(8,128)(2,1)}, u32[]{:S(2)}) copy-start(bf16[1,1,256,128,128]{4,3,2,1,0:T(8,128)(2,1)} %param.8) | copy-start | bytes 25165828
  129.5 2.9 %collective-permute-start.20 = (bf16[8,256,128]{2,1,0:T(8,128)(2,1)S(1)}, bf16[8,256,128]{2,1,0:T(8,128)(2,1)S(1)}, u32[]{:S(2)}, u32[]{:S(2)}) collective-permute-start(bf16[8,256,128]{2,1,0:T(8,128)(2,1)S(1)} %get-tuple-element.52), channel_id=1, source_target_pairs={{0,1},{1,0},{2,3},{3,2},{4,5},{5,4},{6,7},{7,6},{8,9},{9,8},{10,11... | collective-permute-start | bytes 1572872 | tf_op jit(solution)/shard_map/ppermute | solution.py:279
  133.2 20.3 %all-to-all-start.5 = ((bf16[8,256,128]{2,1,0:T(8,128)(2,1)}), bf16[8,256,128]{2,1,0:T(8,128)(2,1)S(1)}, u32[]{:S(2)}, u32[]{:S(2)}) async-start(bf16[8,256,128]{2,1,0:T(8,128)(2,1)} %both.3), calls=%async_computation.5 | async-start | bytes 1048576 | tf_op jit(solution)/shard_map/all_to_all | solution.py:248
  138.1 15.2 %collective-permute-start.21 = (bf16[2,128,128]{2,1,0:T(8,128)(2,1)S(1)}, bf16[2,128,128]{2,1,0:T(8,128)(2,1)S(1)}, u32[]{:S(2)}, u32[]{:S(2)}) collective-permute-start(bf16[2,128,128]{2,1,0:T(8,128)(2,1)S(1)} %gathered.3), channel_id=1, source_target_pairs={{0,0},{16,1},{32,2},{48,3},{64,4},{80,5},{96,6},{112,7},{65,8},{81... | collective-permute-start | bytes 196616 | tf_op jit(solution)/shard_map/ppermute | solution.py:283

commit v10 on v3

--- a/solution.py
+++ b/solution.py
@@ -23,6 +23,8 @@
 ALL = ROWS + COLS
 D_LEN = 9
 M_LEN = 17
+PIECE = (2 * ATOM, VECS)
+BLOCKS = (2, ATOM, VECS)
 
 
 def tables(slot_rows, slot_cols, count, row, col):
@@ -63,41 +65,56 @@
     return (place < jnp.where(atom == 0, widths[0], widths[1])).astype(F32)
 
 
-def send_forms(current, plain_ref, flip_ref):
+def spread(block_ref, copies_ref, sem):
+    copies = [
+        pltpu.make_async_copy(block_ref, copies_ref.at[k], sem.at[k]) for k in range(8)
+    ]
+    for copy in copies:
+        copy.start()
+    return copies
+
+
+def send_forms(current, plain_ref, flip_ref, block, sem):
+    block[...] = jnp.swapaxes(current, 1, 2).astype(BF)
+    copies = spread(block, flip_ref, sem)
     plain_ref[...] = current.reshape(2 * ATOM, VECS).astype(BF)
-    flipped = jnp.swapaxes(current, 1, 2).astype(BF)
-    for k in range(8):
-        flip_ref[k] = flipped
-
-
-def first_kernel(widths, vectors_ref, plain_ref, flip_ref):
-    shape = (2, ATOM, VECS)
-    first = vectors_ref[...].reshape(shape) * keep_of(widths, shape, 1)
-    send_forms(first, plain_ref, flip_ref)
+    return copies
+
+
+def first_kernel(widths, vectors_ref, plain_ref, flip_ref, block, sem):
+    first = vectors_ref[...].reshape(BLOCKS) * keep_of(widths, BLOCKS, 1)
+    for copy in send_forms(first, plain_ref, flip_ref, block, sem):
+        copy.wait()
 
 
 def applied(widths, own_ref, back_ref):
-    shape = (2, ATOM, VECS)
-    total = back_ref[...]
+    total = jnp.swapaxes(back_ref[...], 1, 2).reshape(2 * ATOM, VECS)
     for k in range(8):
         total = total + own_ref[k].astype(F32)
-    return total.reshape(shape) * keep_of(widths, shape, 1)
-
-
-def second_kernel(widths, own_ref, back_ref, vectors_ref, out_ref, plain_ref, flip_ref):
-    shape = (2, ATOM, VECS)
-    first = vectors_ref[...].reshape(shape) * keep_of(widths, shape, 1)
+    return total.reshape(BLOCKS) * keep_of(widths, BLOCKS, 1)
+
+
+def second_kernel(
+    widths, own_ref, back_ref, vectors_ref, out_ref, plain_ref, flip_ref, block, sem
+):
+    first = vectors_ref[...].reshape(BLOCKS) * keep_of(widths, BLOCKS, 1)
     second = applied(widths, own_ref, back_ref) - CENTER * first
+    copies = send_forms(second, plain_ref, flip_ref, block, sem)
     out_ref[...] = second.reshape(2 * ATOM, VECS)
-    send_forms(second, plain_ref, flip_ref)
+    for copy in copies:
+        copy.wait()
 
 
 def last_kernel(widths, own_ref, back_ref, vectors_ref, second_ref, out_ref):
-    shape = (2, ATOM, VECS)
-    first = vectors_ref[...].reshape(shape) * keep_of(widths, shape, 1)
+    first = vectors_ref[...].reshape(BLOCKS) * keep_of(widths, BLOCKS, 1)
     third = applied(widths, own_ref, back_ref)
-    out = 2.0 * (third - CENTER * second_ref[...].reshape(shape)) - first
+    out = 2.0 * (third - CENTER * second_ref[...].reshape(BLOCKS)) - first
     out_ref[...] = out.reshape(2 * ATOM, VECS)
+
+
+def copies_kernel(piece_ref, out_ref, sem):
+    for copy in spread(piece_ref, out_ref, sem):
+        copy.wait()
 
 
 def piece_at(place, i):
@@ -133,7 +150,7 @@
                 out[xz, t * ATOM:(t + 1) * ATOM, :] = total.astype(out.dtype)
         return carry
 
-    lax.fori_loop(0, 8, step, 0)
+    lax.fori_loop(0, 8, step, 0, unroll=True)
 
 
 def mirror_kernel(tab, place, x_ref, y_ref, t_ref, out_ref, held):
@@ -165,14 +182,14 @@
             out_ref[i, t] = total.astype(out_ref.dtype)
         return carry
 
-    lax.fori_loop(0, 8, step, 0)
+    lax.fori_loop(0, 8, step, 0, unroll=True)
 
 
 def gathered_kernel(got_ref, out_ref):
     total = got_ref[0].astype(F32)
     for i in range(1, 8):
         total = total + got_ref[i].astype(F32)
-    out_ref[...] = jnp.swapaxes(total, 1, 2).reshape(2 * ATOM, VECS)
+    out_ref[...] = total.astype(out_ref.dtype)
 
 
 def both_kernel(mine_ref, theirs_ref, out_ref):
@@ -182,21 +199,22 @@
 SMEM = pl.BlockSpec(memory_space=pltpu.SMEM)
 VMEM = pl.BlockSpec(memory_space=pltpu.VMEM)
 PARAMS = pltpu.CompilerParams(vmem_limit_bytes=24 * 1024 * 1024)
-PIECE = (2 * ATOM, VECS)
-BLOCKS = (2, ATOM, VECS)
+ANY = pl.BlockSpec(memory_space=pl.ANY)
 
 
 def like(shape, dtype):
     return jax.ShapeDtypeStruct(shape, dtype)
 
 
-def call(kernel, out_shape, scalars, arrays, scratch=(), flops=0, size=2**20, name=None):
+def call(
+    kernel, out_shape, scalars, arrays, scratch=(), flops=0, size=2**20, name=None, outs=None
+):
     single = not isinstance(out_shape, tuple)
     return pl.pallas_call(
         kernel,
         out_shape=out_shape,
         in_specs=[SMEM] * len(scalars) + [VMEM] * len(arrays),
-        out_specs=VMEM if single else (VMEM,) * len(out_shape),
+        out_specs=outs or (VMEM if single else (VMEM,) * len(out_shape)),
         scratch_shapes=list(scratch),
         compiler_params=PARAMS,
         cost_estimate=pl.CostEstimate(flops=flops, bytes_accessed=size, transcendentals=0),
@@ -233,12 +251,23 @@
     def exchange(x, axes):
         return lax.all_to_all(x, axes, split_axis=0, concat_axis=0, tiled=True)
 
+    def copies(piece):
+        return call(
+            copies_kernel,
+            like((8, *PIECE), BF),
+            (),
+            (piece,),
+            [pltpu.SemaphoreType.DMA((8,))],
+            name="copies",
+            outs=ANY,
+        )
+
     def apply_matrix(plain, flipped):
         piece = lax.ppermute(plain, ALL, TO_COL)
         near = exchange(flipped, ("xh", "z"))
+        piece, near = lax.optimization_barrier((piece, near))
         far = lax.ppermute(near, "co", SWAP)
-        piece, near = lax.optimization_barrier((piece, near))
-        col_block = exchange(jnp.broadcast_to(piece[None], (8, *PIECE)), ROWS)
+        col_block = exchange(copies(piece), ROWS)
         mirror = call(
             mirror_kernel,
             like((8, *BLOCKS), BF),
@@ -263,15 +292,24 @@
         theirs = lax.ppermute(other, "co", SWAP)
         both = call(both_kernel, like((8, *PIECE), BF), (), (mine, theirs), name="both")
         own = exchange(both, ("xh", "z"))
-        gathered = call(gathered_kernel, like(PIECE, F32), (), (got,), name="gathered")
+        gathered = call(gathered_kernel, like(BLOCKS, F32), (), (got,), name="gathered")
         back = lax.ppermute(gathered, ALL, TO_ROW)
         return own, back
 
     forms = (like(PIECE, BF), like((8, *BLOCKS), BF))
-    plain, flipped = call(first_kernel, forms, (widths,), (vectors,), name="first")
+    sent = [pltpu.VMEM(BLOCKS, BF), pltpu.SemaphoreType.DMA((8,))]
+    plain, flipped = call(
+        first_kernel, forms, (widths,), (vectors,), sent, name="first", outs=(VMEM, ANY)
+    )
     parts = apply_matrix(plain, flipped)
     second, plain, flipped = call(
-        second_kernel, (like(PIECE, F32), *forms), (widths,), (*parts, vectors), name="second"
+        second_kernel,
+        (like(PIECE, F32), *forms),
+        (widths,),
+        (*parts, vectors),
+        sent,
+        name="second",
+        outs=(VMEM, VMEM, ANY),
     )
     parts = apply_matrix(plain, flipped)
     return call(

time: 158 us -> 151 us (0.956)
  starting transfers between devices: 67 us -> 80.9 us
  blocking collectives: 13 us -> 0 us
  waiting for transfers between devices: 33 us -> 28.2 us
  Pallas kernels: 24.1 us -> 22.3 us
  local copies, waits for them, and re-layouts: 17.3 us -> 15.5 us
    all_to_all x1 -> x0, blocking collectives: 13 us -> none  [exchange(): return lax.all_to_all(x, axes, split_axis=0, concat_axis=0, tiled=True)]
    all_to_all x7 -> x8, starting transfers between devices: 35.7 us -> 42.7 us  [exchange(): return lax.all_to_all(x, axes, split_axis=0, concat_axis=0, tiled=True)]
    ppermute x2, starting transfers between devices: 11.1 us -> 15.8 us  [apply_matrix(): piece = lax.ppermute(plain, ALL, TO_COL)]
    ppermute x2, waiting for transfers between devices: 7.81 us -> 3.24 us  [apply_matrix(): piece = lax.ppermute(plain, ALL, TO_COL)]
    ppermute x2, starting transfers between devices: 13.7 us -> 16.8 us  [apply_matrix(): back = lax.ppermute(gathered, ALL, TO_ROW)]
    ppermute x2, starting transfers between devices: 3.25 us -> 1.44 us  [apply_matrix(): far = lax.ppermute(near, 'co', SWAP)]
    pallas_call x11 -> x13, Pallas kernels: 24.1 us -> 22.3 us  [call(): pl.pallas_call(kernel, out_shape=out_shape, in_specs=[SMEM] * len(scalars...]
    broadcast_in_dim x2 -> x0, local copies, waits for them, and re-layouts: 1.72 us -> none  [apply_matrix(): col_block = exchange(jnp.broadcast_to(piece[None], (8, *PIECE)), ROWS)]
  transfers between devices with their start and end apart: 15 -> 16, of which waited for: 5 -> 8; matrix products, arithmetic and copies ran while one was open for 2% -> 1% of each run, Pallas kernels for 12% -> 11%
where the time goes in v10:
time: 151 us; the launch traced here: 150 us
  starting transfers between devices  80.9 us (54%)
  waiting for transfers between devices  28.2 us (19%)
  Pallas kernels  22.3 us (15%)
  local copies, waits for them, and re-layouts  15.5 us (10%)
  other arithmetic  1.55 us (1%)
    all_to_all x8, starting transfers between devices, exchange(): return lax.all_to_all(x, axes, split_axis=0, concat_axis=0, tiled=True)  42.7 us
    pallas_call x13, Pallas kernels, call(): pl.pallas_call(kernel, out_shape=out_shape, in_specs=[SMEM] * len(scalars...  22.3 us
    ppermute x2, waiting for transfers between devices, apply_matrix(): back = lax.ppermute(gathered, ALL, TO_ROW)  21 us
    ppermute x2, starting transfers between devices, apply_matrix(): back = lax.ppermute(gathered, ALL, TO_ROW)  16.8 us
    ppermute x2, starting transfers between devices, apply_matrix(): piece = lax.ppermute(plain, ALL, TO_COL)  15.8 us
    unnamed x16, local copies, waits for them, and re-layouts  15.1 us
    ppermute x2, starting transfers between devices, apply_matrix(): theirs = lax.ppermute(other, 'co', SWAP)  4.11 us
    ppermute x2, waiting for transfers between devices, apply_matrix(): piece = lax.ppermute(plain, ALL, TO_COL)  3.24 us
  transfers between devices with their start and end apart: 16, of which 8 were waited for; matrix products, arithmetic and copies ran while one was open for 1% of the time, Pallas kernels for 11%

profile of v10, /device:TPU:25, one launch (start us, length us, event | category | flops | bytes accessed | tf_op | source)
XLA Modules:
  0.0 149.5 jit_solution(13261922956986498667)
XLA Ops:
  0.0 0.9 copy-done.4
  0.9 0.7 copy-done.6
  1.6 1.5 %first.1 = (bf16[256,128]{1,0:T(8,128)(2,1)S(1)}, bf16[8,2,128,128]{3,2,1,0:T(8,128)(2,1)}) custom-call(s32[2]{0:T(128)S(1)} %copy-done.6, f32[256,128]{1,0:T(8,128)S(1)} %copy-done.4), custom_call_target="tpu_custom_call" | custom-call | bytes 1048576 | tf_op jit(solution)/shard_map/first/pallas_call | solution.py:213
  3.1 7.5 %all-to-all-start = ((bf16[8,2,128,128]{3,2,1,0:T(8,128)(2,1)}), bf16[8,2,128,128]{3,2,1,0:T(8,128)(2,1)S(1)}, u32[]{:S(2)}, u32[]{:S(2)}) async-start(bf16[8,2,128,128]{3,2,1,0:T(8,128)(2,1)} %get-tuple-element.27), calls=%async_computation | async-start | bytes 1048576 | tf_op jit(solution)/shard_map/all_to_all | solution.py:252
  10.6 8.8 %collective-permute-start = (bf16[256,128]{1,0:T(8,128)(2,1)S(1)}, bf16[256,128]{1,0:T(8,128)(2,1)S(1)}, u32[]{:S(2)}, u32[]{:S(2)}) collective-permute-start(bf16[256,128]{1,0:T(8,128)(2,1)S(1)} %get-tuple-element.26), channel_id=1, source_target_pairs={{0,0},{1,16},{2,32},{3,48},{4,64},{5,80},{6,96},{7,112},{8,65},{9,... | collective-permute-start | bytes 196616 | tf_op jit(solution)/shard_map/ppermute | solution.py:266
  20.2 0.1 add_select_fusion.1
  20.3 0.1 reshape.355
  20.4 0.1 add.295
  20.5 0.7 multiply_add_fusion.1
  21.2 0.3 select_reduce_fusion.1
  21.5 0.2 collective-permute-done.piece_ref
  21.7 0.0 all-to-all-done.x_ref
  21.7 1.4 collective-permute-start.1
  23.1 0.9 copies.2
  24.0 4.2 %all-to-all-start.1 = ((bf16[8,256,128]{2,1,0:T(8,128)(2,1)}), bf16[8,256,128]{2,1,0:T(8,128)(2,1)S(1)}, u32[]{:S(2)}, u32[]{:S(2)}) async-start(bf16[8,256,128]{2,1,0:T(8,128)(2,1)} %copies.2), calls=%async_computation.1 | async-start | bytes 1048576 | tf_op jit(solution)/shard_map/all_to_all | solution.py:252
  28.2 0.1 pad_add_fusion.place
  28.3 0.1 add_select_fusion
  28.4 0.0 collective-permute-done.1.y_ref
  28.4 0.0 copy-start
  28.4 3.4 %copy-done = bf16[1,1,256,128,128]{4,3,2,1,0:T(8,128)(2,1)S(1)} copy-done((bf16[1,1,256,128,128]{4,3,2,1,0:T(8,128)(2,1)S(1)}, bf16[1,1,256,128,128]{4,3,2,1,0:T(8,128)(2,1)}, u32[]{:S(2)}) %copy-start) | copy-done | bytes 8388632
  31.7 3.9 %mirror.2 = bf16[8,2,128,128]{3,2,1,0:T(8,128)(2,1)} custom-call(s32[272]{0:T(512)S(1)} %broadcast_add_fusion.tab, s32[2]{0:T(128)S(1)} %pad_add_fusion.place, bf16[8,2,128,128]{3,2,1,0:T(8,128)(2,1)S(1)} %all-to-all-done.x_ref, bf16[8,2,128,128]{3,2,1,0:T(8,128)(2,1)S(1)} %collective-permute-done.1.y_ref, bf16[256,128,128]{2,1,0:T(8,128)(2,1)S(1)} %bitcast.6), custom_call_target="tpu_custom_call" | custom-call | flops 1073741824 | bytes 8388608 | tf_op jit(solution)/shard_map/mirror/pallas_call | solution.py:213
  35.7 0.3 all-to-all-done.1.x_ref
  36.0 5.2 %all-to-all-start.2 = ((bf16[8,2,128,128]{3,2,1,0:T(8,128)(2,1)}), bf16[8,2,128,128]{3,2,1,0:T(8,128)(2,1)S(1)}, u32[]{:S(2)}, u32[]{:S(2)}) async-start(bf16[8,2,128,128]{3,2,1,0:T(8,128)(2,1)} %mirror.2), calls=%async_computation.2 | async-start | bytes 1048576 | tf_op jit(solution)/shard_map/all_to_all | solution.py:252
  41.3 0.1 reshape.354
  41.4 0.1 add.260
  41.4 0.1 add.261
  41.6 0.3 select_reduce_fusion
  41.8 0.0 copy-start.1
  41.8 3.4 %copy-done.1 = bf16[1,1,256,128,128]{4,3,2,1,0:T(8,128)(2,1)S(1)} copy-done((bf16[1,1,256,128,128]{4,3,2,1,0:T(8,128)(2,1)S(1)}, bf16[1,1,256,128,128]{4,3,2,1,0:T(8,128)(2,1)}, u32[]{:S(2)}) %copy-start.1) | copy-done | bytes 8388632
  45.2 3.2 %direct.2 = (f32[8,256,128]{2,1,0:T(8,128)S(1)}, bf16[8,256,128]{2,1,0:T(8,128)(2,1)S(1)}) custom-call(s32[288]{0:T(512)S(1)} %broadcast_add_fusion.1.tab, s32[2]{0:T(128)S(1)} %pad_add_fusion.place, bf16[8,256,128]{2,1,0:T(8,128)(2,1)S(1)} %all-to-all-done.1.x_ref, bf16[256,128,128]{2,1,0:T(8,128)(2,1)S(1)} %bitcast.7), custom_call_target="tpu_custom_call" | custom-call | flops 1073741824 | bytes 8388608 | tf_op jit(solution)/shard_map/direct/pallas_call | solution.py:213
  48.4 0.0 all-to-all-done.2.got_ref
  48.4 1.8 %collective-permute-start.2 = (bf16[8,256,128]{2,1,0:T(8,128)(2,1)S(1)}, bf16[8,256,128]{2,1,0:T(8,128)(2,1)S(1)}, u32[]{:S(2)}, u32[]{:S(2)}) collective-permute-start(bf16[8,256,128]{2,1,0:T(8,128)(2,1)S(1)} %get-tuple-element.34), channel_id=1, source_target_pairs={{0,1},{1,0},{2,3},{3,2},{4,5},{5,4},{6,7},{7,6},{8,9},{9,8},{10,11... | collective-permute-start | bytes 1572872 | tf_op jit(solution)/shard_map/ppermute | solution.py:292
  50.2 1.5 %collective-permute-done.2.theirs_ref = bf16[8,256,128]{2,1,0:T(8,128)(2,1)S(1)} collective-permute-done((bf16[8,256,128]{2,1,0:T(8,128)(2,1)S(1)}, bf16[8,256,128]{2,1,0:T(8,128)(2,1)S(1)}, u32[]{:S(2)}, u32[]{:S(2)}) %collective-permute-start.2) | collective-permute-done | bytes 524320 | tf_op jit(solution)/shard_map/ppermute | solution.py:292
  51.7 0.9 both.2
  52.6 6.1 %all-to-all-start.3 = ((bf16[8,256,128]{2,1,0:T(8,128)(2,1)}), bf16[8,256,128]{2,1,0:T(8,128)(2,1)S(1)}, u32[]{:S(2)}, u32[]{:S(2)}) async-start(bf16[8,256,128]{2,1,0:T(8,128)(2,1)} %both.2), calls=%async_computation.3 | async-start | bytes 1048576 | tf_op jit(solution)/shard_map/all_to_all | solution.py:252
  58.7 0.1 gathered.2
  58.8 8.4 %collective-permute-start.3 = (f32[2,128,128]{2,1,0:T(8,128)S(1)}, f32[2,128,128]{2,1,0:T(8,128)S(1)}, u32[]{:S(2)}, u32[]{:S(2)}) collective-permute-start(f32[2,128,128]{2,1,0:T(8,128)S(1)} %gathered.2), channel_id=1, source_target_pairs={{0,0},{16,1},{32,2},{48,3},{64,4},{80,5},{96,6},{112,7},{65,8},{81... | collective-permute-start | bytes 393224 | tf_op jit(solution)/shard_map/ppermute | solution.py:296
  67.2 10.5 %collective-permute-done.3.back_ref = f32[2,128,128]{2,1,0:T(8,128)S(1)} collective-permute-done((f32[2,128,128]{2,1,0:T(8,128)S(1)}, f32[2,128,128]{2,1,0:T(8,128)S(1)}, u32[]{:S(2)}, u32[]{:S(2)}) %collective-permute-start.3) | collective-permute-done | bytes 131104 | tf_op jit(solution)/shard_map/ppermute | solution.py:296
  77.7 0.0 all-to-all-done.3.own_ref
  77.7 1.6 %second.1 = (f32[256,128]{1,0:T(8,128)S(1)}, bf16[256,128]{1,0:T(8,128)(2,1)S(1)}, bf16[8,2,128,128]{3,2,1,0:T(8,128)(2,1)}) custom-call(s32[2]{0:T(128)S(1)} %copy-done.7, bf16[8,256,128]{2,1,0:T(8,128)(2,1)S(1)} %all-to-all-done.3.own_ref, f32[2,128,128]{2,1,0:T(8,128)S(1)} %collective-permute-done.3.back_ref, f32[256,128]{1,0:T(8,128)S(1)} %copy-done.5), custom_call_target="tpu_custom_call" | custom-call | bytes 1048576 | tf_op jit(solution)/shard_map/second/pallas_call | solution.py:213
  79.4 3.5 %all-to-all-start.4 = ((bf16[8,2,128,128]{3,2,1,0:T(8,128)(2,1)}), bf16[8,2,128,128]{3,2,1,0:T(8,128)(2,1)S(1)}, u32[]{:S(2)}, u32[]{:S(2)}) async-start(bf16[8,2,128,128]{3,2,1,0:T(8,128)(2,1)} %get-tuple-element.37), calls=%async_computation.4 | async-start | bytes 1048576 | tf_op jit(solution)/shard_map/all_to_all | solution.py:252
  82.9 7.0 %collective-permute-start.4 = (bf16[256,128]{1,0:T(8,128)(2,1)S(1)}, bf16[256,128]{1,0:T(8,128)(2,1)S(1)}, u32[]{:S(2)}, u32[]{:S(2)}) collective-permute-start(bf16[256,128]{1,0:T(8,128)(2,1)S(1)} %get-tuple-element.36), channel_id=1, source_target_pairs={{0,0},{1,16},{2,32},{3,48},{4,64},{5,80},{6,96},{7,112},{8,65},{9,... | collective-permute-start | bytes 196616 | tf_op jit(solution)/shard_map/ppermute | solution.py:266
  89.9 3.0 %collective-permute-done.4.piece_ref = bf16[256,128]{1,0:T(8,128)(2,1)S(1)} collective-permute-done((bf16[256,128]{1,0:T(8,128)(2,1)S(1)}, bf16[256,128]{1,0:T(8,128)(2,1)S(1)}, u32[]{:S(2)}, u32[]{:S(2)}) %collective-permute-start.4) | collective-permute-done | bytes 65568 | tf_op jit(solution)/shard_map/ppermute | solution.py:266
  93.0 0.0 all-to-all-done.4.x_ref
  93.0 0.0 collective-permute-start.5
  93.0 0.9 copies.3
  93.8 4.9 %all-to-all-start.5 = ((bf16[8,256,128]{2,1,0:T(8,128)(2,1)}), bf16[8,256,128]{2,1,0:T(8,128)(2,1)S(1)}, u32[]{:S(2)}, u32[]{:S(2)}) async-start(bf16[8,256,128]{2,1,0:T(8,128)(2,1)} %copies.3), calls=%async_computation.5 | async-start | bytes 1048576 | tf_op jit(solution)/shard_map/all_to_all | solution.py:252
  98.7 0.0 collective-permute-done.5.y_ref
  98.7 3.4 %copy-done.2 = bf16[1,1,256,128,128]{4,3,2,1,0:T(8,128)(2,1)S(1)} copy-done((bf16[1,1,256,128,128]{4,3,2,1,0:T(8,128)(2,1)S(1)}, bf16[1,1,256,128,128]{4,3,2,1,0:T(8,128)(2,1)}, u32[]{:S(2)}) %copy-start.2) | copy-done | bytes 8388632
  102.1 3.9 %mirror.3 = bf16[8,2,128,128]{3,2,1,0:T(8,128)(2,1)} custom-call(s32[272]{0:T(512)S(1)} %broadcast_add_fusion.tab, s32[2]{0:T(128)S(1)} %pad_add_fusion.place, bf16[8,2,128,128]{3,2,1,0:T(8,128)(2,1)S(1)} %all-to-all-done.4.x_ref, bf16[8,2,128,128]{3,2,1,0:T(8,128)(2,1)S(1)} %collective-permute-done.5.y_ref, bf16[256,128,128]{2,1,0:T(8,128)(2,1)S(1)} %bitcast.8), custom_call_target="tpu_custom_call" | custom-call | flops 1073741824 | bytes 8388608 | tf_op jit(solution)/shard_map/mirror/pallas_call | solution.py:213
  106.1 0.5 all-to-all-done.5.x_ref
  106.6 5.2 %all-to-all-start.6 = ((bf16[8,2,128,128]{3,2,1,0:T(8,128)(2,1)}), bf16[8,2,128,128]{3,2,1,0:T(8,128)(2,1)S(1)}, u32[]{:S(2)}, u32[]{:S(2)}) async-start(bf16[8,2,128,128]{3,2,1,0:T(8,128)(2,1)} %mirror.3), calls=%async_computation.6 | async-start | bytes 1048576 | tf_op jit(solution)/shard_map/all_to_all | solution.py:252
  111.8 3.4 %copy-done.3 = bf16[1,1,256,128,128]{4,3,2,1,0:T(8,128)(2,1)S(1)} copy-done((bf16[1,1,256,128,128]{4,3,2,1,0:T(8,128)(2,1)S(1)}, bf16[1,1,256,128,128]{4,3,2,1,0:T(8,128)(2,1)}, u32[]{:S(2)}) %copy-start.3) | copy-done | bytes 8388632
  115.2 3.2 %direct.3 = (f32[8,256,128]{2,1,0:T(8,128)S(1)}, bf16[8,256,128]{2,1,0:T(8,128)(2,1)S(1)}) custom-call(s32[288]{0:T(512)S(1)} %broadcast_add_fusion.1.tab, s32[2]{0:T(128)S(1)} %pad_add_fusion.place, bf16[8,256,128]{2,1,0:T(8,128)(2,1)S(1)} %all-to-all-done.5.x_ref, bf16[256,128,128]{2,1,0:T(8,128)(2,1)S(1)} %bitcast.9), custom_call_target="tpu_custom_call" | custom-call | flops 1073741824 | bytes 8388608 | tf_op jit(solution)/shard_map/direct/pallas_call | solution.py:213
  118.4 0.0 all-to-all-done.6.got_ref
  118.4 2.3 %collective-permute-start.6 = (bf16[8,256,128]{2,1,0:T(8,128)(2,1)S(1)}, bf16[8,256,128]{2,1,0:T(8,128)(2,1)S(1)}, u32[]{:S(2)}, u32[]{:S(2)}) collective-permute-start(bf16[8,256,128]{2,1,0:T(8,128)(2,1)S(1)} %get-tuple-element.44), channel_id=1, source_target_pairs={{0,1},{1,0},{2,3},{3,2},{4,5},{5,4},{6,7},{7,6},{8,9},{9,8},{10,11... | collective-permute-start | bytes 1572872 | tf_op jit(solution)/shard_map/ppermute | solution.py:292
  120.7 1.5 %collective-permute-done.6.theirs_ref = bf16[8,256,128]{2,1,0:T(8,128)(2,1)S(1)} collective-permute-done((bf16[8,256,128]{2,1,0:T(8,128)(2,1)S(1)}, bf16[8,256,128]{2,1,0:T(8,128)(2,1)S(1)}, u32[]{:S(2)}, u32[]{:S(2)}) %collective-permute-start.6) | collective-permute-done | bytes 524320 | tf_op jit(solution)/shard_map/ppermute | solution.py:292
  122.3 0.9 both.3
  123.1 6.0 %all-to-all-start.7 = ((bf16[8,256,128]{2,1,0:T(8,128)(2,1)}), bf16[8,256,128]{2,1,0:T(8,128)(2,1)S(1)}, u32[]{:S(2)}, u32[]{:S(2)}) async-start(bf16[8,256,128]{2,1,0:T(8,128)(2,1)} %both.3), calls=%async_computation.7 | async-start | bytes 1048576 | tf_op jit(solution)/shard_map/all_to_all | solution.py:252
  129.1 0.1 gathered.3
  129.2 8.4 %collective-permute-start.7 = (f32[2,128,128]{2,1,0:T(8,128)S(1)}, f32[2,128,128]{2,1,0:T(8,128)S(1)}, u32[]{:S(2)}, u32[]{:S(2)}) collective-permute-start(f32[2,128,128]{2,1,0:T(8,128)S(1)} %gathered.3), channel_id=1, source_target_pairs={{0,0},{16,1},{32,2},{48,3},{64,4},{80,5},{96,6},{112,7},{65,8},{81... | collective-permute-start | bytes 393224 | tf_op jit(solution)/shard_map/ppermute | solution.py:296
  137.7 10.5 %collective-permute-done.7.back_ref = f32[2,128,128]{2,1,0:T(8,128)S(1)} collective-permute-done((f32[2,128,128]{2,1,0:T(8,128)S(1)}, f32[2,128,128]{2,1,0:T(8,128)S(1)}, u32[]{:S(2)}, u32[]{:S(2)}) %collective-permute-start.7) | collective-permute-done | bytes 131104 | tf_op jit(solution)/shard_map/ppermute | solution.py:296
  148.1 0.0 all-to-all-done.7.own_ref
  148.1 1.4 last.1
  (25 shorter events, 0.1 us)
Async XLA Ops:
  0.0 0.9 copy-start.4
  0.9 0.7 copy-start.6
  3.1 18.6 %all-to-all-start = ((bf16[8,2,128,128]{3,2,1,0:T(8,128)(2,1)}), bf16[8,2,128,128]{3,2,1,0:T(8,128)(2,1)S(1)}, u32[]{:S(2)}, u32[]{:S(2)}) async-start(bf16[8,2,128,128]{3,2,1,0:T(8,128)(2,1)} %get-tuple-element.27), calls=%async_computation | async-start | bytes 1048576 | tf_op jit(solution)/shard_map/all_to_all | solution.py:252
  10.6 11.1 %collective-permute-start = (bf16[256,128]{1,0:T(8,128)(2,1)S(1)}, bf16[256,128]{1,0:T(8,128)(2,1)S(1)}, u32[]{:S(2)}, u32[]{:S(2)}) collective-permute-start(bf16[256,128]{1,0:T(8,128)(2,1)S(1)} %get-tuple-element.26), channel_id=1, source_target_pairs={{0,0},{1,16},{2,32},{3,48},{4,64},{5,80},{6,96},{7,112},{8,65},{9,... | collective-permute-start | bytes 196616 | tf_op jit(solution)/shard_map/ppermute | solution.py:266
  21.7 6.7 %collective-permute-start.1 = (bf16[8,2,128,128]{3,2,1,0:T(8,128)(2,1)S(1)}, bf16[8,2,128,128]{3,2,1,0:T(8,128)(2,1)S(1)}, u32[]{:S(2)}, u32[]{:S(2)}) collective-permute-start(bf16[8,2,128,128]{3,2,1,0:T(8,128)(2,1)S(1)} %all-to-all-done.x_ref), channel_id=1, source_target_pairs={{0,1},{1,0},{2,3},{3,2},{4,5},{5,4},{6,7},{7,6},{8,9},{9,8},{10,11... | collective-permute-start | bytes 1572872 | tf_op jit(solution)/shard_map/ppermute | solution.py:269
  24.0 12.0 %all-to-all-start.1 = ((bf16[8,256,128]{2,1,0:T(8,128)(2,1)}), bf16[8,256,128]{2,1,0:T(8,128)(2,1)S(1)}, u32[]{:S(2)}, u32[]{:S(2)}) async-start(bf16[8,256,128]{2,1,0:T(8,128)(2,1)} %copies.2), calls=%async_computation.1 | async-start | bytes 1048576 | tf_op jit(solution)/shard_map/all_to_all | solution.py:252
  28.4 3.4 %copy-start = (bf16[1,1,256,128,128]{4,3,2,1,0:T(8,128)(2,1)S(1)}, bf16[1,1,256,128,128]{4,3,2,1,0:T(8,128)(2,1)}, u32[]{:S(2)}) copy-start(bf16[1,1,256,128,128]{4,3,2,1,0:T(8,128)(2,1)} %param.8) | copy-start | bytes 25165828
  35.7 42.0 %copy-start.5 = (f32[256,128]{1,0:T(8,128)S(1)}, f32[256,128]{1,0:T(8,128)}, u32[]{:S(2)}) copy-start(f32[256,128]{1,0:T(8,128)} %vectors_ref.5) | copy-start | bytes 393220
  35.7 42.0 %copy-start.7 = (s32[2]{0:T(128)S(1)}, s32[2]{0:T(128)}, u32[]{:S(2)}) copy-start(s32[2]{0:T(128)} %widths.5) | copy-start | bytes 28
  36.0 12.4 %all-to-all-start.2 = ((bf16[8,2,128,128]{3,2,1,0:T(8,128)(2,1)}), bf16[8,2,128,128]{3,2,1,0:T(8,128)(2,1)S(1)}, u32[]{:S(2)}, u32[]{:S(2)}) async-start(bf16[8,2,128,128]{3,2,1,0:T(8,128)(2,1)} %mirror.2), calls=%async_computation.2 | async-start | bytes 1048576 | tf_op jit(solution)/shard_map/all_to_all | solution.py:252
  41.8 3.4 %copy-start.1 = (bf16[1,1,256,128,128]{4,3,2,1,0:T(8,128)(2,1)S(1)}, bf16[1,1,256,128,128]{4,3,2,1,0:T(8,128)(2,1)}, u32[]{:S(2)}) copy-start(bf16[1,1,256,128,128]{4,3,2,1,0:T(8,128)(2,1)} %param.8) | copy-start | bytes 25165828
  48.4 3.3 %collective-permute-start.2 = (bf16[8,256,128]{2,1,0:T(8,128)(2,1)S(1)}, bf16[8,256,128]{2,1,0:T(8,128)(2,1)S(1)}, u32[]{:S(2)}, u32[]{:S(2)}) collective-permute-start(bf16[8,256,128]{2,1,0:T(8,128)(2,1)S(1)} %get-tuple-element.34), channel_id=1, source_target_pairs={{0,1},{1,0},{2,3},{3,2},{4,5},{5,4},{6,7},{7,6},{8,9},{9,8},{10,11... | collective-permute-start | bytes 1572872 | tf_op jit(solution)/shard_map/ppermute | solution.py:292
  52.6 25.1 %all-to-all-start.3 = ((bf16[8,256,128]{2,1,0:T(8,128)(2,1)}), bf16[8,256,128]{2,1,0:T(8,128)(2,1)S(1)}, u32[]{:S(2)}, u32[]{:S(2)}) async-start(bf16[8,256,128]{2,1,0:T(8,128)(2,1)} %both.2), calls=%async_computation.3 | async-start | bytes 1048576 | tf_op jit(solution)/shard_map/all_to_all | solution.py:252
  58.8 18.9 %collective-permute-start.3 = (f32[2,128,128]{2,1,0:T(8,128)S(1)}, f32[2,128,128]{2,1,0:T(8,128)S(1)}, u32[]{:S(2)}, u32[]{:S(2)}) collective-permute-start(f32[2,128,128]{2,1,0:T(8,128)S(1)} %gathered.2), channel_id=1, source_target_pairs={{0,0},{16,1},{32,2},{48,3},{64,4},{80,5},{96,6},{112,7},{65,8},{81... | collective-permute-start | bytes 393224 | tf_op jit(solution)/shard_map/ppermute | solution.py:296
  79.4 13.6 %all-to-all-start.4 = ((bf16[8,2,128,128]{3,2,1,0:T(8,128)(2,1)}), bf16[8,2,128,128]{3,2,1,0:T(8,128)(2,1)S(1)}, u32[]{:S(2)}, u32[]{:S(2)}) async-start(bf16[8,2,128,128]{3,2,1,0:T(8,128)(2,1)} %get-tuple-element.37), calls=%async_computation.4 | async-start | bytes 1048576 | tf_op jit(solution)/shard_map/all_to_all | solution.py:252
  82.9 10.1 %collective-permute-start.4 = (bf16[256,128]{1,0:T(8,128)(2,1)S(1)}, bf16[256,128]{1,0:T(8,128)(2,1)S(1)}, u32[]{:S(2)}, u32[]{:S(2)}) collective-permute-start(bf16[256,128]{1,0:T(8,128)(2,1)S(1)} %get-tuple-element.36), channel_id=1, source_target_pairs={{0,0},{1,16},{2,32},{3,48},{4,64},{5,80},{6,96},{7,112},{8,65},{9,... | collective-permute-start | bytes 196616 | tf_op jit(solution)/shard_map/ppermute | solution.py:266
  93.0 5.8 %collective-permute-start.5 = (bf16[8,2,128,128]{3,2,1,0:T(8,128)(2,1)S(1)}, bf16[8,2,128,128]{3,2,1,0:T(8,128)(2,1)S(1)}, u32[]{:S(2)}, u32[]{:S(2)}) collective-permute-start(bf16[8,2,128,128]{3,2,1,0:T(8,128)(2,1)S(1)} %all-to-all-done.4.x_ref), channel_id=1, source_target_pairs={{0,1},{1,0},{2,3},{3,2},{4,5},{5,4},{6,7},{7,6},{8,9},{9,8},{10,11... | collective-permute-start | bytes 1572872 | tf_op jit(solution)/shard_map/ppermute | solution.py:269
  93.8 12.7 %all-to-all-start.5 = ((bf16[8,256,128]{2,1,0:T(8,128)(2,1)}), bf16[8,256,128]{2,1,0:T(8,128)(2,1)S(1)}, u32[]{:S(2)}, u32[]{:S(2)}) async-start(bf16[8,256,128]{2,1,0:T(8,128)(2,1)} %copies.3), calls=%async_computation.5 | async-start | bytes 1048576 | tf_op jit(solution)/shard_map/all_to_all | solution.py:252
  98.7 3.4 %copy-start.2 = (bf16[1,1,256,128,128]{4,3,2,1,0:T(8,128)(2,1)S(1)}, bf16[1,1,256,128,128]{4,3,2,1,0:T(8,128)(2,1)}, u32[]{:S(2)}) copy-start(bf16[1,1,256,128,128]{4,3,2,1,0:T(8,128)(2,1)} %param.8) | copy-start | bytes 25165828
  106.6 11.8 %all-to-all-start.6 = ((bf16[8,2,128,128]{3,2,1,0:T(8,128)(2,1)}), bf16[8,2,128,128]{3,2,1,0:T(8,128)(2,1)S(1)}, u32[]{:S(2)}, u32[]{:S(2)}) async-start(bf16[8,2,128,128]{3,2,1,0:T(8,128)(2,1)} %mirror.3), calls=%async_computation.6 | async-start | bytes 1048576 | tf_op jit(solution)/shard_map/all_to_all | solution.py:252
  111.8 3.4 %copy-start.3 = (bf16[1,1,256,128,128]{4,3,2,1,0:T(8,128)(2,1)S(1)}, bf16[1,1,256,128,128]{4,3,2,1,0:T(8,128)(2,1)}, u32[]{:S(2)}) copy-start(bf16[1,1,256,128,128]{4,3,2,1,0:T(8,128)(2,1)} %param.8) | copy-start | bytes 25165828
  118.4 3.9 %collective-permute-start.6 = (bf16[8,256,128]{2,1,0:T(8,128)(2,1)S(1)}, bf16[8,256,128]{2,1,0:T(8,128)(2,1)S(1)}, u32[]{:S(2)}, u32[]{:S(2)}) collective-permute-start(bf16[8,256,128]{2,1,0:T(8,128)(2,1)S(1)} %get-tuple-element.44), channel_id=1, source_target_pairs={{0,1},{1,0},{2,3},{3,2},{4,5},{5,4},{6,7},{7,6},{8,9},{9,8},{10,11... | collective-permute-start | bytes 1572872 | tf_op jit(solution)/shard_map/ppermute | solution.py:292
  123.1 25.0 %all-to-all-start.7 = ((bf16[8,256,128]{2,1,0:T(8,128)(2,1)}), bf16[8,256,128]{2,1,0:T(8,128)(2,1)S(1)}, u32[]{:S(2)}, u32[]{:S(2)}) async-start(bf16[8,256,128]{2,1,0:T(8,128)(2,1)} %both.3), calls=%async_computation.7 | async-start | bytes 1048576 | tf_op jit(solution)/shard_map/all_to_all | solution.py:252
  129.2 18.9 %collective-permute-start.7 = (f32[2,128,128]{2,1,0:T(8,128)S(1)}, f32[2,128,128]{2,1,0:T(8,128)S(1)}, u32[]{:S(2)}, u32[]{:S(2)}) collective-permute-start(f32[2,128,128]{2,1,0:T(8,128)S(1)} %gathered.3), channel_id=1, source_target_pairs={{0,0},{16,1},{32,2},{48,3},{64,4},{80,5},{96,6},{112,7},{65,8},{81... | collective-permute-start | bytes 393224 | tf_op jit(solution)/shard_map/ppermute | solution.py:296

commit v11 on v5

--- a/solution.py
+++ b/solution.py
@@ -237,7 +237,7 @@
     def exchange(x, axes):
         return lax.all_to_all(x, axes, split_axis=0, concat_axis=0, tiled=True)
 
-    def apply_matrix(plain, flipped, sent):
+    def apply_matrix(plain, flipped):
         piece = lax.ppermute(plain, ALL, TO_COL)
         near = exchange(flipped, ("xh", "z"))
         piece, near = lax.optimization_barrier((piece, near))
@@ -267,18 +267,18 @@
         theirs = lax.ppermute(other, "co", SWAP)
         both = call(both_kernel, like((8, *PIECE), BF), (), (mine, theirs), name="both")
         own = exchange(both, ("xh", "z"))
-        gathered = call(gathered_kernel, like(BLOCKS, sent), (), (got,), name="gathered")
+        gathered = call(gathered_kernel, like(BLOCKS, BF), (), (got,), name="gathered")
         back = lax.ppermute(gathered, ALL, TO_ROW)
         turned = call(turned_kernel, like(PIECE, F32), (), (back,), name="turned")
         return own, turned
 
     forms = (like(PIECE, BF), like((8, *BLOCKS), BF))
     plain, flipped = call(first_kernel, forms, (widths,), (vectors,), name="first")
-    parts = apply_matrix(plain, flipped, F32)
+    parts = apply_matrix(plain, flipped)
     second, plain, flipped = call(
         second_kernel, (like(PIECE, F32), *forms), (widths,), (*parts, vectors), name="second"
     )
-    parts = apply_matrix(plain, flipped, BF)
+    parts = apply_matrix(plain, flipped)
     return call(
         last_kernel, like(PIECE, F32), (widths,), (*parts, vectors, second), name="last"
     )

time: 147 us -> 145 us (0.986)
  waiting for transfers between devices: 25.1 us -> 22.2 us
    ppermute x2, waiting for transfers between devices: 17.9 us -> 14.3 us  [apply_matrix(): back = lax.ppermute(gathered, ALL, TO_ROW)]
  transfers between devices with their start and end apart: 16 -> 16, of which waited for: 8 -> 9; matrix products, arithmetic and copies ran while one was open for 3% -> 3% of each run, Pallas kernels for 10% -> 10%
where the time goes in v11:
time: 145 us; the launch traced here: 144 us
  starting transfers between devices  81.7 us (56%)
  waiting for transfers between devices  22.2 us (15%)
  Pallas kernels  20.6 us (14%)
  local copies, waits for them, and re-layouts  17.2 us (12%)
  other arithmetic  1.55 us (1%)
    all_to_all x8, starting transfers between devices, exchange(): return lax.all_to_all(x, axes, split_axis=0, concat_axis=0, tiled=True)  42.5 us
    pallas_call x13, Pallas kernels, call(): pl.pallas_call(kernel, out_shape=out_shape, in_specs=[SMEM] * len(scalars...  20.6 us
    ppermute x2, starting transfers between devices, apply_matrix(): back = lax.ppermute(gathered, ALL, TO_ROW)  16.8 us
    ppermute x2, starting transfers between devices, apply_matrix(): piece = lax.ppermute(plain, ALL, TO_COL)  16.2 us
    unnamed x16, local copies, waits for them, and re-layouts  15.1 us
    ppermute x2, waiting for transfers between devices, apply_matrix(): back = lax.ppermute(gathered, ALL, TO_ROW)  14.3 us
    ppermute x2, starting transfers between devices, apply_matrix(): theirs = lax.ppermute(other, 'co', SWAP)  4.11 us
    ppermute x2, waiting for transfers between devices, apply_matrix(): piece = lax.ppermute(plain, ALL, TO_COL)  3.5 us
  transfers between devices with their start and end apart: 16, of which 9 were waited for; matrix products, arithmetic and copies ran while one was open for 3% of the time, Pallas kernels for 10%

profile of v11, /device:TPU:25, one launch (start us, length us, event | category | flops | bytes accessed | tf_op | source)
XLA Modules:
  0.0 144.2 jit_solution(7255778046242416804)
XLA Ops:
  0.0 0.9 copy-done.4
  0.9 0.7 copy-done.6
  1.6 1.5 %first.1 = (bf16[256,128]{1,0:T(8,128)(2,1)S(1)}, bf16[8,2,128,128]{3,2,1,0:T(8,128)(2,1)}) custom-call(s32[2]{0:T(128)S(1)} %copy-done.6, f32[256,128]{1,0:T(8,128)S(1)} %copy-done.4), custom_call_target="tpu_custom_call" | custom-call | bytes 1048576 | tf_op jit(solution)/shard_map/first/pallas_call | solution.py:199
  3.0 7.5 %all-to-all-start = ((bf16[8,2,128,128]{3,2,1,0:T(8,128)(2,1)}), bf16[8,2,128,128]{3,2,1,0:T(8,128)(2,1)S(1)}, u32[]{:S(2)}, u32[]{:S(2)}) async-start(bf16[8,2,128,128]{3,2,1,0:T(8,128)(2,1)} %get-tuple-element.27), calls=%async_computation | async-start | bytes 1048576 | tf_op jit(solution)/shard_map/all_to_all | solution.py:238
  10.5 8.8 %collective-permute-start = (bf16[256,128]{1,0:T(8,128)(2,1)S(1)}, bf16[256,128]{1,0:T(8,128)(2,1)S(1)}, u32[]{:S(2)}, u32[]{:S(2)}) collective-permute-start(bf16[256,128]{1,0:T(8,128)(2,1)S(1)} %get-tuple-element.26), channel_id=1, source_target_pairs={{0,0},{1,16},{2,32},{3,48},{4,64},{5,80},{6,96},{7,112},{8,65},{9,... | collective-permute-start | bytes 196616 | tf_op jit(solution)/shard_map/ppermute | solution.py:241
  20.1 0.1 add_select_fusion.1
  20.2 0.1 reshape.357
  20.3 0.1 add.295
  20.4 0.7 multiply_add_fusion.1
  21.1 0.3 select_reduce_fusion.1
  21.4 0.2 collective-permute-done
  21.6 0.0 all-to-all-done.x_ref
  21.6 1.4 collective-permute-start.1
  23.1 0.9 broadcast_in_dim.104
  23.9 4.2 %all-to-all-start.1 = ((bf16[8,256,128]{2,1,0:T(8,128)(2,1)}), bf16[8,256,128]{2,1,0:T(8,128)(2,1)S(1)}, u32[]{:S(2)}, u32[]{:S(2)}) async-start(bf16[8,256,128]{2,1,0:T(8,128)(2,1)} %broadcast_in_dim.104), calls=%async_computation.1 | async-start | bytes 1048576 | tf_op jit(solution)/shard_map/all_to_all | solution.py:238
  28.1 0.1 pad_add_fusion.place
  28.2 0.1 add_select_fusion
  28.3 0.0 copy-start
  28.3 3.4 %copy-done = bf16[1,1,256,128,128]{4,3,2,1,0:T(8,128)(2,1)S(1)} copy-done((bf16[1,1,256,128,128]{4,3,2,1,0:T(8,128)(2,1)S(1)}, bf16[1,1,256,128,128]{4,3,2,1,0:T(8,128)(2,1)}, u32[]{:S(2)}) %copy-start) | copy-done | bytes 8388632
  31.7 3.9 %mirror.2 = bf16[8,2,128,128]{3,2,1,0:T(8,128)(2,1)} custom-call(s32[272]{0:T(512)S(1)} %broadcast_add_fusion.tab, s32[2]{0:T(128)S(1)} %pad_add_fusion.place, bf16[8,2,128,128]{3,2,1,0:T(8,128)(2,1)S(1)} %all-to-all-done.x_ref, bf16[8,2,128,128]{3,2,1,0:T(8,128)(2,1)S(1)} %collective-permute-done.1.y_ref, bf16[256,128,128]{2,1,0:T(8,128)(2,1)S(1)} %bitcast.6), custom_call_target="tpu_custom_call" | custom-call | flops 1073741824 | bytes 8388608 | tf_op jit(solution)/shard_map/mirror/pallas_call | solution.py:199
  35.6 0.3 all-to-all-done.1.x_ref
  35.9 5.2 %all-to-all-start.2 = ((bf16[8,2,128,128]{3,2,1,0:T(8,128)(2,1)}), bf16[8,2,128,128]{3,2,1,0:T(8,128)(2,1)S(1)}, u32[]{:S(2)}, u32[]{:S(2)}) async-start(bf16[8,2,128,128]{3,2,1,0:T(8,128)(2,1)} %mirror.2), calls=%async_computation.2 | async-start | bytes 1048576 | tf_op jit(solution)/shard_map/all_to_all | solution.py:238
  41.2 0.1 reshape.356
  41.3 0.1 add.260
  41.3 0.1 add.261
  41.5 0.3 select_reduce_fusion
  41.7 0.0 copy-start.1
  41.7 3.4 %copy-done.1 = bf16[1,1,256,128,128]{4,3,2,1,0:T(8,128)(2,1)S(1)} copy-done((bf16[1,1,256,128,128]{4,3,2,1,0:T(8,128)(2,1)S(1)}, bf16[1,1,256,128,128]{4,3,2,1,0:T(8,128)(2,1)}, u32[]{:S(2)}) %copy-start.1) | copy-done | bytes 8388632
  45.1 3.2 %direct.2 = (f32[8,256,128]{2,1,0:T(8,128)S(1)}, bf16[8,256,128]{2,1,0:T(8,128)(2,1)S(1)}) custom-call(s32[288]{0:T(512)S(1)} %broadcast_add_fusion.1.tab, s32[2]{0:T(128)S(1)} %pad_add_fusion.place, bf16[8,256,128]{2,1,0:T(8,128)(2,1)S(1)} %all-to-all-done.1.x_ref, bf16[256,128,128]{2,1,0:T(8,128)(2,1)S(1)} %bitcast.7), custom_call_target="tpu_custom_call" | custom-call | flops 1073741824 | bytes 8388608 | tf_op jit(solution)/shard_map/direct/pallas_call | solution.py:199
  48.3 0.0 all-to-all-done.2.got_ref
  48.3 1.8 %collective-permute-start.2 = (bf16[8,256,128]{2,1,0:T(8,128)(2,1)S(1)}, bf16[8,256,128]{2,1,0:T(8,128)(2,1)S(1)}, u32[]{:S(2)}, u32[]{:S(2)}) collective-permute-start(bf16[8,256,128]{2,1,0:T(8,128)(2,1)S(1)} %get-tuple-element.34), channel_id=1, source_target_pairs={{0,1},{1,0},{2,3},{3,2},{4,5},{5,4},{6,7},{7,6},{8,9},{9,8},{10,11... | collective-permute-start | bytes 1572872 | tf_op jit(solution)/shard_map/ppermute | solution.py:267
  50.1 1.5 %collective-permute-done.2.theirs_ref = bf16[8,256,128]{2,1,0:T(8,128)(2,1)S(1)} collective-permute-done((bf16[8,256,128]{2,1,0:T(8,128)(2,1)S(1)}, bf16[8,256,128]{2,1,0:T(8,128)(2,1)S(1)}, u32[]{:S(2)}, u32[]{:S(2)}) %collective-permute-start.2) | collective-permute-done | bytes 524320 | tf_op jit(solution)/shard_map/ppermute | solution.py:267
  51.6 0.9 both.2
  52.5 6.1 %all-to-all-start.3 = ((bf16[8,256,128]{2,1,0:T(8,128)(2,1)}), bf16[8,256,128]{2,1,0:T(8,128)(2,1)S(1)}, u32[]{:S(2)}, u32[]{:S(2)}) async-start(bf16[8,256,128]{2,1,0:T(8,128)(2,1)} %both.2), calls=%async_computation.3 | async-start | bytes 1048576 | tf_op jit(solution)/shard_map/all_to_all | solution.py:238
  58.6 0.1 gathered.2
  58.7 8.4 %collective-permute-start.3 = (bf16[2,128,128]{2,1,0:T(8,128)(2,1)S(1)}, bf16[2,128,128]{2,1,0:T(8,128)(2,1)S(1)}, u32[]{:S(2)}, u32[]{:S(2)}) collective-permute-start(bf16[2,128,128]{2,1,0:T(8,128)(2,1)S(1)} %gathered.2), channel_id=1, source_target_pairs={{0,0},{16,1},{32,2},{48,3},{64,4},{80,5},{96,6},{112,7},{65,8},{81... | collective-permute-start | bytes 196616 | tf_op jit(solution)/shard_map/ppermute | solution.py:271
  67.1 7.4 %collective-permute-done.3.sum_ref = bf16[2,128,128]{2,1,0:T(8,128)(2,1)S(1)} collective-permute-done((bf16[2,128,128]{2,1,0:T(8,128)(2,1)S(1)}, bf16[2,128,128]{2,1,0:T(8,128)(2,1)S(1)}, u32[]{:S(2)}, u32[]{:S(2)}) %collective-permute-start.3) | collective-permute-done | bytes 65568 | tf_op jit(solution)/shard_map/ppermute | solution.py:271
  74.5 0.1 turned.2.back_ref
  74.6 1.5 %second.1 = (f32[256,128]{1,0:T(8,128)S(1)}, bf16[256,128]{1,0:T(8,128)(2,1)S(1)}, bf16[8,2,128,128]{3,2,1,0:T(8,128)(2,1)}) custom-call(s32[2]{0:T(128)S(1)} %copy-done.7, bf16[8,256,128]{2,1,0:T(8,128)(2,1)S(1)} %all-to-all-done.3.own_ref, f32[256,128]{1,0:T(8,128)S(1)} %turned.2.back_ref, f32[256,128]{1,0:T(8,128)S(1)} %copy-done.5), custom_call_target="tpu_custom_call" | custom-call | bytes 1048576 | tf_op jit(solution)/shard_map/second/pallas_call | solution.py:199
  76.2 3.5 %all-to-all-start.4 = ((bf16[8,2,128,128]{3,2,1,0:T(8,128)(2,1)}), bf16[8,2,128,128]{3,2,1,0:T(8,128)(2,1)S(1)}, u32[]{:S(2)}, u32[]{:S(2)}) async-start(bf16[8,2,128,128]{3,2,1,0:T(8,128)(2,1)} %get-tuple-element.37), calls=%async_computation.4 | async-start | bytes 1048576 | tf_op jit(solution)/shard_map/all_to_all | solution.py:238
  79.7 7.4 %collective-permute-start.4 = (bf16[256,128]{1,0:T(8,128)(2,1)S(1)}, bf16[256,128]{1,0:T(8,128)(2,1)S(1)}, u32[]{:S(2)}, u32[]{:S(2)}) collective-permute-start(bf16[256,128]{1,0:T(8,128)(2,1)S(1)} %get-tuple-element.36), channel_id=1, source_target_pairs={{0,0},{1,16},{2,32},{3,48},{4,64},{5,80},{6,96},{7,112},{8,65},{9,... | collective-permute-start | bytes 196616 | tf_op jit(solution)/shard_map/ppermute | solution.py:241
  87.0 3.3 %collective-permute-done.4 = bf16[256,128]{1,0:T(8,128)(2,1)S(1)} collective-permute-done((bf16[256,128]{1,0:T(8,128)(2,1)S(1)}, bf16[256,128]{1,0:T(8,128)(2,1)S(1)}, u32[]{:S(2)}, u32[]{:S(2)}) %collective-permute-start.4) | collective-permute-done | bytes 65568 | tf_op jit(solution)/shard_map/ppermute | solution.py:241
  90.3 0.4 all-to-all-done.4.x_ref
  90.7 0.6 collective-permute-start.5
  91.4 0.9 broadcast_in_dim.112
  92.2 4.1 %all-to-all-start.5 = ((bf16[8,256,128]{2,1,0:T(8,128)(2,1)}), bf16[8,256,128]{2,1,0:T(8,128)(2,1)S(1)}, u32[]{:S(2)}, u32[]{:S(2)}) async-start(bf16[8,256,128]{2,1,0:T(8,128)(2,1)} %broadcast_in_dim.112), calls=%async_computation.5 | async-start | bytes 1048576 | tf_op jit(solution)/shard_map/all_to_all | solution.py:238
  96.3 0.0 collective-permute-done.5.y_ref
  96.3 3.4 %copy-done.2 = bf16[1,1,256,128,128]{4,3,2,1,0:T(8,128)(2,1)S(1)} copy-done((bf16[1,1,256,128,128]{4,3,2,1,0:T(8,128)(2,1)S(1)}, bf16[1,1,256,128,128]{4,3,2,1,0:T(8,128)(2,1)}, u32[]{:S(2)}) %copy-start.2) | copy-done | bytes 8388632
  99.7 3.9 %mirror.3 = bf16[8,2,128,128]{3,2,1,0:T(8,128)(2,1)} custom-call(s32[272]{0:T(512)S(1)} %broadcast_add_fusion.tab, s32[2]{0:T(128)S(1)} %pad_add_fusion.place, bf16[8,2,128,128]{3,2,1,0:T(8,128)(2,1)S(1)} %all-to-all-done.4.x_ref, bf16[8,2,128,128]{3,2,1,0:T(8,128)(2,1)S(1)} %collective-permute-done.5.y_ref, bf16[256,128,128]{2,1,0:T(8,128)(2,1)S(1)} %bitcast.8), custom_call_target="tpu_custom_call" | custom-call | flops 1073741824 | bytes 8388608 | tf_op jit(solution)/shard_map/mirror/pallas_call | solution.py:199
  103.6 0.5 all-to-all-done.5.x_ref
  104.1 5.2 %all-to-all-start.6 = ((bf16[8,2,128,128]{3,2,1,0:T(8,128)(2,1)}), bf16[8,2,128,128]{3,2,1,0:T(8,128)(2,1)S(1)}, u32[]{:S(2)}, u32[]{:S(2)}) async-start(bf16[8,2,128,128]{3,2,1,0:T(8,128)(2,1)} %mirror.3), calls=%async_computation.6 | async-start | bytes 1048576 | tf_op jit(solution)/shard_map/all_to_all | solution.py:238
  109.4 3.4 %copy-done.3 = bf16[1,1,256,128,128]{4,3,2,1,0:T(8,128)(2,1)S(1)} copy-done((bf16[1,1,256,128,128]{4,3,2,1,0:T(8,128)(2,1)S(1)}, bf16[1,1,256,128,128]{4,3,2,1,0:T(8,128)(2,1)}, u32[]{:S(2)}) %copy-start.3) | copy-done | bytes 8388632
  112.8 3.2 %direct.3 = (f32[8,256,128]{2,1,0:T(8,128)S(1)}, bf16[8,256,128]{2,1,0:T(8,128)(2,1)S(1)}) custom-call(s32[288]{0:T(512)S(1)} %broadcast_add_fusion.1.tab, s32[2]{0:T(128)S(1)} %pad_add_fusion.place, bf16[8,256,128]{2,1,0:T(8,128)(2,1)S(1)} %all-to-all-done.5.x_ref, bf16[256,128,128]{2,1,0:T(8,128)(2,1)S(1)} %bitcast.9), custom_call_target="tpu_custom_call" | custom-call | flops 1073741824 | bytes 8388608 | tf_op jit(solution)/shard_map/direct/pallas_call | solution.py:199
  115.9 0.0 all-to-all-done.6.got_ref
  116.0 2.3 %collective-permute-start.6 = (bf16[8,256,128]{2,1,0:T(8,128)(2,1)S(1)}, bf16[8,256,128]{2,1,0:T(8,128)(2,1)S(1)}, u32[]{:S(2)}, u32[]{:S(2)}) collective-permute-start(bf16[8,256,128]{2,1,0:T(8,128)(2,1)S(1)} %get-tuple-element.44), channel_id=1, source_target_pairs={{0,1},{1,0},{2,3},{3,2},{4,5},{5,4},{6,7},{7,6},{8,9},{9,8},{10,11... | collective-permute-start | bytes 1572872 | tf_op jit(solution)/shard_map/ppermute | solution.py:267
  118.3 1.5 %collective-permute-done.6.theirs_ref = bf16[8,256,128]{2,1,0:T(8,128)(2,1)S(1)} collective-permute-done((bf16[8,256,128]{2,1,0:T(8,128)(2,1)S(1)}, bf16[8,256,128]{2,1,0:T(8,128)(2,1)S(1)}, u32[]{:S(2)}, u32[]{:S(2)}) %collective-permute-start.6) | collective-permute-done | bytes 524320 | tf_op jit(solution)/shard_map/ppermute | solution.py:267
  119.8 0.9 both.3
  120.7 6.6 %all-to-all-start.7 = ((bf16[8,256,128]{2,1,0:T(8,128)(2,1)}), bf16[8,256,128]{2,1,0:T(8,128)(2,1)S(1)}, u32[]{:S(2)}, u32[]{:S(2)}) async-start(bf16[8,256,128]{2,1,0:T(8,128)(2,1)} %both.3), calls=%async_computation.7 | async-start | bytes 1048576 | tf_op jit(solution)/shard_map/all_to_all | solution.py:238
  127.4 0.1 gathered.3
  127.4 8.4 %collective-permute-start.7 = (bf16[2,128,128]{2,1,0:T(8,128)(2,1)S(1)}, bf16[2,128,128]{2,1,0:T(8,128)(2,1)S(1)}, u32[]{:S(2)}, u32[]{:S(2)}) collective-permute-start(bf16[2,128,128]{2,1,0:T(8,128)(2,1)S(1)} %gathered.3), channel_id=1, source_target_pairs={{0,0},{16,1},{32,2},{48,3},{64,4},{80,5},{96,6},{112,7},{65,8},{81... | collective-permute-start | bytes 196616 | tf_op jit(solution)/shard_map/ppermute | solution.py:271
  135.9 7.0 %collective-permute-done.7.sum_ref = bf16[2,128,128]{2,1,0:T(8,128)(2,1)S(1)} collective-permute-done((bf16[2,128,128]{2,1,0:T(8,128)(2,1)S(1)}, bf16[2,128,128]{2,1,0:T(8,128)(2,1)S(1)}, u32[]{:S(2)}, u32[]{:S(2)}) %collective-permute-start.7) | collective-permute-done | bytes 65568 | tf_op jit(solution)/shard_map/ppermute | solution.py:271
  142.8 0.1 turned.3.back_ref
  142.9 0.0 all-to-all-done.7.own_ref
  142.9 1.3 last.1
  (27 shorter events, 0.1 us)
Async XLA Ops:
  0.0 0.9 copy-start.4
  0.9 0.7 copy-start.6
  3.0 18.6 %all-to-all-start = ((bf16[8,2,128,128]{3,2,1,0:T(8,128)(2,1)}), bf16[8,2,128,128]{3,2,1,0:T(8,128)(2,1)S(1)}, u32[]{:S(2)}, u32[]{:S(2)}) async-start(bf16[8,2,128,128]{3,2,1,0:T(8,128)(2,1)} %get-tuple-element.27), calls=%async_computation | async-start | bytes 1048576 | tf_op jit(solution)/shard_map/all_to_all | solution.py:238
  10.5 11.1 %collective-permute-start = (bf16[256,128]{1,0:T(8,128)(2,1)S(1)}, bf16[256,128]{1,0:T(8,128)(2,1)S(1)}, u32[]{:S(2)}, u32[]{:S(2)}) collective-permute-start(bf16[256,128]{1,0:T(8,128)(2,1)S(1)} %get-tuple-element.26), channel_id=1, source_target_pairs={{0,0},{1,16},{2,32},{3,48},{4,64},{5,80},{6,96},{7,112},{8,65},{9,... | collective-permute-start | bytes 196616 | tf_op jit(solution)/shard_map/ppermute | solution.py:241
  21.6 6.7 %collective-permute-start.1 = (bf16[8,2,128,128]{3,2,1,0:T(8,128)(2,1)S(1)}, bf16[8,2,128,128]{3,2,1,0:T(8,128)(2,1)S(1)}, u32[]{:S(2)}, u32[]{:S(2)}) collective-permute-start(bf16[8,2,128,128]{3,2,1,0:T(8,128)(2,1)S(1)} %all-to-all-done.x_ref), channel_id=1, source_target_pairs={{0,1},{1,0},{2,3},{3,2},{4,5},{5,4},{6,7},{7,6},{8,9},{9,8},{10,11... | collective-permute-start | bytes 1572872 | tf_op jit(solution)/shard_map/ppermute | solution.py:244
  23.9 12.0 %all-to-all-start.1 = ((bf16[8,256,128]{2,1,0:T(8,128)(2,1)}), bf16[8,256,128]{2,1,0:T(8,128)(2,1)S(1)}, u32[]{:S(2)}, u32[]{:S(2)}) async-start(bf16[8,256,128]{2,1,0:T(8,128)(2,1)} %broadcast_in_dim.104), calls=%async_computation.1 | async-start | bytes 1048576 | tf_op jit(solution)/shard_map/all_to_all | solution.py:238
  28.3 3.4 %copy-start = (bf16[1,1,256,128,128]{4,3,2,1,0:T(8,128)(2,1)S(1)}, bf16[1,1,256,128,128]{4,3,2,1,0:T(8,128)(2,1)}, u32[]{:S(2)}) copy-start(bf16[1,1,256,128,128]{4,3,2,1,0:T(8,128)(2,1)} %param.8) | copy-start | bytes 25165828
  35.6 39.0 %copy-start.5 = (f32[256,128]{1,0:T(8,128)S(1)}, f32[256,128]{1,0:T(8,128)}, u32[]{:S(2)}) copy-start(f32[256,128]{1,0:T(8,128)} %vectors_ref.5) | copy-start | bytes 393220
  35.6 39.0 %copy-start.7 = (s32[2]{0:T(128)S(1)}, s32[2]{0:T(128)}, u32[]{:S(2)}) copy-start(s32[2]{0:T(128)} %widths.5) | copy-start | bytes 28
  35.9 12.4 %all-to-all-start.2 = ((bf16[8,2,128,128]{3,2,1,0:T(8,128)(2,1)}), bf16[8,2,128,128]{3,2,1,0:T(8,128)(2,1)S(1)}, u32[]{:S(2)}, u32[]{:S(2)}) async-start(bf16[8,2,128,128]{3,2,1,0:T(8,128)(2,1)} %mirror.2), calls=%async_computation.2 | async-start | bytes 1048576 | tf_op jit(solution)/shard_map/all_to_all | solution.py:238
  41.7 3.4 %copy-start.1 = (bf16[1,1,256,128,128]{4,3,2,1,0:T(8,128)(2,1)S(1)}, bf16[1,1,256,128,128]{4,3,2,1,0:T(8,128)(2,1)}, u32[]{:S(2)}) copy-start(bf16[1,1,256,128,128]{4,3,2,1,0:T(8,128)(2,1)} %param.8) | copy-start | bytes 25165828
  48.3 3.3 %collective-permute-start.2 = (bf16[8,256,128]{2,1,0:T(8,128)(2,1)S(1)}, bf16[8,256,128]{2,1,0:T(8,128)(2,1)S(1)}, u32[]{:S(2)}, u32[]{:S(2)}) collective-permute-start(bf16[8,256,128]{2,1,0:T(8,128)(2,1)S(1)} %get-tuple-element.34), channel_id=1, source_target_pairs={{0,1},{1,0},{2,3},{3,2},{4,5},{5,4},{6,7},{7,6},{8,9},{9,8},{10,11... | collective-permute-start | bytes 1572872 | tf_op jit(solution)/shard_map/ppermute | solution.py:267
  52.5 22.1 %all-to-all-start.3 = ((bf16[8,256,128]{2,1,0:T(8,128)(2,1)}), bf16[8,256,128]{2,1,0:T(8,128)(2,1)S(1)}, u32[]{:S(2)}, u32[]{:S(2)}) async-start(bf16[8,256,128]{2,1,0:T(8,128)(2,1)} %both.2), calls=%async_computation.3 | async-start | bytes 1048576 | tf_op jit(solution)/shard_map/all_to_all | solution.py:238
  58.7 15.8 %collective-permute-start.3 = (bf16[2,128,128]{2,1,0:T(8,128)(2,1)S(1)}, bf16[2,128,128]{2,1,0:T(8,128)(2,1)S(1)}, u32[]{:S(2)}, u32[]{:S(2)}) collective-permute-start(bf16[2,128,128]{2,1,0:T(8,128)(2,1)S(1)} %gathered.2), channel_id=1, source_target_pairs={{0,0},{16,1},{32,2},{48,3},{64,4},{80,5},{96,6},{112,7},{65,8},{81... | collective-permute-start | bytes 196616 | tf_op jit(solution)/shard_map/ppermute | solution.py:271
  76.2 14.6 %all-to-all-start.4 = ((bf16[8,2,128,128]{3,2,1,0:T(8,128)(2,1)}), bf16[8,2,128,128]{3,2,1,0:T(8,128)(2,1)S(1)}, u32[]{:S(2)}, u32[]{:S(2)}) async-start(bf16[8,2,128,128]{3,2,1,0:T(8,128)(2,1)} %get-tuple-element.37), calls=%async_computation.4 | async-start | bytes 1048576 | tf_op jit(solution)/shard_map/all_to_all | solution.py:238
  79.7 10.7 %collective-permute-start.4 = (bf16[256,128]{1,0:T(8,128)(2,1)S(1)}, bf16[256,128]{1,0:T(8,128)(2,1)S(1)}, u32[]{:S(2)}, u32[]{:S(2)}) collective-permute-start(bf16[256,128]{1,0:T(8,128)(2,1)S(1)} %get-tuple-element.36), channel_id=1, source_target_pairs={{0,0},{1,16},{2,32},{3,48},{4,64},{5,80},{6,96},{7,112},{8,65},{9,... | collective-permute-start | bytes 196616 | tf_op jit(solution)/shard_map/ppermute | solution.py:241
  90.7 5.6 %collective-permute-start.5 = (bf16[8,2,128,128]{3,2,1,0:T(8,128)(2,1)S(1)}, bf16[8,2,128,128]{3,2,1,0:T(8,128)(2,1)S(1)}, u32[]{:S(2)}, u32[]{:S(2)}) collective-permute-start(bf16[8,2,128,128]{3,2,1,0:T(8,128)(2,1)S(1)} %all-to-all-done.4.x_ref), channel_id=1, source_target_pairs={{0,1},{1,0},{2,3},{3,2},{4,5},{5,4},{6,7},{7,6},{8,9},{9,8},{10,11... | collective-permute-start | bytes 1572872 | tf_op jit(solution)/shard_map/ppermute | solution.py:244
  92.2 11.9 %all-to-all-start.5 = ((bf16[8,256,128]{2,1,0:T(8,128)(2,1)}), bf16[8,256,128]{2,1,0:T(8,128)(2,1)S(1)}, u32[]{:S(2)}, u32[]{:S(2)}) async-start(bf16[8,256,128]{2,1,0:T(8,128)(2,1)} %broadcast_in_dim.112), calls=%async_computation.5 | async-start | bytes 1048576 | tf_op jit(solution)/shard_map/all_to_all | solution.py:238
  96.3 3.4 %copy-start.2 = (bf16[1,1,256,128,128]{4,3,2,1,0:T(8,128)(2,1)S(1)}, bf16[1,1,256,128,128]{4,3,2,1,0:T(8,128)(2,1)}, u32[]{:S(2)}) copy-start(bf16[1,1,256,128,128]{4,3,2,1,0:T(8,128)(2,1)} %param.8) | copy-start | bytes 25165828
  104.1 11.8 %all-to-all-start.6 = ((bf16[8,2,128,128]{3,2,1,0:T(8,128)(2,1)}), bf16[8,2,128,128]{3,2,1,0:T(8,128)(2,1)S(1)}, u32[]{:S(2)}, u32[]{:S(2)}) async-start(bf16[8,2,128,128]{3,2,1,0:T(8,128)(2,1)} %mirror.3), calls=%async_computation.6 | async-start | bytes 1048576 | tf_op jit(solution)/shard_map/all_to_all | solution.py:238
  109.4 3.4 %copy-start.3 = (bf16[1,1,256,128,128]{4,3,2,1,0:T(8,128)(2,1)S(1)}, bf16[1,1,256,128,128]{4,3,2,1,0:T(8,128)(2,1)}, u32[]{:S(2)}) copy-start(bf16[1,1,256,128,128]{4,3,2,1,0:T(8,128)(2,1)} %param.8) | copy-start | bytes 25165828
  116.0 3.9 %collective-permute-start.6 = (bf16[8,256,128]{2,1,0:T(8,128)(2,1)S(1)}, bf16[8,256,128]{2,1,0:T(8,128)(2,1)S(1)}, u32[]{:S(2)}, u32[]{:S(2)}) collective-permute-start(bf16[8,256,128]{2,1,0:T(8,128)(2,1)S(1)} %get-tuple-element.44), channel_id=1, source_target_pairs={{0,1},{1,0},{2,3},{3,2},{4,5},{5,4},{6,7},{7,6},{8,9},{9,8},{10,11... | collective-permute-start | bytes 1572872 | tf_op jit(solution)/shard_map/ppermute | solution.py:267
  120.7 22.2 %all-to-all-start.7 = ((bf16[8,256,128]{2,1,0:T(8,128)(2,1)}), bf16[8,256,128]{2,1,0:T(8,128)(2,1)S(1)}, u32[]{:S(2)}, u32[]{:S(2)}) async-start(bf16[8,256,128]{2,1,0:T(8,128)(2,1)} %both.3), calls=%async_computation.7 | async-start | bytes 1048576 | tf_op jit(solution)/shard_map/all_to_all | solution.py:238
  127.4 15.4 %collective-permute-start.7 = (bf16[2,128,128]{2,1,0:T(8,128)(2,1)S(1)}, bf16[2,128,128]{2,1,0:T(8,128)(2,1)S(1)}, u32[]{:S(2)}, u32[]{:S(2)}) collective-permute-start(bf16[2,128,128]{2,1,0:T(8,128)(2,1)S(1)} %gathered.3), channel_id=1, source_target_pairs={{0,0},{16,1},{32,2},{48,3},{64,4},{80,5},{96,6},{112,7},{65,8},{81... | collective-permute-start | bytes 196616 | tf_op jit(solution)/shard_map/ppermute | solution.py:271

commit v12 on v11

--- a/solution.py
+++ b/solution.py
@@ -70,9 +70,17 @@
         flip_ref[k] = flipped
 
 
-def first_kernel(widths, vectors_ref, plain_ref, flip_ref):
+def first_kernel(widths_ref, vectors_ref, plain_ref, flip_ref, widths, vectors, sem):
+    copies = [
+        pltpu.make_async_copy(vectors_ref, vectors, sem.at[0]),
+        pltpu.make_async_copy(widths_ref, widths, sem.at[1]),
+    ]
+    for copy in copies:
+        copy.start()
+    for copy in copies:
+        copy.wait()
     shape = (2, ATOM, VECS)
-    first = vectors_ref[...].reshape(shape) * keep_of(widths, shape, 1)
+    first = vectors[...].reshape(shape) * keep_of(widths, shape, 1)
     send_forms(first, plain_ref, flip_ref)
 
 
@@ -273,7 +281,19 @@
         return own, turned
 
     forms = (like(PIECE, BF), like((8, *BLOCKS), BF))
-    plain, flipped = call(first_kernel, forms, (widths,), (vectors,), name="first")
+    plain, flipped = pl.pallas_call(
+        first_kernel,
+        out_shape=forms,
+        in_specs=[pl.BlockSpec(memory_space=pl.ANY)] * 2,
+        out_specs=(VMEM, VMEM),
+        scratch_shapes=[
+            pltpu.SMEM((2,), jnp.int32),
+            pltpu.VMEM(PIECE, F32),
+            pltpu.SemaphoreType.DMA((2,)),
+        ],
+        compiler_params=pltpu.CompilerParams(vmem_limit_bytes=56 * 1024 * 1024),
+        name="first",
+    )(widths, vectors)
     parts = apply_matrix(plain, flipped)
     second, plain, flipped = call(
         second_kernel, (like(PIECE, F32), *forms), (widths,), (*parts, vectors), name="second"

time: 145 us -> 144 us (level)
  local copies, waits for them, and re-layouts: 17.2 us -> 15.7 us
    pallas_call x0 -> x1, Pallas kernels: none -> 1.85 us  [local(): pl.pallas_call(first_kernel, out_shape=forms, in_specs=[pl.BlockSpec(memo...]
    pallas_call x13 -> x12, Pallas kernels: 20.6 us -> 18.8 us  [call(): pl.pallas_call(kernel, out_shape=out_shape, in_specs=[SMEM] * len(scalars...]
    unnamed x16 -> x12, local copies, waits for them, and re-layouts: 15.1 us -> 13.5 us
  transfers between devices with their start and end apart: 16 -> 16, of which waited for: 9 -> 10; matrix products, arithmetic and copies ran while one was open for 3% -> 3% of each run, Pallas kernels for 10% -> 10%
where the time goes in v12:
time: 144 us; the launch traced here: 143 us
  starting transfers between devices  82 us (57%)
  waiting for transfers between devices  22.5 us (16%)
  Pallas kernels  20.6 us (14%)
  local copies, waits for them, and re-layouts  15.7 us (11%)
  other arithmetic  1.55 us (1%)
    all_to_all x8, starting transfers between devices, exchange(): return lax.all_to_all(x, axes, split_axis=0, concat_axis=0, tiled=True)  42.7 us
    pallas_call x12, Pallas kernels, call(): pl.pallas_call(kernel, out_shape=out_shape, in_specs=[SMEM] * len(scalars...  18.8 us
    ppermute x2, starting transfers between devices, apply_matrix(): back = lax.ppermute(gathered, ALL, TO_ROW)  16.8 us
    ppermute x2, starting transfers between devices, apply_matrix(): piece = lax.ppermute(plain, ALL, TO_COL)  16.2 us
    ppermute x2, waiting for transfers between devices, apply_matrix(): back = lax.ppermute(gathered, ALL, TO_ROW)  14.3 us
    unnamed x12, local copies, waits for them, and re-layouts  13.5 us
    ppermute x2, starting transfers between devices, apply_matrix(): theirs = lax.ppermute(other, 'co', SWAP)  4.21 us
    ppermute x2, waiting for transfers between devices, apply_matrix(): piece = lax.ppermute(plain, ALL, TO_COL)  3.5 us
  transfers between devices with their start and end apart: 16, of which 10 were waited for; matrix products, arithmetic and copies ran while one was open for 3% of the time, Pallas kernels for 10%

profile of v12, /device:TPU:25, one launch (start us, length us, event | category | flops | bytes accessed | tf_op | source)
XLA Modules:
  0.0 143.4 jit_solution(5707260418777966657)
XLA Ops:
  0.0 1.8 %first.1 = (bf16[256,128]{1,0:T(8,128)(2,1)}, bf16[8,2,128,128]{3,2,1,0:T(8,128)(2,1)}) custom-call(s32[2]{0:T(128)} %widths.3, f32[256,128]{1,0:T(8,128)} %vectors_ref.5), custom_call_target="tpu_custom_call" | custom-call | tf_op jit(solution)/shard_map/first/pallas_call | solution.py:284
  1.9 7.5 %all-to-all-start = ((bf16[8,2,128,128]{3,2,1,0:T(8,128)(2,1)}), bf16[8,2,128,128]{3,2,1,0:T(8,128)(2,1)S(1)}, u32[]{:S(2)}, u32[]{:S(2)}) async-start(bf16[8,2,128,128]{3,2,1,0:T(8,128)(2,1)} %get-tuple-element.27), calls=%async_computation | async-start | bytes 1048576 | tf_op jit(solution)/shard_map/all_to_all | solution.py:246
  9.4 8.8 %collective-permute-start = (bf16[256,128]{1,0:T(8,128)(2,1)}, bf16[256,128]{1,0:T(8,128)(2,1)S(1)}, u32[]{:S(2)}, u32[]{:S(2)}) collective-permute-start(bf16[256,128]{1,0:T(8,128)(2,1)} %get-tuple-element.26), channel_id=1, source_target_pairs={{0,0},{1,16},{2,32},{3,48},{4,64},{5,80},{6,96},{7,112},{8,65},{9,... | collective-permute-start | bytes 196616 | tf_op jit(solution)/shard_map/ppermute | solution.py:249
  19.0 0.1 add_select_fusion.1
  19.1 0.1 reshape.357
  19.2 0.1 add.295
  19.3 0.7 multiply_add_fusion.1
  20.0 0.3 select_reduce_fusion.1
  20.3 0.2 collective-permute-done
  20.5 0.0 all-to-all-done.x_ref
  20.5 1.4 %collective-permute-start.1 = (bf16[8,2,128,128]{3,2,1,0:T(8,128)(2,1)S(1)}, bf16[8,2,128,128]{3,2,1,0:T(8,128)(2,1)S(1)}, u32[]{:S(2)}, u32[]{:S(2)}) collective-permute-start(bf16[8,2,128,128]{3,2,1,0:T(8,128)(2,1)S(1)} %all-to-all-done.x_ref), channel_id=1, source_target_pairs={{0,1},{1,0},{2,3},{3,2},{4,5},{5,4},{6,7},{7,6},{8,9},{9,8},{10,11... | collective-permute-start | bytes 1572872 | tf_op jit(solution)/shard_map/ppermute | solution.py:252
  21.9 0.9 broadcast_in_dim.104
  22.8 4.2 %all-to-all-start.1 = ((bf16[8,256,128]{2,1,0:T(8,128)(2,1)}), bf16[8,256,128]{2,1,0:T(8,128)(2,1)S(1)}, u32[]{:S(2)}, u32[]{:S(2)}) async-start(bf16[8,256,128]{2,1,0:T(8,128)(2,1)} %broadcast_in_dim.104), calls=%async_computation.1 | async-start | bytes 1048576 | tf_op jit(solution)/shard_map/all_to_all | solution.py:246
  27.0 0.1 pad_add_fusion.place
  27.1 0.1 add_select_fusion
  27.2 0.0 collective-permute-done.1.y_ref
  27.2 0.0 copy-start
  27.2 3.4 %copy-done = bf16[1,1,256,128,128]{4,3,2,1,0:T(8,128)(2,1)S(1)} copy-done((bf16[1,1,256,128,128]{4,3,2,1,0:T(8,128)(2,1)S(1)}, bf16[1,1,256,128,128]{4,3,2,1,0:T(8,128)(2,1)}, u32[]{:S(2)}) %copy-start) | copy-done | bytes 8388632
  30.6 3.8 %mirror.2 = bf16[8,2,128,128]{3,2,1,0:T(8,128)(2,1)} custom-call(s32[272]{0:T(512)S(1)} %broadcast_add_fusion.tab, s32[2]{0:T(128)S(1)} %pad_add_fusion.place, bf16[8,2,128,128]{3,2,1,0:T(8,128)(2,1)S(1)} %all-to-all-done.x_ref, bf16[8,2,128,128]{3,2,1,0:T(8,128)(2,1)S(1)} %collective-permute-done.1.y_ref, bf16[256,128,128]{2,1,0:T(8,128)(2,1)S(1)} %bitcast.6), custom_call_target="tpu_custom_call" | custom-call | flops 1073741824 | bytes 8388608 | tf_op jit(solution)/shard_map/mirror/pallas_call | solution.py:207
  34.4 0.4 all-to-all-done.1.x_ref
  34.8 5.2 %all-to-all-start.2 = ((bf16[8,2,128,128]{3,2,1,0:T(8,128)(2,1)}), bf16[8,2,128,128]{3,2,1,0:T(8,128)(2,1)S(1)}, u32[]{:S(2)}, u32[]{:S(2)}) async-start(bf16[8,2,128,128]{3,2,1,0:T(8,128)(2,1)} %mirror.2), calls=%async_computation.2 | async-start | bytes 1048576 | tf_op jit(solution)/shard_map/all_to_all | solution.py:246
  40.1 0.1 reshape.356
  40.2 0.1 add.260
  40.3 0.1 add.261
  40.4 0.3 select_reduce_fusion
  40.6 0.0 copy-start.1
  40.7 3.4 %copy-done.1 = bf16[1,1,256,128,128]{4,3,2,1,0:T(8,128)(2,1)S(1)} copy-done((bf16[1,1,256,128,128]{4,3,2,1,0:T(8,128)(2,1)S(1)}, bf16[1,1,256,128,128]{4,3,2,1,0:T(8,128)(2,1)}, u32[]{:S(2)}) %copy-start.1) | copy-done | bytes 8388632
  44.0 3.1 %direct.2 = (f32[8,256,128]{2,1,0:T(8,128)S(1)}, bf16[8,256,128]{2,1,0:T(8,128)(2,1)S(1)}) custom-call(s32[288]{0:T(512)S(1)} %broadcast_add_fusion.1.tab, s32[2]{0:T(128)S(1)} %pad_add_fusion.place, bf16[8,256,128]{2,1,0:T(8,128)(2,1)S(1)} %all-to-all-done.1.x_ref, bf16[256,128,128]{2,1,0:T(8,128)(2,1)S(1)} %bitcast.7), custom_call_target="tpu_custom_call" | custom-call | flops 1073741824 | bytes 8388608 | tf_op jit(solution)/shard_map/direct/pallas_call | solution.py:207
  47.1 0.0 all-to-all-done.2.got_ref
  47.1 1.9 %collective-permute-start.2 = (bf16[8,256,128]{2,1,0:T(8,128)(2,1)S(1)}, bf16[8,256,128]{2,1,0:T(8,128)(2,1)S(1)}, u32[]{:S(2)}, u32[]{:S(2)}) collective-permute-start(bf16[8,256,128]{2,1,0:T(8,128)(2,1)S(1)} %get-tuple-element.34), channel_id=1, source_target_pairs={{0,1},{1,0},{2,3},{3,2},{4,5},{5,4},{6,7},{7,6},{8,9},{9,8},{10,11... | collective-permute-start | bytes 1572872 | tf_op jit(solution)/shard_map/ppermute | solution.py:275
  49.0 1.5 %collective-permute-done.2.theirs_ref = bf16[8,256,128]{2,1,0:T(8,128)(2,1)S(1)} collective-permute-done((bf16[8,256,128]{2,1,0:T(8,128)(2,1)S(1)}, bf16[8,256,128]{2,1,0:T(8,128)(2,1)S(1)}, u32[]{:S(2)}, u32[]{:S(2)}) %collective-permute-start.2) | collective-permute-done | bytes 524320 | tf_op jit(solution)/shard_map/ppermute | solution.py:275
  50.5 0.9 both.2
  51.4 6.3 %all-to-all-start.3 = ((bf16[8,256,128]{2,1,0:T(8,128)(2,1)}), bf16[8,256,128]{2,1,0:T(8,128)(2,1)S(1)}, u32[]{:S(2)}, u32[]{:S(2)}) async-start(bf16[8,256,128]{2,1,0:T(8,128)(2,1)} %both.2), calls=%async_computation.3 | async-start | bytes 1048576 | tf_op jit(solution)/shard_map/all_to_all | solution.py:246
  57.7 0.1 gathered.2
  57.8 8.4 %collective-permute-start.3 = (bf16[2,128,128]{2,1,0:T(8,128)(2,1)S(1)}, bf16[2,128,128]{2,1,0:T(8,128)(2,1)S(1)}, u32[]{:S(2)}, u32[]{:S(2)}) collective-permute-start(bf16[2,128,128]{2,1,0:T(8,128)(2,1)S(1)} %gathered.2), channel_id=1, source_target_pairs={{0,0},{16,1},{32,2},{48,3},{64,4},{80,5},{96,6},{112,7},{65,8},{81... | collective-permute-start | bytes 196616 | tf_op jit(solution)/shard_map/ppermute | solution.py:279
  66.2 7.4 %collective-permute-done.3.sum_ref = bf16[2,128,128]{2,1,0:T(8,128)(2,1)S(1)} collective-permute-done((bf16[2,128,128]{2,1,0:T(8,128)(2,1)S(1)}, bf16[2,128,128]{2,1,0:T(8,128)(2,1)S(1)}, u32[]{:S(2)}, u32[]{:S(2)}) %collective-permute-start.3) | collective-permute-done | bytes 65568 | tf_op jit(solution)/shard_map/ppermute | solution.py:279
  73.6 0.1 turned.2.back_ref
  73.7 0.0 all-to-all-done.3.own_ref
  73.7 1.5 %second.1 = (f32[256,128]{1,0:T(8,128)S(1)}, bf16[256,128]{1,0:T(8,128)(2,1)S(1)}, bf16[8,2,128,128]{3,2,1,0:T(8,128)(2,1)}) custom-call(s32[2]{0:T(128)S(1)} %copy-done.5, bf16[8,256,128]{2,1,0:T(8,128)(2,1)S(1)} %all-to-all-done.3.own_ref, f32[256,128]{1,0:T(8,128)S(1)} %turned.2.back_ref, f32[256,128]{1,0:T(8,128)S(1)} %copy-done.4), custom_call_target="tpu_custom_call" | custom-call | bytes 1048576 | tf_op jit(solution)/shard_map/second/pallas_call | solution.py:207
  75.2 3.5 %all-to-all-start.4 = ((bf16[8,2,128,128]{3,2,1,0:T(8,128)(2,1)}), bf16[8,2,128,128]{3,2,1,0:T(8,128)(2,1)S(1)}, u32[]{:S(2)}, u32[]{:S(2)}) async-start(bf16[8,2,128,128]{3,2,1,0:T(8,128)(2,1)} %get-tuple-element.37), calls=%async_computation.4 | async-start | bytes 1048576 | tf_op jit(solution)/shard_map/all_to_all | solution.py:246
  78.7 7.4 %collective-permute-start.4 = (bf16[256,128]{1,0:T(8,128)(2,1)S(1)}, bf16[256,128]{1,0:T(8,128)(2,1)S(1)}, u32[]{:S(2)}, u32[]{:S(2)}) collective-permute-start(bf16[256,128]{1,0:T(8,128)(2,1)S(1)} %get-tuple-element.36), channel_id=1, source_target_pairs={{0,0},{1,16},{2,32},{3,48},{4,64},{5,80},{6,96},{7,112},{8,65},{9,... | collective-permute-start | bytes 196616 | tf_op jit(solution)/shard_map/ppermute | solution.py:249
  86.1 3.3 %collective-permute-done.4 = bf16[256,128]{1,0:T(8,128)(2,1)S(1)} collective-permute-done((bf16[256,128]{1,0:T(8,128)(2,1)S(1)}, bf16[256,128]{1,0:T(8,128)(2,1)S(1)}, u32[]{:S(2)}, u32[]{:S(2)}) %collective-permute-start.4) | collective-permute-done | bytes 65568 | tf_op jit(solution)/shard_map/ppermute | solution.py:249
  89.4 0.4 all-to-all-done.4.x_ref
  89.8 0.6 collective-permute-start.5
  90.5 0.9 broadcast_in_dim.112
  91.3 4.1 %all-to-all-start.5 = ((bf16[8,256,128]{2,1,0:T(8,128)(2,1)}), bf16[8,256,128]{2,1,0:T(8,128)(2,1)S(1)}, u32[]{:S(2)}, u32[]{:S(2)}) async-start(bf16[8,256,128]{2,1,0:T(8,128)(2,1)} %broadcast_in_dim.112), calls=%async_computation.5 | async-start | bytes 1048576 | tf_op jit(solution)/shard_map/all_to_all | solution.py:246
  95.4 0.0 collective-permute-done.5.y_ref
  95.4 3.4 %copy-done.2 = bf16[1,1,256,128,128]{4,3,2,1,0:T(8,128)(2,1)S(1)} copy-done((bf16[1,1,256,128,128]{4,3,2,1,0:T(8,128)(2,1)S(1)}, bf16[1,1,256,128,128]{4,3,2,1,0:T(8,128)(2,1)}, u32[]{:S(2)}) %copy-start.2) | copy-done | bytes 8388632
  98.8 3.8 %mirror.3 = bf16[8,2,128,128]{3,2,1,0:T(8,128)(2,1)} custom-call(s32[272]{0:T(512)S(1)} %broadcast_add_fusion.tab, s32[2]{0:T(128)S(1)} %pad_add_fusion.place, bf16[8,2,128,128]{3,2,1,0:T(8,128)(2,1)S(1)} %all-to-all-done.4.x_ref, bf16[8,2,128,128]{3,2,1,0:T(8,128)(2,1)S(1)} %collective-permute-done.5.y_ref, bf16[256,128,128]{2,1,0:T(8,128)(2,1)S(1)} %bitcast.8), custom_call_target="tpu_custom_call" | custom-call | flops 1073741824 | bytes 8388608 | tf_op jit(solution)/shard_map/mirror/pallas_call | solution.py:207
  102.6 0.6 all-to-all-done.5.x_ref
  103.2 5.2 %all-to-all-start.6 = ((bf16[8,2,128,128]{3,2,1,0:T(8,128)(2,1)}), bf16[8,2,128,128]{3,2,1,0:T(8,128)(2,1)S(1)}, u32[]{:S(2)}, u32[]{:S(2)}) async-start(bf16[8,2,128,128]{3,2,1,0:T(8,128)(2,1)} %mirror.3), calls=%async_computation.6 | async-start | bytes 1048576 | tf_op jit(solution)/shard_map/all_to_all | solution.py:246
  108.5 3.4 %copy-done.3 = bf16[1,1,256,128,128]{4,3,2,1,0:T(8,128)(2,1)S(1)} copy-done((bf16[1,1,256,128,128]{4,3,2,1,0:T(8,128)(2,1)S(1)}, bf16[1,1,256,128,128]{4,3,2,1,0:T(8,128)(2,1)}, u32[]{:S(2)}) %copy-start.3) | copy-done | bytes 8388632
  111.8 3.1 %direct.3 = (f32[8,256,128]{2,1,0:T(8,128)S(1)}, bf16[8,256,128]{2,1,0:T(8,128)(2,1)S(1)}) custom-call(s32[288]{0:T(512)S(1)} %broadcast_add_fusion.1.tab, s32[2]{0:T(128)S(1)} %pad_add_fusion.place, bf16[8,256,128]{2,1,0:T(8,128)(2,1)S(1)} %all-to-all-done.5.x_ref, bf16[256,128,128]{2,1,0:T(8,128)(2,1)S(1)} %bitcast.9), custom_call_target="tpu_custom_call" | custom-call | flops 1073741824 | bytes 8388608 | tf_op jit(solution)/shard_map/direct/pallas_call | solution.py:207
  114.9 0.1 all-to-all-done.6.got_ref
  115.1 2.3 %collective-permute-start.6 = (bf16[8,256,128]{2,1,0:T(8,128)(2,1)S(1)}, bf16[8,256,128]{2,1,0:T(8,128)(2,1)S(1)}, u32[]{:S(2)}, u32[]{:S(2)}) collective-permute-start(bf16[8,256,128]{2,1,0:T(8,128)(2,1)S(1)} %get-tuple-element.44), channel_id=1, source_target_pairs={{0,1},{1,0},{2,3},{3,2},{4,5},{5,4},{6,7},{7,6},{8,9},{9,8},{10,11... | collective-permute-start | bytes 1572872 | tf_op jit(solution)/shard_map/ppermute | solution.py:275
  117.4 1.5 %collective-permute-done.6.theirs_ref = bf16[8,256,128]{2,1,0:T(8,128)(2,1)S(1)} collective-permute-done((bf16[8,256,128]{2,1,0:T(8,128)(2,1)S(1)}, bf16[8,256,128]{2,1,0:T(8,128)(2,1)S(1)}, u32[]{:S(2)}, u32[]{:S(2)}) %collective-permute-start.6) | collective-permute-done | bytes 524320 | tf_op jit(solution)/shard_map/ppermute | solution.py:275
  118.9 0.9 both.3
  119.8 6.6 %all-to-all-start.7 = ((bf16[8,256,128]{2,1,0:T(8,128)(2,1)}), bf16[8,256,128]{2,1,0:T(8,128)(2,1)S(1)}, u32[]{:S(2)}, u32[]{:S(2)}) async-start(bf16[8,256,128]{2,1,0:T(8,128)(2,1)} %both.3), calls=%async_computation.7 | async-start | bytes 1048576 | tf_op jit(solution)/shard_map/all_to_all | solution.py:246
  126.5 0.1 gathered.3
  126.5 8.4 %collective-permute-start.7 = (bf16[2,128,128]{2,1,0:T(8,128)(2,1)S(1)}, bf16[2,128,128]{2,1,0:T(8,128)(2,1)S(1)}, u32[]{:S(2)}, u32[]{:S(2)}) collective-permute-start(bf16[2,128,128]{2,1,0:T(8,128)(2,1)S(1)} %gathered.3), channel_id=1, source_target_pairs={{0,0},{16,1},{32,2},{48,3},{64,4},{80,5},{96,6},{112,7},{65,8},{81... | collective-permute-start | bytes 196616 | tf_op jit(solution)/shard_map/ppermute | solution.py:279
  135.0 7.0 %collective-permute-done.7.sum_ref = bf16[2,128,128]{2,1,0:T(8,128)(2,1)S(1)} collective-permute-done((bf16[2,128,128]{2,1,0:T(8,128)(2,1)S(1)}, bf16[2,128,128]{2,1,0:T(8,128)(2,1)S(1)}, u32[]{:S(2)}, u32[]{:S(2)}) %collective-permute-start.7) | collective-permute-done | bytes 65568 | tf_op jit(solution)/shard_map/ppermute | solution.py:279
  141.9 0.1 turned.3.back_ref
  142.0 0.0 all-to-all-done.7.own_ref
  142.0 1.3 last.1
  (23 shorter events, 0.1 us)
Async XLA Ops:
  1.9 18.6 %all-to-all-start = ((bf16[8,2,128,128]{3,2,1,0:T(8,128)(2,1)}), bf16[8,2,128,128]{3,2,1,0:T(8,128)(2,1)S(1)}, u32[]{:S(2)}, u32[]{:S(2)}) async-start(bf16[8,2,128,128]{3,2,1,0:T(8,128)(2,1)} %get-tuple-element.27), calls=%async_computation | async-start | bytes 1048576 | tf_op jit(solution)/shard_map/all_to_all | solution.py:246
  9.4 11.1 %collective-permute-start = (bf16[256,128]{1,0:T(8,128)(2,1)}, bf16[256,128]{1,0:T(8,128)(2,1)S(1)}, u32[]{:S(2)}, u32[]{:S(2)}) collective-permute-start(bf16[256,128]{1,0:T(8,128)(2,1)} %get-tuple-element.26), channel_id=1, source_target_pairs={{0,0},{1,16},{2,32},{3,48},{4,64},{5,80},{6,96},{7,112},{8,65},{9,... | collective-permute-start | bytes 196616 | tf_op jit(solution)/shard_map/ppermute | solution.py:249
  20.5 6.7 %collective-permute-start.1 = (bf16[8,2,128,128]{3,2,1,0:T(8,128)(2,1)S(1)}, bf16[8,2,128,128]{3,2,1,0:T(8,128)(2,1)S(1)}, u32[]{:S(2)}, u32[]{:S(2)}) collective-permute-start(bf16[8,2,128,128]{3,2,1,0:T(8,128)(2,1)S(1)} %all-to-all-done.x_ref), channel_id=1, source_target_pairs={{0,1},{1,0},{2,3},{3,2},{4,5},{5,4},{6,7},{7,6},{8,9},{9,8},{10,11... | collective-permute-start | bytes 1572872 | tf_op jit(solution)/shard_map/ppermute | solution.py:252
  22.8 12.1 %all-to-all-start.1 = ((bf16[8,256,128]{2,1,0:T(8,128)(2,1)}), bf16[8,256,128]{2,1,0:T(8,128)(2,1)S(1)}, u32[]{:S(2)}, u32[]{:S(2)}) async-start(bf16[8,256,128]{2,1,0:T(8,128)(2,1)} %broadcast_in_dim.104), calls=%async_computation.1 | async-start | bytes 1048576 | tf_op jit(solution)/shard_map/all_to_all | solution.py:246
  27.2 3.4 %copy-start = (bf16[1,1,256,128,128]{4,3,2,1,0:T(8,128)(2,1)S(1)}, bf16[1,1,256,128,128]{4,3,2,1,0:T(8,128)(2,1)}, u32[]{:S(2)}) copy-start(bf16[1,1,256,128,128]{4,3,2,1,0:T(8,128)(2,1)} %param.8) | copy-start | bytes 25165828
  34.4 39.3 %copy-start.4 = (f32[256,128]{1,0:T(8,128)S(1)}, f32[256,128]{1,0:T(8,128)}, u32[]{:S(2)}) copy-start(f32[256,128]{1,0:T(8,128)} %vectors_ref.5) | copy-start | bytes 393220
  34.4 39.3 %copy-start.5 = (s32[2]{0:T(128)S(1)}, s32[2]{0:T(128)}, u32[]{:S(2)}) copy-start(s32[2]{0:T(128)} %widths.3) | copy-start | bytes 28
  34.8 12.3 %all-to-all-start.2 = ((bf16[8,2,128,128]{3,2,1,0:T(8,128)(2,1)}), bf16[8,2,128,128]{3,2,1,0:T(8,128)(2,1)S(1)}, u32[]{:S(2)}, u32[]{:S(2)}) async-start(bf16[8,2,128,128]{3,2,1,0:T(8,128)(2,1)} %mirror.2), calls=%async_computation.2 | async-start | bytes 1048576 | tf_op jit(solution)/shard_map/all_to_all | solution.py:246
  40.6 3.4 %copy-start.1 = (bf16[1,1,256,128,128]{4,3,2,1,0:T(8,128)(2,1)S(1)}, bf16[1,1,256,128,128]{4,3,2,1,0:T(8,128)(2,1)}, u32[]{:S(2)}) copy-start(bf16[1,1,256,128,128]{4,3,2,1,0:T(8,128)(2,1)} %param.8) | copy-start | bytes 25165828
  47.1 3.4 %collective-permute-start.2 = (bf16[8,256,128]{2,1,0:T(8,128)(2,1)S(1)}, bf16[8,256,128]{2,1,0:T(8,128)(2,1)S(1)}, u32[]{:S(2)}, u32[]{:S(2)}) collective-permute-start(bf16[8,256,128]{2,1,0:T(8,128)(2,1)S(1)} %get-tuple-element.34), channel_id=1, source_target_pairs={{0,1},{1,0},{2,3},{3,2},{4,5},{5,4},{6,7},{7,6},{8,9},{9,8},{10,11... | collective-permute-start | bytes 1572872 | tf_op jit(solution)/shard_map/ppermute | solution.py:275
  51.4 22.3 %all-to-all-start.3 = ((bf16[8,256,128]{2,1,0:T(8,128)(2,1)}), bf16[8,256,128]{2,1,0:T(8,128)(2,1)S(1)}, u32[]{:S(2)}, u32[]{:S(2)}) async-start(bf16[8,256,128]{2,1,0:T(8,128)(2,1)} %both.2), calls=%async_computation.3 | async-start | bytes 1048576 | tf_op jit(solution)/shard_map/all_to_all | solution.py:246
  57.8 15.8 %collective-permute-start.3 = (bf16[2,128,128]{2,1,0:T(8,128)(2,1)S(1)}, bf16[2,128,128]{2,1,0:T(8,128)(2,1)S(1)}, u32[]{:S(2)}, u32[]{:S(2)}) collective-permute-start(bf16[2,128,128]{2,1,0:T(8,128)(2,1)S(1)} %gathered.2), channel_id=1, source_target_pairs={{0,0},{16,1},{32,2},{48,3},{64,4},{80,5},{96,6},{112,7},{65,8},{81... | collective-permute-start | bytes 196616 | tf_op jit(solution)/shard_map/ppermute | solution.py:279
  75.2 14.6 %all-to-all-start.4 = ((bf16[8,2,128,128]{3,2,1,0:T(8,128)(2,1)}), bf16[8,2,128,128]{3,2,1,0:T(8,128)(2,1)S(1)}, u32[]{:S(2)}, u32[]{:S(2)}) async-start(bf16[8,2,128,128]{3,2,1,0:T(8,128)(2,1)} %get-tuple-element.37), calls=%async_computation.4 | async-start | bytes 1048576 | tf_op jit(solution)/shard_map/all_to_all | solution.py:246
  78.7 10.7 %collective-permute-start.4 = (bf16[256,128]{1,0:T(8,128)(2,1)S(1)}, bf16[256,128]{1,0:T(8,128)(2,1)S(1)}, u32[]{:S(2)}, u32[]{:S(2)}) collective-permute-start(bf16[256,128]{1,0:T(8,128)(2,1)S(1)} %get-tuple-element.36), channel_id=1, source_target_pairs={{0,0},{1,16},{2,32},{3,48},{4,64},{5,80},{6,96},{7,112},{8,65},{9,... | collective-permute-start | bytes 196616 | tf_op jit(solution)/shard_map/ppermute | solution.py:249
  89.8 5.6 %collective-permute-start.5 = (bf16[8,2,128,128]{3,2,1,0:T(8,128)(2,1)S(1)}, bf16[8,2,128,128]{3,2,1,0:T(8,128)(2,1)S(1)}, u32[]{:S(2)}, u32[]{:S(2)}) collective-permute-start(bf16[8,2,128,128]{3,2,1,0:T(8,128)(2,1)S(1)} %all-to-all-done.4.x_ref), channel_id=1, source_target_pairs={{0,1},{1,0},{2,3},{3,2},{4,5},{5,4},{6,7},{7,6},{8,9},{9,8},{10,11... | collective-permute-start | bytes 1572872 | tf_op jit(solution)/shard_map/ppermute | solution.py:252
  91.3 11.9 %all-to-all-start.5 = ((bf16[8,256,128]{2,1,0:T(8,128)(2,1)}), bf16[8,256,128]{2,1,0:T(8,128)(2,1)S(1)}, u32[]{:S(2)}, u32[]{:S(2)}) async-start(bf16[8,256,128]{2,1,0:T(8,128)(2,1)} %broadcast_in_dim.112), calls=%async_computation.5 | async-start | bytes 1048576 | tf_op jit(solution)/shard_map/all_to_all | solution.py:246
  95.4 3.4 %copy-start.2 = (bf16[1,1,256,128,128]{4,3,2,1,0:T(8,128)(2,1)S(1)}, bf16[1,1,256,128,128]{4,3,2,1,0:T(8,128)(2,1)}, u32[]{:S(2)}) copy-start(bf16[1,1,256,128,128]{4,3,2,1,0:T(8,128)(2,1)} %param.8) | copy-start | bytes 25165828
  103.2 11.8 %all-to-all-start.6 = ((bf16[8,2,128,128]{3,2,1,0:T(8,128)(2,1)}), bf16[8,2,128,128]{3,2,1,0:T(8,128)(2,1)S(1)}, u32[]{:S(2)}, u32[]{:S(2)}) async-start(bf16[8,2,128,128]{3,2,1,0:T(8,128)(2,1)} %mirror.3), calls=%async_computation.6 | async-start | bytes 1048576 | tf_op jit(solution)/shard_map/all_to_all | solution.py:246
  108.5 3.4 %copy-start.3 = (bf16[1,1,256,128,128]{4,3,2,1,0:T(8,128)(2,1)S(1)}, bf16[1,1,256,128,128]{4,3,2,1,0:T(8,128)(2,1)}, u32[]{:S(2)}) copy-start(bf16[1,1,256,128,128]{4,3,2,1,0:T(8,128)(2,1)} %param.8) | copy-start | bytes 25165828
  115.1 3.9 %collective-permute-start.6 = (bf16[8,256,128]{2,1,0:T(8,128)(2,1)S(1)}, bf16[8,256,128]{2,1,0:T(8,128)(2,1)S(1)}, u32[]{:S(2)}, u32[]{:S(2)}) collective-permute-start(bf16[8,256,128]{2,1,0:T(8,128)(2,1)S(1)} %get-tuple-element.44), channel_id=1, source_target_pairs={{0,1},{1,0},{2,3},{3,2},{4,5},{5,4},{6,7},{7,6},{8,9},{9,8},{10,11... | collective-permute-start | bytes 1572872 | tf_op jit(solution)/shard_map/ppermute | solution.py:275
  119.8 22.2 %all-to-all-start.7 = ((bf16[8,256,128]{2,1,0:T(8,128)(2,1)}), bf16[8,256,128]{2,1,0:T(8,128)(2,1)S(1)}, u32[]{:S(2)}, u32[]{:S(2)}) async-start(bf16[8,256,128]{2,1,0:T(8,128)(2,1)} %both.3), calls=%async_computation.7 | async-start | bytes 1048576 | tf_op jit(solution)/shard_map/all_to_all | solution.py:246
  126.5 15.4 %collective-permute-start.7 = (bf16[2,128,128]{2,1,0:T(8,128)(2,1)S(1)}, bf16[2,128,128]{2,1,0:T(8,128)(2,1)S(1)}, u32[]{:S(2)}, u32[]{:S(2)}) collective-permute-start(bf16[2,128,128]{2,1,0:T(8,128)(2,1)S(1)} %gathered.3), channel_id=1, source_target_pairs={{0,0},{16,1},{32,2},{48,3},{64,4},{80,5},{96,6},{112,7},{65,8},{81... | collective-permute-start | bytes 196616 | tf_op jit(solution)/shard_map/ppermute | solution.py:279

commit v13 on v12

--- a/solution.py
+++ b/solution.py
@@ -70,7 +70,9 @@
         flip_ref[k] = flipped
 
 
-def first_kernel(widths_ref, vectors_ref, plain_ref, flip_ref, widths, vectors, sem):
+def first_kernel(
+    widths_ref, vectors_ref, plain_ref, flip_ref, keep_ref, widths, vectors, sem
+):
     copies = [
         pltpu.make_async_copy(vectors_ref, vectors, sem.at[0]),
         pltpu.make_async_copy(widths_ref, widths, sem.at[1]),
@@ -80,30 +82,32 @@
     for copy in copies:
         copy.wait()
     shape = (2, ATOM, VECS)
-    first = vectors[...].reshape(shape) * keep_of(widths, shape, 1)
+    keep = keep_of(widths, shape, 1)
+    keep_ref[...] = keep
+    first = vectors[...].reshape(shape) * keep
     send_forms(first, plain_ref, flip_ref)
 
 
-def applied(widths, own_ref, back_ref):
+def applied(keep_ref, own_ref, back_ref):
     shape = (2, ATOM, VECS)
     total = back_ref[...]
     for k in range(8):
         total = total + own_ref[k].astype(F32)
-    return total.reshape(shape) * keep_of(widths, shape, 1)
-
-
-def second_kernel(widths, own_ref, back_ref, vectors_ref, out_ref, plain_ref, flip_ref):
+    return total.reshape(shape) * keep_ref[...]
+
+
+def second_kernel(keep_ref, own_ref, back_ref, vectors_ref, out_ref, plain_ref, flip_ref):
     shape = (2, ATOM, VECS)
-    first = vectors_ref[...].reshape(shape) * keep_of(widths, shape, 1)
-    second = applied(widths, own_ref, back_ref) - CENTER * first
+    first = vectors_ref[...].reshape(shape) * keep_ref[...]
+    second = applied(keep_ref, own_ref, back_ref) - CENTER * first
     out_ref[...] = second.reshape(2 * ATOM, VECS)
     send_forms(second, plain_ref, flip_ref)
 
 
-def last_kernel(widths, own_ref, back_ref, vectors_ref, second_ref, out_ref):
+def last_kernel(keep_ref, own_ref, back_ref, vectors_ref, second_ref, out_ref):
     shape = (2, ATOM, VECS)
-    first = vectors_ref[...].reshape(shape) * keep_of(widths, shape, 1)
-    third = applied(widths, own_ref, back_ref)
+    first = vectors_ref[...].reshape(shape) * keep_ref[...]
+    third = applied(keep_ref, own_ref, back_ref)
     out = 2.0 * (third - CENTER * second_ref[...].reshape(shape)) - first
     out_ref[...] = out.reshape(2 * ATOM, VECS)
 
@@ -281,11 +285,11 @@
         return own, turned
 
     forms = (like(PIECE, BF), like((8, *BLOCKS), BF))
-    plain, flipped = pl.pallas_call(
+    plain, flipped, keep = pl.pallas_call(
         first_kernel,
-        out_shape=forms,
+        out_shape=(*forms, like((2, ATOM, VECS), F32)),
         in_specs=[pl.BlockSpec(memory_space=pl.ANY)] * 2,
-        out_specs=(VMEM, VMEM),
+        out_specs=(VMEM,) * 3,
         scratch_shapes=[
             pltpu.SMEM((2,), jnp.int32),
             pltpu.VMEM(PIECE, F32),
@@ -296,11 +300,11 @@
     )(widths, vectors)
     parts = apply_matrix(plain, flipped)
     second, plain, flipped = call(
-        second_kernel, (like(PIECE, F32), *forms), (widths,), (*parts, vectors), name="second"
+        second_kernel, (like(PIECE, F32), *forms), (), (keep, *parts, vectors), name="second"
     )
     parts = apply_matrix(plain, flipped)
     return call(
-        last_kernel, like(PIECE, F32), (widths,), (*parts, vectors, second), name="last"
+        last_kernel, like(PIECE, F32), (), (keep, *parts, vectors, second), name="last"
     )
 
 def solution(mesh):

time: 144 us -> 143 us (level)
  no operation moved by 1% of the time
where the time goes in v13:
time: 143 us; the launch traced here: 142 us
  starting transfers between devices  82 us (57%)
  waiting for transfers between devices  22.5 us (16%)
  Pallas kernels  19.6 us (14%)
  local copies, waits for them, and re-layouts  15.7 us (11%)
  other arithmetic  1.55 us (1%)
    all_to_all x8, starting transfers between devices, exchange(): return lax.all_to_all(x, axes, split_axis=0, concat_axis=0, tiled=True)  42.7 us
    pallas_call x12, Pallas kernels, call(): pl.pallas_call(kernel, out_shape=out_shape, in_specs=[SMEM] * len(scalars...  17.7 us
    ppermute x2, starting transfers between devices, apply_matrix(): back = lax.ppermute(gathered, ALL, TO_ROW)  16.8 us
    ppermute x2, starting transfers between devices, apply_matrix(): piece = lax.ppermute(plain, ALL, TO_COL)  16.2 us
    ppermute x2, waiting for transfers between devices, apply_matrix(): back = lax.ppermute(gathered, ALL, TO_ROW)  14.3 us
    unnamed x12, local copies, waits for them, and re-layouts  13.5 us
    ppermute x2, starting transfers between devices, apply_matrix(): theirs = lax.ppermute(other, 'co', SWAP)  4.2 us
    ppermute x2, waiting for transfers between devices, apply_matrix(): piece = lax.ppermute(plain, ALL, TO_COL)  3.5 us
  transfers between devices with their start and end apart: 16, of which 10 were waited for; matrix products, arithmetic and copies ran while one was open for 3% of the time, Pallas kernels for 10%

profile of v13, /device:TPU:25, one launch (start us, length us, event | category | flops | bytes accessed | tf_op | source)
XLA Modules:
  0.0 142.3 jit_solution(10896226782849477199)
XLA Ops:
  0.0 1.9 %first.1 = (bf16[256,128]{1,0:T(8,128)(2,1)}, bf16[8,2,128,128]{3,2,1,0:T(8,128)(2,1)}, f32[2,128,128]{2,1,0:T(8,128)}) custom-call(s32[2]{0:T(128)} %widths_ref.1, f32[256,128]{1,0:T(8,128)} %vectors_ref.5), custom_call_target="tpu_custom_call" | custom-call | tf_op jit(solution)/shard_map/first/pallas_call | solution.py:288
  1.9 7.5 %all-to-all-start = ((bf16[8,2,128,128]{3,2,1,0:T(8,128)(2,1)}), bf16[8,2,128,128]{3,2,1,0:T(8,128)(2,1)S(1)}, u32[]{:S(2)}, u32[]{:S(2)}) async-start(bf16[8,2,128,128]{3,2,1,0:T(8,128)(2,1)} %get-tuple-element.29), calls=%async_computation | async-start | bytes 1048576 | tf_op jit(solution)/shard_map/all_to_all | solution.py:250
  9.4 8.8 %collective-permute-start = (bf16[256,128]{1,0:T(8,128)(2,1)}, bf16[256,128]{1,0:T(8,128)(2,1)S(1)}, u32[]{:S(2)}, u32[]{:S(2)}) collective-permute-start(bf16[256,128]{1,0:T(8,128)(2,1)} %get-tuple-element.28), channel_id=1, source_target_pairs={{0,0},{1,16},{2,32},{3,48},{4,64},{5,80},{6,96},{7,112},{8,65},{9,... | collective-permute-start | bytes 196616 | tf_op jit(solution)/shard_map/ppermute | solution.py:253
  19.0 0.1 add_select_fusion.1
  19.1 0.1 reshape.357
  19.2 0.1 add.295
  19.3 0.7 multiply_add_fusion.1
  20.0 0.3 select_reduce_fusion.1
  20.3 0.2 collective-permute-done
  20.5 0.0 all-to-all-done.x_ref
  20.5 1.4 %collective-permute-start.1 = (bf16[8,2,128,128]{3,2,1,0:T(8,128)(2,1)S(1)}, bf16[8,2,128,128]{3,2,1,0:T(8,128)(2,1)S(1)}, u32[]{:S(2)}, u32[]{:S(2)}) collective-permute-start(bf16[8,2,128,128]{3,2,1,0:T(8,128)(2,1)S(1)} %all-to-all-done.x_ref), channel_id=1, source_target_pairs={{0,1},{1,0},{2,3},{3,2},{4,5},{5,4},{6,7},{7,6},{8,9},{9,8},{10,11... | collective-permute-start | bytes 1572872 | tf_op jit(solution)/shard_map/ppermute | solution.py:256
  21.9 0.9 broadcast_in_dim.104
  22.8 4.2 %all-to-all-start.1 = ((bf16[8,256,128]{2,1,0:T(8,128)(2,1)}), bf16[8,256,128]{2,1,0:T(8,128)(2,1)S(1)}, u32[]{:S(2)}, u32[]{:S(2)}) async-start(bf16[8,256,128]{2,1,0:T(8,128)(2,1)} %broadcast_in_dim.104), calls=%async_computation.1 | async-start | bytes 1048576 | tf_op jit(solution)/shard_map/all_to_all | solution.py:250
  27.0 0.1 pad_add_fusion.place
  27.1 0.1 add_select_fusion
  27.2 0.0 collective-permute-done.1.y_ref
  27.2 0.0 copy-start
  27.2 3.4 %copy-done = bf16[1,1,256,128,128]{4,3,2,1,0:T(8,128)(2,1)S(1)} copy-done((bf16[1,1,256,128,128]{4,3,2,1,0:T(8,128)(2,1)S(1)}, bf16[1,1,256,128,128]{4,3,2,1,0:T(8,128)(2,1)}, u32[]{:S(2)}) %copy-start) | copy-done | bytes 8388632
  30.6 3.8 %mirror.2 = bf16[8,2,128,128]{3,2,1,0:T(8,128)(2,1)} custom-call(s32[272]{0:T(512)S(1)} %broadcast_add_fusion.tab, s32[2]{0:T(128)S(1)} %pad_add_fusion.place, bf16[8,2,128,128]{3,2,1,0:T(8,128)(2,1)S(1)} %all-to-all-done.x_ref, bf16[8,2,128,128]{3,2,1,0:T(8,128)(2,1)S(1)} %collective-permute-done.1.y_ref, bf16[256,128,128]{2,1,0:T(8,128)(2,1)S(1)} %bitcast.6), custom_call_target="tpu_custom_call" | custom-call | flops 1073741824 | bytes 8388608 | tf_op jit(solution)/shard_map/mirror/pallas_call | solution.py:211
  34.5 0.4 all-to-all-done.1.x_ref
  34.9 5.2 %all-to-all-start.2 = ((bf16[8,2,128,128]{3,2,1,0:T(8,128)(2,1)}), bf16[8,2,128,128]{3,2,1,0:T(8,128)(2,1)S(1)}, u32[]{:S(2)}, u32[]{:S(2)}) async-start(bf16[8,2,128,128]{3,2,1,0:T(8,128)(2,1)} %mirror.2), calls=%async_computation.2 | async-start | bytes 1048576 | tf_op jit(solution)/shard_map/all_to_all | solution.py:250
  40.1 0.1 reshape.356
  40.2 0.1 add.260
  40.3 0.1 add.261
  40.4 0.3 select_reduce_fusion
  40.7 0.0 copy-start.1
  40.7 3.4 %copy-done.1 = bf16[1,1,256,128,128]{4,3,2,1,0:T(8,128)(2,1)S(1)} copy-done((bf16[1,1,256,128,128]{4,3,2,1,0:T(8,128)(2,1)S(1)}, bf16[1,1,256,128,128]{4,3,2,1,0:T(8,128)(2,1)}, u32[]{:S(2)}) %copy-start.1) | copy-done | bytes 8388632
  44.1 3.1 %direct.2 = (f32[8,256,128]{2,1,0:T(8,128)S(1)}, bf16[8,256,128]{2,1,0:T(8,128)(2,1)S(1)}) custom-call(s32[288]{0:T(512)S(1)} %broadcast_add_fusion.1.tab, s32[2]{0:T(128)S(1)} %pad_add_fusion.place, bf16[8,256,128]{2,1,0:T(8,128)(2,1)S(1)} %all-to-all-done.1.x_ref, bf16[256,128,128]{2,1,0:T(8,128)(2,1)S(1)} %bitcast.7), custom_call_target="tpu_custom_call" | custom-call | flops 1073741824 | bytes 8388608 | tf_op jit(solution)/shard_map/direct/pallas_call | solution.py:211
  47.2 0.0 all-to-all-done.2.got_ref
  47.2 1.9 %collective-permute-start.2 = (bf16[8,256,128]{2,1,0:T(8,128)(2,1)S(1)}, bf16[8,256,128]{2,1,0:T(8,128)(2,1)S(1)}, u32[]{:S(2)}, u32[]{:S(2)}) collective-permute-start(bf16[8,256,128]{2,1,0:T(8,128)(2,1)S(1)} %get-tuple-element.36), channel_id=1, source_target_pairs={{0,1},{1,0},{2,3},{3,2},{4,5},{5,4},{6,7},{7,6},{8,9},{9,8},{10,11... | collective-permute-start | bytes 1572872 | tf_op jit(solution)/shard_map/ppermute | solution.py:279
  49.0 1.5 %collective-permute-done.2.theirs_ref = bf16[8,256,128]{2,1,0:T(8,128)(2,1)S(1)} collective-permute-done((bf16[8,256,128]{2,1,0:T(8,128)(2,1)S(1)}, bf16[8,256,128]{2,1,0:T(8,128)(2,1)S(1)}, u32[]{:S(2)}, u32[]{:S(2)}) %collective-permute-start.2) | collective-permute-done | bytes 524320 | tf_op jit(solution)/shard_map/ppermute | solution.py:279
  50.6 0.9 both.2
  51.5 6.3 %all-to-all-start.3 = ((bf16[8,256,128]{2,1,0:T(8,128)(2,1)}), bf16[8,256,128]{2,1,0:T(8,128)(2,1)S(1)}, u32[]{:S(2)}, u32[]{:S(2)}) async-start(bf16[8,256,128]{2,1,0:T(8,128)(2,1)} %both.2), calls=%async_computation.3 | async-start | bytes 1048576 | tf_op jit(solution)/shard_map/all_to_all | solution.py:250
  57.7 0.1 gathered.2
  57.8 8.4 %collective-permute-start.3 = (bf16[2,128,128]{2,1,0:T(8,128)(2,1)S(1)}, bf16[2,128,128]{2,1,0:T(8,128)(2,1)S(1)}, u32[]{:S(2)}, u32[]{:S(2)}) collective-permute-start(bf16[2,128,128]{2,1,0:T(8,128)(2,1)S(1)} %gathered.2), channel_id=1, source_target_pairs={{0,0},{16,1},{32,2},{48,3},{64,4},{80,5},{96,6},{112,7},{65,8},{81... | collective-permute-start | bytes 196616 | tf_op jit(solution)/shard_map/ppermute | solution.py:283
  66.3 7.4 %collective-permute-done.3.sum_ref = bf16[2,128,128]{2,1,0:T(8,128)(2,1)S(1)} collective-permute-done((bf16[2,128,128]{2,1,0:T(8,128)(2,1)S(1)}, bf16[2,128,128]{2,1,0:T(8,128)(2,1)S(1)}, u32[]{:S(2)}, u32[]{:S(2)}) %collective-permute-start.3) | collective-permute-done | bytes 65568 | tf_op jit(solution)/shard_map/ppermute | solution.py:283
  73.6 0.1 turned.2.back_ref
  73.7 0.0 all-to-all-done.3.own_ref
  73.7 1.0 second.1
  74.7 3.5 %all-to-all-start.4 = ((bf16[8,2,128,128]{3,2,1,0:T(8,128)(2,1)}), bf16[8,2,128,128]{3,2,1,0:T(8,128)(2,1)S(1)}, u32[]{:S(2)}, u32[]{:S(2)}) async-start(bf16[8,2,128,128]{3,2,1,0:T(8,128)(2,1)} %get-tuple-element.39), calls=%async_computation.4 | async-start | bytes 1048576 | tf_op jit(solution)/shard_map/all_to_all | solution.py:250
  78.2 7.4 %collective-permute-start.4 = (bf16[256,128]{1,0:T(8,128)(2,1)S(1)}, bf16[256,128]{1,0:T(8,128)(2,1)S(1)}, u32[]{:S(2)}, u32[]{:S(2)}) collective-permute-start(bf16[256,128]{1,0:T(8,128)(2,1)S(1)} %get-tuple-element.38), channel_id=1, source_target_pairs={{0,0},{1,16},{2,32},{3,48},{4,64},{5,80},{6,96},{7,112},{8,65},{9,... | collective-permute-start | bytes 196616 | tf_op jit(solution)/shard_map/ppermute | solution.py:253
  85.6 3.3 %collective-permute-done.4 = bf16[256,128]{1,0:T(8,128)(2,1)S(1)} collective-permute-done((bf16[256,128]{1,0:T(8,128)(2,1)S(1)}, bf16[256,128]{1,0:T(8,128)(2,1)S(1)}, u32[]{:S(2)}, u32[]{:S(2)}) %collective-permute-start.4) | collective-permute-done | bytes 65568 | tf_op jit(solution)/shard_map/ppermute | solution.py:253
  88.9 0.4 all-to-all-done.4.x_ref
  89.3 0.6 collective-permute-start.5
  89.9 0.9 broadcast_in_dim.112
  90.8 4.1 %all-to-all-start.5 = ((bf16[8,256,128]{2,1,0:T(8,128)(2,1)}), bf16[8,256,128]{2,1,0:T(8,128)(2,1)S(1)}, u32[]{:S(2)}, u32[]{:S(2)}) async-start(bf16[8,256,128]{2,1,0:T(8,128)(2,1)} %broadcast_in_dim.112), calls=%async_computation.5 | async-start | bytes 1048576 | tf_op jit(solution)/shard_map/all_to_all | solution.py:250
  94.9 0.0 collective-permute-done.5.y_ref
  94.9 3.4 %copy-done.2 = bf16[1,1,256,128,128]{4,3,2,1,0:T(8,128)(2,1)S(1)} copy-done((bf16[1,1,256,128,128]{4,3,2,1,0:T(8,128)(2,1)S(1)}, bf16[1,1,256,128,128]{4,3,2,1,0:T(8,128)(2,1)}, u32[]{:S(2)}) %copy-start.2) | copy-done | bytes 8388632
  98.3 3.8 %mirror.3 = bf16[8,2,128,128]{3,2,1,0:T(8,128)(2,1)} custom-call(s32[272]{0:T(512)S(1)} %broadcast_add_fusion.tab, s32[2]{0:T(128)S(1)} %pad_add_fusion.place, bf16[8,2,128,128]{3,2,1,0:T(8,128)(2,1)S(1)} %all-to-all-done.4.x_ref, bf16[8,2,128,128]{3,2,1,0:T(8,128)(2,1)S(1)} %collective-permute-done.5.y_ref, bf16[256,128,128]{2,1,0:T(8,128)(2,1)S(1)} %bitcast.8), custom_call_target="tpu_custom_call" | custom-call | flops 1073741824 | bytes 8388608 | tf_op jit(solution)/shard_map/mirror/pallas_call | solution.py:211
  102.1 0.6 all-to-all-done.5.x_ref
  102.7 5.2 %all-to-all-start.6 = ((bf16[8,2,128,128]{3,2,1,0:T(8,128)(2,1)}), bf16[8,2,128,128]{3,2,1,0:T(8,128)(2,1)S(1)}, u32[]{:S(2)}, u32[]{:S(2)}) async-start(bf16[8,2,128,128]{3,2,1,0:T(8,128)(2,1)} %mirror.3), calls=%async_computation.6 | async-start | bytes 1048576 | tf_op jit(solution)/shard_map/all_to_all | solution.py:250
  108.0 3.4 %copy-done.3 = bf16[1,1,256,128,128]{4,3,2,1,0:T(8,128)(2,1)S(1)} copy-done((bf16[1,1,256,128,128]{4,3,2,1,0:T(8,128)(2,1)S(1)}, bf16[1,1,256,128,128]{4,3,2,1,0:T(8,128)(2,1)}, u32[]{:S(2)}) %copy-start.3) | copy-done | bytes 8388632
  111.3 3.1 %direct.3 = (f32[8,256,128]{2,1,0:T(8,128)S(1)}, bf16[8,256,128]{2,1,0:T(8,128)(2,1)S(1)}) custom-call(s32[288]{0:T(512)S(1)} %broadcast_add_fusion.1.tab, s32[2]{0:T(128)S(1)} %pad_add_fusion.place, bf16[8,256,128]{2,1,0:T(8,128)(2,1)S(1)} %all-to-all-done.5.x_ref, bf16[256,128,128]{2,1,0:T(8,128)(2,1)S(1)} %bitcast.9), custom_call_target="tpu_custom_call" | custom-call | flops 1073741824 | bytes 8388608 | tf_op jit(solution)/shard_map/direct/pallas_call | solution.py:211
  114.4 0.1 all-to-all-done.6.got_ref
  114.6 2.3 %collective-permute-start.6 = (bf16[8,256,128]{2,1,0:T(8,128)(2,1)S(1)}, bf16[8,256,128]{2,1,0:T(8,128)(2,1)S(1)}, u32[]{:S(2)}, u32[]{:S(2)}) collective-permute-start(bf16[8,256,128]{2,1,0:T(8,128)(2,1)S(1)} %get-tuple-element.46), channel_id=1, source_target_pairs={{0,1},{1,0},{2,3},{3,2},{4,5},{5,4},{6,7},{7,6},{8,9},{9,8},{10,11... | collective-permute-start | bytes 1572872 | tf_op jit(solution)/shard_map/ppermute | solution.py:279
  116.9 1.5 %collective-permute-done.6.theirs_ref = bf16[8,256,128]{2,1,0:T(8,128)(2,1)S(1)} collective-permute-done((bf16[8,256,128]{2,1,0:T(8,128)(2,1)S(1)}, bf16[8,256,128]{2,1,0:T(8,128)(2,1)S(1)}, u32[]{:S(2)}, u32[]{:S(2)}) %collective-permute-start.6) | collective-permute-done | bytes 524320 | tf_op jit(solution)/shard_map/ppermute | solution.py:279
  118.4 0.9 both.3
  119.3 6.6 %all-to-all-start.7 = ((bf16[8,256,128]{2,1,0:T(8,128)(2,1)}), bf16[8,256,128]{2,1,0:T(8,128)(2,1)S(1)}, u32[]{:S(2)}, u32[]{:S(2)}) async-start(bf16[8,256,128]{2,1,0:T(8,128)(2,1)} %both.3), calls=%async_computation.7 | async-start | bytes 1048576 | tf_op jit(solution)/shard_map/all_to_all | solution.py:250
  125.9 0.1 gathered.3
  126.0 8.4 %collective-permute-start.7 = (bf16[2,128,128]{2,1,0:T(8,128)(2,1)S(1)}, bf16[2,128,128]{2,1,0:T(8,128)(2,1)S(1)}, u32[]{:S(2)}, u32[]{:S(2)}) collective-permute-start(bf16[2,128,128]{2,1,0:T(8,128)(2,1)S(1)} %gathered.3), channel_id=1, source_target_pairs={{0,0},{16,1},{32,2},{48,3},{64,4},{80,5},{96,6},{112,7},{65,8},{81... | collective-permute-start | bytes 196616 | tf_op jit(solution)/shard_map/ppermute | solution.py:283
  134.5 7.0 %collective-permute-done.7.sum_ref = bf16[2,128,128]{2,1,0:T(8,128)(2,1)S(1)} collective-permute-done((bf16[2,128,128]{2,1,0:T(8,128)(2,1)S(1)}, bf16[2,128,128]{2,1,0:T(8,128)(2,1)S(1)}, u32[]{:S(2)}, u32[]{:S(2)}) %collective-permute-start.7) | collective-permute-done | bytes 65568 | tf_op jit(solution)/shard_map/ppermute | solution.py:283
  141.4 0.1 turned.3.back_ref
  141.5 0.0 all-to-all-done.7.own_ref
  141.5 0.8 last.1
  (23 shorter events, 0.1 us)
Async XLA Ops:
  1.9 18.6 %all-to-all-start = ((bf16[8,2,128,128]{3,2,1,0:T(8,128)(2,1)}), bf16[8,2,128,128]{3,2,1,0:T(8,128)(2,1)S(1)}, u32[]{:S(2)}, u32[]{:S(2)}) async-start(bf16[8,2,128,128]{3,2,1,0:T(8,128)(2,1)} %get-tuple-element.29), calls=%async_computation | async-start | bytes 1048576 | tf_op jit(solution)/shard_map/all_to_all | solution.py:250
  9.4 11.1 %collective-permute-start = (bf16[256,128]{1,0:T(8,128)(2,1)}, bf16[256,128]{1,0:T(8,128)(2,1)S(1)}, u32[]{:S(2)}, u32[]{:S(2)}) collective-permute-start(bf16[256,128]{1,0:T(8,128)(2,1)} %get-tuple-element.28), channel_id=1, source_target_pairs={{0,0},{1,16},{2,32},{3,48},{4,64},{5,80},{6,96},{7,112},{8,65},{9,... | collective-permute-start | bytes 196616 | tf_op jit(solution)/shard_map/ppermute | solution.py:253
  20.5 6.7 %collective-permute-start.1 = (bf16[8,2,128,128]{3,2,1,0:T(8,128)(2,1)S(1)}, bf16[8,2,128,128]{3,2,1,0:T(8,128)(2,1)S(1)}, u32[]{:S(2)}, u32[]{:S(2)}) collective-permute-start(bf16[8,2,128,128]{3,2,1,0:T(8,128)(2,1)S(1)} %all-to-all-done.x_ref), channel_id=1, source_target_pairs={{0,1},{1,0},{2,3},{3,2},{4,5},{5,4},{6,7},{7,6},{8,9},{9,8},{10,11... | collective-permute-start | bytes 1572872 | tf_op jit(solution)/shard_map/ppermute | solution.py:256
  22.8 12.1 %all-to-all-start.1 = ((bf16[8,256,128]{2,1,0:T(8,128)(2,1)}), bf16[8,256,128]{2,1,0:T(8,128)(2,1)S(1)}, u32[]{:S(2)}, u32[]{:S(2)}) async-start(bf16[8,256,128]{2,1,0:T(8,128)(2,1)} %broadcast_in_dim.104), calls=%async_computation.1 | async-start | bytes 1048576 | tf_op jit(solution)/shard_map/all_to_all | solution.py:250
  27.2 3.4 %copy-start = (bf16[1,1,256,128,128]{4,3,2,1,0:T(8,128)(2,1)S(1)}, bf16[1,1,256,128,128]{4,3,2,1,0:T(8,128)(2,1)}, u32[]{:S(2)}) copy-start(bf16[1,1,256,128,128]{4,3,2,1,0:T(8,128)(2,1)} %param.8) | copy-start | bytes 25165828
  34.5 39.3 %copy-start.4 = (f32[256,128]{1,0:T(8,128)S(1)}, f32[256,128]{1,0:T(8,128)}, u32[]{:S(2)}) copy-start(f32[256,128]{1,0:T(8,128)} %vectors_ref.5) | copy-start | bytes 393220
  34.5 39.3 %copy-start.5 = (f32[2,128,128]{2,1,0:T(8,128)S(1)}, f32[2,128,128]{2,1,0:T(8,128)}, u32[]{:S(2)}) copy-start(f32[2,128,128]{2,1,0:T(8,128)} %get-tuple-element.27.keep_ref) | copy-start | bytes 393220
  34.9 12.3 %all-to-all-start.2 = ((bf16[8,2,128,128]{3,2,1,0:T(8,128)(2,1)}), bf16[8,2,128,128]{3,2,1,0:T(8,128)(2,1)S(1)}, u32[]{:S(2)}, u32[]{:S(2)}) async-start(bf16[8,2,128,128]{3,2,1,0:T(8,128)(2,1)} %mirror.2), calls=%async_computation.2 | async-start | bytes 1048576 | tf_op jit(solution)/shard_map/all_to_all | solution.py:250
  40.7 3.4 %copy-start.1 = (bf16[1,1,256,128,128]{4,3,2,1,0:T(8,128)(2,1)S(1)}, bf16[1,1,256,128,128]{4,3,2,1,0:T(8,128)(2,1)}, u32[]{:S(2)}) copy-start(bf16[1,1,256,128,128]{4,3,2,1,0:T(8,128)(2,1)} %param.8) | copy-start | bytes 25165828
  47.2 3.4 %collective-permute-start.2 = (bf16[8,256,128]{2,1,0:T(8,128)(2,1)S(1)}, bf16[8,256,128]{2,1,0:T(8,128)(2,1)S(1)}, u32[]{:S(2)}, u32[]{:S(2)}) collective-permute-start(bf16[8,256,128]{2,1,0:T(8,128)(2,1)S(1)} %get-tuple-element.36), channel_id=1, source_target_pairs={{0,1},{1,0},{2,3},{3,2},{4,5},{5,4},{6,7},{7,6},{8,9},{9,8},{10,11... | collective-permute-start | bytes 1572872 | tf_op jit(solution)/shard_map/ppermute | solution.py:279
  51.5 22.3 %all-to-all-start.3 = ((bf16[8,256,128]{2,1,0:T(8,128)(2,1)}), bf16[8,256,128]{2,1,0:T(8,128)(2,1)S(1)}, u32[]{:S(2)}, u32[]{:S(2)}) async-start(bf16[8,256,128]{2,1,0:T(8,128)(2,1)} %both.2), calls=%async_computation.3 | async-start | bytes 1048576 | tf_op jit(solution)/shard_map/all_to_all | solution.py:250
  57.8 15.8 %collective-permute-start.3 = (bf16[2,128,128]{2,1,0:T(8,128)(2,1)S(1)}, bf16[2,128,128]{2,1,0:T(8,128)(2,1)S(1)}, u32[]{:S(2)}, u32[]{:S(2)}) collective-permute-start(bf16[2,128,128]{2,1,0:T(8,128)(2,1)S(1)} %gathered.2), channel_id=1, source_target_pairs={{0,0},{16,1},{32,2},{48,3},{64,4},{80,5},{96,6},{112,7},{65,8},{81... | collective-permute-start | bytes 196616 | tf_op jit(solution)/shard_map/ppermute | solution.py:283
  74.7 14.6 %all-to-all-start.4 = ((bf16[8,2,128,128]{3,2,1,0:T(8,128)(2,1)}), bf16[8,2,128,128]{3,2,1,0:T(8,128)(2,1)S(1)}, u32[]{:S(2)}, u32[]{:S(2)}) async-start(bf16[8,2,128,128]{3,2,1,0:T(8,128)(2,1)} %get-tuple-element.39), calls=%async_computation.4 | async-start | bytes 1048576 | tf_op jit(solution)/shard_map/all_to_all | solution.py:250
  78.2 10.7 %collective-permute-start.4 = (bf16[256,128]{1,0:T(8,128)(2,1)S(1)}, bf16[256,128]{1,0:T(8,128)(2,1)S(1)}, u32[]{:S(2)}, u32[]{:S(2)}) collective-permute-start(bf16[256,128]{1,0:T(8,128)(2,1)S(1)} %get-tuple-element.38), channel_id=1, source_target_pairs={{0,0},{1,16},{2,32},{3,48},{4,64},{5,80},{6,96},{7,112},{8,65},{9,... | collective-permute-start | bytes 196616 | tf_op jit(solution)/shard_map/ppermute | solution.py:253
  89.3 5.6 %collective-permute-start.5 = (bf16[8,2,128,128]{3,2,1,0:T(8,128)(2,1)S(1)}, bf16[8,2,128,128]{3,2,1,0:T(8,128)(2,1)S(1)}, u32[]{:S(2)}, u32[]{:S(2)}) collective-permute-start(bf16[8,2,128,128]{3,2,1,0:T(8,128)(2,1)S(1)} %all-to-all-done.4.x_ref), channel_id=1, source_target_pairs={{0,1},{1,0},{2,3},{3,2},{4,5},{5,4},{6,7},{7,6},{8,9},{9,8},{10,11... | collective-permute-start | bytes 1572872 | tf_op jit(solution)/shard_map/ppermute | solution.py:256
  90.8 11.9 %all-to-all-start.5 = ((bf16[8,256,128]{2,1,0:T(8,128)(2,1)}), bf16[8,256,128]{2,1,0:T(8,128)(2,1)S(1)}, u32[]{:S(2)}, u32[]{:S(2)}) async-start(bf16[8,256,128]{2,1,0:T(8,128)(2,1)} %broadcast_in_dim.112), calls=%async_computation.5 | async-start | bytes 1048576 | tf_op jit(solution)/shard_map/all_to_all | solution.py:250
  94.9 3.4 %copy-start.2 = (bf16[1,1,256,128,128]{4,3,2,1,0:T(8,128)(2,1)S(1)}, bf16[1,1,256,128,128]{4,3,2,1,0:T(8,128)(2,1)}, u32[]{:S(2)}) copy-start(bf16[1,1,256,128,128]{4,3,2,1,0:T(8,128)(2,1)} %param.8) | copy-start | bytes 25165828
  102.7 11.8 %all-to-all-start.6 = ((bf16[8,2,128,128]{3,2,1,0:T(8,128)(2,1)}), bf16[8,2,128,128]{3,2,1,0:T(8,128)(2,1)S(1)}, u32[]{:S(2)}, u32[]{:S(2)}) async-start(bf16[8,2,128,128]{3,2,1,0:T(8,128)(2,1)} %mirror.3), calls=%async_computation.6 | async-start | bytes 1048576 | tf_op jit(solution)/shard_map/all_to_all | solution.py:250
  108.0 3.4 %copy-start.3 = (bf16[1,1,256,128,128]{4,3,2,1,0:T(8,128)(2,1)S(1)}, bf16[1,1,256,128,128]{4,3,2,1,0:T(8,128)(2,1)}, u32[]{:S(2)}) copy-start(bf16[1,1,256,128,128]{4,3,2,1,0:T(8,128)(2,1)} %param.8) | copy-start | bytes 25165828
  114.6 3.9 %collective-permute-start.6 = (bf16[8,256,128]{2,1,0:T(8,128)(2,1)S(1)}, bf16[8,256,128]{2,1,0:T(8,128)(2,1)S(1)}, u32[]{:S(2)}, u32[]{:S(2)}) collective-permute-start(bf16[8,256,128]{2,1,0:T(8,128)(2,1)S(1)} %get-tuple-element.46), channel_id=1, source_target_pairs={{0,1},{1,0},{2,3},{3,2},{4,5},{5,4},{6,7},{7,6},{8,9},{9,8},{10,11... | collective-permute-start | bytes 1572872 | tf_op jit(solution)/shard_map/ppermute | solution.py:279
  119.3 22.2 %all-to-all-start.7 = ((bf16[8,256,128]{2,1,0:T(8,128)(2,1)}), bf16[8,256,128]{2,1,0:T(8,128)(2,1)S(1)}, u32[]{:S(2)}, u32[]{:S(2)}) async-start(bf16[8,256,128]{2,1,0:T(8,128)(2,1)} %both.3), calls=%async_computation.7 | async-start | bytes 1048576 | tf_op jit(solution)/shard_map/all_to_all | solution.py:250
  126.0 15.4 %collective-permute-start.7 = (bf16[2,128,128]{2,1,0:T(8,128)(2,1)S(1)}, bf16[2,128,128]{2,1,0:T(8,128)(2,1)S(1)}, u32[]{:S(2)}, u32[]{:S(2)}) collective-permute-start(bf16[2,128,128]{2,1,0:T(8,128)(2,1)S(1)} %gathered.3), channel_id=1, source_target_pairs={{0,0},{16,1},{32,2},{48,3},{64,4},{80,5},{96,6},{112,7},{65,8},{81... | collective-permute-start | bytes 196616 | tf_op jit(solution)/shard_map/ppermute | solution.py:283

commit v14 on v13

--- a/solution.py
+++ b/solution.py
@@ -222,7 +222,7 @@
 
 def shift_of(column):
     r = column // 2
-    return (r // 2 - r % 4 + 2 * (column % 2)) % 4
+    return (r // 2 + 2 * (column % 2)) % 4
 
 
 def owners(r, c):

time: 143 us -> 141 us (0.986)
  waiting for transfers between devices: 22.5 us -> 19.4 us
    ppermute x2, waiting for transfers between devices: 14.3 us -> 12.4 us  [apply_matrix(): back = lax.ppermute(gathered, ALL, TO_ROW)]
  transfers between devices with their start and end apart: 16 -> 16, of which waited for: 10 -> 8; matrix products, arithmetic and copies ran while one was open for 3% -> 3% of each run, Pallas kernels for 10% -> 10%
where the time goes in v14:
time: 141 us; the launch traced here: 140 us
  starting transfers between devices  83.2 us (59%)
  Pallas kernels  19.6 us (14%)
  waiting for transfers between devices  19.4 us (14%)
  local copies, waits for them, and re-layouts  15.7 us (11%)
  other arithmetic  1.55 us (1%)
    all_to_all x8, starting transfers between devices, exchange(): return lax.all_to_all(x, axes, split_axis=0, concat_axis=0, tiled=True)  43.2 us
    pallas_call x12, Pallas kernels, call(): pl.pallas_call(kernel, out_shape=out_shape, in_specs=[SMEM] * len(scalars...  17.7 us
    ppermute x2, starting transfers between devices, apply_matrix(): back = lax.ppermute(gathered, ALL, TO_ROW)  16.8 us
    ppermute x2, starting transfers between devices, apply_matrix(): piece = lax.ppermute(plain, ALL, TO_COL)  16.7 us
    unnamed x12, local copies, waits for them, and re-layouts  13.5 us
    ppermute x2, waiting for transfers between devices, apply_matrix(): back = lax.ppermute(gathered, ALL, TO_ROW)  12.4 us
    ppermute x2, starting transfers between devices, apply_matrix(): theirs = lax.ppermute(other, 'co', SWAP)  4.34 us
    ppermute x2, waiting for transfers between devices, apply_matrix(): theirs = lax.ppermute(other, 'co', SWAP)  3.07 us
  transfers between devices with their start and end apart: 16, of which 8 were waited for; matrix products, arithmetic and copies ran while one was open for 3% of the time, Pallas kernels for 10%

profile of v14, /device:TPU:25, one launch (start us, length us, event | category | flops | bytes accessed | tf_op | source)
XLA Modules:
  0.0 140.4 jit_solution(550618487868696932)
XLA Ops:
  0.0 1.9 %first.1 = (bf16[256,128]{1,0:T(8,128)(2,1)}, bf16[8,2,128,128]{3,2,1,0:T(8,128)(2,1)}, f32[2,128,128]{2,1,0:T(8,128)}) custom-call(s32[2]{0:T(128)} %widths_ref.1, f32[256,128]{1,0:T(8,128)} %vectors_ref.5), custom_call_target="tpu_custom_call" | custom-call | tf_op jit(solution)/shard_map/first/pallas_call | solution.py:288
  1.9 7.5 %all-to-all-start = ((bf16[8,2,128,128]{3,2,1,0:T(8,128)(2,1)}), bf16[8,2,128,128]{3,2,1,0:T(8,128)(2,1)S(1)}, u32[]{:S(2)}, u32[]{:S(2)}) async-start(bf16[8,2,128,128]{3,2,1,0:T(8,128)(2,1)} %get-tuple-element.29), calls=%async_computation | async-start | bytes 1048576 | tf_op jit(solution)/shard_map/all_to_all | solution.py:250
  9.4 8.1 %collective-permute-start = (bf16[256,128]{1,0:T(8,128)(2,1)}, bf16[256,128]{1,0:T(8,128)(2,1)S(1)}, u32[]{:S(2)}, u32[]{:S(2)}) collective-permute-start(bf16[256,128]{1,0:T(8,128)(2,1)} %get-tuple-element.28), channel_id=1, source_target_pairs={{0,0},{1,16},{2,32},{3,48},{4,64},{5,80},{6,96},{7,112},{8,65},{9,... | collective-permute-start | bytes 196616 | tf_op jit(solution)/shard_map/ppermute | solution.py:253
  18.4 0.1 add_select_fusion.1
  18.4 0.1 reshape.357
  18.5 0.1 add.291
  18.6 0.7 multiply_add_fusion.1
  19.3 0.3 select_reduce_fusion.1
  19.6 0.9 collective-permute-done
  20.5 0.0 all-to-all-done.x_ref
  20.5 1.4 %collective-permute-start.1 = (bf16[8,2,128,128]{3,2,1,0:T(8,128)(2,1)S(1)}, bf16[8,2,128,128]{3,2,1,0:T(8,128)(2,1)S(1)}, u32[]{:S(2)}, u32[]{:S(2)}) collective-permute-start(bf16[8,2,128,128]{3,2,1,0:T(8,128)(2,1)S(1)} %all-to-all-done.x_ref), channel_id=1, source_target_pairs={{0,1},{1,0},{2,3},{3,2},{4,5},{5,4},{6,7},{7,6},{8,9},{9,8},{10,11... | collective-permute-start | bytes 1572872 | tf_op jit(solution)/shard_map/ppermute | solution.py:256
  21.9 0.9 broadcast_in_dim.104
  22.8 4.2 %all-to-all-start.1 = ((bf16[8,256,128]{2,1,0:T(8,128)(2,1)}), bf16[8,256,128]{2,1,0:T(8,128)(2,1)S(1)}, u32[]{:S(2)}, u32[]{:S(2)}) async-start(bf16[8,256,128]{2,1,0:T(8,128)(2,1)} %broadcast_in_dim.104), calls=%async_computation.1 | async-start | bytes 1048576 | tf_op jit(solution)/shard_map/all_to_all | solution.py:250
  27.0 0.1 pad_add_fusion.place
  27.1 0.1 add_select_fusion
  27.2 0.0 collective-permute-done.1.y_ref
  27.2 0.0 copy-start
  27.2 3.4 %copy-done = bf16[1,1,256,128,128]{4,3,2,1,0:T(8,128)(2,1)S(1)} copy-done((bf16[1,1,256,128,128]{4,3,2,1,0:T(8,128)(2,1)S(1)}, bf16[1,1,256,128,128]{4,3,2,1,0:T(8,128)(2,1)}, u32[]{:S(2)}) %copy-start) | copy-done | bytes 8388632
  30.6 3.8 %mirror.2 = bf16[8,2,128,128]{3,2,1,0:T(8,128)(2,1)} custom-call(s32[272]{0:T(512)S(1)} %broadcast_add_fusion.tab, s32[2]{0:T(128)S(1)} %pad_add_fusion.place, bf16[8,2,128,128]{3,2,1,0:T(8,128)(2,1)S(1)} %all-to-all-done.x_ref, bf16[8,2,128,128]{3,2,1,0:T(8,128)(2,1)S(1)} %collective-permute-done.1.y_ref, bf16[256,128,128]{2,1,0:T(8,128)(2,1)S(1)} %bitcast.6), custom_call_target="tpu_custom_call" | custom-call | flops 1073741824 | bytes 8388608 | tf_op jit(solution)/shard_map/mirror/pallas_call | solution.py:211
  34.5 0.4 all-to-all-done.1.x_ref
  34.9 5.2 %all-to-all-start.2 = ((bf16[8,2,128,128]{3,2,1,0:T(8,128)(2,1)}), bf16[8,2,128,128]{3,2,1,0:T(8,128)(2,1)S(1)}, u32[]{:S(2)}, u32[]{:S(2)}) async-start(bf16[8,2,128,128]{3,2,1,0:T(8,128)(2,1)} %mirror.2), calls=%async_computation.2 | async-start | bytes 1048576 | tf_op jit(solution)/shard_map/all_to_all | solution.py:250
  40.1 0.1 reshape.356
  40.2 0.1 add.257
  40.3 0.1 add.258
  40.4 0.3 select_reduce_fusion
  40.7 0.0 copy-start.1
  40.7 3.4 %copy-done.1 = bf16[1,1,256,128,128]{4,3,2,1,0:T(8,128)(2,1)S(1)} copy-done((bf16[1,1,256,128,128]{4,3,2,1,0:T(8,128)(2,1)S(1)}, bf16[1,1,256,128,128]{4,3,2,1,0:T(8,128)(2,1)}, u32[]{:S(2)}) %copy-start.1) | copy-done | bytes 8388632
  44.1 3.1 %direct.2 = (f32[8,256,128]{2,1,0:T(8,128)S(1)}, bf16[8,256,128]{2,1,0:T(8,128)(2,1)S(1)}) custom-call(s32[288]{0:T(512)S(1)} %broadcast_add_fusion.1.tab, s32[2]{0:T(128)S(1)} %pad_add_fusion.place, bf16[8,256,128]{2,1,0:T(8,128)(2,1)S(1)} %all-to-all-done.1.x_ref, bf16[256,128,128]{2,1,0:T(8,128)(2,1)S(1)} %bitcast.7), custom_call_target="tpu_custom_call" | custom-call | flops 1073741824 | bytes 8388608 | tf_op jit(solution)/shard_map/direct/pallas_call | solution.py:211
  47.1 0.0 all-to-all-done.2.got_ref
  47.1 1.9 %collective-permute-start.2 = (bf16[8,256,128]{2,1,0:T(8,128)(2,1)S(1)}, bf16[8,256,128]{2,1,0:T(8,128)(2,1)S(1)}, u32[]{:S(2)}, u32[]{:S(2)}) collective-permute-start(bf16[8,256,128]{2,1,0:T(8,128)(2,1)S(1)} %get-tuple-element.36), channel_id=1, source_target_pairs={{0,1},{1,0},{2,3},{3,2},{4,5},{5,4},{6,7},{7,6},{8,9},{9,8},{10,11... | collective-permute-start | bytes 1572872 | tf_op jit(solution)/shard_map/ppermute | solution.py:279
  49.0 1.5 %collective-permute-done.2.theirs_ref = bf16[8,256,128]{2,1,0:T(8,128)(2,1)S(1)} collective-permute-done((bf16[8,256,128]{2,1,0:T(8,128)(2,1)S(1)}, bf16[8,256,128]{2,1,0:T(8,128)(2,1)S(1)}, u32[]{:S(2)}, u32[]{:S(2)}) %collective-permute-start.2) | collective-permute-done | bytes 524320 | tf_op jit(solution)/shard_map/ppermute | solution.py:279
  50.6 0.9 both.2
  51.4 5.8 %all-to-all-start.3 = ((bf16[8,256,128]{2,1,0:T(8,128)(2,1)}), bf16[8,256,128]{2,1,0:T(8,128)(2,1)S(1)}, u32[]{:S(2)}, u32[]{:S(2)}) async-start(bf16[8,256,128]{2,1,0:T(8,128)(2,1)} %both.2), calls=%async_computation.3 | async-start | bytes 1048576 | tf_op jit(solution)/shard_map/all_to_all | solution.py:250
  57.2 0.1 gathered.2
  57.3 8.4 %collective-permute-start.3 = (bf16[2,128,128]{2,1,0:T(8,128)(2,1)S(1)}, bf16[2,128,128]{2,1,0:T(8,128)(2,1)S(1)}, u32[]{:S(2)}, u32[]{:S(2)}) collective-permute-start(bf16[2,128,128]{2,1,0:T(8,128)(2,1)S(1)} %gathered.2), channel_id=1, source_target_pairs={{0,0},{16,1},{32,2},{48,3},{64,4},{80,5},{96,6},{112,7},{65,8},{81... | collective-permute-start | bytes 196616 | tf_op jit(solution)/shard_map/ppermute | solution.py:283
  65.8 6.1 %collective-permute-done.3.sum_ref = bf16[2,128,128]{2,1,0:T(8,128)(2,1)S(1)} collective-permute-done((bf16[2,128,128]{2,1,0:T(8,128)(2,1)S(1)}, bf16[2,128,128]{2,1,0:T(8,128)(2,1)S(1)}, u32[]{:S(2)}, u32[]{:S(2)}) %collective-permute-start.3) | collective-permute-done | bytes 65568 | tf_op jit(solution)/shard_map/ppermute | solution.py:283
  71.9 0.1 turned.2.back_ref
  72.0 0.0 all-to-all-done.3.own_ref
  72.0 1.0 second.1
  73.0 3.5 %all-to-all-start.4 = ((bf16[8,2,128,128]{3,2,1,0:T(8,128)(2,1)}), bf16[8,2,128,128]{3,2,1,0:T(8,128)(2,1)S(1)}, u32[]{:S(2)}, u32[]{:S(2)}) async-start(bf16[8,2,128,128]{3,2,1,0:T(8,128)(2,1)} %get-tuple-element.39), calls=%async_computation.4 | async-start | bytes 1048576 | tf_op jit(solution)/shard_map/all_to_all | solution.py:250
  76.5 8.5 %collective-permute-start.4 = (bf16[256,128]{1,0:T(8,128)(2,1)S(1)}, bf16[256,128]{1,0:T(8,128)(2,1)S(1)}, u32[]{:S(2)}, u32[]{:S(2)}) collective-permute-start(bf16[256,128]{1,0:T(8,128)(2,1)S(1)} %get-tuple-element.38), channel_id=1, source_target_pairs={{0,0},{1,16},{2,32},{3,48},{4,64},{5,80},{6,96},{7,112},{8,65},{9,... | collective-permute-start | bytes 196616 | tf_op jit(solution)/shard_map/ppermute | solution.py:253
  85.1 2.0 %collective-permute-done.4 = bf16[256,128]{1,0:T(8,128)(2,1)S(1)} collective-permute-done((bf16[256,128]{1,0:T(8,128)(2,1)S(1)}, bf16[256,128]{1,0:T(8,128)(2,1)S(1)}, u32[]{:S(2)}, u32[]{:S(2)}) %collective-permute-start.4) | collective-permute-done | bytes 65568 | tf_op jit(solution)/shard_map/ppermute | solution.py:253
  87.0 0.6 all-to-all-done.4.x_ref
  87.7 0.7 collective-permute-start.5
  88.3 0.9 broadcast_in_dim.112
  89.2 4.3 %all-to-all-start.5 = ((bf16[8,256,128]{2,1,0:T(8,128)(2,1)}), bf16[8,256,128]{2,1,0:T(8,128)(2,1)S(1)}, u32[]{:S(2)}, u32[]{:S(2)}) async-start(bf16[8,256,128]{2,1,0:T(8,128)(2,1)} %broadcast_in_dim.112), calls=%async_computation.5 | async-start | bytes 1048576 | tf_op jit(solution)/shard_map/all_to_all | solution.py:250
  93.5 0.0 collective-permute-done.5.y_ref
  93.5 3.4 %copy-done.2 = bf16[1,1,256,128,128]{4,3,2,1,0:T(8,128)(2,1)S(1)} copy-done((bf16[1,1,256,128,128]{4,3,2,1,0:T(8,128)(2,1)S(1)}, bf16[1,1,256,128,128]{4,3,2,1,0:T(8,128)(2,1)}, u32[]{:S(2)}) %copy-start.2) | copy-done | bytes 8388632
  96.9 3.8 %mirror.3 = bf16[8,2,128,128]{3,2,1,0:T(8,128)(2,1)} custom-call(s32[272]{0:T(512)S(1)} %broadcast_add_fusion.tab, s32[2]{0:T(128)S(1)} %pad_add_fusion.place, bf16[8,2,128,128]{3,2,1,0:T(8,128)(2,1)S(1)} %all-to-all-done.4.x_ref, bf16[8,2,128,128]{3,2,1,0:T(8,128)(2,1)S(1)} %collective-permute-done.5.y_ref, bf16[256,128,128]{2,1,0:T(8,128)(2,1)S(1)} %bitcast.8), custom_call_target="tpu_custom_call" | custom-call | flops 1073741824 | bytes 8388608 | tf_op jit(solution)/shard_map/mirror/pallas_call | solution.py:211
  100.7 0.0 all-to-all-done.5.x_ref
  100.7 5.5 %all-to-all-start.6 = ((bf16[8,2,128,128]{3,2,1,0:T(8,128)(2,1)}), bf16[8,2,128,128]{3,2,1,0:T(8,128)(2,1)S(1)}, u32[]{:S(2)}, u32[]{:S(2)}) async-start(bf16[8,2,128,128]{3,2,1,0:T(8,128)(2,1)} %mirror.3), calls=%async_computation.6 | async-start | bytes 1048576 | tf_op jit(solution)/shard_map/all_to_all | solution.py:250
  106.3 3.4 %copy-done.3 = bf16[1,1,256,128,128]{4,3,2,1,0:T(8,128)(2,1)S(1)} copy-done((bf16[1,1,256,128,128]{4,3,2,1,0:T(8,128)(2,1)S(1)}, bf16[1,1,256,128,128]{4,3,2,1,0:T(8,128)(2,1)}, u32[]{:S(2)}) %copy-start.3) | copy-done | bytes 8388632
  109.7 3.1 %direct.3 = (f32[8,256,128]{2,1,0:T(8,128)S(1)}, bf16[8,256,128]{2,1,0:T(8,128)(2,1)S(1)}) custom-call(s32[288]{0:T(512)S(1)} %broadcast_add_fusion.1.tab, s32[2]{0:T(128)S(1)} %pad_add_fusion.place, bf16[8,256,128]{2,1,0:T(8,128)(2,1)S(1)} %all-to-all-done.5.x_ref, bf16[256,128,128]{2,1,0:T(8,128)(2,1)S(1)} %bitcast.9), custom_call_target="tpu_custom_call" | custom-call | flops 1073741824 | bytes 8388608 | tf_op jit(solution)/shard_map/direct/pallas_call | solution.py:211
  112.7 0.0 all-to-all-done.6.got_ref
  112.8 2.5 %collective-permute-start.6 = (bf16[8,256,128]{2,1,0:T(8,128)(2,1)S(1)}, bf16[8,256,128]{2,1,0:T(8,128)(2,1)S(1)}, u32[]{:S(2)}, u32[]{:S(2)}) collective-permute-start(bf16[8,256,128]{2,1,0:T(8,128)(2,1)S(1)} %get-tuple-element.46), channel_id=1, source_target_pairs={{0,1},{1,0},{2,3},{3,2},{4,5},{5,4},{6,7},{7,6},{8,9},{9,8},{10,11... | collective-permute-start | bytes 1572872 | tf_op jit(solution)/shard_map/ppermute | solution.py:279
  115.2 1.5 %collective-permute-done.6.theirs_ref = bf16[8,256,128]{2,1,0:T(8,128)(2,1)S(1)} collective-permute-done((bf16[8,256,128]{2,1,0:T(8,128)(2,1)S(1)}, bf16[8,256,128]{2,1,0:T(8,128)(2,1)S(1)}, u32[]{:S(2)}, u32[]{:S(2)}) %collective-permute-start.6) | collective-permute-done | bytes 524320 | tf_op jit(solution)/shard_map/ppermute | solution.py:279
  116.7 0.9 both.3
  117.6 7.1 %all-to-all-start.7 = ((bf16[8,256,128]{2,1,0:T(8,128)(2,1)}), bf16[8,256,128]{2,1,0:T(8,128)(2,1)S(1)}, u32[]{:S(2)}, u32[]{:S(2)}) async-start(bf16[8,256,128]{2,1,0:T(8,128)(2,1)} %both.3), calls=%async_computation.7 | async-start | bytes 1048576 | tf_op jit(solution)/shard_map/all_to_all | solution.py:250
  124.8 0.1 gathered.3
  124.8 8.4 %collective-permute-start.7 = (bf16[2,128,128]{2,1,0:T(8,128)(2,1)S(1)}, bf16[2,128,128]{2,1,0:T(8,128)(2,1)S(1)}, u32[]{:S(2)}, u32[]{:S(2)}) collective-permute-start(bf16[2,128,128]{2,1,0:T(8,128)(2,1)S(1)} %gathered.3), channel_id=1, source_target_pairs={{0,0},{16,1},{32,2},{48,3},{64,4},{80,5},{96,6},{112,7},{65,8},{81... | collective-permute-start | bytes 196616 | tf_op jit(solution)/shard_map/ppermute | solution.py:283
  133.3 6.2 %collective-permute-done.7.sum_ref = bf16[2,128,128]{2,1,0:T(8,128)(2,1)S(1)} collective-permute-done((bf16[2,128,128]{2,1,0:T(8,128)(2,1)S(1)}, bf16[2,128,128]{2,1,0:T(8,128)(2,1)S(1)}, u32[]{:S(2)}, u32[]{:S(2)}) %collective-permute-start.7) | collective-permute-done | bytes 65568 | tf_op jit(solution)/shard_map/ppermute | solution.py:283
  139.5 0.1 turned.3.back_ref
  139.6 0.0 all-to-all-done.7.own_ref
  139.6 0.8 last.1
  (23 shorter events, 0.1 us)
Async XLA Ops:
  1.9 18.6 %all-to-all-start = ((bf16[8,2,128,128]{3,2,1,0:T(8,128)(2,1)}), bf16[8,2,128,128]{3,2,1,0:T(8,128)(2,1)S(1)}, u32[]{:S(2)}, u32[]{:S(2)}) async-start(bf16[8,2,128,128]{3,2,1,0:T(8,128)(2,1)} %get-tuple-element.29), calls=%async_computation | async-start | bytes 1048576 | tf_op jit(solution)/shard_map/all_to_all | solution.py:250
  9.4 11.1 %collective-permute-start = (bf16[256,128]{1,0:T(8,128)(2,1)}, bf16[256,128]{1,0:T(8,128)(2,1)S(1)}, u32[]{:S(2)}, u32[]{:S(2)}) collective-permute-start(bf16[256,128]{1,0:T(8,128)(2,1)} %get-tuple-element.28), channel_id=1, source_target_pairs={{0,0},{1,16},{2,32},{3,48},{4,64},{5,80},{6,96},{7,112},{8,65},{9,... | collective-permute-start | bytes 196616 | tf_op jit(solution)/shard_map/ppermute | solution.py:253
  20.5 6.7 %collective-permute-start.1 = (bf16[8,2,128,128]{3,2,1,0:T(8,128)(2,1)S(1)}, bf16[8,2,128,128]{3,2,1,0:T(8,128)(2,1)S(1)}, u32[]{:S(2)}, u32[]{:S(2)}) collective-permute-start(bf16[8,2,128,128]{3,2,1,0:T(8,128)(2,1)S(1)} %all-to-all-done.x_ref), channel_id=1, source_target_pairs={{0,1},{1,0},{2,3},{3,2},{4,5},{5,4},{6,7},{7,6},{8,9},{9,8},{10,11... | collective-permute-start | bytes 1572872 | tf_op jit(solution)/shard_map/ppermute | solution.py:256
  22.8 12.1 %all-to-all-start.1 = ((bf16[8,256,128]{2,1,0:T(8,128)(2,1)}), bf16[8,256,128]{2,1,0:T(8,128)(2,1)S(1)}, u32[]{:S(2)}, u32[]{:S(2)}) async-start(bf16[8,256,128]{2,1,0:T(8,128)(2,1)} %broadcast_in_dim.104), calls=%async_computation.1 | async-start | bytes 1048576 | tf_op jit(solution)/shard_map/all_to_all | solution.py:250
  27.2 3.4 %copy-start = (bf16[1,1,256,128,128]{4,3,2,1,0:T(8,128)(2,1)S(1)}, bf16[1,1,256,128,128]{4,3,2,1,0:T(8,128)(2,1)}, u32[]{:S(2)}) copy-start(bf16[1,1,256,128,128]{4,3,2,1,0:T(8,128)(2,1)} %param.8) | copy-start | bytes 25165828
  34.5 37.6 %copy-start.4 = (f32[256,128]{1,0:T(8,128)S(1)}, f32[256,128]{1,0:T(8,128)}, u32[]{:S(2)}) copy-start(f32[256,128]{1,0:T(8,128)} %vectors_ref.5) | copy-start | bytes 393220
  34.5 37.6 %copy-start.5 = (f32[2,128,128]{2,1,0:T(8,128)S(1)}, f32[2,128,128]{2,1,0:T(8,128)}, u32[]{:S(2)}) copy-start(f32[2,128,128]{2,1,0:T(8,128)} %get-tuple-element.27.keep_ref) | copy-start | bytes 393220
  34.9 12.3 %all-to-all-start.2 = ((bf16[8,2,128,128]{3,2,1,0:T(8,128)(2,1)}), bf16[8,2,128,128]{3,2,1,0:T(8,128)(2,1)S(1)}, u32[]{:S(2)}, u32[]{:S(2)}) async-start(bf16[8,2,128,128]{3,2,1,0:T(8,128)(2,1)} %mirror.2), calls=%async_computation.2 | async-start | bytes 1048576 | tf_op jit(solution)/shard_map/all_to_all | solution.py:250
  40.7 3.4 %copy-start.1 = (bf16[1,1,256,128,128]{4,3,2,1,0:T(8,128)(2,1)S(1)}, bf16[1,1,256,128,128]{4,3,2,1,0:T(8,128)(2,1)}, u32[]{:S(2)}) copy-start(bf16[1,1,256,128,128]{4,3,2,1,0:T(8,128)(2,1)} %param.8) | copy-start | bytes 25165828
  47.1 3.4 %collective-permute-start.2 = (bf16[8,256,128]{2,1,0:T(8,128)(2,1)S(1)}, bf16[8,256,128]{2,1,0:T(8,128)(2,1)S(1)}, u32[]{:S(2)}, u32[]{:S(2)}) collective-permute-start(bf16[8,256,128]{2,1,0:T(8,128)(2,1)S(1)} %get-tuple-element.36), channel_id=1, source_target_pairs={{0,1},{1,0},{2,3},{3,2},{4,5},{5,4},{6,7},{7,6},{8,9},{9,8},{10,11... | collective-permute-start | bytes 1572872 | tf_op jit(solution)/shard_map/ppermute | solution.py:279
  51.4 20.6 %all-to-all-start.3 = ((bf16[8,256,128]{2,1,0:T(8,128)(2,1)}), bf16[8,256,128]{2,1,0:T(8,128)(2,1)S(1)}, u32[]{:S(2)}, u32[]{:S(2)}) async-start(bf16[8,256,128]{2,1,0:T(8,128)(2,1)} %both.2), calls=%async_computation.3 | async-start | bytes 1048576 | tf_op jit(solution)/shard_map/all_to_all | solution.py:250
  57.3 14.6 %collective-permute-start.3 = (bf16[2,128,128]{2,1,0:T(8,128)(2,1)S(1)}, bf16[2,128,128]{2,1,0:T(8,128)(2,1)S(1)}, u32[]{:S(2)}, u32[]{:S(2)}) collective-permute-start(bf16[2,128,128]{2,1,0:T(8,128)(2,1)S(1)} %gathered.2), channel_id=1, source_target_pairs={{0,0},{16,1},{32,2},{48,3},{64,4},{80,5},{96,6},{112,7},{65,8},{81... | collective-permute-start | bytes 196616 | tf_op jit(solution)/shard_map/ppermute | solution.py:283
  73.0 14.6 %all-to-all-start.4 = ((bf16[8,2,128,128]{3,2,1,0:T(8,128)(2,1)}), bf16[8,2,128,128]{3,2,1,0:T(8,128)(2,1)S(1)}, u32[]{:S(2)}, u32[]{:S(2)}) async-start(bf16[8,2,128,128]{3,2,1,0:T(8,128)(2,1)} %get-tuple-element.39), calls=%async_computation.4 | async-start | bytes 1048576 | tf_op jit(solution)/shard_map/all_to_all | solution.py:250
  76.5 10.5 %collective-permute-start.4 = (bf16[256,128]{1,0:T(8,128)(2,1)S(1)}, bf16[256,128]{1,0:T(8,128)(2,1)S(1)}, u32[]{:S(2)}, u32[]{:S(2)}) collective-permute-start(bf16[256,128]{1,0:T(8,128)(2,1)S(1)} %get-tuple-element.38), channel_id=1, source_target_pairs={{0,0},{1,16},{2,32},{3,48},{4,64},{5,80},{6,96},{7,112},{8,65},{9,... | collective-permute-start | bytes 196616 | tf_op jit(solution)/shard_map/ppermute | solution.py:253
  87.7 5.8 %collective-permute-start.5 = (bf16[8,2,128,128]{3,2,1,0:T(8,128)(2,1)S(1)}, bf16[8,2,128,128]{3,2,1,0:T(8,128)(2,1)S(1)}, u32[]{:S(2)}, u32[]{:S(2)}) collective-permute-start(bf16[8,2,128,128]{3,2,1,0:T(8,128)(2,1)S(1)} %all-to-all-done.4.x_ref), channel_id=1, source_target_pairs={{0,1},{1,0},{2,3},{3,2},{4,5},{5,4},{6,7},{7,6},{8,9},{9,8},{10,11... | collective-permute-start | bytes 1572872 | tf_op jit(solution)/shard_map/ppermute | solution.py:256
  89.2 11.6 %all-to-all-start.5 = ((bf16[8,256,128]{2,1,0:T(8,128)(2,1)}), bf16[8,256,128]{2,1,0:T(8,128)(2,1)S(1)}, u32[]{:S(2)}, u32[]{:S(2)}) async-start(bf16[8,256,128]{2,1,0:T(8,128)(2,1)} %broadcast_in_dim.112), calls=%async_computation.5 | async-start | bytes 1048576 | tf_op jit(solution)/shard_map/all_to_all | solution.py:250
  93.5 3.4 %copy-start.2 = (bf16[1,1,256,128,128]{4,3,2,1,0:T(8,128)(2,1)S(1)}, bf16[1,1,256,128,128]{4,3,2,1,0:T(8,128)(2,1)}, u32[]{:S(2)}) copy-start(bf16[1,1,256,128,128]{4,3,2,1,0:T(8,128)(2,1)} %param.8) | copy-start | bytes 25165828
  100.7 12.0 %all-to-all-start.6 = ((bf16[8,2,128,128]{3,2,1,0:T(8,128)(2,1)}), bf16[8,2,128,128]{3,2,1,0:T(8,128)(2,1)S(1)}, u32[]{:S(2)}, u32[]{:S(2)}) async-start(bf16[8,2,128,128]{3,2,1,0:T(8,128)(2,1)} %mirror.3), calls=%async_computation.6 | async-start | bytes 1048576 | tf_op jit(solution)/shard_map/all_to_all | solution.py:250
  106.3 3.4 %copy-start.3 = (bf16[1,1,256,128,128]{4,3,2,1,0:T(8,128)(2,1)S(1)}, bf16[1,1,256,128,128]{4,3,2,1,0:T(8,128)(2,1)}, u32[]{:S(2)}) copy-start(bf16[1,1,256,128,128]{4,3,2,1,0:T(8,128)(2,1)} %param.8) | copy-start | bytes 25165828
  112.8 4.0 %collective-permute-start.6 = (bf16[8,256,128]{2,1,0:T(8,128)(2,1)S(1)}, bf16[8,256,128]{2,1,0:T(8,128)(2,1)S(1)}, u32[]{:S(2)}, u32[]{:S(2)}) collective-permute-start(bf16[8,256,128]{2,1,0:T(8,128)(2,1)S(1)} %get-tuple-element.46), channel_id=1, source_target_pairs={{0,1},{1,0},{2,3},{3,2},{4,5},{5,4},{6,7},{7,6},{8,9},{9,8},{10,11... | collective-permute-start | bytes 1572872 | tf_op jit(solution)/shard_map/ppermute | solution.py:279
  117.6 22.0 %all-to-all-start.7 = ((bf16[8,256,128]{2,1,0:T(8,128)(2,1)}), bf16[8,256,128]{2,1,0:T(8,128)(2,1)S(1)}, u32[]{:S(2)}, u32[]{:S(2)}) async-start(bf16[8,256,128]{2,1,0:T(8,128)(2,1)} %both.3), calls=%async_computation.7 | async-start | bytes 1048576 | tf_op jit(solution)/shard_map/all_to_all | solution.py:250
  124.8 14.7 %collective-permute-start.7 = (bf16[2,128,128]{2,1,0:T(8,128)(2,1)S(1)}, bf16[2,128,128]{2,1,0:T(8,128)(2,1)S(1)}, u32[]{:S(2)}, u32[]{:S(2)}) collective-permute-start(bf16[2,128,128]{2,1,0:T(8,128)(2,1)S(1)} %gathered.3), channel_id=1, source_target_pairs={{0,0},{16,1},{32,2},{48,3},{64,4},{80,5},{96,6},{112,7},{65,8},{81... | collective-permute-start | bytes 196616 | tf_op jit(solution)/shard_map/ppermute | solution.py:283
